TPU v7x, 32 devices: a whole 2x2x4 slice. The times are simulated.
32 devices in a mesh: seq: 8 (over z, y), fsdp: 4 (over x, core).
Axes of the slice: x: 2, y: 2, z: 4, core: 2. Of those that a mesh axis runs over, the one named last changes fastest.
Arguments:
- layer_in: bfloat16 [4, 1024, 1536], P('fsdp', 'seq'), may hold values from -6 to 6
- cotangent: bfloat16 [4, 1024, 1536], P('fsdp', 'seq'), may hold values from -6 to 6
- doc_starts: int32 [4, 4], P('fsdp'), may hold values from 0 to 1023, as said below
- routes: int32 [4, 1024, 8], P('fsdp', 'seq'), may hold values from 0 to 23, all different within a row; in each aligned block of 128 rows (0 to 127, 128 to 255, ..., all dimensions but the last counted through in order) at most 57 rows name the same one
- attn_gain: bfloat16 [2, 1536], P(None, ('seq', 'fsdp')), may hold values from 0.5 to 1.5
- ffn_gain: bfloat16 [2, 1536], P(None, ('seq', 'fsdp')), may hold values from 0.5 to 1.5
- query_weight: bfloat16 [2, 1536, 1536], P(None, ('seq', 'fsdp')), may hold values from -0.15625 to 0.15625
- key_matrix: bfloat16 [2, 1536, 512], P(None, ('seq', 'fsdp')), may hold values from -0.15625 to 0.15625
- value_matrix: bfloat16 [2, 1536, 512], P(None, ('seq', 'fsdp')), may hold values from -0.15625 to 0.15625
- out_weight: bfloat16 [2, 1536, 1536], P(None, ('seq', 'fsdp')), may hold values from -0.875 to 0.875
- router_weight: bfloat16 [2, 1536, 24], P(None, ('seq', 'fsdp')), may hold values from -0.078125 to 0.078125
- gate_weight: bfloat16 [2, 24, 1536, 512], P(None, 'seq', 'fsdp'), may hold values from -0.15625 to 0.15625
- up_weight: bfloat16 [2, 24, 1536, 512], P(None, 'seq', 'fsdp'), may hold values from -0.15625 to 0.15625
- down_weight: bfloat16 [2, 24, 512, 1536], P(None, 'seq', None, 'fsdp'), may hold values from -1 to 1
Outputs:
- layer_out: bfloat16 [4, 1024, 1536], P('fsdp', 'seq')
- input_grad: float32 [4, 1024, 1536], P('fsdp', 'seq')
- attn_gain_grad: float32 [2, 1536], P(None, ('seq', 'fsdp'))
- ffn_gain_grad: float32 [2, 1536], P(None, ('seq', 'fsdp'))
- query_grad: float32 [2, 1536, 1536], P(None, ('seq', 'fsdp'))
- key_grad: float32 [2, 1536, 512], P(None, ('seq', 'fsdp'))
- value_grad: float32 [2, 1536, 512], P(None, ('seq', 'fsdp'))
- out_grad: float32 [2, 1536, 1536], P(None, ('seq', 'fsdp'))
- router_grad: float32 [2, 1536, 24], P(None, ('seq', 'fsdp'))
- gate_grad: float32 [2, 24, 1536, 512], P(None, 'seq', 'fsdp')
- up_grad: float32 [2, 24, 1536, 512], P(None, 'seq', 'fsdp')
- down_grad: float32 [2, 24, 512, 1536], P(None, 'seq', None, 'fsdp')
Inputs may be any that keep to these rules, and one draw needn't show every extreme that they name: `doc_starts`: in each stream the 4 starts rise strictly and the first is 0; a document runs from its start to the next start, the last one to the end of the stream, and may be a single position. `routes`: the 8 experts of a position are distinct; among the 128 positions of a stream that one device holds (aligned blocks) no expert is named more than 57 times.
All inputs are finite; a program needn't handle non-finite values.
Results may differ from a plain program's by a relative error of at most 0.025.
Values may be sent and summed in bfloat16 or wider, within the bound.
A program may use at most 384 MiB of HBM per device.

v0:
```python
import math

import jax
import jax.numpy as jnp
from jax import lax
from jax.sharding import PartitionSpec as P

HEAD_SIZE = 64


EPSILON = 1e-05
HIGHEST = lax.Precision.HIGHEST


def norm_factor(stream):
    return lax.rsqrt(jnp.mean(stream * stream, axis=-1, keepdims=True) + EPSILON)


def norm_back(stream, factor, gain_row, upstream):
    scaled = gain_row * upstream
    inner_mean = jnp.mean(stream * scaled, axis=-1, keepdims=True)
    return factor * scaled - stream * (factor * factor * factor) * inner_mean


def rotation_apply(source, token_positions, head_count, head_size, sign_factor):
    half_size = head_size // 2
    inverse = 10000.0 ** (-2.0 * jnp.arange(half_size, dtype=jnp.float32) / head_size)
    angle_table = token_positions.astype(jnp.float32)[:, None] * inverse[None, :]
    cosine = jnp.cos(angle_table)[:, None, :]
    sine_part = sign_factor * jnp.sin(angle_table)[:, None, :]
    shaped = source.reshape(source.shape[:-1] + (head_count, head_size))
    first_half = shaped[..., :half_size]
    second = shaped[..., half_size:]
    turned = jnp.concatenate(
        [first_half * cosine - second * sine_part, second * cosine + first_half * sine_part],
        axis=-1,
    )
    return turned.reshape(source.shape)


def fetch_layer(shards, layer_id):
    dense = (
        lax.all_gather(shards[0][layer_id], ("seq", "fsdp"), axis=0, tiled=True),
        lax.all_gather(shards[1][layer_id], ("seq", "fsdp"), axis=0, tiled=True),
        lax.all_gather(shards[2][layer_id], ("seq", "fsdp"), axis=0, tiled=True),
        lax.all_gather(shards[3][layer_id], ("seq", "fsdp"), axis=0, tiled=True),
        lax.all_gather(shards[4][layer_id], ("seq", "fsdp"), axis=0, tiled=True),
        lax.all_gather(shards[5][layer_id], ("seq", "fsdp"), axis=0, tiled=True),
        lax.all_gather(shards[6][layer_id], ("seq", "fsdp"), axis=0, tiled=True),
    )
    experts = (
        lax.all_gather(shards[7][layer_id], "fsdp", axis=1, tiled=True),
        lax.all_gather(shards[8][layer_id], "fsdp", axis=1, tiled=True),
        lax.all_gather(shards[9][layer_id], "fsdp", axis=2, tiled=True),
    )
    return tuple(dense) + tuple(experts)


def dispatch_tables(chosen, experts_all, local_count, seq_count, capacity):
    token_count, top_count = chosen.shape
    flat_routes = chosen.reshape(-1)
    onehot = (flat_routes[:, None] == jnp.arange(experts_all, dtype=jnp.int32)[None, :]).astype(
        jnp.int32
    )
    slot_ids = jnp.sum((jnp.cumsum(onehot, axis=0) - onehot) * onehot, axis=1)
    places = (
        flat_routes % local_count * seq_count + flat_routes // local_count
    ) * capacity + slot_ids
    entries = (
        jnp.full((experts_all * capacity,), token_count * top_count, jnp.int32)
        .at[places]
        .set(jnp.arange(token_count * top_count, dtype=jnp.int32))
    )
    return (places, entries)


def block_layout(query_side, pair_side):
    seq_length = query_side.shape[0]
    kv_heads = pair_side.shape[1] // (2 * HEAD_SIZE)
    query_group_width = query_side.shape[1] // (kv_heads * HEAD_SIZE)
    block_rows = min(512, seq_length)
    block_count = seq_length // block_rows
    pair_rows = pair_side.reshape(seq_length, kv_heads, 2, HEAD_SIZE)
    return (
        seq_length,
        kv_heads,
        query_group_width,
        block_rows,
        block_count,
        pair_rows[:, :, 0],
        pair_rows[:, :, 1],
    )


def masked_scores(block_index, query_rows, keys_part, documents, block_rows):
    key_count = keys_part.shape[0]
    row_start = block_index * block_rows
    row_ids = row_start + jnp.arange(block_rows, dtype=jnp.int32)
    row_docs = documents[row_start : row_start + block_rows]
    key_positions = jnp.arange(key_count, dtype=jnp.int32)
    allowed = (row_docs[:, None] == documents[None, :key_count]) & (
        key_positions[None, :] <= row_ids[:, None]
    )
    scores = jnp.einsum(
        "qhgd,khd->hgqk", query_rows, keys_part, preferred_element_type=jnp.float32
    ) * (1.0 / math.sqrt(HEAD_SIZE))
    return jnp.where(allowed[None, None], scores, -1e30)


def attention_forward(query_side, pair_side, documents):
    (
        seq_length,
        kv_heads,
        query_group_width,
        block_rows,
        block_count,
        key_token_rows,
        value_token_rows,
    ) = block_layout(query_side, pair_side)
    blocked = query_side.reshape(block_count, block_rows, kv_heads, query_group_width, HEAD_SIZE)
    mixed_list = []
    log_list = []
    for block_index in range(block_count):
        key_end = (block_index + 1) * block_rows
        scores = masked_scores(
            block_index, blocked[block_index], key_token_rows[:key_end], documents, block_rows
        )
        highest = jnp.max(scores, axis=-1, keepdims=True)
        weights = jnp.exp(scores - highest)
        totals = jnp.sum(weights, axis=-1, keepdims=True)
        probs_low = (weights / totals).astype(jnp.bfloat16)
        mixed_rows = jnp.einsum(
            "hgqk,khd->qhgd",
            probs_low,
            value_token_rows[:key_end],
            preferred_element_type=jnp.float32,
        )
        mixed_list.append(mixed_rows.astype(jnp.bfloat16).reshape(block_rows, -1))
        log_list.append((highest + jnp.log(totals))[..., 0])
    return (jnp.concatenate(mixed_list, axis=0), log_list)


def attention_backward(query_side, pair_side, documents, log_totals, heads_grad):
    (
        seq_length,
        kv_heads,
        query_group_width,
        block_rows,
        block_count,
        key_token_rows,
        value_token_rows,
    ) = block_layout(query_side, pair_side)
    score_scale = 1.0 / math.sqrt(HEAD_SIZE)
    blocked = query_side.reshape(block_count, block_rows, kv_heads, query_group_width, HEAD_SIZE)
    grads_blocked = heads_grad.reshape(
        block_count, block_rows, kv_heads, query_group_width, HEAD_SIZE
    )
    key_sum = jnp.zeros((seq_length, kv_heads, HEAD_SIZE), jnp.float32)
    value_sum = jnp.zeros((seq_length, kv_heads, HEAD_SIZE), jnp.float32)
    query_list = []
    for block_index in range(block_count):
        key_end = (block_index + 1) * block_rows
        query_rows = blocked[block_index]
        upstream = grads_blocked[block_index]
        keys_part = key_token_rows[:key_end]
        values_part = value_token_rows[:key_end]
        scores = masked_scores(block_index, query_rows, keys_part, documents, block_rows)
        probs = jnp.exp(scores - log_totals[block_index][..., None])
        probs_low = probs.astype(jnp.bfloat16)
        prob_grad = jnp.einsum(
            "qhgd,khd->hgqk", upstream, values_part, preferred_element_type=jnp.float32
        )
        centre = jnp.sum(probs * prob_grad, axis=-1, keepdims=True)
        score_grad = (probs * (prob_grad - centre)).astype(jnp.bfloat16)
        query_part = (
            jnp.einsum("hgqk,khd->qhgd", score_grad, keys_part, preferred_element_type=jnp.float32)
            * score_scale
        )
        key_sum = key_sum.at[:key_end].add(
            jnp.einsum("hgqk,qhgd->khd", score_grad, query_rows, preferred_element_type=jnp.float32)
            * score_scale
        )
        value_sum = value_sum.at[:key_end].add(
            jnp.einsum("hgqk,qhgd->khd", probs_low, upstream, preferred_element_type=jnp.float32)
        )
        query_list.append(query_part.astype(jnp.bfloat16).reshape(block_rows, -1))
    pair_grad = (
        jnp.concatenate([key_sum, value_sum], axis=2).astype(jnp.bfloat16).reshape(seq_length, -1)
    )
    return (jnp.concatenate(query_list, axis=0), pair_grad)


def expert_capacity(token_count, top_count, experts_all):
    return token_count * top_count * 4 // (3 * experts_all) + 1


def forward_layer(stream, params, context):
    (
        attn_gain,
        ffn_gain,
        query_weight,
        key_matrix,
        value_matrix,
        out_weight,
        router_weight,
        gate_weight,
        up_weight,
        down_weight,
    ) = params
    token_positions, documents, chosen, seq_count = context
    token_count, top_count = chosen.shape
    query_heads = query_weight.shape[1] // HEAD_SIZE
    kv_heads = key_matrix.shape[1] // HEAD_SIZE
    local_count = gate_weight.shape[0]
    experts_all = router_weight.shape[1]
    capacity = expert_capacity(token_count, top_count, experts_all)
    factor_one = norm_factor(stream)
    normed_one = (stream * factor_one * attn_gain.astype(jnp.float32)).astype(jnp.bfloat16)
    query_raw = jnp.dot(normed_one, query_weight, preferred_element_type=jnp.float32)
    key_unrotated = jnp.dot(normed_one, key_matrix, preferred_element_type=jnp.float32)
    value_low = jnp.dot(normed_one, value_matrix, preferred_element_type=jnp.float32).astype(
        jnp.bfloat16
    )
    query_low = rotation_apply(query_raw, token_positions, query_heads, HEAD_SIZE, 1.0).astype(
        jnp.bfloat16
    )
    key_low = rotation_apply(key_unrotated, token_positions, kv_heads, HEAD_SIZE, 1.0).astype(
        jnp.bfloat16
    )
    paired = jnp.concatenate(
        [
            key_low.reshape(token_count, kv_heads, HEAD_SIZE),
            value_low.reshape(token_count, kv_heads, HEAD_SIZE),
        ],
        axis=2,
    ).reshape(token_count, kv_heads * 2 * HEAD_SIZE)
    query_side, pair_side = (
        lax.all_to_all(query_low, "seq", split_axis=1, concat_axis=0, tiled=True),
        lax.all_to_all(paired, "seq", split_axis=1, concat_axis=0, tiled=True),
    )
    mixed_heads, log_totals = attention_forward(query_side, pair_side, documents)
    mixed_tokens = lax.all_to_all(mixed_heads, "seq", split_axis=0, concat_axis=1, tiled=True)
    middle = stream + jnp.dot(mixed_tokens, out_weight, preferred_element_type=jnp.float32)
    factor_two = norm_factor(middle)
    normed_two = (middle * factor_two * ffn_gain.astype(jnp.float32)).astype(jnp.bfloat16)
    logits = jnp.dot(normed_two, router_weight, preferred_element_type=jnp.float32)
    route_mask = (
        chosen[:, :, None] == jnp.arange(experts_all, dtype=jnp.int32)[None, None, :]
    ).astype(jnp.float32)
    selected = jnp.sum(route_mask * logits[:, None, :], axis=2)
    highest = jnp.max(selected, axis=-1, keepdims=True)
    weights = jnp.exp(selected - highest)
    gate_probs = weights / jnp.sum(weights, axis=-1, keepdims=True)
    places, entries = dispatch_tables(chosen, experts_all, local_count, seq_count, capacity)
    padded = jnp.concatenate(
        [normed_two, jnp.zeros((1, normed_two.shape[1]), jnp.bfloat16)], axis=0
    )
    sending = padded[entries // top_count].reshape(local_count, seq_count, capacity, -1)
    arrived = lax.all_to_all(sending, "seq", split_axis=1, concat_axis=1, tiled=True)
    expert_rows = arrived.reshape(local_count, seq_count * capacity, -1)
    gate_part = jnp.einsum(
        "erd,edf->erf", expert_rows, gate_weight, preferred_element_type=jnp.float32
    )
    up_part = jnp.einsum("erd,edf->erf", expert_rows, up_weight, preferred_element_type=jnp.float32)
    hidden = (gate_part * jax.nn.sigmoid(gate_part) * up_part).astype(jnp.bfloat16)
    produced = jnp.einsum(
        "erf,efd->erd", hidden, down_weight, preferred_element_type=jnp.float32
    ).astype(jnp.bfloat16)
    returned = lax.all_to_all(
        produced.reshape(local_count, seq_count, capacity, -1),
        "seq",
        split_axis=1,
        concat_axis=1,
        tiled=True,
    )
    picked = returned.reshape(experts_all * capacity, -1)[places].reshape(
        token_count, top_count, -1
    )
    following = middle + jnp.sum(gate_probs[:, :, None] * picked, axis=1)
    saved_state = (
        stream,
        factor_one,
        normed_one,
        query_side,
        pair_side,
        log_totals,
        mixed_tokens,
        middle,
        factor_two,
        normed_two,
        route_mask,
        gate_probs,
        places,
        entries,
        picked,
        expert_rows,
        gate_part,
        up_part,
        hidden,
    )
    return (saved_state, following)


def backward_layer(upstream, params, saved_state, context):
    (
        attn_gain,
        ffn_gain,
        query_weight,
        key_matrix,
        value_matrix,
        out_weight,
        router_weight,
        gate_weight,
        up_weight,
        down_weight,
    ) = params
    (
        stream,
        factor_one,
        normed_one,
        query_side,
        pair_side,
        log_totals,
        mixed_tokens,
        middle,
        factor_two,
        normed_two,
        route_mask,
        gate_probs,
        places,
        entries,
        picked,
        expert_rows,
        gate_part,
        up_part,
        hidden,
    ) = saved_state
    token_positions, documents, chosen, seq_count = context
    token_count, top_count = chosen.shape
    query_heads = query_weight.shape[1] // HEAD_SIZE
    kv_heads = key_matrix.shape[1] // HEAD_SIZE
    local_count = gate_weight.shape[0]
    experts_all = router_weight.shape[1]
    capacity = expert_capacity(token_count, top_count, experts_all)
    gate_dot = jnp.sum(upstream[:, None, :] * picked, axis=2)
    select_grad = gate_probs * (gate_dot - jnp.sum(gate_probs * gate_dot, axis=1, keepdims=True))
    logit_grad = jnp.sum(route_mask * select_grad[:, :, None], axis=1)
    router_term = jnp.einsum(
        "td,te->de", normed_two.astype(jnp.float32), logit_grad, precision=HIGHEST
    )
    normed_two_grad = jnp.einsum(
        "te,de->td", logit_grad, router_weight.astype(jnp.float32), precision=HIGHEST
    )
    gate_padded = jnp.concatenate([gate_probs.reshape(-1), jnp.zeros((1,), jnp.float32)])
    upstream_padded = jnp.concatenate(
        [upstream, jnp.zeros((1, upstream.shape[1]), jnp.float32)], axis=0
    )
    output_grad = (gate_padded[entries][:, None] * upstream_padded[entries // top_count]).astype(
        jnp.bfloat16
    )
    arriving = lax.all_to_all(
        output_grad.reshape(local_count, seq_count, capacity, -1),
        "seq",
        split_axis=1,
        concat_axis=1,
        tiled=True,
    )
    arriving = arriving.reshape(local_count, seq_count * capacity, -1)
    hidden_grad = jnp.einsum(
        "erd,efd->erf", arriving, down_weight, preferred_element_type=jnp.float32
    )
    down_term = jnp.einsum("erf,erd->efd", hidden, arriving, preferred_element_type=jnp.float32)
    logistic = jax.nn.sigmoid(gate_part)
    gate_low = (hidden_grad * up_part * logistic * (1.0 + gate_part * (1.0 - logistic))).astype(
        jnp.bfloat16
    )
    up_low = (hidden_grad * gate_part * logistic).astype(jnp.bfloat16)
    gate_term = jnp.einsum(
        "erd,erf->edf", expert_rows, gate_low, preferred_element_type=jnp.float32
    )
    up_term = jnp.einsum("erd,erf->edf", expert_rows, up_low, preferred_element_type=jnp.float32)
    rows_grad = jnp.einsum(
        "erf,edf->erd", gate_low, gate_weight, preferred_element_type=jnp.float32
    )
    rows_grad = (
        rows_grad
        + jnp.einsum("erf,edf->erd", up_low, up_weight, preferred_element_type=jnp.float32)
    ).astype(jnp.bfloat16)
    leaving = lax.all_to_all(
        rows_grad.reshape(local_count, seq_count, capacity, -1),
        "seq",
        split_axis=1,
        concat_axis=1,
        tiled=True,
    )
    gathered_grad = leaving.reshape(experts_all * capacity, -1)[places].reshape(
        token_count, top_count, -1
    )
    normed_two_grad = normed_two_grad + jnp.sum(gathered_grad.astype(jnp.float32), axis=1)
    ffn_gain_term = jnp.sum(normed_two_grad * middle * factor_two, axis=0)
    middle_grad = upstream + norm_back(
        middle, factor_two, ffn_gain.astype(jnp.float32), normed_two_grad
    )
    branch_low = middle_grad.astype(jnp.bfloat16)
    out_term = jnp.einsum("tc,td->cd", mixed_tokens, branch_low, preferred_element_type=jnp.float32)
    mixed_grad = jnp.einsum(
        "td,cd->tc", branch_low, out_weight, preferred_element_type=jnp.float32
    ).astype(jnp.bfloat16)
    heads_grad = lax.all_to_all(mixed_grad, "seq", split_axis=1, concat_axis=0, tiled=True)
    query_heads_grad, pair_heads_grad = attention_backward(
        query_side, pair_side, documents, log_totals, heads_grad
    )
    query_tokens, pair_tokens = (
        lax.all_to_all(query_heads_grad, "seq", split_axis=0, concat_axis=1, tiled=True),
        lax.all_to_all(pair_heads_grad, "seq", split_axis=0, concat_axis=1, tiled=True),
    )
    pair_rows = pair_tokens.reshape(token_count, kv_heads, 2, HEAD_SIZE)
    key_turned = pair_rows[:, :, 0].reshape(token_count, -1)
    value_low = pair_rows[:, :, 1].reshape(token_count, -1)
    query_low = rotation_apply(
        query_tokens.astype(jnp.float32), token_positions, query_heads, HEAD_SIZE, -1.0
    ).astype(jnp.bfloat16)
    key_low = rotation_apply(
        key_turned.astype(jnp.float32), token_positions, kv_heads, HEAD_SIZE, -1.0
    ).astype(jnp.bfloat16)
    query_term = jnp.einsum("td,tc->dc", normed_one, query_low, preferred_element_type=jnp.float32)
    key_term = jnp.einsum("td,tc->dc", normed_one, key_low, preferred_element_type=jnp.float32)
    value_term = jnp.einsum("td,tc->dc", normed_one, value_low, preferred_element_type=jnp.float32)
    normed_one_grad = jnp.einsum(
        "tc,dc->td", query_low, query_weight, preferred_element_type=jnp.float32
    )
    normed_one_grad = normed_one_grad + jnp.einsum(
        "tc,dc->td", key_low, key_matrix, preferred_element_type=jnp.float32
    )
    normed_one_grad = normed_one_grad + jnp.einsum(
        "tc,dc->td", value_low, value_matrix, preferred_element_type=jnp.float32
    )
    attn_gain_term = jnp.sum(normed_one_grad * stream * factor_one, axis=0)
    stream_grad = middle_grad + norm_back(
        stream, factor_one, attn_gain.astype(jnp.float32), normed_one_grad
    )
    dense_terms = (
        attn_gain_term,
        ffn_gain_term,
        query_term,
        key_term,
        value_term,
        out_term,
        router_term,
    )
    expert_terms = (gate_term, up_term, down_term)
    return (stream_grad, dense_terms, expert_terms)


def per_device(
    layer_in,
    cotangent,
    doc_starts,
    routes,
    attn_gain,
    ffn_gain,
    query_weight,
    key_matrix,
    value_matrix,
    out_weight,
    router_weight,
    gate_weight,
    up_weight,
    down_weight,
):
    seq_count = lax.axis_size("seq")
    seq_index = lax.axis_index("seq")
    token_count = layer_in.shape[1]
    seq_length = token_count * seq_count
    token_positions = seq_index * token_count + jnp.arange(token_count, dtype=jnp.int32)
    all_positions = jnp.arange(seq_length, dtype=jnp.int32)
    documents = (
        jnp.sum((doc_starts[0][None, :] <= all_positions[:, None]).astype(jnp.int32), axis=1) - 1
    )
    context = (token_positions, documents, routes[0], seq_count)
    shards = (
        attn_gain,
        ffn_gain,
        query_weight,
        key_matrix,
        value_matrix,
        out_weight,
        router_weight,
        gate_weight,
        up_weight,
        down_weight,
    )
    layer_count = attn_gain.shape[0]
    stream = layer_in[0].astype(jnp.float32)
    inputs_kept = []
    states = []
    params = None
    for layer_id in range(layer_count):
        params = fetch_layer(shards, layer_id)
        inputs_kept.append(stream)
        saved_state, stream = forward_layer(stream, params, context)
        states.append(saved_state)
    result = stream.astype(jnp.bfloat16)[None]
    upstream = cotangent[0].astype(jnp.float32)
    dense_out = [None] * layer_count
    expert_out = [None] * layer_count
    for layer_id in reversed(range(layer_count)):
        params = fetch_layer(shards, layer_id)
        saved_state = states[layer_id]
        upstream, dense_terms, expert_terms = backward_layer(upstream, params, saved_state, context)
        dense_out[layer_id] = (
            lax.psum_scatter(dense_terms[0], ("seq", "fsdp"), scatter_dimension=0, tiled=True),
            lax.psum_scatter(dense_terms[1], ("seq", "fsdp"), scatter_dimension=0, tiled=True),
            lax.psum_scatter(dense_terms[2], ("seq", "fsdp"), scatter_dimension=0, tiled=True),
            lax.psum_scatter(dense_terms[3], ("seq", "fsdp"), scatter_dimension=0, tiled=True),
            lax.psum_scatter(dense_terms[4], ("seq", "fsdp"), scatter_dimension=0, tiled=True),
            lax.psum_scatter(dense_terms[5], ("seq", "fsdp"), scatter_dimension=0, tiled=True),
            lax.psum_scatter(dense_terms[6], ("seq", "fsdp"), scatter_dimension=0, tiled=True),
        )
        expert_out[layer_id] = (
            lax.psum_scatter(
                expert_terms[0].astype(jnp.bfloat16), "fsdp", scatter_dimension=1, tiled=True
            ).astype(jnp.float32),
            lax.psum_scatter(
                expert_terms[1].astype(jnp.bfloat16), "fsdp", scatter_dimension=1, tiled=True
            ).astype(jnp.float32),
            lax.psum_scatter(
                expert_terms[2].astype(jnp.bfloat16), "fsdp", scatter_dimension=2, tiled=True
            ).astype(jnp.float32),
        )
    dense_stacked = [
        jnp.stack([dense_out[layer_id][position] for layer_id in range(layer_count)])
        for position in range(7)
    ]
    expert_stacked = [
        jnp.stack([expert_out[layer_id][position] for layer_id in range(layer_count)])
        for position in range(3)
    ]
    return (
        result,
        upstream[None],
        dense_stacked[0],
        dense_stacked[1],
        dense_stacked[2],
        dense_stacked[3],
        dense_stacked[4],
        dense_stacked[5],
        dense_stacked[6],
        expert_stacked[0],
        expert_stacked[1],
        expert_stacked[2],
    )


def solution(mesh):
    return jax.shard_map(
        per_device,
        mesh=mesh,
        in_specs=(
            P("fsdp", "seq", None),
            P("fsdp", "seq", None),
            P("fsdp", None),
            P("fsdp", "seq", None),
            P(None, ("seq", "fsdp")),
            P(None, ("seq", "fsdp")),
            P(None, ("seq", "fsdp"), None),
            P(None, ("seq", "fsdp"), None),
            P(None, ("seq", "fsdp"), None),
            P(None, ("seq", "fsdp"), None),
            P(None, ("seq", "fsdp"), None),
            P(None, "seq", "fsdp", None),
            P(None, "seq", "fsdp", None),
            P(None, "seq", None, "fsdp"),
        ),
        out_specs=(
            P("fsdp", "seq", None),
            P("fsdp", "seq", None),
            P(None, ("seq", "fsdp")),
            P(None, ("seq", "fsdp")),
            P(None, ("seq", "fsdp"), None),
            P(None, ("seq", "fsdp"), None),
            P(None, ("seq", "fsdp"), None),
            P(None, ("seq", "fsdp"), None),
            P(None, ("seq", "fsdp"), None),
            P(None, "seq", "fsdp", None),
            P(None, "seq", "fsdp", None),
            P(None, "seq", None, "fsdp"),
        ),
        check_vma=False,
    )
```

profile of v0, /device:TPU:9, one launch (start us, length us, event | category | flops | bytes accessed | tf_op | source)
XLA Modules:
  0.0 2829.7 jit_solution(9956031070566437901)
XLA Ops:
  25.1 40.7 %all-reduce.17 = (bf16[1536]{0:T(1024)(128)(2,1)S(1)}, bf16[1536]{0:T(1024)(128)(2,1)S(1)}, bf16[1536]{0:T(1024)(128)(2,1)S(1)}, bf16[1536]{0:T(1024)(128)(2,1)S(1)}) all-reduce(bf16[1536]{0:T(1024)(128)(2,1)S(1)} %dynamic-update-slice.20, bf16[1536]{0:T(1024)(128)(2,1)S(1)} %dynamic-update-slice.21, ...), channel_id=2, replica_groups=mesh['seq'=8,'fsdp'=4] {'seq','fsdp'}, use_global_device_ids=true, to_apply=%add.8 | all-reduce | flops 6144 | bytes 24576
  77.1 47.4 %all-gather.37.cloned.1.call-done = bf16[1,1536,512]{2,1,0:T(8,128)(2,1)} async-done(((bf16[1,48,512]{2,1,0:T(8,128)(2,1)}), bf16[1,1536,512]{2,1,0:T(8,128)(2,1)}) %all-gather.37.cloned.1.call-update) | async-done | bytes 1572880 | tf_op jit(solution)/shard_map/all_gather | solution.py:47
  132.5 59.6 %all-gather.39.cloned.1.call-done = bf16[1,1536,1536]{2,1,0:T(8,128)(2,1)} async-done(((bf16[1,48,1536]{2,1,0:T(8,128)(2,1)}), bf16[1,1536,1536]{2,1,0:T(8,128)(2,1)}) %all-gather.39.cloned.1.call-update) | async-done | bytes 4718608 | tf_op jit(solution)/shard_map/all_gather | solution.py:45
  208.6 9.4 all-to-all-done.1
  239.2 21.1 all-gather.41.cloned.1.call-done
  288.0 102.5 %all-to-all-done.3 = bf16[3,8,57,1536]{3,2,0,1:T(8,128)(2,1)} async-done(((bf16[3,8,57,1536]{3,2,0,1:T(8,128)(2,1)}), bf16[3,8,57,1536]{3,2,0,1:T(8,128)(2,1)}, u32[]{:S(2)}, u32[]{:S(2)}) %all-to-all-start.3) | async-done | bytes 4202528 | tf_op jit(solution)/shard_map/all_to_all | solution.py:259
  401.4 7.6 fusion.42
  409.0 8.7 multiply_convert_fusion.7
  417.7 7.2 fusion.50
  443.3 134.5 %all-gather.6 = bf16[1,1536,24]{2,0,1:T(2,128)(2,1)S(1)} all-gather(bf16[1,48,24]{2,0,1:T(2,128)(2,1)S(1)} %copy.495), channel_id=8, replica_groups=mesh['seq'=8,'fsdp'=4] {'seq','fsdp'}, dimensions={1}, use_global_device_ids=true | all-gather | bytes 76032 | tf_op jit(solution)/shard_map/all_gather | solution.py:49
  589.5 9.4 gather_fusion.1
  612.1 24.0 all-gather.53.cloned.1.call-done
  645.7 10.6 all-to-all-done.6
  670.9 43.0 %all-gather.16 = bf16[1,1536,24]{2,0,1:T(2,128)(2,1)S(1)} all-gather(bf16[1,48,24]{2,0,1:T(2,128)(2,1)S(1)} %copy.496), channel_id=18, replica_groups=mesh['seq'=8,'fsdp'=4] {'seq','fsdp'}, dimensions={1}, use_global_device_ids=true | all-gather | bytes 76032 | tf_op jit(solution)/shard_map/all_gather | solution.py:49
  721.6 8.2 gather.40
  736.7 7.8 gather_fusion.4
  751.4 10.3 all-to-all-start.10
  779.4 85.0 %all-to-all-done.10 = bf16[3,8,57,1536]{3,2,0,1:T(8,128)(2,1)} async-done(((bf16[3,8,57,1536]{3,2,0,1:T(8,128)(2,1)}), bf16[3,8,57,1536]{3,2,0,1:T(8,128)(2,1)}, u32[]{:S(2)}, u32[]{:S(2)}) %all-to-all-start.10) | async-done | bytes 4202528 | tf_op jit(solution)/shard_map/all_to_all | solution.py:361
  882.2 91.3 %all-to-all-done.8 = bf16[3,8,57,1536]{3,2,0,1:T(8,128)(2,1)} async-done(((bf16[3,8,57,1536]{3,2,0,1:T(8,128)(2,1)}), bf16[3,8,57,1536]{3,2,0,1:T(8,128)(2,1)}, u32[]{:S(2)}, u32[]{:S(2)}) %all-to-all-start.8) | async-done | bytes 4202528 | tf_op jit(solution)/shard_map/all_to_all | solution.py:259
  984.2 7.5 fusion.19
  991.7 7.5 fusion.23
  999.2 9.8 multiply_convert_fusion.4
  1051.4 82.5 %all-to-all-done.9 = bf16[3,8,57,1536]{3,2,0,1:T(8,128)(2,1)} async-done(((bf16[3,8,57,1536]{3,2,0,1:T(8,128)(2,1)}), bf16[3,8,57,1536]{3,2,0,1:T(8,128)(2,1)}, u32[]{:S(2)}, u32[]{:S(2)}) %all-to-all-start.9) | async-done | bytes 4202528 | tf_op jit(solution)/shard_map/all_to_all | solution.py:269
  1150.3 9.4 gather_fusion.3
  1167.1 75.2 %all-to-all-done.11 = bf16[3,8,57,1536]{3,2,0,1:T(8,128)(2,1)} async-done(((bf16[3,8,57,1536]{3,2,0,1:T(8,128)(2,1)}), bf16[3,8,57,1536]{3,2,0,1:T(8,128)(2,1)}, u32[]{:S(2)}, u32[]{:S(2)}) %all-to-all-start.11) | async-done | bytes 4202528 | tf_op jit(solution)/shard_map/all_to_all | solution.py:389
  1253.0 9.4 gather_fusion.6
  1350.6 10.9 copy.493
  1369.6 7.8 gather_fusion.7
  1383.9 8.2 gather.44
  1396.8 113.1 %all_to_all.214 = bf16[3,8,57,1536]{3,2,0,1:T(8,128)(2,1)S(1)} all-to-all(bf16[3,8,57,1536]{3,2,0,1:T(8,128)(2,1)S(1)} %copy.452), channel_id=1, replica_groups=mesh['seq'=8,'fsdp'=4] {'seq'}, dimensions={1} | all-to-all | bytes 8404992 | tf_op jit(solution)/shard_map/all_to_all | solution.py:361
  1524.9 10.9 copy.491
  1544.4 7.5 convolution_convert_fusion.2
  1552.0 10.2 multiply_convert_fusion.2
  1569.0 7.2 convolution_convert_fusion.4
  1606.9 7.2 convolution_convert_fusion.5
  1614.2 95.1 %all-to-all-done.16 = bf16[3,8,57,1536]{3,2,0,1:T(8,128)(2,1)} async-done(((bf16[3,8,57,1536]{3,2,0,1:T(8,128)(2,1)}), bf16[3,8,57,1536]{3,2,0,1:T(8,128)(2,1)}, u32[]{:S(2)}, u32[]{:S(2)}) %all-to-all-start.16) | async-done | bytes 4202528 | tf_op jit(solution)/shard_map/all_to_all | solution.py:389
  1720.1 10.1 gather_fusion.9
  1773.7 12.1 all_to_all.215
  1815.7 16.0 all_to_all.216
  1849.0 40.1 %all-reduce.16 = (f32[1536]{0:T(1024)S(1)}, f32[1536]{0:T(1024)S(1)}, f32[1536]{0:T(1024)S(1)}, f32[1536]{0:T(1024)S(1)}) all-reduce(f32[1536]{0:T(1024)S(1)} %copy-done.131, f32[1536]{0:T(1024)S(1)} %get-tuple-element.148, f32[1536]{0:T(1024)S(1)} %copy-done.130, ...), channel_id=23, replica_groups=mesh['seq'=8,'fsdp'=4] {'seq','fsdp'}, use_global_device_ids=true, to_apply=%region_44.45.clone | all-reduce | flops 6144 | bytes 49152
  1908.7 31.5 %reduce-scatter.35.cloned.1.call-done = f32[48,512]{1,0:T(8,128)} async-done(((f32[1536,512]{1,0:T(8,128)}), f32[48,512]{1,0:T(8,128)}) %reduce-scatter.35.cloned.1.call-update) | async-done | bytes 98320 | tf_op jit(solution)/shard_map/reduce_scatter | solution.py:516
  1940.2 105.8 %reduce-scatter.33.cloned.1.call-done = f32[48,512]{1,0:T(8,128)} async-done(((f32[1536,512]{1,0:T(8,128)}), f32[48,512]{1,0:T(8,128)}) %reduce-scatter.33.cloned.1.call-update) | async-done | bytes 98320 | tf_op jit(solution)/shard_map/reduce_scatter | solution.py:516
  2047.6 104.2 %reduce-scatter.31.cloned.1.call-done = f32[48,512]{1,0:T(8,128)} async-done(((f32[1536,512]{1,0:T(8,128)}), f32[48,512]{1,0:T(8,128)}) %reduce-scatter.31.cloned.1.call-update) | async-done | bytes 98320 | tf_op jit(solution)/shard_map/reduce_scatter | solution.py:515
  2151.8 105.8 %reduce-scatter.29.cloned.1.call-done = f32[48,512]{1,0:T(8,128)} async-done(((f32[1536,512]{1,0:T(8,128)}), f32[48,512]{1,0:T(8,128)}) %reduce-scatter.29.cloned.1.call-update) | async-done | bytes 98320 | tf_op jit(solution)/shard_map/reduce_scatter | solution.py:515
  2259.2 138.4 %reduce-scatter.39.cloned.1.call-done = f32[48,1536]{1,0:T(8,128)} async-done(((f32[1536,1536]{1,0:T(8,128)}), f32[48,1536]{1,0:T(8,128)}) %reduce-scatter.39.cloned.1.call-update) | async-done | bytes 294928 | tf_op jit(solution)/shard_map/reduce_scatter | solution.py:517
  2397.7 141.4 %reduce-scatter.37.cloned.1.call-done = f32[48,1536]{1,0:T(8,128)} async-done(((f32[1536,1536]{1,0:T(8,128)}), f32[48,1536]{1,0:T(8,128)}) %reduce-scatter.37.cloned.1.call-update) | async-done | bytes 294928 | tf_op jit(solution)/shard_map/reduce_scatter | solution.py:517
  2540.9 138.3 %reduce-scatter.27.cloned.1.call-done = f32[48,1536]{1,0:T(8,128)} async-done(((f32[1536,1536]{1,0:T(8,128)}), f32[48,1536]{1,0:T(8,128)}) %reduce-scatter.27.cloned.1.call-update) | async-done | bytes 294928 | tf_op jit(solution)/shard_map/reduce_scatter | solution.py:514
  2679.2 141.5 %reduce-scatter.25.cloned.1.call-done = f32[48,1536]{1,0:T(8,128)} async-done(((f32[1536,1536]{1,0:T(8,128)}), f32[48,1536]{1,0:T(8,128)}) %reduce-scatter.25.cloned.1.call-update) | async-done | bytes 294928 | tf_op jit(solution)/shard_map/reduce_scatter | solution.py:514
  (757 shorter events, 619.6 us)
Async XLA Ops:
  7.2 67.5 %all-gather.35.cloned.1.call-start = ((), (), s32[]{:S(2)}) async-start(), calls=%async_computation.48 | async-start | bytes 1622016 | tf_op jit(solution)/shard_map/all_gather | solution.py:46
  8.7 115.7 %all-gather.37.cloned.1.call-start = ((), (), s32[]{:S(2)}) async-start(), calls=%async_computation.49 | async-start | bytes 1622016 | tf_op jit(solution)/shard_map/all_gather | solution.py:47
  10.3 181.9 %all-gather.39.cloned.1.call-start = ((), (), s32[]{:S(2)}) async-start(), calls=%async_computation.50 | async-start | bytes 4866048 | tf_op jit(solution)/shard_map/all_gather | solution.py:45
  12.0 248.3 %all-gather.41.cloned.1.call-start = ((), (), s32[]{:S(2)}) async-start(), calls=%async_computation.51 | async-start | bytes 4866048 | tf_op jit(solution)/shard_map/all_gather | solution.py:48
  13.8 387.6 %all-gather.43.cloned.1.call-start = ((), (), s32[]{:S(2)}) async-start(), calls=%async_computation.52 | async-start | bytes 5898240 | tf_op jit(solution)/shard_map/all_gather | solution.py:52
  17.4 391.6 %all-gather.45.cloned.1.call-start = ((), (), s32[]{:S(2)}) async-start(), calls=%async_computation.53 | async-start | bytes 5898240 | tf_op jit(solution)/shard_map/all_gather | solution.py:53
  19.0 398.7 %all-gather.47.cloned.1.call-start = ((), (), s32[]{:S(2)}) async-start(), calls=%async_computation.54 | async-start | bytes 5898240 | tf_op jit(solution)/shard_map/all_gather | solution.py:54
  22.5 580.5 %all-gather.51.cloned.1.call-start = ((), (), s32[]{:S(2)}) async-start(), calls=%async_computation.56 | async-start | bytes 1622016 | tf_op jit(solution)/shard_map/all_gather | solution.py:47
  23.2 581.9 %all-gather.49.cloned.1.call-start = ((), (), s32[]{:S(2)}) async-start(), calls=%async_computation.55 | async-start | bytes 1622016 | tf_op jit(solution)/shard_map/all_gather | solution.py:46
  74.7 565.6 %copy-start.63 = (f32[128,32]{0,1:T(8,128)}, f32[128,32]{0,1:T(8,128)S(1)}, u32[]{:S(2)}) copy-start(f32[128,32]{0,1:T(8,128)S(1)} %get-tuple-element.219) | copy-start | bytes 49156
  127.2 76.3 %all-to-all-start = ((bf16[128,8,128]{0,2,1:T(8,128)(2,1)}), bf16[128,8,128]{0,2,1:T(8,128)(2,1)S(1)}, u32[]{:S(2)}, u32[]{:S(2)}) async-start(bf16[128,8,128]{0,2,1:T(8,128)(2,1)} %pad_maximum_fusion.5), calls=%async_computation | async-start | bytes 524288 | tf_op jit(solution)/shard_map/all_to_all | solution.py:239
  203.5 14.5 all-to-all-start.1
  226.9 33.4 %all-to-all-start.2 = ((bf16[8,128,192]{1,2,0:T(8,128)(2,1)}), bf16[8,128,192]{1,2,0:T(8,128)(2,1)S(1)}, u32[]{:S(2)}, u32[]{:S(2)}) async-start(bf16[8,128,192]{1,2,0:T(8,128)(2,1)} %copy_bitcast_fusion.3), calls=%async_computation.2 | async-start | bytes 786432 | tf_op jit(solution)/shard_map/all_to_all | solution.py:242
  281.6 108.9 %all-to-all-start.3 = ((bf16[3,8,57,1536]{3,2,0,1:T(8,128)(2,1)}), bf16[3,8,57,1536]{3,2,0,1:T(8,128)(2,1)}, u32[]{:S(2)}, u32[]{:S(2)}) async-start(bf16[3,8,57,1536]{3,2,0,1:T(8,128)(2,1)} %copy.409), calls=%async_computation.3 | async-start | bytes 9437184 | tf_op jit(solution)/shard_map/all_to_all | solution.py:259
  287.5 348.6 %all-gather.53.cloned.1.call-start = ((), (), s32[]{:S(2)}) async-start(), calls=%async_computation.57 | async-start | bytes 4866048 | tf_op jit(solution)/shard_map/all_gather | solution.py:45
  435.6 143.0 %all-to-all-start.4 = ((bf16[3,8,57,1536]{3,2,0,1:T(8,128)(2,1)}), bf16[3,8,57,1536]{3,2,0,1:T(8,128)(2,1)}, u32[]{:S(2)}, u32[]{:S(2)}) async-start(bf16[3,8,57,1536]{3,2,0,1:T(8,128)(2,1)} %copy.411), calls=%async_computation.4 | async-start | bytes 9437184 | tf_op jit(solution)/shard_map/all_to_all | solution.py:269
  441.8 288.0 %all-gather.55.cloned.1.call-start = ((), (), s32[]{:S(2)}) async-start(), calls=%async_computation.58 | async-start | bytes 4866048 | tf_op jit(solution)/shard_map/all_gather | solution.py:48
  608.0 33.3 %all-to-all-start.5 = ((bf16[128,8,128]{0,2,1:T(8,128)(2,1)}), bf16[128,8,128]{0,2,1:T(8,128)(2,1)S(1)}, u32[]{:S(2)}, u32[]{:S(2)}) async-start(bf16[128,8,128]{0,2,1:T(8,128)(2,1)} %pad_maximum_fusion.6), calls=%async_computation.5 | async-start | bytes 524288 | tf_op jit(solution)/shard_map/all_to_all | solution.py:239
  641.3 15.0 all-to-all-start.6
  644.8 339.5 %all-gather.59.cloned.1.call-start = ((), (), s32[]{:S(2)}) async-start(), calls=%async_computation.60 | async-start | bytes 5898240 | tf_op jit(solution)/shard_map/all_gather | solution.py:53
  663.6 66.2 %all-to-all-start.7 = ((bf16[8,128,192]{1,2,0:T(8,128)(2,1)}), bf16[8,128,192]{1,2,0:T(8,128)(2,1)S(1)}, u32[]{:S(2)}, u32[]{:S(2)}) async-start(bf16[8,128,192]{1,2,0:T(8,128)(2,1)} %copy_bitcast_fusion.2), calls=%async_computation.7 | async-start | bytes 786432 | tf_op jit(solution)/shard_map/all_to_all | solution.py:242
  751.4 113.1 %all-to-all-start.10 = ((bf16[3,8,57,1536]{3,2,0,1:T(8,128)(2,1)}), bf16[3,8,57,1536]{3,2,0,1:T(8,128)(2,1)}, u32[]{:S(2)}, u32[]{:S(2)}) async-start(bf16[3,8,57,1536]{3,2,0,1:T(8,128)(2,1)} %copy.432), calls=%async_computation.10 | async-start | bytes 9437184 | tf_op jit(solution)/shard_map/all_to_all | solution.py:361
  761.7 230.0 %all-gather.57.cloned.1.call-start = ((), (), s32[]{:S(2)}) async-start(), calls=%async_computation.59 | async-start | bytes 5898240 | tf_op jit(solution)/shard_map/all_gather | solution.py:52
  864.5 109.0 %all-to-all-start.8 = ((bf16[3,8,57,1536]{3,2,0,1:T(8,128)(2,1)}), bf16[3,8,57,1536]{3,2,0,1:T(8,128)(2,1)}, u32[]{:S(2)}, u32[]{:S(2)}) async-start(bf16[3,8,57,1536]{3,2,0,1:T(8,128)(2,1)} %copy.425), calls=%async_computation.8 | async-start | bytes 9437184 | tf_op jit(solution)/shard_map/all_to_all | solution.py:259
  870.7 128.5 %all-gather.61.cloned.1.call-start = ((), (), s32[]{:S(2)}) async-start(), calls=%async_computation.61 | async-start | bytes 5898240 | tf_op jit(solution)/shard_map/all_gather | solution.py:54
  1025.3 108.6 %all-to-all-start.9 = ((bf16[3,8,57,1536]{3,2,0,1:T(8,128)(2,1)}), bf16[3,8,57,1536]{3,2,0,1:T(8,128)(2,1)}, u32[]{:S(2)}, u32[]{:S(2)}) async-start(bf16[3,8,57,1536]{3,2,0,1:T(8,128)(2,1)} %copy.427), calls=%async_computation.9 | async-start | bytes 9437184 | tf_op jit(solution)/shard_map/all_to_all | solution.py:269
  1133.9 108.4 %all-to-all-start.11 = ((bf16[3,8,57,1536]{3,2,0,1:T(8,128)(2,1)}), bf16[3,8,57,1536]{3,2,0,1:T(8,128)(2,1)}, u32[]{:S(2)}, u32[]{:S(2)}) async-start(bf16[3,8,57,1536]{3,2,0,1:T(8,128)(2,1)} %copy.434), calls=%async_computation.11 | async-start | bytes 9437184 | tf_op jit(solution)/shard_map/all_to_all | solution.py:389
  1274.7 14.1 all-to-all-start.12
  1307.8 12.2 all-to-all-start.14
  1320.0 14.3 all-to-all-start.13
  1326.5 510.5 %reduce-scatter.51.cloned.1.call-start = ((), (), s32[]{:S(2)}) async-start(), calls=%async_computation.63 | async-start | bytes 811008
  1328.7 509.2 %reduce-scatter.49.cloned.1.call-start = ((), (), s32[]{:S(2)}) async-start(), calls=%async_computation.62 | async-start | bytes 811008
  1344.0 495.3 %reduce-scatter.55.cloned.1.call-start = ((), (), s32[]{:S(2)}) async-start(), calls=%async_computation.65 | async-start | bytes 5898240
  1368.6 523.2 %reduce-scatter.53.cloned.1.call-start = ((), (), s32[]{:S(2)}) async-start(), calls=%async_computation.64 | async-start | bytes 5898240
  1542.8 357.6 %reduce-scatter.47.cloned.1.call-start = ((), (), s32[]{:S(2)}) async-start(), calls=%async_computation.47 | async-start | bytes 5898240 | tf_op jit(solution)/shard_map/reduce_scatter | solution.py:524
  1551.9 348.5 %reduce-scatter.45.cloned.1.call-start = ((), (), s32[]{:S(2)}) async-start(), calls=%async_computation.46 | async-start | bytes 5898240 | tf_op jit(solution)/shard_map/reduce_scatter | solution.py:524
  1567.7 336.9 %reduce-scatter.43.cloned.1.call-start = ((), (), s32[]{:S(2)}) async-start(), calls=%async_computation.45 | async-start | bytes 5898240 | tf_op jit(solution)/shard_map/reduce_scatter | solution.py:521
  1600.4 108.9 %all-to-all-start.16 = ((bf16[3,8,57,1536]{3,2,0,1:T(8,128)(2,1)}), bf16[3,8,57,1536]{3,2,0,1:T(8,128)(2,1)}, u32[]{:S(2)}, u32[]{:S(2)}) async-start(bf16[3,8,57,1536]{3,2,0,1:T(8,128)(2,1)} %copy.454), calls=%async_computation.16 | async-start | bytes 9437184 | tf_op jit(solution)/shard_map/all_to_all | solution.py:389
  1606.5 298.0 %reduce-scatter.41.cloned.1.call-start = ((), (), s32[]{:S(2)}) async-start(), calls=%async_computation.44 | async-start | bytes 5898240 | tf_op jit(solution)/shard_map/reduce_scatter | solution.py:521
  1741.1 13.8 all-to-all-start.17
  1746.7 193.5 %reduce-scatter.35.cloned.1.call-start = ((), (), s32[]{:S(2)}) async-start(), calls=%async_computation.41 | async-start | bytes 3244032 | tf_op jit(solution)/shard_map/reduce_scatter | solution.py:516
  1749.1 296.9 %reduce-scatter.33.cloned.1.call-start = ((), (), s32[]{:S(2)}) async-start(), calls=%async_computation.40 | async-start | bytes 3244032 | tf_op jit(solution)/shard_map/reduce_scatter | solution.py:516
  1788.3 363.5 %reduce-scatter.31.cloned.1.call-start = ((), (), s32[]{:S(2)}) async-start(), calls=%async_computation.39 | async-start | bytes 3244032 | tf_op jit(solution)/shard_map/reduce_scatter | solution.py:515
  1790.7 466.9 %reduce-scatter.29.cloned.1.call-start = ((), (), s32[]{:S(2)}) async-start(), calls=%async_computation.38 | async-start | bytes 3244032 | tf_op jit(solution)/shard_map/reduce_scatter | solution.py:515
  1793.3 604.3 %reduce-scatter.39.cloned.1.call-start = ((), (), s32[]{:S(2)}) async-start(), calls=%async_computation.43 | async-start | bytes 9732096 | tf_op jit(solution)/shard_map/reduce_scatter | solution.py:517
  1799.4 739.6 %reduce-scatter.37.cloned.1.call-start = ((), (), s32[]{:S(2)}) async-start(), calls=%async_computation.42 | async-start | bytes 9732096 | tf_op jit(solution)/shard_map/reduce_scatter | solution.py:517
  1805.7 873.5 %reduce-scatter.27.cloned.1.call-start = ((), (), s32[]{:S(2)}) async-start(), calls=%async_computation.37 | async-start | bytes 9732096 | tf_op jit(solution)/shard_map/reduce_scatter | solution.py:514
  1811.7 1009.1 %reduce-scatter.25.cloned.1.call-start = ((), (), s32[]{:S(2)}) async-start(), calls=%async_computation.36 | async-start | bytes 9732096 | tf_op jit(solution)/shard_map/reduce_scatter | solution.py:514
  (170 other events, 2311.1 us)
Sparse Core Ops, SparseCore 0:
  11.4 55.6 all-gather.34
  70.6 53.8 all-gather.36
  127.9 64.1 all-gather.38
  195.4 64.8 all-gather.40
  262.3 36.3 all-gather.42
  300.1 37.4 all-gather.44
  339.2 37.3 all-gather.46
  379.5 54.0 all-gather.50
  436.5 131.0 all-gather.48
  570.9 65.1 all-gather.52
  638.9 69.4 all-gather.54
  709.9 36.8 all-gather.58
  764.1 37.6 all-gather.56
  872.8 38.3 all-gather.60
  1332.1 98.1 reduce-scatter.50
  1435.3 95.8 reduce-scatter.48
  1533.5 48.6 reduce-scatter.54
  1584.8 47.8 reduce-scatter.52
  1635.2 47.8 reduce-scatter.46
  1685.6 47.8 reduce-scatter.44
  1736.6 47.8 reduce-scatter.42
  1787.1 47.8 reduce-scatter.40
  1840.4 99.7 reduce-scatter.34
  1945.5 100.4 reduce-scatter.32
  2051.4 100.3 reduce-scatter.30
  2157.1 100.4 reduce-scatter.28
  2263.3 134.2 reduce-scatter.38
  2404.6 134.4 reduce-scatter.36
  2544.9 134.2 reduce-scatter.26
  2686.0 134.7 reduce-scatter.24
where the time goes:
time: 2850 us; the launch traced here: 2830 us
  waiting for transfers between devices  1630 us (57%)
  blocking collectives  399 us (14%)
  local copies, waits for them, and re-layouts  362 us (13%)
  matrix products  235 us (8%)
  starting transfers between devices  105 us (4%)
  other arithmetic  78.5 us (3%)
    reduce_scatter x2, waiting for transfers between devices, per_device(): lax.psum_scatter(dense_terms[5], ('seq', 'fsdp'), scatter_dimension=0, ti...  280 us
    reduce_scatter x2, waiting for transfers between devices, per_device(): lax.psum_scatter(dense_terms[2], ('seq', 'fsdp'), scatter_dimension=0, ti...  280 us
    reduce_scatter x2, waiting for transfers between devices, per_device(): lax.psum_scatter(dense_terms[3], ('seq', 'fsdp'), scatter_dimension=0, ti...  210 us
    all_to_all x2, waiting for transfers between devices, forward_layer(): lax.all_to_all(sending, 'seq', split_axis=1, concat_axis=1, tiled=True)  194 us
    all_gather x2, blocking collectives, fetch_layer(): lax.all_gather(shards[6][layer_id], ('seq', 'fsdp'), axis=0, tiled=True)  177 us
    all_to_all x2, waiting for transfers between devices, backward_layer(): lax.all_to_all(rows_grad.reshape(local_count, seq_count, capacity, -1), '...  170 us
    reduce_scatter x2, waiting for transfers between devices, per_device(): lax.psum_scatter(dense_terms[4], ('seq', 'fsdp'), scatter_dimension=0, ti...  137 us
    all_to_all x1, blocking collectives, backward_layer(): lax.all_to_all(output_grad.reshape(local_count, seq_count, capacity, -1),...  113 us
  transfers between devices with their start and end apart: 47, of which 24 were waited for; matrix products, arithmetic and copies ran while one was open for 20% of the time, Pallas kernels for 0%

commit v1 on v0

v1 whole, which is shorter than its diff:
```python
import functools, math
import jax, jax.numpy as jnp
from jax import lax
from jax.experimental import pallas as pl
from jax.experimental.pallas import tpu as pltpu
from jax.sharding import Mesh, PartitionSpec as P
MESH = pl.DeviceIdType.MESH
AX=("za","yb","grp","xh","co")

class Ring8:
    def __init__(self, na):
        self.n=2*na; self.na=na
        za=lax.axis_index("za"); yb=lax.axis_index("yb")
        self.rho = za + yb*(2*na-1-2*za)
    def pos(self, r):
        r = lax.rem(r+2*self.n, self.n)
        yb = r//self.na
        za = r + yb*(2*self.na-1-2*r)
        return za, yb
    def dev(self, r):
        za,yb=self.pos(r); return {"za":za,"yb":yb}
    def slot(self, r):
        za,yb=self.pos(r); return za*2+yb

class Ring4:
    def __init__(self):
        self.n=4
        x=lax.axis_index("xh"); b=lax.axis_index("yb"); self.c=lax.axis_index("co")
        self.rho = 2*x + (x+b-2*x*b)
    def pos(self, r):
        r = lax.rem(r+2*self.n, self.n)
        x = r//2; m=lax.rem(r,2)
        return x, m+x-2*x*m
    def dev(self, r):
        x,b=self.pos(r); return {"xh":x,"yb":b}
    def slot(self, r, sib=False):
        x,b=self.pos(r); c = (1-self.c) if sib else self.c
        return (x*2+c)*2+b
    def sib_dev(self):
        return {"co":1-self.c}

def barrier(devs):
    sem = pltpu.get_barrier_semaphore()
    for d in devs:
        pl.semaphore_signal(sem, inc=1, device_id=d, device_id_type=MESH)
    pl.semaphore_wait(sem, len(devs))

def rcopy(src, dst, ss, rs, dev):
    return pltpu.make_async_remote_copy(src_ref=src, dst_ref=dst, send_sem=ss, recv_sem=rs, device_id=dev, device_id_type=MESH)

def ag_ring(ring, K, own, out, send, recv, sib=None):
    n=ring.n; S=n//2; T=own.shape[0]; rows=T//K; rho=ring.rho
    def chunks(d,s): return range(K) if s<S else (range(K//2) if d==0 else range(K//2,K))
    def mk(d,s,c):
        sg=1-2*d
        slot=ring.slot(rho-(s-1)*sg)
        sl=pl.ds(c*rows,rows)
        src = own.at[sl] if s==1 else out.at[slot,sl]
        return rcopy(src, out.at[slot,sl], send.at[d,s-1,c], recv.at[d,s-1,c], ring.dev(rho+sg))
    def rd(d,s,c):
        sg=1-2*d
        slot=ring.slot(rho-s*sg); sl=pl.ds(c*rows,rows)
        return rcopy(out.at[slot,sl], out.at[slot,sl], send.at[d,s-1,c], recv.at[d,s-1,c], ring.dev(rho-sg))
    started=[]
    def sibcopy(slot, slot_src, c, idx, src):
        ss,rs=sib
        cp=rcopy(src, out.at[slot,pl.ds(c*rows,rows)], ss.at[idx,c], rs.at[idx,c], ring.sib_dev())
        cp.start(); started.append(cp)
    def arrived(d,s,c):
        rd(d,s,c).wait_recv()
        if sib is not None:
            sg=1-2*d
            slot=ring.slot(rho-s*sg)
            idx = s*sg % n
            sibcopy(slot, None, c, idx, out.at[slot,pl.ds(c*rows,rows)])
    sends=[]
    for s in range(1,S+1):
        for c in range(K):
            for d in (0,1):
                if c in chunks(d,s):
                    if s>1: arrived(d,s-1,c)
                    cp=mk(d,s,c); cp.start(); sends.append(cp)
        if s==1 and sib is not None:
            for c in range(K): sibcopy(ring.slot(rho), None, c, 0, own.at[pl.ds(c*rows,rows)])
    for s in (S-1,S):
        for c in range(K):
            for d in (0,1):
                if s==S and c in chunks(d,S): arrived(d,S,c)
                if s==S-1 and S>1 and c not in chunks(d,S): arrived(d,S-1,c)
    if sib is not None:
        ss,rs=sib
        for idx in range(n):
            for c in range(K):
                slot=ring.slot(rho-idx, True); sl=pl.ds(c*rows,rows)
                rcopy(out.at[slot,sl],out.at[slot,sl],ss.at[idx,c],rs.at[idx,c],ring.sib_dev()).wait_recv()
    for cp in sends+started: cp.wait_send()

def rs_ring(ring, K, part, buf, send, recv, slotf):
    n=ring.n; S=n//2; T=buf.shape[2]; rows=T//K; rho=ring.rho
    def chunks(d,s): return range(K) if s>1 else (range(K//2) if d==0 else range(K//2,K))
    sends=[]
    def rd(d,s,c):
        sl=pl.ds(c*rows,rows)
        return rcopy(buf.at[d,s-1,sl],buf.at[d,s-1,sl],send.at[d,s-1,c],recv.at[d,s-1,c],ring.dev(rho-(1-2*d)))
    for s in range(1,S+1):
        order=list(range(K))
        if s==2:
            pass
        for c in order:
            for d in (0,1):
                if c not in chunks(d,s): continue
                sg=1-2*d
                dest=rho+sg*(S+1-s)
                sl=pl.ds(c*rows,rows)
                if s>1 and c in chunks(d,s-1):
                    rd(d,s-1,c).wait_recv()
                    buf[d,s-2,sl,:] = (buf[d,s-2,sl,:].astype(jnp.float32)+part[slotf(dest),sl,:].astype(jnp.float32)).astype(buf.dtype)
                    src=buf.at[d,s-2,sl]
                else:
                    src=part.at[slotf(dest),sl]
                cp=rcopy(src,buf.at[d,s-1,sl],send.at[d,s-1,c],recv.at[d,s-1,c],ring.dev(rho+sg))
                cp.start(); sends.append(cp)
    for c in range(K):
        for d in (0,1):
            rd(d,S,c).wait_recv()
    for cp in sends: cp.wait_send()

HEAD_SIZE = 64
EPSILON = 1e-05
HIGHEST = lax.Precision.HIGHEST
F32 = jnp.float32
BF16 = jnp.bfloat16
ANY_SPEC = pl.BlockSpec(memory_space=pl.ANY)
VMEM_SPEC = pl.BlockSpec(memory_space=pltpu.VMEM)
CHUNKS = 4
DMA = pltpu.SemaphoreType.DMA


def comm_params(number):
    return pltpu.CompilerParams(
        collective_id=number, has_side_effects=True, vmem_limit_bytes=40 << 20
    )


def gather_group(rows, planes):
    count, width = rows.shape

    def kernel(x_ref, o_ref, send, recv, own):
        ring = Ring8(planes)
        barrier([ring.dev(ring.rho + 1), ring.dev(ring.rho - 1)])
        local = pltpu.make_async_copy(x_ref, o_ref.at[ring.slot(ring.rho)], own)
        local.start()
        ag_ring(ring, CHUNKS, x_ref, o_ref, send, recv)
        local.wait()

    return pl.pallas_call(
        kernel,
        out_shape=jax.ShapeDtypeStruct((2 * planes, count, width), BF16),
        in_specs=[VMEM_SPEC],
        out_specs=ANY_SPEC,
        scratch_shapes=[DMA((2, planes, CHUNKS)), DMA((2, planes, CHUNKS)), DMA],
        compiler_params=comm_params(0),
        name="gather_group",
    )(rows)


def scatter_group(parts, planes, number):
    _, count, width = parts.shape

    def kernel(p_ref, o_ref, buf, send, recv):
        ring = Ring8(planes)
        barrier([ring.dev(ring.rho + 1), ring.dev(ring.rho - 1)])
        rs_ring(ring, CHUNKS, p_ref, buf, send, recv, ring.slot)
        last = planes - 1
        o_ref[...] = (
            buf[0, last].astype(F32) + buf[1, last].astype(F32)
        ) + p_ref[ring.slot(ring.rho)].astype(F32)

    return pl.pallas_call(
        kernel,
        out_shape=jax.ShapeDtypeStruct((count, width), F32),
        in_specs=[VMEM_SPEC],
        out_specs=VMEM_SPEC,
        scratch_shapes=[
            pltpu.VMEM((2, planes, count, width), BF16),
            DMA((2, planes, CHUNKS)),
            DMA((2, planes, CHUNKS)),
        ],
        compiler_params=comm_params(number),
        name="scatter_group",
    )(parts)


def gather_plane(rows):
    count, width = rows.shape

    def kernel(x_ref, o_ref, send, recv, sib_send, sib_recv, own):
        ring = Ring4()
        barrier([ring.dev(ring.rho + 1), ring.dev(ring.rho - 1), ring.sib_dev()])
        local = pltpu.make_async_copy(x_ref, o_ref.at[ring.slot(ring.rho)], own)
        local.start()
        ag_ring(ring, CHUNKS, x_ref, o_ref, send, recv, (sib_send, sib_recv))
        local.wait()

    return pl.pallas_call(
        kernel,
        out_shape=jax.ShapeDtypeStruct((8, count, width), BF16),
        in_specs=[VMEM_SPEC],
        out_specs=ANY_SPEC,
        scratch_shapes=[
            DMA((2, 2, CHUNKS)),
            DMA((2, 2, CHUNKS)),
            DMA((4, CHUNKS)),
            DMA((4, CHUNKS)),
            DMA,
        ],
        compiler_params=comm_params(3),
        name="gather_plane",
    )(rows)


def scatter_plane(parts):
    _, count, width = parts.shape

    def kernel(p_ref, o_ref, pair, buf, send, recv, sib_send, sib_recv):
        ring = Ring4()
        barrier([ring.dev(ring.rho + 1), ring.dev(ring.rho - 1), ring.sib_dev()])

        def chip(r):
            x, b = ring.pos(r)
            return x * 2 + b

        copies = []
        for i in (2, 1, 3, 0):
            copy = rcopy(
                p_ref.at[ring.slot(ring.rho + i, True)],
                pair.at[chip(ring.rho + i)],
                sib_send.at[i],
                sib_recv.at[i],
                ring.sib_dev(),
            )
            copy.start()
            copies.append(copy)
        for i, copy in zip((2, 1, 3, 0), copies):
            place = chip(ring.rho + i)
            copy.wait_recv()
            pair[place] = (
                pair[place].astype(F32) + p_ref[ring.slot(ring.rho + i)].astype(F32)
            ).astype(BF16)
        rs_ring(ring, CHUNKS, pair, buf, send, recv, chip)
        o_ref[...] = (
            buf[0, 1].astype(F32) + buf[1, 1].astype(F32)
        ) + pair[chip(ring.rho)].astype(F32)
        for copy in copies:
            copy.wait_send()

    return pl.pallas_call(
        kernel,
        out_shape=jax.ShapeDtypeStruct((count, width), F32),
        in_specs=[VMEM_SPEC],
        out_specs=VMEM_SPEC,
        scratch_shapes=[
            pltpu.VMEM((4, count, width), BF16),
            pltpu.VMEM((2, 2, count, width), BF16),
            DMA((2, 2, CHUNKS)),
            DMA((2, 2, CHUNKS)),
            DMA((4,)),
            DMA((4,)),
        ],
        compiler_params=comm_params(4),
        name="scatter_plane",
    )(parts)


def norm_factor(stream):
    return lax.rsqrt(jnp.mean(stream * stream, axis=-1, keepdims=True) + EPSILON)


def norm_back(stream, factor, gain_row, upstream):
    scaled = gain_row * upstream
    inner_mean = jnp.mean(stream * scaled, axis=-1, keepdims=True)
    return factor * scaled - stream * (factor * factor * factor) * inner_mean


def rotate(source, cosine, sine):
    half = HEAD_SIZE // 2
    shaped = source.reshape(source.shape[0], -1, HEAD_SIZE)
    first, second = shaped[..., :half], shaped[..., half:]
    c, s = cosine[:, None, :], sine[:, None, :]
    turned = jnp.concatenate([first * c - second * s, second * c + first * s], axis=-1)
    return turned.reshape(source.shape)


def attend_blocks(length):
    rows = min(512, length)
    return [(i * rows, (i + 1) * rows) for i in range(length // rows)]


def masked(scores, documents, start, stop):
    ids = jnp.arange(stop, dtype=jnp.int32)
    allowed = (documents[start:stop, None] == documents[None, :stop]) & (
        ids[None, :] <= ids[start:stop, None]
    )
    return jnp.where(allowed[None], scores * (1.0 / math.sqrt(HEAD_SIZE)), -1e30)


def attend(queries, keys, values, documents):
    mixed, logs = [], []
    for start, stop in attend_blocks(queries.shape[0]):
        scores = masked(
            jnp.einsum(
                "qhd,kd->hqk", queries[start:stop], keys[:stop], preferred_element_type=F32
            ),
            documents,
            start,
            stop,
        )
        highest = jnp.max(scores, axis=-1, keepdims=True)
        weights = jnp.exp(scores - highest)
        totals = jnp.sum(weights, axis=-1, keepdims=True)
        probs = (weights / totals).astype(BF16)
        mixed.append(
            jnp.einsum("hqk,kd->qhd", probs, values[:stop], preferred_element_type=F32).astype(BF16)
        )
        logs.append(highest + jnp.log(totals))
    return jnp.concatenate(mixed, axis=0), logs


def attend_back(queries, keys, values, documents, logs, mixed_grad):
    scale = 1.0 / math.sqrt(HEAD_SIZE)
    key_sum = jnp.zeros(keys.shape, F32)
    value_sum = jnp.zeros(values.shape, F32)
    query_list = []
    for (start, stop), log in zip(attend_blocks(queries.shape[0]), logs):
        query_rows, upstream = queries[start:stop], mixed_grad[start:stop]
        scores = masked(
            jnp.einsum("qhd,kd->hqk", query_rows, keys[:stop], preferred_element_type=F32),
            documents,
            start,
            stop,
        )
        probs = jnp.exp(scores - log)
        prob_grad = jnp.einsum("qhd,kd->hqk", upstream, values[:stop], preferred_element_type=F32)
        centre = jnp.sum(probs * prob_grad, axis=-1, keepdims=True)
        score_grad = (probs * (prob_grad - centre)).astype(BF16)
        query_list.append(
            jnp.einsum("hqk,kd->qhd", score_grad, keys[:stop], preferred_element_type=F32) * scale
        )
        key_sum = key_sum.at[:stop].add(
            jnp.einsum("hqk,qhd->kd", score_grad, query_rows, preferred_element_type=F32) * scale
        )
        value_sum = value_sum.at[:stop].add(
            jnp.einsum("hqk,qhd->kd", probs.astype(BF16), upstream, preferred_element_type=F32)
        )
    return jnp.concatenate(query_list, axis=0).astype(BF16), key_sum.astype(BF16), value_sum.astype(BF16)


def per_device(
    layer_in,
    cotangent,
    doc_starts,
    routes,
    attn_gain,
    ffn_gain,
    query_weight,
    key_matrix,
    value_matrix,
    out_weight,
    router_weight,
    gate_weight,
    up_weight,
    down_weight,
):
    planes, groups = lax.axis_size("za"), lax.axis_size("grp")
    seq_count = 2 * planes
    place = lax.axis_index("za") * 2 + lax.axis_index("yb")
    count, width = layer_in.shape[1:]
    length = count * seq_count
    layers = attn_gain.shape[0]
    experts_all = router_weight.shape[2]
    local = gate_weight.shape[1]
    top = routes.shape[2]
    slots = -(-(count * top * 4 // (3 * experts_all) + 1) // 16) * 16
    heads = query_weight.shape[2] // HEAD_SIZE // 8
    columns = heads * HEAD_SIZE
    kv = key_matrix.shape[2] // 8
    bands = query_weight.shape[1]

    swap = [(a * 4 + f, f * 4 + a) for a in range(planes) for f in range(4)]

    def exchange(array):
        return lax.ppermute(array, ("za", "xh", "co"), swap)

    stream = exchange(layer_in[0]).astype(F32)
    upstream_low = exchange(cotangent[0])
    starts = exchange(doc_starts)[0]
    chosen = exchange(routes[0])

    small = jnp.stack([attn_gain, ffn_gain], axis=-1)
    pieces = jnp.concatenate(
        [
            jnp.moveaxis(query_weight.reshape(layers, bands, 8, columns), 2, 0),
            jnp.moveaxis(key_matrix.reshape(layers, bands, 8, kv), 2, 0),
            jnp.moveaxis(value_matrix.reshape(layers, bands, 8, kv), 2, 0),
            jnp.broadcast_to(
                jnp.concatenate([router_weight, small], axis=-1)[None],
                (8, layers, bands, experts_all + 2),
            ),
        ],
        axis=-1,
    )
    used = pieces.shape[-1]
    slab = lax.all_to_all(pieces, ("xh", "co", "yb"), 0, 0)
    slab = lax.all_gather(slab, ("za", "grp"))
    slab = slab.reshape(planes, groups, 4, 2, layers, bands, used)
    slab = jnp.transpose(slab, (4, 0, 3, 1, 2, 5, 6)).reshape(layers, width, used)
    qkv_weight = slab[:, :, : columns + 2 * kv]
    router_full = slab[:, :, columns + 2 * kv : columns + 2 * kv + experts_all]
    gains = slab[:, :, columns + 2 * kv + experts_all :].astype(F32)
    out_rows = lax.all_gather(out_weight, ("za", "grp"))
    out_rows = lax.all_to_all(
        out_rows.reshape(planes, groups, layers, bands, width), ("xh", "co"), 0, 0
    )
    out_rows = jnp.transpose(out_rows, (2, 1, 0, 3, 4)).reshape(layers, columns, width)

    def fetch_experts(layer):
        return (
            lax.all_gather(gate_weight[layer], ("grp", "xh", "co"), axis=1, tiled=True),
            lax.all_gather(up_weight[layer], ("grp", "xh", "co"), axis=1, tiled=True),
            lax.all_gather(down_weight[layer], ("grp", "xh", "co"), axis=2, tiled=True),
        )

    named = jnp.sum(
        (chosen[:, :, None] == jnp.arange(experts_all, dtype=jnp.int32)).astype(F32), axis=1
    )
    ids = jnp.arange(count, dtype=jnp.int32)
    before = (ids[None, :] < ids[:, None]).astype(BF16)
    rank = jnp.dot(before, named.astype(BF16), preferred_element_type=F32)
    codes = lax.all_gather(jnp.where(named > 0, rank, -1.0).astype(BF16), ("za", "yb"))
    routed = (codes >= 0).reshape(length, experts_all)
    mine = lax.dynamic_slice_in_dim(codes, place * local, local, axis=2).astype(F32)
    slot_ids = jnp.arange(slots, dtype=jnp.int32).astype(F32)
    spread = mine[:, :, :, None] == slot_ids
    back_ones = spread.reshape(seq_count, count, local * slots).astype(BF16)
    row_ones = jnp.transpose(spread, (0, 2, 3, 1)).reshape(seq_count, local * slots, count)
    row_ones = row_ones.astype(BF16)

    def to_experts(rows):
        shaped = rows.reshape(seq_count, local, slots, -1)
        return jnp.moveaxis(shaped, 1, 0).reshape(local, seq_count * slots, -1)

    def from_experts(rows):
        shaped = rows.reshape(local, seq_count, slots, -1)
        return jnp.moveaxis(shaped, 0, 1).reshape(seq_count, local * slots, -1)

    positions = jnp.arange(length, dtype=jnp.int32)
    documents = jnp.sum((starts[None, :] <= positions[:, None]).astype(jnp.int32), axis=1) - 1
    inverse = 10000.0 ** (
        -2.0 * jnp.arange(HEAD_SIZE // 2, dtype=F32) / HEAD_SIZE
    )
    angles = positions.astype(F32)[:, None] * inverse[None, :]
    cosine, sine = jnp.cos(angles), jnp.sin(angles)

    states = []
    for layer in range(layers):
        gate_w, up_w, down_w = fetch_experts(layer)
        attn_row, ffn_row = gains[layer, :, 0], gains[layer, :, 1]
        factor_one = norm_factor(stream)
        normed_one = gather_plane((stream * factor_one * attn_row).astype(BF16))
        normed_one = normed_one.reshape(length, width)
        qkv = jnp.dot(normed_one, qkv_weight[layer], preferred_element_type=F32)
        queries = rotate(qkv[:, :columns], cosine, sine).astype(BF16)
        keys = rotate(qkv[:, columns : columns + kv], cosine, sine).astype(BF16)
        values = qkv[:, columns + kv :].astype(BF16)
        queries = queries.reshape(length, heads, HEAD_SIZE)
        mixed, logs = attend(queries, keys, values, documents)
        mixed = mixed.reshape(length, columns)
        branch = jnp.dot(mixed, out_rows[layer], preferred_element_type=F32).astype(BF16)
        middle = stream + scatter_plane(branch.reshape(8, count, width))
        factor_two = norm_factor(middle)
        own_two = (middle * factor_two * ffn_row).astype(BF16)
        normed_two = gather_group(own_two, planes)
        logits = jnp.dot(
            normed_two.reshape(length, width), router_full[layer], preferred_element_type=F32
        )
        highest = jnp.max(jnp.where(routed, logits, -1e30), axis=-1, keepdims=True)
        raised = jnp.where(routed, jnp.exp(jnp.where(routed, logits - highest, 0.0)), 0.0)
        gate_probs = raised / jnp.sum(raised, axis=-1, keepdims=True)
        gate_probs = gate_probs.reshape(seq_count, count, experts_all)
        own_probs = lax.dynamic_index_in_dim(gate_probs, place, 0, keepdims=False)
        my_probs = lax.dynamic_slice_in_dim(gate_probs, place * local, local, axis=2)
        back_probs = jnp.where(spread, my_probs[..., None], 0.0)
        row_probs = jnp.transpose(back_probs, (0, 2, 3, 1)).reshape(
            seq_count, local * slots, count
        )
        back_probs = back_probs.reshape(seq_count, count, local * slots).astype(BF16)
        rows = to_experts(
            jnp.einsum("brt,btd->brd", row_ones, normed_two, preferred_element_type=BF16)
        )
        gate_part = jnp.einsum("erd,edf->erf", rows, gate_w, preferred_element_type=F32)
        up_part = jnp.einsum("erd,edf->erf", rows, up_w, preferred_element_type=F32)
        hidden = (gate_part * jax.nn.sigmoid(gate_part) * up_part).astype(BF16)
        produced = jnp.einsum("erf,efd->erd", hidden, down_w, preferred_element_type=F32)
        total = jnp.einsum(
            "btr,brd->btd",
            back_probs,
            from_experts(produced.astype(BF16)),
            preferred_element_type=F32,
        ).astype(BF16)
        states.append(
            (
                stream, factor_one, normed_one, queries, keys, values, logs, mixed, middle,
                factor_two, own_two, own_probs, row_probs, rows, gate_part, up_part, hidden,
                gate_w, up_w, down_w,
            )
        )
        stream = middle + scatter_group(total, planes, 1)

    result = exchange(stream.astype(BF16))[None]

    upstream = upstream_low.astype(F32)
    dense_out, expert_out, small_out = [None] * layers, [None] * layers, [None] * layers
    for layer in reversed(range(layers)):
        (
            stream, factor_one, normed_one, queries, keys, values, logs, mixed, middle,
            factor_two, own_two, own_probs, row_probs, rows, gate_part, up_part, hidden,
            gate_w, up_w, down_w,
        ) = states[layer]
        attn_row, ffn_row = gains[layer, :, 0], gains[layer, :, 1]
        arrived = gather_group(upstream.astype(BF16), planes)
        out_rows_grad = to_experts(
            jnp.einsum(
                "brt,btd->brd", row_probs.astype(BF16), arrived, preferred_element_type=F32
            ).astype(BF16)
        )
        hidden_grad = jnp.einsum("erd,efd->erf", out_rows_grad, down_w, preferred_element_type=F32)
        down_term = jnp.einsum("erf,erd->efd", hidden, out_rows_grad, preferred_element_type=F32)
        weighted = jnp.sum(hidden.astype(F32) * hidden_grad, axis=-1)
        logistic = jax.nn.sigmoid(gate_part)
        gate_low = (
            hidden_grad * up_part * logistic * (1.0 + gate_part * (1.0 - logistic))
        ).astype(BF16)
        up_low = (hidden_grad * gate_part * logistic).astype(BF16)
        gate_term = jnp.einsum("erd,erf->edf", rows, gate_low, preferred_element_type=F32)
        up_term = jnp.einsum("erd,erf->edf", rows, up_low, preferred_element_type=F32)
        rows_grad = jnp.einsum("erf,edf->erd", gate_low, gate_w, preferred_element_type=F32)
        rows_grad = (
            rows_grad + jnp.einsum("erf,edf->erd", up_low, up_w, preferred_element_type=F32)
        ).astype(BF16)
        row_sums = jnp.einsum(
            "btr,brd->btd", back_ones, from_experts(rows_grad), preferred_element_type=F32
        ).astype(BF16)
        by_row = jnp.moveaxis(weighted.reshape(local, seq_count, slots), 1, 0)
        by_token = jnp.sum(jnp.where(spread, by_row[:, None], 0.0), axis=-1)
        extra = jnp.zeros((seq_count, count, 64), F32)
        extra = lax.dynamic_update_slice_in_dim(extra, by_token, place * local, axis=2)
        high = extra.astype(BF16)
        rest = (extra - high.astype(F32)).astype(BF16)
        summed = scatter_group(
            jnp.concatenate([row_sums, high, rest], axis=2), planes, 2
        )
        weighted = summed[:, width : width + experts_all]
        weighted = weighted + summed[:, width + 64 : width + 64 + experts_all]
        logit_grad = weighted - own_probs * jnp.sum(weighted, axis=-1, keepdims=True)
        router_term = jnp.einsum("td,te->ed", own_two.astype(F32), logit_grad, precision=HIGHEST)
        normed_two_grad = summed[:, :width] + jnp.einsum(
            "te,de->td", logit_grad, router_full[layer].astype(F32), precision=HIGHEST
        )
        ffn_gain_term = jnp.sum(normed_two_grad * middle * factor_two, axis=0)
        middle_grad = upstream + norm_back(middle, factor_two, ffn_row, normed_two_grad)
        branch_low = gather_plane(middle_grad.astype(BF16)).reshape(length, width)
        out_term = jnp.einsum("tc,td->cd", mixed, branch_low, preferred_element_type=F32)
        mixed_grad = jnp.einsum(
            "td,cd->tc", branch_low, out_rows[layer], preferred_element_type=F32
        ).astype(BF16)
        query_grad, key_grad, value_grad = attend_back(
            queries, keys, values, documents, logs, mixed_grad.reshape(length, heads, HEAD_SIZE)
        )
        query_grad = query_grad.reshape(length, columns)
        low = jnp.concatenate(
            [
                rotate(query_grad.astype(F32), cosine, -sine).astype(BF16),
                rotate(key_grad.astype(F32), cosine, -sine).astype(BF16),
                value_grad,
            ],
            axis=1,
        )
        qkv_term = jnp.einsum("td,tc->dc", normed_one, low, preferred_element_type=F32)
        partial = jnp.einsum(
            "tc,dc->td", low, qkv_weight[layer], preferred_element_type=F32
        ).astype(BF16)
        normed_one_grad = scatter_plane(partial.reshape(8, count, width))
        attn_gain_term = jnp.sum(normed_one_grad * stream * factor_one, axis=0)
        upstream = middle_grad + norm_back(stream, factor_one, attn_row, normed_one_grad)

        expert_out[layer] = (
            lax.psum_scatter(
                gate_term.astype(BF16), ("grp", "xh", "co"), scatter_dimension=1, tiled=True
            ).astype(F32),
            lax.psum_scatter(
                up_term.astype(BF16), ("grp", "xh", "co"), scatter_dimension=1, tiled=True
            ).astype(F32),
            lax.psum_scatter(
                down_term.astype(BF16), ("grp", "xh", "co"), scatter_dimension=2, tiled=True
            ).astype(F32),
        )
        wide = qkv_term.astype(BF16).reshape(planes, 2, groups, 4, bands, columns + 2 * kv)
        wide = jnp.transpose(wide, (0, 2, 3, 1, 4, 5)).reshape(
            planes * groups, 8, bands, columns + 2 * kv
        )
        wide = lax.psum_scatter(wide, ("za", "grp"), scatter_dimension=0)
        wide = lax.all_to_all(wide, ("xh", "co", "yb"), 0, 0)
        tall = out_term.astype(BF16).reshape(groups, 4, bands, width)
        tall = lax.all_to_all(jnp.moveaxis(tall, 1, 0), ("xh", "co"), 0, 0)
        tall = lax.psum_scatter(
            tall.reshape(planes * groups, bands, width), ("za", "grp"), scatter_dimension=0
        )
        dense_out[layer] = (
            jnp.moveaxis(wide[..., :columns], 0, 1).reshape(bands, -1).astype(F32),
            jnp.moveaxis(wide[..., columns : columns + kv], 0, 1).reshape(bands, -1).astype(F32),
            jnp.moveaxis(wide[..., columns + kv :], 0, 1).reshape(bands, -1).astype(F32),
            tall.astype(F32),
        )
        small_out[layer] = jnp.concatenate(
            [router_term, attn_gain_term[None], ffn_gain_term[None]], axis=0
        )

    rest = jnp.stack(small_out)
    kinds = rest.shape[1]
    rest = jnp.moveaxis(rest.reshape(layers, kinds, width // bands, bands), 2, 0)
    rest = lax.psum_scatter(
        rest.reshape(width // bands, layers * kinds, bands),
        ("za", "yb", "grp", "xh", "co"),
        scatter_dimension=0,
    ).reshape(layers, kinds, bands)

    def stacked(lists, i):
        return jnp.stack([lists[layer][i] for layer in range(layers)])

    return (
        result,
        exchange(upstream)[None],
        rest[:, experts_all],
        rest[:, experts_all + 1],
        stacked(dense_out, 0),
        stacked(dense_out, 1),
        stacked(dense_out, 2),
        stacked(dense_out, 3),
        jnp.moveaxis(rest[:, :experts_all], 1, 2),
        stacked(expert_out, 0),
        stacked(expert_out, 1),
        stacked(expert_out, 2),
    )


def solution(mesh):
    seq, fsdp = mesh.shape["seq"], mesh.shape["fsdp"]
    split = Mesh(mesh.devices.reshape(seq // 2, 2, fsdp // 4, 2, 2), AX)
    s, f = ("za", "yb"), ("grp", "xh", "co")
    token = P(f, s, None)
    dense = P(None, s + f, None)
    gain = P(None, s + f)
    wide, tall = P(None, s, f, None), P(None, s, None, f)
    return jax.shard_map(
        per_device,
        mesh=split,
        in_specs=(token, token, P(f, None), token, gain, gain, dense, dense, dense, dense, dense, wide, wide, tall),
        out_specs=(token, token, gain, gain, dense, dense, dense, dense, dense, wide, wide, tall),
        check_vma=False,
    )
```

time: 2850 us -> 1390 us (0.49)
  waiting for transfers between devices: 1630 us -> 299 us
  Pallas kernels: 0 us -> 460 us
  blocking collectives: 399 us -> 63.6 us
  local copies, waits for them, and re-layouts: 362 us -> 147 us
  matrix products: 235 us -> 192 us
    reduce_scatter x12 -> x9, waiting for transfers between devices: 907 us -> 209 us  [the longest x2 97.3 us: per_device(): lax.psum_scatter(gate_term.astype(BF16), ('grp', 'xh', 'co'), scatter_dim...]
    all_to_all x17 -> x3, waiting for transfers between devices: 569 us -> 5.95 us  [the longest x2 5.94 us: per_device(): wide = lax.all_to_all(wide, ('xh', 'co', 'yb'), 0, 0)]
    pallas_call x0 -> x16, Pallas kernels: none -> 460 us  [the longest x4 128 us: gather_group(): pl.pallas_call(kernel, out_shape=jax.ShapeDtypeStruct((2 * planes, count,...]
    all_gather x2 -> x1, blocking collectives: 177 us -> 23.9 us  [per_device(): lax.all_gather(jnp.where(named > 0, rank, -1.0).astype(BF16), ('za', 'yb'))]
    all_gather x14 -> x8, waiting for transfers between devices: 152 us -> 0.01 us  [the longest x2 0.01 us: fetch_experts(): lax.all_gather(gate_weight[layer], ('grp', 'xh', 'co'), axis=1, tiled=True)]
    all_to_all x3, blocking collectives: 141 us -> 39.7 us  [the longest x2 25.5 us: per_device(): tall = lax.all_to_all(jnp.moveaxis(tall, 1, 0), ('xh', 'co'), 0, 0)]
    reshape x22 -> x10, local copies, waits for them, and re-layouts: 112 us -> 11.5 us  [the longest x2 5.28 us: to_experts(): shaped = rows.reshape(seq_count, local, slots, -1)]
    gather x12 -> x0, local copies, waits for them, and re-layouts: 94.9 us -> none  [the longest x4 29.1 us: backward_layer(): upstream_padded[entries // top_count]]
  transfers between devices with their start and end apart: 47 -> 28, of which waited for: 24 -> 8; matrix products, arithmetic and copies ran while one was open for 20% -> 17% of each run, Pallas kernels for 0% -> 18%
where the time goes in v1:
time: 1390 us; the launch traced here: 1380 us
  Pallas kernels  460 us (33%)
  waiting for transfers between devices  299 us (22%)
  matrix products  192 us (14%)
  local copies, waits for them, and re-layouts  147 us (11%)
  starting transfers between devices  133 us (10%)
  blocking collectives  63.6 us (5%)
  other arithmetic  63.3 us (5%)
  between operations  16.9 us (1%)
    pallas_call x4, Pallas kernels, gather_group(): pl.pallas_call(kernel, out_shape=jax.ShapeDtypeStruct((2 * planes, count,...  128 us
    pallas_call x4, Pallas kernels, scatter_group(): pl.pallas_call(kernel, out_shape=jax.ShapeDtypeStruct((count, width), F32...  128 us
    pallas_call x4, Pallas kernels, gather_plane(): pl.pallas_call(kernel, out_shape=jax.ShapeDtypeStruct((8, count, width),...  116 us
    reduce_scatter x2, waiting for transfers between devices, per_device(): lax.psum_scatter(gate_term.astype(BF16), ('grp', 'xh', 'co'), scatter_dim...  97.3 us
    reduce_scatter x2, waiting for transfers between devices, per_device(): lax.psum_scatter(up_term.astype(BF16), ('grp', 'xh', 'co'), scatter_dimen...  92.1 us
    pallas_call x4, Pallas kernels, scatter_plane(): pl.pallas_call(kernel, out_shape=jax.ShapeDtypeStruct((count, width), F32...  88.1 us
    unnamed x21, waiting for transfers between devices  84.6 us
    unnamed x327, local copies, waits for them, and re-layouts  83 us
  transfers between devices with their start and end apart: 28, of which 8 were waited for; matrix products, arithmetic and copies ran while one was open for 17% of the time, Pallas kernels for 18%

profile of v1, /device:TPU:9, one launch (start us, length us, event | category | flops | bytes accessed | tf_op | source)
XLA Modules:
  0.0 1376.1 jit_solution(8560398241496305737)
XLA Ops:
  14.0 14.2 %all_to_all.30 = bf16[8,2,48,346]{3,2,1,0:T(8,128)(2,1)} all-to-all(bf16[8,2,48,346]{3,2,1,0:T(8,128)(2,1)S(1)} %copy.454), channel_id=1, replica_groups=mesh['za'=4,'yb'=2,'grp'=1,'xh'=2,'co'=2] {'xh','co','yb'}, dimensions={0} | all-to-all | bytes 1062912 | tf_op jit(solution)/shard_map/all_to_all | solution.py:413
  51.5 48.1 %all-to-all-start.1 = ((bf16[4,1,2,48,1536]{4,3,2,1,0:T(8,128)(2,1)}), bf16[4,1,2,48,1536]{4,3,2,1,0:T(8,128)(2,1)}, u32[]{:S(2)}, u32[]{:S(2)}) async-start(bf16[4,1,2,48,1536]{4,3,2,1,0:T(8,128)(2,1)} %bitcast.632), calls=%async_computation.1 | async-start | bytes 2359296 | tf_op jit(solution)/shard_map/all_to_all | solution.py:421
  99.7 23.9 %all-gather.2 = bf16[1024,24]{0,1:T(8,128)(2,1)S(1)} all-gather(bf16[128,24]{0,1:T(8,128)(2,1)S(1)} %select_convert_fusion), channel_id=4, replica_groups=mesh['za'=4,'yb'=2,'grp'=1,'xh'=2,'co'=2] {'za','yb'}, dimensions={0}, use_global_device_ids=true | all-gather | bytes 55296 | tf_op jit(solution)/shard_map/all_gather | solution.py:439
  124.3 30.9 %gather_group.6 = bf16[8,128,1536]{2,1,0:T(8,128)(2,1)S(1)} custom-call(bf16[128,1536]{1,0:T(8,128)(2,1)S(1)} %collective-permute-done.4.x_ref), custom_call_target="tpu_custom_call" | custom-call | tf_op jit(solution)/shard_map/gather_group/pallas_call | solution.py:156
  164.2 40.9 %gather_plane.4 = bf16[8,128,1536]{2,1,0:T(8,128)(2,1)S(1)} custom-call(bf16[128,1536]{1,0:T(8,128)(2,1)S(1)} %fusion.124.x_ref), custom_call_target="tpu_custom_call" | custom-call | tf_op jit(solution)/shard_map/gather_plane/pallas_call | solution.py:205
  217.8 31.7 %scatter_plane.4 = f32[128,1536]{1,0:T(8,128)S(1)} custom-call(bf16[8,128,1536]{2,1,0:T(8,128)(2,1)S(1)} %bitcast.534), custom_call_target="tpu_custom_call" | custom-call | tf_op jit(solution)/shard_map/scatter_plane/pallas_call | solution.py:257
  251.4 33.3 %gather_group.4 = bf16[8,128,1536]{2,1,0:T(8,128)(2,1)S(1)} custom-call(bf16[128,1536]{1,0:T(8,128)(2,1)S(1)} %multiply_convert_fusion.8.x_ref), custom_call_target="tpu_custom_call" | custom-call | tf_op jit(solution)/shard_map/gather_group/pallas_call | solution.py:156
  294.1 8.1 fusion.30
  302.2 9.8 multiply_convert_fusion.5
  312.0 5.5 fusion.32
  319.6 31.7 %scatter_group.4 = f32[128,1536]{1,0:T(8,128)S(1)} custom-call(bf16[8,128,1536]{2,1,0:T(8,128)(2,1)S(1)} %convolution_convert_fusion.12.p_ref), custom_call_target="tpu_custom_call" | custom-call | tf_op jit(solution)/shard_map/scatter_group/pallas_call | solution.py:179
  352.2 32.6 %gather_plane.5 = bf16[8,128,1536]{2,1,0:T(8,128)(2,1)S(1)} custom-call(bf16[128,1536]{1,0:T(8,128)(2,1)S(1)} %multiply_convert_fusion.7.x_ref), custom_call_target="tpu_custom_call" | custom-call | tf_op jit(solution)/shard_map/gather_plane/pallas_call | solution.py:205
  395.3 18.7 %scatter_plane.5 = f32[128,1536]{1,0:T(8,128)S(1)} custom-call(bf16[8,128,1536]{2,1,0:T(8,128)(2,1)S(1)} %bitcast.535), custom_call_target="tpu_custom_call" | custom-call | tf_op jit(solution)/shard_map/scatter_plane/pallas_call | solution.py:257
  415.4 32.0 %gather_group.5 = bf16[8,128,1536]{2,1,0:T(8,128)(2,1)S(1)} custom-call(bf16[128,1536]{1,0:T(8,128)(2,1)S(1)} %multiply_convert_fusion.6.x_ref), custom_call_target="tpu_custom_call" | custom-call | tf_op jit(solution)/shard_map/gather_group/pallas_call | solution.py:156
  460.5 8.1 fusion.19
  468.6 8.0 fusion.15
  476.6 10.8 multiply_reduce_fusion.1
  492.6 31.3 %scatter_group.5 = f32[128,1536]{1,0:T(8,128)S(1)} custom-call(bf16[8,128,1536]{2,1,0:T(8,128)(2,1)S(1)} %convolution_convert_fusion.10.p_ref), custom_call_target="tpu_custom_call" | custom-call | tf_op jit(solution)/shard_map/scatter_group/pallas_call | solution.py:179
  548.6 32.5 %scatter_group.6 = f32[128,1664]{1,0:T(8,128)S(1)} custom-call(bf16[8,128,1664]{2,1,0:T(8,128)(2,1)S(1)} %concatenate.143.p_ref), custom_call_target="tpu_custom_call" | custom-call | tf_op jit(solution)/shard_map/scatter_group/pallas_call | solution.py:179
  588.7 21.4 %gather_plane.6 = bf16[8,128,1536]{2,1,0:T(8,128)(2,1)S(1)} custom-call(bf16[128,1536]{1,0:T(8,128)(2,1)S(1)} %get-tuple-element.158.x_ref), custom_call_target="tpu_custom_call" | custom-call | tf_op jit(solution)/shard_map/gather_plane/pallas_call | solution.py:205
  629.0 18.8 %scatter_plane.6 = f32[128,1536]{1,0:T(8,128)S(1)} custom-call(bf16[8,128,1536]{2,1,0:T(8,128)(2,1)S(1)} %bitcast.545), custom_call_target="tpu_custom_call" | custom-call | tf_op jit(solution)/shard_map/scatter_plane/pallas_call | solution.py:257
  649.8 32.0 %gather_group.7 = bf16[8,128,1536]{2,1,0:T(8,128)(2,1)S(1)} custom-call(bf16[128,1536]{1,0:T(8,128)(2,1)S(1)} %get-tuple-element.156.x_ref), custom_call_target="tpu_custom_call" | custom-call | tf_op jit(solution)/shard_map/gather_group/pallas_call | solution.py:156
  687.6 6.2 multiply_convert_fusion
  703.1 5.3 add_convert_fusion
  716.8 32.0 %scatter_group.7 = f32[128,1664]{1,0:T(8,128)S(1)} custom-call(bf16[8,128,1664]{2,1,0:T(8,128)(2,1)S(1)} %concatenate.148.p_ref), custom_call_target="tpu_custom_call" | custom-call | tf_op jit(solution)/shard_map/scatter_group/pallas_call | solution.py:179
  752.6 21.5 %gather_plane.7 = bf16[8,128,1536]{2,1,0:T(8,128)(2,1)S(1)} custom-call(bf16[128,1536]{1,0:T(8,128)(2,1)S(1)} %get-tuple-element.152.x_ref), custom_call_target="tpu_custom_call" | custom-call | tf_op jit(solution)/shard_map/gather_plane/pallas_call | solution.py:205
  800.9 18.9 %scatter_plane.7 = f32[128,1536]{1,0:T(8,128)S(1)} custom-call(bf16[8,128,1536]{2,1,0:T(8,128)(2,1)S(1)} %bitcast.544), custom_call_target="tpu_custom_call" | custom-call | tf_op jit(solution)/shard_map/scatter_plane/pallas_call | solution.py:257
  841.4 12.9 all_to_all.31
  856.1 12.6 all_to_all.32
  874.7 6.5 convolution_convert_fusion.3
  881.2 10.9 copy.563
  892.1 6.9 copy.577
  900.5 7.0 convolution_convert_fusion.2
  907.4 10.9 copy.565
  918.3 6.9 copy.578
  926.7 7.3 convolution_convert_fusion.5
  935.5 7.4 convolution_convert_fusion.4
  944.2 7.3 convolution_convert_fusion.7
  953.0 7.3 convolution_convert_fusion.6
  966.9 72.1 %all-to-all-start.2 = ((bf16[8,48,320]{2,1,0:T(8,128)(2,1)}), bf16[8,48,320]{2,1,0:T(8,128)(2,1)S(1)}, u32[]{:S(2)}, u32[]{:S(2)}) async-start(bf16[8,48,320]{2,1,0:T(8,128)(2,1)} %bitcast.645), calls=%async_computation.4 | async-start | bytes 589824 | tf_op jit(solution)/shard_map/all_to_all | solution.py:612
  1040.9 19.3 %reduce-scatter.20.cloned.1.call-done = bf16[1,8,48,320]{3,2,1,0:T(8,128)(2,1)} async-done(((bf16[4,8,48,320]{3,2,1,0:T(8,128)(2,1)}), bf16[1,8,48,320]{3,2,1,0:T(8,128)(2,1)}) %reduce-scatter.20.cloned.1.call-update) | async-done | bytes 245776 | tf_op jit(solution)/shard_map/reduce_scatter | solution.py:611
  1064.8 5.9 all-to-all-done.3
  1074.1 37.0 %reduce-scatter.34.cloned.1.call-done = bf16[384,1536]{1,0:T(8,128)(2,1)} async-done(((bf16[1536,1536]{1,0:T(8,128)(2,1)}), bf16[384,1536]{1,0:T(8,128)(2,1)}) %reduce-scatter.34.cloned.1.call-update) | async-done | bytes 1179664
  1115.0 46.6 %reduce-scatter.36.cloned.1.call-done = bf16[384,1536]{1,0:T(8,128)(2,1)} async-done(((bf16[1536,1536]{1,0:T(8,128)(2,1)}), bf16[384,1536]{1,0:T(8,128)(2,1)}) %reduce-scatter.36.cloned.1.call-update) | async-done | bytes 1179664
  1170.1 41.7 %reduce-scatter.30.cloned.1.call-done = bf16[3,384,512]{2,1,0:T(8,128)(2,1)} async-done(((bf16[3,1536,512]{2,1,0:T(8,128)(2,1)}), bf16[3,384,512]{2,1,0:T(8,128)(2,1)}) %reduce-scatter.30.cloned.1.call-update) | async-done | bytes 1179664 | tf_op jit(solution)/shard_map/reduce_scatter | solution.py:600
  1211.8 50.4 %reduce-scatter.32.cloned.1.call-done = bf16[3,384,512]{2,1,0:T(8,128)(2,1)} async-done(((bf16[3,1536,512]{2,1,0:T(8,128)(2,1)}), bf16[3,384,512]{2,1,0:T(8,128)(2,1)}) %reduce-scatter.32.cloned.1.call-update) | async-done | bytes 1179664 | tf_op jit(solution)/shard_map/reduce_scatter | solution.py:600
  1266.3 46.1 %reduce-scatter.26.cloned.1.call-done = bf16[3,384,512]{2,1,0:T(8,128)(2,1)} async-done(((bf16[3,1536,512]{2,1,0:T(8,128)(2,1)}), bf16[3,384,512]{2,1,0:T(8,128)(2,1)}) %reduce-scatter.26.cloned.1.call-update) | async-done | bytes 1179664 | tf_op jit(solution)/shard_map/reduce_scatter | solution.py:597
  1312.4 51.1 %reduce-scatter.28.cloned.1.call-done = bf16[3,384,512]{2,1,0:T(8,128)(2,1)} async-done(((bf16[3,1536,512]{2,1,0:T(8,128)(2,1)}), bf16[3,384,512]{2,1,0:T(8,128)(2,1)}) %reduce-scatter.28.cloned.1.call-update) | async-done | bytes 1179664 | tf_op jit(solution)/shard_map/reduce_scatter | solution.py:597
  (620 shorter events, 276.8 us)
Async XLA Ops:
  7.2 44.3 %all-gather.20.cloned.1.call-start = ((), (), s32[]{:S(2)}) async-start(), calls=%async_computation.27 | async-start | bytes 1474560 | tf_op jit(solution)/shard_map/all_gather | solution.py:420
  7.9 151.3 %all-gather.18.cloned.1.call-start = ((), (), s32[]{:S(2)}) async-start(), calls=%async_computation.26 | async-start | bytes 2949120 | tf_op jit(solution)/shard_map/all_gather | solution.py:414
  28.2 265.9 %all-gather.22.cloned.1.call-start = ((), (), s32[]{:S(2)}) async-start(), calls=%async_computation.28 | async-start | bytes 5898240 | tf_op jit(solution)/shard_map/all_gather | solution.py:428
  31.5 270.7 %all-gather.24.cloned.1.call-start = ((), (), s32[]{:S(2)}) async-start(), calls=%async_computation.29 | async-start | bytes 5898240 | tf_op jit(solution)/shard_map/all_gather | solution.py:429
  34.7 277.3 %all-gather.26.cloned.1.call-start = ((), (), s32[]{:S(2)}) async-start(), calls=%async_computation.30 | async-start | bytes 5898240 | tf_op jit(solution)/shard_map/all_gather | solution.py:430
  38.1 422.4 %all-gather.28.cloned.1.call-start = ((), (), s32[]{:S(2)}) async-start(), calls=%async_computation.31 | async-start | bytes 5898240 | tf_op jit(solution)/shard_map/all_gather | solution.py:428
  39.6 428.9 %all-gather.30.cloned.1.call-start = ((), (), s32[]{:S(2)}) async-start(), calls=%async_computation.32 | async-start | bytes 5898240 | tf_op jit(solution)/shard_map/all_gather | solution.py:429
  41.1 435.5 %all-gather.32.cloned.1.call-start = ((), (), s32[]{:S(2)}) async-start(), calls=%async_computation.33 | async-start | bytes 5898240 | tf_op jit(solution)/shard_map/all_gather | solution.py:430
  41.2 114.0 %collective-permute-start = (bf16[128,1536]{1,0:T(8,128)(2,1)}, bf16[128,1536]{1,0:T(8,128)(2,1)}, u32[]{:S(2)}, u32[]{:S(2)}) collective-permute-start(bf16[128,1536]{1,0:T(8,128)(2,1)} %bitcast), channel_id=1, source_target_pairs={{0,0},{1,8},{2,16},{3,24},{8,1},{9,9},{10,17},{11,25},{16,2},{17,1... | collective-permute-start | bytes 1179656 | tf_op jit(solution)/shard_map/ppermute | solution.py:392
  45.7 3.6 collective-permute-start.1
  46.3 53.2 %collective-permute-start.2 = (s32[128,8]{0,1:T(8,128)S(1)}, s32[128,8]{0,1:T(8,128)S(1)}, u32[]{:S(2)}, u32[]{:S(2)}) collective-permute-start(s32[128,8]{0,1:T(8,128)S(1)} %bitcast.663), channel_id=1, source_target_pairs={{0,0},{1,8},{2,16},{3,24},{8,1},{9,9},{10,17},{11,25},{16,2},{17,1... | collective-permute-start | bytes 12296 | tf_op jit(solution)/shard_map/ppermute | solution.py:392
  47.0 77.3 %collective-permute-start.4 = (bf16[128,1536]{1,0:T(8,128)(2,1)S(1)}, bf16[128,1536]{1,0:T(8,128)(2,1)S(1)}, u32[]{:S(2)}, u32[]{:S(2)}) collective-permute-start(bf16[128,1536]{1,0:T(8,128)(2,1)S(1)} %bitcast.662), channel_id=1, source_target_pairs={{0,0},{1,8},{2,16},{3,24},{8,1},{9,9},{10,17},{11,25},{16,2},{17,1... | collective-permute-start | bytes 1179656 | tf_op jit(solution)/shard_map/ppermute | solution.py:392
  47.7 159.1 %copy-start.91 = (f32[1024]{0:T(1024)}, f32[1024]{0:T(1024)S(1)}, u32[]{:S(2)}) copy-start(f32[1024]{0:T(1024)S(1)} %iota_convert_fusion) | copy-start | bytes 12292
  47.8 159.1 %copy-start.116 = (f32[32]{0:T(128)}, f32[32]{0:T(128)S(1)}, u32[]{:S(2)}) copy-start(f32[32]{0:T(128)S(1)} %multiply_power_fusion) | copy-start | bytes 388
  47.8 76.5 %copy-start.127 = (f32[64]{0:T(128)}, f32[64]{0:T(128)S(1)}, u32[]{:S(2)}) copy-start(f32[64]{0:T(128)S(1)} %iota_convert_fusion.1) | copy-start | bytes 772
  47.9 238.8 %copy-start.111 = (f32[192]{0:T(256)}, f32[192]{0:T(256)S(1)}, u32[]{:S(2)}) copy-start(f32[192]{0:T(256)S(1)} %eq.147) | copy-start | bytes 2308
  51.5 105.4 %all-to-all-start.1 = ((bf16[4,1,2,48,1536]{4,3,2,1,0:T(8,128)(2,1)}), bf16[4,1,2,48,1536]{4,3,2,1,0:T(8,128)(2,1)}, u32[]{:S(2)}, u32[]{:S(2)}) async-start(bf16[4,1,2,48,1536]{4,3,2,1,0:T(8,128)(2,1)} %bitcast.632), calls=%async_computation.1 | async-start | bytes 2359296 | tf_op jit(solution)/shard_map/all_to_all | solution.py:421
  99.6 865.3 %reduce-scatter.16.cloned.1.call-start = ((), (), s32[]{:S(2)}) async-start(), calls=%async_computation.17 | async-start | bytes 811008 | tf_op jit(solution)/shard_map/reduce_scatter | solution.py:631
  124.3 35.0 %copy-start.13 = (bf16[128,1536]{1,0:T(8,128)(2,1)}, bf16[128,1536]{1,0:T(8,128)(2,1)S(1)}, u32[]{:S(2)}) copy-start(bf16[128,1536]{1,0:T(8,128)(2,1)S(1)} %collective-permute-done.4.x_ref) | copy-start | bytes 1179652
  161.3 123.5 %copy-start.27 = (bf16[2,4,2,1,4,48,346]{6,5,4,2,1,0,3:T(8,128)(2,1)}, bf16[2,4,2,1,4,48,346]{6,5,4,2,1,0,3:T(8,128)(2,1)S(1)}, u32[]{:S(2)}) copy-start(bf16[2,4,2,1,4,48,346]{6,5,4,2,1,0,3:T(8,128)(2,1)S(1)} %copy.455) | copy-start | bytes 6377476
  163.1 43.3 %copy-start.95 = (f32[1536]{0:T(1024)}, f32[1536]{0:T(1024)S(1)}, u32[]{:S(2)}) copy-start(f32[1536]{0:T(1024)S(1)} %get-tuple-element.149) | copy-start | bytes 18436
  163.1 88.2 %copy-start.97 = (f32[1536]{0:T(1024)}, f32[1536]{0:T(1024)S(1)}, u32[]{:S(2)}) copy-start(f32[1536]{0:T(1024)S(1)} %get-tuple-element.148) | copy-start | bytes 18436
  249.5 35.3 %copy-start.63 = (pred[8,128,24]{1,0,2:T(8,128)(4,1)S(1)}, pred[8,128,24]{1,0,2:T(8,128)(4,1)}, u32[]{:S(2)}) copy-start(pred[8,128,24]{1,0,2:T(8,128)(4,1)} %broadcast_compare_fusion) | copy-start | bytes 73732
  250.7 35.1 %copy-start.21 = (f32[128,1536]{1,0:T(8,128)}, f32[128,1536]{1,0:T(8,128)S(1)}, u32[]{:S(2)}) copy-start(f32[128,1536]{1,0:T(8,128)S(1)} %get-tuple-element.169) | copy-start | bytes 2359300
  251.3 33.5 %copy-start.120 = (f32[128]{0:T(128)}, f32[128]{0:T(128)S(1)}, u32[]{:S(2)}) copy-start(f32[128]{0:T(128)S(1)} %get-tuple-element.222) | copy-start | bytes 1540
  251.4 34.4 %copy-start.5 = (bf16[128,1536]{1,0:T(8,128)(2,1)}, bf16[128,1536]{1,0:T(8,128)(2,1)S(1)}, u32[]{:S(2)}) copy-start(bf16[128,1536]{1,0:T(8,128)(2,1)S(1)} %multiply_convert_fusion.8.x_ref) | copy-start | bytes 1179652
  351.3 33.6 %copy-start.28 = (bf16[2,4,2,1,4,48,346]{6,5,4,2,1,0,3:T(8,128)(2,1)S(1)}, bf16[2,4,2,1,4,48,346]{6,5,4,2,1,0,3:T(8,128)(2,1)}, u32[]{:S(2)}) copy-start(bf16[2,4,2,1,4,48,346]{6,5,4,2,1,0,3:T(8,128)(2,1)} %copy-done.27) | copy-start | bytes 6377476
  351.5 62.5 %copy-start.24 = (f32[128,1536]{1,0:T(8,128)}, f32[128,1536]{1,0:T(8,128)S(1)}, u32[]{:S(2)}) copy-start(f32[128,1536]{1,0:T(8,128)S(1)} %get-tuple-element.167) | copy-start | bytes 2359300
  414.2 34.3 %copy-start.26 = (f32[128,1536]{1,0:T(8,128)}, f32[128,1536]{1,0:T(8,128)S(1)}, u32[]{:S(2)}) copy-start(f32[128,1536]{1,0:T(8,128)S(1)} %get-tuple-element.165) | copy-start | bytes 2359300
  415.4 33.2 %copy-start.113 = (f32[192]{0:T(256)S(1)}, f32[192]{0:T(256)}, u32[]{:S(2)}) copy-start(f32[192]{0:T(256)} %copy-done.111) | copy-start | bytes 2308
  487.4 49.8 %copy-start.38 = (bf16[3,512,512]{1,2,0:T(8,128)(2,1)}, bf16[3,512,512]{1,2,0:T(8,128)(2,1)S(1)}, u32[]{:S(2)}) copy-start(bf16[3,512,512]{1,2,0:T(8,128)(2,1)S(1)} %get-tuple-element.173) | copy-start | bytes 4718596
  648.6 33.2 %copy-start.58 = (bf16[8,192,128]{2,1,0:T(8,128)(2,1)S(1)}, bf16[8,192,128]{2,1,0:T(8,128)(2,1)}, u32[]{:S(2)}) copy-start(bf16[8,192,128]{2,1,0:T(8,128)(2,1)} %get-tuple-element.212) | copy-start | bytes 1179652
  716.8 34.7 %copy-start.37 = (f32[128,1536]{1,0:T(8,128)S(1)}, f32[128,1536]{1,0:T(8,128)}, u32[]{:S(2)}) copy-start(f32[128,1536]{1,0:T(8,128)} %get-tuple-element.157) | copy-start | bytes 2359300
  716.8 34.7 %copy-start.133 = (f32[128]{0:T(128)S(1)}, f32[128]{0:T(128)}, u32[]{:S(2)}) copy-start(f32[128]{0:T(128)} %get-tuple-element.221) | copy-start | bytes 1540
  832.2 134.7 %reduce-scatter.18.cloned.1.call-start = ((), (), s32[]{:S(2)}) async-start(), calls=%async_computation.18 | async-start | bytes 1474560 | tf_op jit(solution)/shard_map/reduce_scatter | solution.py:611
  838.5 200.5 %reduce-scatter.22.cloned.1.call-start = ((), (), s32[]{:S(2)}) async-start(), calls=%async_computation.20 | async-start | bytes 737280 | tf_op jit(solution)/shard_map/reduce_scatter | solution.py:615
  854.3 184.7 %reduce-scatter.24.cloned.1.call-start = ((), (), s32[]{:S(2)}) async-start(), calls=%async_computation.21 | async-start | bytes 737280 | tf_op jit(solution)/shard_map/reduce_scatter | solution.py:615
  868.8 191.3 %reduce-scatter.20.cloned.1.call-start = ((), (), s32[]{:S(2)}) async-start(), calls=%async_computation.19 | async-start | bytes 1474560 | tf_op jit(solution)/shard_map/reduce_scatter | solution.py:611
  874.0 237.1 %reduce-scatter.34.cloned.1.call-start = ((), (), s32[]{:S(2)}) async-start(), calls=%async_computation.34 | async-start | bytes 5898240
  899.1 262.4 %reduce-scatter.36.cloned.1.call-start = ((), (), s32[]{:S(2)}) async-start(), calls=%async_computation.35 | async-start | bytes 5898240
  925.3 286.5 %reduce-scatter.30.cloned.1.call-start = ((), (), s32[]{:S(2)}) async-start(), calls=%async_computation.24 | async-start | bytes 5898240 | tf_op jit(solution)/shard_map/reduce_scatter | solution.py:600
  934.0 328.2 %reduce-scatter.32.cloned.1.call-start = ((), (), s32[]{:S(2)}) async-start(), calls=%async_computation.25 | async-start | bytes 5898240 | tf_op jit(solution)/shard_map/reduce_scatter | solution.py:600
  942.9 369.6 %reduce-scatter.26.cloned.1.call-start = ((), (), s32[]{:S(2)}) async-start(), calls=%async_computation.22 | async-start | bytes 5898240 | tf_op jit(solution)/shard_map/reduce_scatter | solution.py:597
  951.6 412.0 %reduce-scatter.28.cloned.1.call-start = ((), (), s32[]{:S(2)}) async-start(), calls=%async_computation.23 | async-start | bytes 5898240 | tf_op jit(solution)/shard_map/reduce_scatter | solution.py:597
  961.3 2.8 collective-permute-start.3
  963.3 3.5 collective-permute-start.5
  966.9 93.3 %all-to-all-start.2 = ((bf16[8,48,320]{2,1,0:T(8,128)(2,1)}), bf16[8,48,320]{2,1,0:T(8,128)(2,1)S(1)}, u32[]{:S(2)}, u32[]{:S(2)}) async-start(bf16[8,48,320]{2,1,0:T(8,128)(2,1)} %bitcast.645), calls=%async_computation.4 | async-start | bytes 589824 | tf_op jit(solution)/shard_map/all_to_all | solution.py:612
  1060.2 10.5 all-to-all-start.3
  (134 other events, 845.7 us)
Sparse Core Ops, SparseCore 0:
  9.6 30.8 all-gather.19
  42.1 70.5 all-gather.17
  114.8 43.9 all-gather.21
  160.9 50.0 all-gather.23
  212.3 50.0 all-gather.25
  263.9 36.4 all-gather.27
  301.9 37.3 all-gather.29
  340.9 50.0 all-gather.31
  832.3 93.0 reduce-scatter.15
  927.5 28.0 reduce-scatter.17
  957.9 49.0 reduce-scatter.21
  1009.1 22.7 reduce-scatter.23
  1034.2 25.9 reduce-scatter.19
  1062.5 48.5 reduce-scatter.33
  1113.6 47.8 reduce-scatter.35
  1163.9 47.8 reduce-scatter.29
  1214.3 47.8 reduce-scatter.31
  1264.6 47.8 reduce-scatter.25
  1315.7 47.8 reduce-scatter.27

commit v2 on v1

--- a/solution.py
+++ b/solution.py
@@ -48,7 +48,7 @@
 def rcopy(src, dst, ss, rs, dev):
     return pltpu.make_async_remote_copy(src_ref=src, dst_ref=dst, send_sem=ss, recv_sem=rs, device_id=dev, device_id_type=MESH)
 
-def ag_ring(ring, K, own, out, send, recv, sib=None):
+def ag_ring(ring, K, own, out, send, recv, sib=None, beside=None):
     n=ring.n; S=n//2; T=own.shape[0]; rows=T//K; rho=ring.rho
     def chunks(d,s): return range(K) if s<S else (range(K//2) if d==0 else range(K//2,K))
     def mk(d,s,c):
@@ -80,6 +80,7 @@
                 if c in chunks(d,s):
                     if s>1: arrived(d,s-1,c)
                     cp=mk(d,s,c); cp.start(); sends.append(cp)
+        if beside is not None: beside(s)
         if s==1 and sib is not None:
             for c in range(K): sibcopy(ring.slot(rho), None, c, 0, own.at[pl.ds(c*rows,rows)])
     for s in (S-1,S):
@@ -142,7 +143,11 @@
     )
 
 
-def gather_group(rows, planes):
+def busy(microseconds):
+    return pl.CostEstimate(flops=0, bytes_accessed=microseconds * 3_690_000, transcendentals=0)
+
+
+def gather_group(rows, planes, number=0):
     count, width = rows.shape
 
     def kernel(x_ref, o_ref, send, recv, own):
@@ -159,7 +164,8 @@
         in_specs=[VMEM_SPEC],
         out_specs=ANY_SPEC,
         scratch_shapes=[DMA((2, planes, CHUNKS)), DMA((2, planes, CHUNKS)), DMA],
-        compiler_params=comm_params(0),
+        compiler_params=comm_params(number),
+        cost_estimate=busy(33),
         name="gather_group",
     )(rows)
 
@@ -187,6 +193,7 @@
             DMA((2, planes, CHUNKS)),
         ],
         compiler_params=comm_params(number),
+        cost_estimate=busy(32),
         name="scatter_group",
     )(parts)
 
@@ -215,6 +222,7 @@
             DMA,
         ],
         compiler_params=comm_params(3),
+        cost_estimate=busy(20),
         name="gather_plane",
     )(rows)
 
@@ -268,8 +276,661 @@
             DMA((4,)),
         ],
         compiler_params=comm_params(4),
+        cost_estimate=busy(20),
         name="scatter_plane",
     )(parts)
+
+
+def plane_peers():
+    x, c, b = lax.axis_index("xh"), lax.axis_index("co"), lax.axis_index("yb")
+    peers = []
+    for k in range(1, 8):
+        px = x + (k // 4) * (1 - 2 * x)
+        pc = c + (k // 2 % 2) * (1 - 2 * c)
+        pb = b + (k % 2) * (1 - 2 * b)
+        peers.append(
+            ({"xh": px, "co": pc, "yb": pb}, (px * 2 + pc) * 2 + pb, pb * 4 + px * 2 + pc)
+        )
+    return peers
+
+
+def own_places():
+    x, c, b = lax.axis_index("xh"), lax.axis_index("co"), lax.axis_index("yb")
+    return (x * 2 + c) * 2 + b, b * 4 + x * 2 + c
+
+
+def line_barrier(planes, devices):
+    za = lax.axis_index("za")
+    sem = pltpu.get_barrier_semaphore()
+    for device in devices:
+        pl.semaphore_signal(sem, inc=1, device_id=device, device_id_type=MESH)
+
+    @pl.when(za > 0)
+    def _():
+        pl.semaphore_signal(sem, inc=1, device_id={"za": za - 1}, device_id_type=MESH)
+
+    @pl.when(za < planes - 1)
+    def _():
+        pl.semaphore_signal(sem, inc=1, device_id={"za": za + 1}, device_id_type=MESH)
+
+    below, above = (za + planes - 1) // planes, (2 * planes - 2 - za) // planes
+    pl.semaphore_wait(sem, len(devices) + below + above)
+
+
+class LineGather:
+    def __init__(self, planes, stores, send, recv):
+        self.planes, self.stores, self.send, self.recv = planes, stores, send, recv
+        self.za = lax.axis_index("za")
+
+    def copy(self, i, d, s):
+        sign = 1 - 2 * d
+        block = self.za - (s - 1) * sign
+        return rcopy(
+            self.stores[i].at[block],
+            self.stores[i].at[block],
+            self.send.at[i, d, s - 1],
+            self.recv.at[i, d, s - 1],
+            {"za": self.za + sign},
+        )
+
+    def sends(self, d, s):
+        za, last = self.za, self.planes - 1
+        if d == 0:
+            return (za < last) & (za >= s - 1)
+        return (za > 0) & (za <= last - (s - 1))
+
+    def step(self, s):
+        for i in range(len(self.stores)):
+            for d in (0, 1):
+                if s > 1:
+                    self.wait_arrival(i, d, s - 1)
+
+                @pl.when(self.sends(d, s))
+                def _():
+                    self.copy(i, d, s).start()
+
+    def wait_arrival(self, i, d, s):
+        za, last, sign = self.za, self.planes - 1, 1 - 2 * d
+        has = (za >= s) if d == 0 else (za <= last - s)
+
+        @pl.when(has)
+        def _():
+            block = za - s * sign
+            ref = self.stores[i].at[block]
+            rcopy(
+                ref, ref, self.send.at[i, d, s - 1], self.recv.at[i, d, s - 1],
+                {"za": za - sign},
+            ).wait_recv()
+
+    def finish(self):
+        for i in range(len(self.stores)):
+            for d in (0, 1):
+                self.wait_arrival(i, d, self.planes - 1)
+        self.finish_sends()
+
+    def finish_sends(self):
+        for i in range(len(self.stores)):
+            for d in (0, 1):
+                for s in range(1, self.planes):
+
+                    @pl.when(self.sends(d, s))
+                    def _():
+                        self.copy(i, d, s).wait_send()
+
+
+def spread_first(pieces, planes):
+    _, layers, count, width = pieces.shape
+
+    def kernel(p_ref, a_ref, *refs):
+        later, (send, recv, own, z_send, z_recv) = refs[: layers - 1], refs[layers - 1 :]
+        za = lax.axis_index("za")
+        peers = plane_peers()
+        line_barrier(planes, [peer[0] for peer in peers])
+        group, place = own_places()
+        copies = []
+
+        def target(layer, at):
+            return a_ref.at[za, at] if layer == 0 else later[layer - 1].at[at]
+
+        for layer in range(layers):
+            for k, (device, their_group, _) in enumerate(peers):
+                copy = rcopy(
+                    p_ref.at[their_group, layer], target(layer, place),
+                    send.at[layer, k], recv.at[layer, k], device,
+                )
+                copy.start()
+                copies.append(copy)
+        locals_ = [
+            pltpu.make_async_copy(p_ref.at[group, layer], target(layer, place), own.at[layer])
+            for layer in range(layers)
+        ]
+        for copy in locals_:
+            copy.start()
+
+        def arrivals(layer):
+            for k, (device, _, their_place) in enumerate(peers):
+                ref = target(layer, their_place)
+                rcopy(ref, ref, send.at[layer, k], recv.at[layer, k], device).wait_recv()
+            locals_[layer].wait()
+
+        arrivals(0)
+        line = LineGather(planes, [a_ref], z_send, z_recv)
+        for s in range(1, planes):
+            line.step(s)
+            if s == 1:
+                for layer in range(1, layers):
+                    arrivals(layer)
+        line.finish()
+        for copy in copies:
+            copy.wait_send()
+
+    return pl.pallas_call(
+        kernel,
+        out_shape=[jax.ShapeDtypeStruct((planes, 8, count, width), BF16)]
+        + [jax.ShapeDtypeStruct((8, count, width), BF16)] * (layers - 1),
+        in_specs=[VMEM_SPEC],
+        out_specs=[VMEM_SPEC] * layers,
+        scratch_shapes=[
+            DMA((layers, 7)),
+            DMA((layers, 7)),
+            DMA((layers,)),
+            DMA((1, 2, planes - 1)),
+            DMA((1, 2, planes - 1)),
+        ],
+        compiler_params=comm_params(5),
+        cost_estimate=busy(20),
+        name="spread_first",
+    )(pieces)
+
+
+def gather_plane_first(rows, later, out_weight, planes):
+    count, width = rows.shape
+    extra = len(later)
+
+    def kernel(x_ref, w_ref, *refs):
+        l_refs, refs = refs[:extra], refs[extra:]
+        o_ref, t_ref, refs = refs[0], refs[1], refs[2:]
+        s_refs, refs = refs[:extra], refs[extra:]
+        stage, send, recv, sib_send, sib_recv, own, put, z_send, z_recv, f_send, f_recv = refs
+        za = lax.axis_index("za")
+        x, c = lax.axis_index("xh"), lax.axis_index("co")
+        mine = x * 2 + c
+        ring = Ring4()
+        peers = plane_peers()
+        line_barrier(planes, [peer[0] for peer in peers])
+        puts = [
+            pltpu.make_async_copy(src, dst.at[za], put.at[i])
+            for i, (src, dst) in enumerate(
+                [(w_ref, stage)] + [(l_refs[i], s_refs[i]) for i in range(extra)]
+            )
+        ]
+        for copy in puts:
+            copy.start()
+        local = pltpu.make_async_copy(x_ref, o_ref.at[ring.slot(ring.rho)], own)
+        local.start()
+        line = LineGather(planes, [stage] + list(s_refs), z_send, z_recv)
+
+        def beside(turn):
+            if turn == 1:
+                for copy in puts:
+                    copy.wait()
+            line.step(turn)
+
+        ag_ring(ring, CHUNKS, x_ref, o_ref, send, recv, (sib_send, sib_recv), beside)
+        for turn in range(3, planes):
+            beside(turn)
+        local.wait()
+        for d in (0, 1):
+            line.wait_arrival(0, d, planes - 1)
+        copies = []
+        for k in (1, 2, 3):
+            px = x + (k // 2) * (1 - 2 * x)
+            pc = c + (k % 2) * (1 - 2 * c)
+            copies.append(
+                rcopy(
+                    stage.at[px * 2 + pc], t_ref.at[mine], f_send.at[k - 1], f_recv.at[k - 1],
+                    {"xh": px, "co": pc},
+                )
+            )
+            copies[-1].start()
+        keep = pltpu.make_async_copy(stage.at[mine], t_ref.at[mine], own)
+        keep.start()
+        keep.wait()
+        for k in (1, 2, 3):
+            px = x + (k // 2) * (1 - 2 * x)
+            pc = c + (k % 2) * (1 - 2 * c)
+            ref = t_ref.at[px * 2 + pc]
+            rcopy(ref, ref, f_send.at[k - 1], f_recv.at[k - 1], {"xh": px, "co": pc}).wait_recv()
+        for copy in copies:
+            copy.wait_send()
+        for i in range(1 + extra):
+            for d in (0, 1):
+                if i > 0:
+                    line.wait_arrival(i, d, planes - 1)
+        line.finish_sends()
+
+    return pl.pallas_call(
+        kernel,
+        out_shape=[
+            jax.ShapeDtypeStruct((8, count, width), BF16),
+            jax.ShapeDtypeStruct((4,) + out_weight.shape, BF16),
+        ]
+        + [jax.ShapeDtypeStruct((planes,) + array.shape, BF16) for array in later],
+        in_specs=[VMEM_SPEC] * (2 + extra),
+        out_specs=[ANY_SPEC] + [VMEM_SPEC] * (1 + extra),
+        scratch_shapes=[
+            pltpu.VMEM((planes,) + out_weight.shape, BF16),
+            DMA((2, 2, CHUNKS)),
+            DMA((2, 2, CHUNKS)),
+            DMA((4, CHUNKS)),
+            DMA((4, CHUNKS)),
+            DMA,
+            DMA((1 + extra,)),
+            DMA((1 + extra, 2, planes - 1)),
+            DMA((1 + extra, 2, planes - 1)),
+            DMA((3,)),
+            DMA((3,)),
+        ],
+        compiler_params=comm_params(6),
+        cost_estimate=busy(30),
+        name="gather_plane_first",
+    )(rows, out_weight, *later)
+
+
+def collect(wide, tall, planes):
+    layers = len(wide)
+    count, width = wide[0].shape[2:]
+    depth = tall[0].shape[2]
+
+    def kernel(*refs):
+        w_in, refs = refs[:layers], refs[layers:]
+        t_in, refs = refs[:layers], refs[layers:]
+        w_out, refs = refs[:layers], refs[layers:]
+        t_out, refs = refs[:layers], refs[layers:]
+        w_up, t_own, t_up, summed, own, f_send, f_recv, z_send, z_recv, p_send, p_recv = refs
+        za = lax.axis_index("za")
+        x, c = lax.axis_index("xh"), lax.axis_index("co")
+        mine = x * 2 + c
+        peers = plane_peers()
+        line_barrier(planes, [peer[0] for peer in peers])
+        group, place = own_places()
+        firsts, keeps = [], []
+        for l in range(layers):
+            for k in (1, 2, 3):
+                px = x + (k // 2) * (1 - 2 * x)
+                pc = c + (k % 2) * (1 - 2 * c)
+                copy = rcopy(
+                    t_in[l].at[px * 2 + pc], t_own.at[l, mine], f_send.at[l, k - 1],
+                    f_recv.at[l, k - 1], {"xh": px, "co": pc},
+                )
+                copy.start()
+                firsts.append(copy)
+            keep = pltpu.make_async_copy(t_in[l].at[mine], t_own.at[l, mine], own.at[l])
+            keep.start()
+            keeps.append(keep)
+
+        def arrive(l):
+            for k in (1, 2, 3):
+                px = x + (k // 2) * (1 - 2 * x)
+                pc = c + (k % 2) * (1 - 2 * c)
+                ref = t_own.at[l, px * 2 + pc]
+                rcopy(
+                    ref, ref, f_send.at[l, k - 1], f_recv.at[l, k - 1], {"xh": px, "co": pc}
+                ).wait_recv()
+            keeps[l].wait()
+
+        def parts(l, kind):
+            if kind == 0:
+                return w_in[l], w_up.at[l]
+            return t_own.at[l], t_up.at[l]
+
+        def along(l, kind, d, dest):
+            _, came = parts(l, kind)
+            ref = came.at[d, dest]
+            return ref, rcopy(
+                ref, ref, z_send.at[l, kind, d, dest], z_recv.at[l, kind, d, dest],
+                {"za": za + (1 - 2 * d)},
+            )
+
+        last = planes - 1
+        for kind in (0, 1):
+            if kind == 1:
+                for l in range(layers):
+                    arrive(l)
+            for far in range(last):
+                for l in reversed(range(layers)):
+                    for d in (0, 1):
+                        dest = last - far if d == 0 else far
+                        held, came = parts(l, kind)
+                        sends = (za < dest) if d == 0 else (za > dest)
+                        inner = (za > 0) if d == 0 else (za < last)
+                        ref, copy = along(l, kind, d, dest)
+
+                        @pl.when(sends & inner)
+                        def _():
+                            copy.wait_recv()
+                            came[d, dest] = (
+                                came[d, dest].astype(F32) + held[dest].astype(F32)
+                            ).astype(BF16)
+                            copy.start()
+
+                        @pl.when(sends & jnp.logical_not(inner))
+                        def _():
+                            rcopy(
+                                held.at[dest], ref, z_send.at[l, kind, d, dest],
+                                z_recv.at[l, kind, d, dest], {"za": za + (1 - 2 * d)},
+                            ).start()
+
+        def total(l, kind, result):
+            _, came = parts(l, kind)
+            for d in (0, 1):
+
+                @pl.when((za > 0) if d == 0 else (za < last))
+                def _():
+                    ref = came.at[d, za]
+                    rcopy(
+                        ref, ref, z_send.at[l, kind, d, za], z_recv.at[l, kind, d, za],
+                        {"za": za - (1 - 2 * d)},
+                    ).wait_recv()
+                    result[...] = (result[...].astype(F32) + came[d, za].astype(F32)).astype(BF16)
+
+        outs = []
+        for l in reversed(range(layers)):
+            summed[l] = w_in[l][za]
+            total(l, 0, summed.at[l])
+            for k, (device, _, their_place) in enumerate(peers):
+                copy = rcopy(
+                    summed.at[l, their_place], w_out[l].at[group], p_send.at[l, k],
+                    p_recv.at[l, k], device,
+                )
+                copy.start()
+                outs.append(copy)
+            w_out[l][group] = summed[l, place]
+        for l in reversed(range(layers)):
+            t_out[l][...] = t_own[l, za]
+            total(l, 1, t_out[l])
+        for l in reversed(range(layers)):
+            for k, (device, their_group, _) in enumerate(peers):
+                ref = w_out[l].at[their_group]
+                rcopy(ref, ref, p_send.at[l, k], p_recv.at[l, k], device).wait_recv()
+        for copy in firsts + outs:
+            copy.wait_send()
+        for kind in (0, 1):
+            for l in range(layers):
+                for d in (0, 1):
+                    for far in range(last):
+                        dest = last - far if d == 0 else far
+
+                        @pl.when((za < dest) if d == 0 else (za > dest))
+                        def _():
+                            along(l, kind, d, dest)[1].wait_send()
+
+    return pl.pallas_call(
+        kernel,
+        out_shape=[jax.ShapeDtypeStruct((8, count, width), BF16)] * layers
+        + [jax.ShapeDtypeStruct((count, depth), BF16)] * layers,
+        in_specs=[VMEM_SPEC] * (2 * layers),
+        out_specs=[VMEM_SPEC] * (2 * layers),
+        scratch_shapes=[
+            pltpu.VMEM((layers, 2, planes, 8, count, width), BF16),
+            pltpu.VMEM((layers, 4, count, depth), BF16),
+            pltpu.VMEM((layers, 2, planes, count, depth), BF16),
+            pltpu.VMEM((layers, 8, count, width), BF16),
+            DMA((layers,)),
+            DMA((layers, 3)),
+            DMA((layers, 3)),
+            DMA((layers, 2, 2, planes)),
+            DMA((layers, 2, 2, planes)),
+            DMA((layers, 7)),
+            DMA((layers, 7)),
+        ],
+        compiler_params=comm_params(7),
+        cost_estimate=busy(40),
+        name="collect",
+    )(*wide, *tall)
+
+
+def row_codes(code_rows, first, local, slots, weights=None):
+    blocks = []
+    for e in range(local):
+        code = code_rows(first + e)
+        ids = lax.broadcasted_iota(jnp.int32, (slots, code.shape[1]), 0).astype(F32)
+        value = 1.0 if weights is None else weights(first + e)
+        blocks.append(jnp.where(ids == code, value, 0.0))
+    return jnp.concatenate(blocks, axis=0).astype(BF16)
+
+
+def column_codes(code, first, local, slots, weights=None):
+    lanes = lax.broadcasted_iota(jnp.int32, code.shape, 1)
+    blocks = []
+    for e in range(local):
+        chosen = lanes == first + e
+        column = jnp.sum(jnp.where(chosen, code, 0.0), axis=1, keepdims=True)
+        ids = lax.broadcasted_iota(jnp.int32, (code.shape[0], slots), 1).astype(F32)
+        value = 1.0
+        if weights is not None:
+            value = jnp.sum(jnp.where(chosen, weights, 0.0), axis=1, keepdims=True)
+        blocks.append(jnp.where(ids == column, value, 0.0))
+    return jnp.concatenate(blocks, axis=1).astype(BF16)
+
+
+def dot(a, b):
+    return jnp.dot(a, b, preferred_element_type=F32)
+
+
+def dot_t(a, b):
+    return lax.dot_general(a, b, (((1,), (1,)), ((), ())), preferred_element_type=F32)
+
+
+def plain_params(megabytes):
+    return pltpu.CompilerParams(
+        vmem_limit_bytes=megabytes << 20, dimension_semantics=("arbitrary",)
+    )
+
+
+def once(shape):
+    return pl.BlockSpec(shape, lambda e: (0,) * len(shape), pipeline_mode=pl.Buffered(1))
+
+
+def per_expert(shape):
+    return pl.BlockSpec((1,) + shape, lambda e: (e,) + (0,) * len(shape))
+
+
+def experts_forward(normed, codes, codes_t, router, gate_w, up_w, down_w, slots):
+    blocks, count, width = normed.shape
+    local, _, hidden_size = gate_w.shape
+    lines = local * slots
+    halves = 2
+    share = blocks // halves
+
+    def kernel(n_ref, c_ref, ct_ref, r_ref, gw_ref, uw_ref, dw_ref, out, g_out, u_out, p_out, pt_out, rows, back):
+        e = pl.program_id(0)
+        first = (lax.axis_index("za") * 2 + lax.axis_index("yb")) * local
+
+        @pl.when(e == 0)
+        def _():
+            @pl.loop(0, blocks)
+            def _(b):
+                tokens = n_ref[b]
+                logits = dot(tokens, r_ref[...])
+                code = c_ref[b]
+                routed = code >= 0.0
+                highest = jnp.max(jnp.where(routed, logits, -1e30), axis=1, keepdims=True)
+                raised = jnp.where(routed, jnp.exp(logits - highest), 0.0)
+                probs = raised / jnp.sum(raised, axis=1, keepdims=True)
+                p_out[b] = probs
+                pt_out[b] = probs.T[: pt_out.shape[1]]
+                back[b] = column_codes(code, first, local, slots, probs)
+                ones = row_codes(lambda i: ct_ref[b, pl.ds(i, 1), :], first, local, slots)
+                rows[b] = dot(ones, tokens).astype(BF16)
+
+        mine = pl.ds(pl.multiple_of(e * slots, slots), slots)
+        for h in range(halves):
+            part = pl.ds(h * share, share)
+            held = rows[part, mine, :].reshape(share * slots, width)
+            gate = dot(held, gw_ref[0])
+            up = dot(held, uw_ref[0])
+            at = pl.ds(h * share * slots, share * slots)
+            g_out[0, at, :] = gate
+            u_out[0, at, :] = up
+            hidden = (gate * jax.nn.sigmoid(gate) * up).astype(BF16)
+            made = dot(hidden, dw_ref[0]).astype(BF16)
+            rows[part, mine, :] = made.reshape(share, slots, width)
+
+        @pl.when(e == local - 1)
+        def _():
+            @pl.loop(0, blocks)
+            def _(b):
+                out[b] = dot(back[b], rows[b]).astype(BF16)
+
+    wide = (local, blocks * slots, hidden_size)
+    return pl.pallas_call(
+        kernel,
+        grid=(local,),
+        out_shape=[
+            jax.ShapeDtypeStruct(normed.shape, BF16),
+            jax.ShapeDtypeStruct(wide, F32),
+            jax.ShapeDtypeStruct(wide, F32),
+            jax.ShapeDtypeStruct(codes.shape, F32),
+            jax.ShapeDtypeStruct(codes_t.shape, F32),
+        ],
+        in_specs=[
+            once(normed.shape),
+            once(codes.shape),
+            once(codes_t.shape),
+            once(router.shape),
+            per_expert(gate_w.shape[1:]),
+            per_expert(up_w.shape[1:]),
+            per_expert(down_w.shape[1:]),
+        ],
+        out_specs=[
+            once(normed.shape),
+            per_expert(wide[1:]),
+            per_expert(wide[1:]),
+            once(codes.shape),
+            once(codes_t.shape),
+        ],
+        scratch_shapes=[
+            pltpu.VMEM((blocks, lines, width), BF16),
+            pltpu.VMEM((blocks, count, lines), BF16),
+        ],
+        compiler_params=plain_params(56),
+        cost_estimate=busy(16),
+        name="experts_forward",
+    )(normed, codes, codes_t, router, gate_w, up_w, down_w)
+
+
+def experts_backward(
+    normed, arrived, codes, codes_t, probs_t, gate_w, up_w, down_w, gate_part, up_part, slots, shares
+):
+    blocks, count, width = normed.shape
+    local, _, hidden_size = gate_w.shape
+    lines = local * slots
+    total = blocks * slots
+    band = width // shares
+    split = band % 128 == 0
+
+    def kernel(
+        n_ref, a_ref, c_ref, ct_ref, pt_ref, gw_ref, uw_ref, dw_ref, g_ref, u_ref,
+        out, dg_out, du_out, dd_out, rows, outs, back, marks,
+    ):
+        e = pl.program_id(0)
+        first = (lax.axis_index("za") * 2 + lax.axis_index("yb")) * local
+
+        @pl.when(e == 0)
+        def _():
+            @pl.loop(0, blocks)
+            def _(b):
+                def code(i):
+                    return ct_ref[b, pl.ds(i, 1), :]
+
+                def prob(i):
+                    return pt_ref[b, pl.ds(i, 1), :]
+
+                back[b] = column_codes(c_ref[b], first, local, slots)
+                rows[b] = dot(row_codes(code, first, local, slots), n_ref[b]).astype(BF16)
+                outs[b] = dot(row_codes(code, first, local, slots, prob), a_ref[b]).astype(BF16)
+
+        mine = pl.ds(pl.multiple_of(e * slots, slots), slots)
+        upstream = outs[:, mine, :].reshape(total, width)
+        hidden_grad = dot_t(upstream, dw_ref[0])
+        gate, up = g_ref[0], u_ref[0]
+        logistic = jax.nn.sigmoid(gate)
+        hidden = (gate * logistic * up).astype(BF16)
+        gate_low = (hidden_grad * up * logistic * (1.0 + gate * (1.0 - logistic))).astype(BF16)
+        up_low = (hidden_grad * gate * logistic).astype(BF16)
+        weighted = jnp.sum(hidden.astype(F32) * hidden_grad, axis=1, keepdims=True)
+        high = weighted.astype(BF16).astype(F32)
+        lanes = lax.broadcasted_iota(jnp.int32, (total, 128), 1)
+        mark = jnp.where(lanes == first + e, high, 0.0)
+        mark = mark + jnp.where(lanes == first + e + 64, weighted - high, 0.0)
+        marks[:, mine, :] = mark.astype(BF16).reshape(blocks, slots, 128)
+        turned = rows[:, mine, :].reshape(total, width).T
+        for f in range(shares):
+            cut = turned[f * band : (f + 1) * band]
+            dg_out[f, 0] = dot(cut, gate_low).astype(BF16)
+            du_out[f, 0] = dot(cut, up_low).astype(BF16)
+        down = dot(hidden.T, upstream).astype(BF16)
+        if split:
+            for f in range(shares):
+                dd_out[f, 0] = down[:, f * band : (f + 1) * band]
+        else:
+            dd_out[0] = down
+        back_rows = dot_t(gate_low, gw_ref[0]) + dot_t(up_low, uw_ref[0])
+        rows[:, mine, :] = back_rows.astype(BF16).reshape(blocks, slots, width)
+
+        @pl.when(e == local - 1)
+        def _():
+            @pl.loop(0, blocks)
+            def _(b):
+                out[b, :, :width] = dot(back[b], rows[b]).astype(BF16)
+                out[b, :, width:] = dot(back[b], marks[b]).astype(BF16)
+
+    cut_shape = (shares, local, band, hidden_size)
+    cut_spec = pl.BlockSpec((shares, 1, band, hidden_size), lambda e: (0, e, 0, 0))
+    if split:
+        down_shape = (shares, local, hidden_size, band)
+        down_spec = pl.BlockSpec((shares, 1, hidden_size, band), lambda e: (0, e, 0, 0))
+    else:
+        down_shape, down_spec = down_w.shape, per_expert(down_w.shape[1:])
+    results = pl.pallas_call(
+        kernel,
+        grid=(local,),
+        out_shape=[
+            jax.ShapeDtypeStruct((blocks, count, width + 128), BF16),
+            jax.ShapeDtypeStruct(cut_shape, BF16),
+            jax.ShapeDtypeStruct(cut_shape, BF16),
+            jax.ShapeDtypeStruct(down_shape, BF16),
+        ],
+        in_specs=[
+            once(normed.shape),
+            once(arrived.shape),
+            once(codes.shape),
+            once(codes_t.shape),
+            once(probs_t.shape),
+            per_expert(gate_w.shape[1:]),
+            per_expert(up_w.shape[1:]),
+            per_expert(down_w.shape[1:]),
+            per_expert(gate_part.shape[1:]),
+            per_expert(up_part.shape[1:]),
+        ],
+        out_specs=[once((blocks, count, width + 128)), cut_spec, cut_spec, down_spec],
+        scratch_shapes=[
+            pltpu.VMEM((blocks, lines, width), BF16),
+            pltpu.VMEM((blocks, lines, width), BF16),
+            pltpu.VMEM((blocks, count, lines), BF16),
+            pltpu.VMEM((blocks, lines, 128), BF16),
+        ],
+        compiler_params=plain_params(60),
+        cost_estimate=busy(30),
+        name="experts_backward",
+    )(normed, arrived, codes, codes_t, probs_t, gate_w, up_w, down_w, gate_part, up_part)
+    row_sums, gate_term, up_term, down_term = results
+    if not split:
+        down_term = jnp.moveaxis(
+            down_term.reshape(local, hidden_size, shares, band), 2, 0
+        )
+    return row_sums, gate_term, up_term, down_term
 
 
 def norm_factor(stream):
@@ -397,37 +1058,59 @@
     chosen = exchange(routes[0])
 
     small = jnp.stack([attn_gain, ffn_gain], axis=-1)
-    pieces = jnp.concatenate(
+    used = columns + 2 * kv + experts_all + 2
+    padded = -(-used // 128) * 128
+
+    def whole_rows(array):
+        if groups == 1:
+            return array
+        return jnp.moveaxis(lax.all_gather(array, "grp"), 0, 1).reshape(
+            layers, groups * bands, array.shape[-1]
+        )
+
+    packed = jnp.concatenate(
         [
             jnp.moveaxis(query_weight.reshape(layers, bands, 8, columns), 2, 0),
             jnp.moveaxis(key_matrix.reshape(layers, bands, 8, kv), 2, 0),
             jnp.moveaxis(value_matrix.reshape(layers, bands, 8, kv), 2, 0),
             jnp.broadcast_to(
-                jnp.concatenate([router_weight, small], axis=-1)[None],
-                (8, layers, bands, experts_all + 2),
+                jnp.concatenate(
+                    [router_weight, small, jnp.zeros((layers, bands, padded - used), BF16)], axis=-1
+                )[None],
+                (8, layers, bands, padded - columns - 2 * kv),
             ),
         ],
         axis=-1,
     )
-    used = pieces.shape[-1]
-    slab = lax.all_to_all(pieces, ("xh", "co", "yb"), 0, 0)
-    slab = lax.all_gather(slab, ("za", "grp"))
-    slab = slab.reshape(planes, groups, 4, 2, layers, bands, used)
-    slab = jnp.transpose(slab, (4, 0, 3, 1, 2, 5, 6)).reshape(layers, width, used)
-    qkv_weight = slab[:, :, : columns + 2 * kv]
-    router_full = slab[:, :, columns + 2 * kv : columns + 2 * kv + experts_all]
-    gains = slab[:, :, columns + 2 * kv + experts_all :].astype(F32)
-    out_rows = lax.all_gather(out_weight, ("za", "grp"))
-    out_rows = lax.all_to_all(
-        out_rows.reshape(planes, groups, layers, bands, width), ("xh", "co"), 0, 0
-    )
-    out_rows = jnp.transpose(out_rows, (2, 1, 0, 3, 4)).reshape(layers, columns, width)
+    pieces = packed
+    if groups > 1:
+        pieces = jnp.transpose(lax.all_gather(packed, "grp"), (1, 2, 0, 3, 4)).reshape(
+            8, layers, groups * bands, padded
+        )
+    band_rows = groups * bands
+
+    def in_order(array):
+        if groups > 1:
+            array = array.reshape(planes, 2, 4, groups, bands, padded)
+            array = jnp.swapaxes(array, 2, 3)
+        return array.reshape(width, padded)
+
+    first, *later = spread_first(pieces, planes)
+    slabs = [in_order(first)]
 
     def fetch_experts(layer):
         return (
             lax.all_gather(gate_weight[layer], ("grp", "xh", "co"), axis=1, tiled=True),
             lax.all_gather(up_weight[layer], ("grp", "xh", "co"), axis=1, tiled=True),
             lax.all_gather(down_weight[layer], ("grp", "xh", "co"), axis=2, tiled=True),
+        )
+
+    def sum_experts(gate_term, up_term, down_term):
+        axes = ("grp", "xh", "co")
+        return (
+            lax.psum_scatter(gate_term, axes, scatter_dimension=0),
+            lax.psum_scatter(up_term, axes, scatter_dimension=0),
+            lax.psum_scatter(down_term, axes, scatter_dimension=0),
         )
 
     named = jnp.sum(
@@ -436,22 +1119,9 @@
     ids = jnp.arange(count, dtype=jnp.int32)
     before = (ids[None, :] < ids[:, None]).astype(BF16)
     rank = jnp.dot(before, named.astype(BF16), preferred_element_type=F32)
-    codes = lax.all_gather(jnp.where(named > 0, rank, -1.0).astype(BF16), ("za", "yb"))
-    routed = (codes >= 0).reshape(length, experts_all)
-    mine = lax.dynamic_slice_in_dim(codes, place * local, local, axis=2).astype(F32)
-    slot_ids = jnp.arange(slots, dtype=jnp.int32).astype(F32)
-    spread = mine[:, :, :, None] == slot_ids
-    back_ones = spread.reshape(seq_count, count, local * slots).astype(BF16)
-    row_ones = jnp.transpose(spread, (0, 2, 3, 1)).reshape(seq_count, local * slots, count)
-    row_ones = row_ones.astype(BF16)
-
-    def to_experts(rows):
-        shaped = rows.reshape(seq_count, local, slots, -1)
-        return jnp.moveaxis(shaped, 1, 0).reshape(local, seq_count * slots, -1)
-
-    def from_experts(rows):
-        shaped = rows.reshape(local, seq_count, slots, -1)
-        return jnp.moveaxis(shaped, 0, 1).reshape(seq_count, local * slots, -1)
+    codes = jnp.where(named > 0, rank, -1.0)
+    codes = jnp.pad(codes, ((0, 0), (0, 128 - experts_all)), constant_values=-1.0).astype(BF16)
+    codes_t = None
 
     positions = jnp.arange(length, dtype=jnp.int32)
     documents = jnp.sum((starts[None, :] <= positions[:, None]).astype(jnp.int32), axis=1) - 1
@@ -462,13 +1132,27 @@
     cosine, sine = jnp.cos(angles), jnp.sin(angles)
 
     states = []
+    out_rows = None
     for layer in range(layers):
         gate_w, up_w, down_w = fetch_experts(layer)
-        attn_row, ffn_row = gains[layer, :, 0], gains[layer, :, 1]
+        small_part = slabs[layer][:, columns + 2 * kv :]
+        attn_row = small_part[:, experts_all].astype(F32)
+        ffn_row = small_part[:, experts_all + 1].astype(F32)
+        qkv_w = slabs[layer][:, : columns + 2 * kv]
+        router_w = jnp.pad(small_part[:, :experts_all], ((0, 0), (0, 128 - experts_all)))
         factor_one = norm_factor(stream)
-        normed_one = gather_plane((stream * factor_one * attn_row).astype(BF16))
+        own_one = (stream * factor_one * attn_row).astype(BF16)
+        if layer == 0:
+            normed_one, tall_rows, *rest = gather_plane_first(
+                own_one, later, whole_rows(out_weight), planes
+            )
+            slabs += [in_order(array) for array in rest]
+            tall_rows = tall_rows.reshape(4, layers, groups, bands, width)
+            out_rows = jnp.transpose(tall_rows, (1, 2, 0, 3, 4)).reshape(layers, columns, width)
+        else:
+            normed_one = gather_plane(own_one)
         normed_one = normed_one.reshape(length, width)
-        qkv = jnp.dot(normed_one, qkv_weight[layer], preferred_element_type=F32)
+        qkv = jnp.dot(normed_one, qkv_w, preferred_element_type=F32)
         queries = rotate(qkv[:, :columns], cosine, sine).astype(BF16)
         keys = rotate(qkv[:, columns : columns + kv], cosine, sine).astype(BF16)
         values = qkv[:, columns + kv :].astype(BF16)
@@ -479,39 +1163,21 @@
         middle = stream + scatter_plane(branch.reshape(8, count, width))
         factor_two = norm_factor(middle)
         own_two = (middle * factor_two * ffn_row).astype(BF16)
-        normed_two = gather_group(own_two, planes)
-        logits = jnp.dot(
-            normed_two.reshape(length, width), router_full[layer], preferred_element_type=F32
-        )
-        highest = jnp.max(jnp.where(routed, logits, -1e30), axis=-1, keepdims=True)
-        raised = jnp.where(routed, jnp.exp(jnp.where(routed, logits - highest, 0.0)), 0.0)
-        gate_probs = raised / jnp.sum(raised, axis=-1, keepdims=True)
-        gate_probs = gate_probs.reshape(seq_count, count, experts_all)
-        own_probs = lax.dynamic_index_in_dim(gate_probs, place, 0, keepdims=False)
-        my_probs = lax.dynamic_slice_in_dim(gate_probs, place * local, local, axis=2)
-        back_probs = jnp.where(spread, my_probs[..., None], 0.0)
-        row_probs = jnp.transpose(back_probs, (0, 2, 3, 1)).reshape(
-            seq_count, local * slots, count
-        )
-        back_probs = back_probs.reshape(seq_count, count, local * slots).astype(BF16)
-        rows = to_experts(
-            jnp.einsum("brt,btd->brd", row_ones, normed_two, preferred_element_type=BF16)
-        )
-        gate_part = jnp.einsum("erd,edf->erf", rows, gate_w, preferred_element_type=F32)
-        up_part = jnp.einsum("erd,edf->erf", rows, up_w, preferred_element_type=F32)
-        hidden = (gate_part * jax.nn.sigmoid(gate_part) * up_part).astype(BF16)
-        produced = jnp.einsum("erf,efd->erd", hidden, down_w, preferred_element_type=F32)
-        total = jnp.einsum(
-            "btr,brd->btd",
-            back_probs,
-            from_experts(produced.astype(BF16)),
-            preferred_element_type=F32,
-        ).astype(BF16)
+        if layer == 0:
+            both = gather_group(jnp.concatenate([own_two, codes], axis=1), planes, 8)
+            normed_two, codes = both[..., :width], both[..., width:].astype(F32)
+            codes_t = jnp.swapaxes(codes[..., :32], 1, 2)
+        else:
+            normed_two = gather_group(own_two, planes)
+        total, gate_part, up_part, gate_probs, probs_t = experts_forward(
+            normed_two, codes, codes_t, router_w, gate_w, up_w, down_w, slots
+        )
+        own_probs = lax.dynamic_index_in_dim(gate_probs, place, 0, keepdims=False)[:, :experts_all]
         states.append(
             (
                 stream, factor_one, normed_one, queries, keys, values, logs, mixed, middle,
-                factor_two, own_two, own_probs, row_probs, rows, gate_part, up_part, hidden,
-                gate_w, up_w, down_w,
+                factor_two, own_two, normed_two, own_probs, probs_t, gate_part, up_part,
+                gate_w, up_w, down_w, attn_row, ffn_row, qkv_w, router_w,
             )
         )
         stream = middle + scatter_group(total, planes, 1)
@@ -519,52 +1185,30 @@
     result = exchange(stream.astype(BF16))[None]
 
     upstream = upstream_low.astype(F32)
-    dense_out, expert_out, small_out = [None] * layers, [None] * layers, [None] * layers
+    expert_out, previous = [None] * layers, None
+    wide_terms, tall_terms = [None] * layers, [None] * layers
     for layer in reversed(range(layers)):
         (
             stream, factor_one, normed_one, queries, keys, values, logs, mixed, middle,
-            factor_two, own_two, own_probs, row_probs, rows, gate_part, up_part, hidden,
-            gate_w, up_w, down_w,
+            factor_two, own_two, normed_two, own_probs, probs_t, gate_part, up_part,
+            gate_w, up_w, down_w, attn_row, ffn_row, qkv_w, router_w,
         ) = states[layer]
-        attn_row, ffn_row = gains[layer, :, 0], gains[layer, :, 1]
         arrived = gather_group(upstream.astype(BF16), planes)
-        out_rows_grad = to_experts(
-            jnp.einsum(
-                "brt,btd->brd", row_probs.astype(BF16), arrived, preferred_element_type=F32
-            ).astype(BF16)
-        )
-        hidden_grad = jnp.einsum("erd,efd->erf", out_rows_grad, down_w, preferred_element_type=F32)
-        down_term = jnp.einsum("erf,erd->efd", hidden, out_rows_grad, preferred_element_type=F32)
-        weighted = jnp.sum(hidden.astype(F32) * hidden_grad, axis=-1)
-        logistic = jax.nn.sigmoid(gate_part)
-        gate_low = (
-            hidden_grad * up_part * logistic * (1.0 + gate_part * (1.0 - logistic))
-        ).astype(BF16)
-        up_low = (hidden_grad * gate_part * logistic).astype(BF16)
-        gate_term = jnp.einsum("erd,erf->edf", rows, gate_low, preferred_element_type=F32)
-        up_term = jnp.einsum("erd,erf->edf", rows, up_low, preferred_element_type=F32)
-        rows_grad = jnp.einsum("erf,edf->erd", gate_low, gate_w, preferred_element_type=F32)
-        rows_grad = (
-            rows_grad + jnp.einsum("erf,edf->erd", up_low, up_w, preferred_element_type=F32)
-        ).astype(BF16)
-        row_sums = jnp.einsum(
-            "btr,brd->btd", back_ones, from_experts(rows_grad), preferred_element_type=F32
-        ).astype(BF16)
-        by_row = jnp.moveaxis(weighted.reshape(local, seq_count, slots), 1, 0)
-        by_token = jnp.sum(jnp.where(spread, by_row[:, None], 0.0), axis=-1)
-        extra = jnp.zeros((seq_count, count, 64), F32)
-        extra = lax.dynamic_update_slice_in_dim(extra, by_token, place * local, axis=2)
-        high = extra.astype(BF16)
-        rest = (extra - high.astype(F32)).astype(BF16)
-        summed = scatter_group(
-            jnp.concatenate([row_sums, high, rest], axis=2), planes, 2
-        )
+        row_sums, gate_term, up_term, down_term = experts_backward(
+            normed_two, arrived, codes, codes_t, probs_t, gate_w, up_w, down_w, gate_part, up_part,
+            slots, 4 * groups,
+        )
+        terms = (gate_term, up_term, down_term)
+        if previous is not None:
+            terms, expert_out[layer + 1] = lax.optimization_barrier((terms, previous))
+        previous = expert_out[layer] = sum_experts(*terms)
+        summed = scatter_group(row_sums, planes, 2)
         weighted = summed[:, width : width + experts_all]
         weighted = weighted + summed[:, width + 64 : width + 64 + experts_all]
         logit_grad = weighted - own_probs * jnp.sum(weighted, axis=-1, keepdims=True)
-        router_term = jnp.einsum("td,te->ed", own_two.astype(F32), logit_grad, precision=HIGHEST)
+        router_term = jnp.einsum("td,te->de", own_two.astype(F32), logit_grad, precision=HIGHEST)
         normed_two_grad = summed[:, :width] + jnp.einsum(
-            "te,de->td", logit_grad, router_full[layer].astype(F32), precision=HIGHEST
+            "te,de->td", logit_grad, router_w[:, :experts_all].astype(F32), precision=HIGHEST
         )
         ffn_gain_term = jnp.sum(normed_two_grad * middle * factor_two, axis=0)
         middle_grad = upstream + norm_back(middle, factor_two, ffn_row, normed_two_grad)
@@ -587,66 +1231,61 @@
         )
         qkv_term = jnp.einsum("td,tc->dc", normed_one, low, preferred_element_type=F32)
         partial = jnp.einsum(
-            "tc,dc->td", low, qkv_weight[layer], preferred_element_type=F32
+            "tc,dc->td", low, qkv_w, preferred_element_type=F32
         ).astype(BF16)
+        rest = jnp.concatenate([router_term, ffn_gain_term[:, None]], axis=1)
+        rest = jnp.pad(rest, ((0, 0), (0, 32 - experts_all - 1)))
+        high = rest.astype(BF16)
+        low_part = (rest - high.astype(F32)).astype(BF16)
+        qkv_term = jnp.concatenate([qkv_term.astype(BF16), high, low_part], axis=1)
+        partial, qkv_term, out_term = lax.optimization_barrier(
+            (partial, qkv_term, out_term.astype(BF16))
+        )
         normed_one_grad = scatter_plane(partial.reshape(8, count, width))
-        attn_gain_term = jnp.sum(normed_one_grad * stream * factor_one, axis=0)
         upstream = middle_grad + norm_back(stream, factor_one, attn_row, normed_one_grad)
-
-        expert_out[layer] = (
-            lax.psum_scatter(
-                gate_term.astype(BF16), ("grp", "xh", "co"), scatter_dimension=1, tiled=True
-            ).astype(F32),
-            lax.psum_scatter(
-                up_term.astype(BF16), ("grp", "xh", "co"), scatter_dimension=1, tiled=True
-            ).astype(F32),
-            lax.psum_scatter(
-                down_term.astype(BF16), ("grp", "xh", "co"), scatter_dimension=2, tiled=True
-            ).astype(F32),
-        )
-        wide = qkv_term.astype(BF16).reshape(planes, 2, groups, 4, bands, columns + 2 * kv)
-        wide = jnp.transpose(wide, (0, 2, 3, 1, 4, 5)).reshape(
-            planes * groups, 8, bands, columns + 2 * kv
-        )
-        wide = lax.psum_scatter(wide, ("za", "grp"), scatter_dimension=0)
-        wide = lax.all_to_all(wide, ("xh", "co", "yb"), 0, 0)
-        tall = out_term.astype(BF16).reshape(groups, 4, bands, width)
-        tall = lax.all_to_all(jnp.moveaxis(tall, 1, 0), ("xh", "co"), 0, 0)
-        tall = lax.psum_scatter(
-            tall.reshape(planes * groups, bands, width), ("za", "grp"), scatter_dimension=0
-        )
-        dense_out[layer] = (
-            jnp.moveaxis(wide[..., :columns], 0, 1).reshape(bands, -1).astype(F32),
-            jnp.moveaxis(wide[..., columns : columns + kv], 0, 1).reshape(bands, -1).astype(F32),
-            jnp.moveaxis(wide[..., columns + kv :], 0, 1).reshape(bands, -1).astype(F32),
-            tall.astype(F32),
-        )
-        small_out[layer] = jnp.concatenate(
-            [router_term, attn_gain_term[None], ffn_gain_term[None]], axis=0
-        )
-
-    rest = jnp.stack(small_out)
-    kinds = rest.shape[1]
-    rest = jnp.moveaxis(rest.reshape(layers, kinds, width // bands, bands), 2, 0)
-    rest = lax.psum_scatter(
-        rest.reshape(width // bands, layers * kinds, bands),
-        ("za", "yb", "grp", "xh", "co"),
-        scatter_dimension=0,
-    ).reshape(layers, kinds, bands)
+        if groups > 1:
+            qkv_term = jnp.swapaxes(
+                qkv_term.reshape(planes, 2, groups, 4, bands, padded), 2, 3
+            )
+            out_term = jnp.swapaxes(out_term.reshape(groups, 4, bands, width), 0, 1)
+        wide_terms[layer] = qkv_term.reshape(planes, 8, band_rows, padded)
+        tall_terms[layer] = out_term.reshape(4, band_rows, width)
+
+    sums = collect(wide_terms, tall_terms, planes)
+    if groups > 1:
+        sums = [
+            lax.psum_scatter(array, "grp", scatter_dimension=array.ndim - 2, tiled=True)
+            for array in sums
+        ]
+    wide_sums = jnp.stack(sums[:layers]).astype(F32)
+
+    def by_heads(start, stop):
+        return jnp.swapaxes(wide_sums[..., start:stop], 1, 2).reshape(layers, bands, -1)
+
+    query_out = by_heads(0, columns)
+    key_out = by_heads(columns, columns + kv)
+    value_out = by_heads(columns + kv, columns + 2 * kv)
+    rest = jnp.sum(wide_sums[..., columns + 2 * kv :], axis=1)
+    rest = rest[..., :32] + rest[..., 32:64]
+    attn_out = (
+        jnp.sum(query_weight.astype(F32) * query_out, axis=-1)
+        + jnp.sum(key_matrix.astype(F32) * key_out, axis=-1)
+        + jnp.sum(value_matrix.astype(F32) * value_out, axis=-1)
+    ) / attn_gain.astype(F32)
 
     def stacked(lists, i):
-        return jnp.stack([lists[layer][i] for layer in range(layers)])
+        return jnp.stack([lists[layer][i] for layer in range(layers)]).astype(F32)
 
     return (
         result,
-        exchange(upstream)[None],
-        rest[:, experts_all],
-        rest[:, experts_all + 1],
-        stacked(dense_out, 0),
-        stacked(dense_out, 1),
-        stacked(dense_out, 2),
-        stacked(dense_out, 3),
-        jnp.moveaxis(rest[:, :experts_all], 1, 2),
+        exchange(upstream.astype(BF16)).astype(F32)[None],
+        attn_out,
+        rest[..., experts_all],
+        query_out,
+        key_out,
+        value_out,
+        jnp.stack(sums[layers:]).astype(F32),
+        rest[..., :experts_all],
         stacked(expert_out, 0),
         stacked(expert_out, 1),
         stacked(expert_out, 2),

time: 1390 us -> 966 us (0.69)
  Pallas kernels: 460 us -> 768 us
  waiting for transfers between devices: 299 us -> 2.64 us
  matrix products: 192 us -> 55.9 us
  starting transfers between devices: 133 us -> 14.2 us
  local copies, waits for them, and re-layouts: 147 us -> 50.1 us
  blocking collectives: 63.6 us -> 0 us
    pallas_call x0 -> x7, Pallas kernels: none -> 299 us  [the longest x1 77.8 us: collect(): pl.pallas_call(kernel, out_shape=[jax.ShapeDtypeStruct((8, count, width),...]
    reduce_scatter x9 -> x6, waiting for transfers between devices: 209 us -> 0.05 us  [the longest x2 0.02 us: sum_experts(): lax.psum_scatter(up_term, axes, scatter_dimension=0)]
    dot_general x36 -> x8, matrix products: 151 us -> 13.7 us  [the longest x2 4.32 us: per_device(): jnp.einsum('tc,dc->td', low, qkv_w, preferred_element_type=F32).astype(BF16)]
    all_to_all x3 -> x0, starting transfers between devices: 125 us -> none  [the longest x2 76.4 us: per_device(): wide = lax.all_to_all(wide, ('xh', 'co', 'yb'), 0, 0)]
    unnamed x21 -> x12, waiting for transfers between devices: 84.6 us -> 2.56 us
    unnamed x327 -> x330, local copies, waits for them, and re-layouts: 83 us -> 23.7 us
    all_to_all x3 -> x0, blocking collectives: 39.7 us -> none  [the longest x2 25.5 us: per_device(): tall = lax.all_to_all(jnp.moveaxis(tall, 1, 0), ('xh', 'co'), 0, 0)]
    pallas_call x4 -> x3, Pallas kernels: 116 us -> 79.6 us  [gather_plane(): pl.pallas_call(kernel, out_shape=jax.ShapeDtypeStruct((8, count, width),...]
  transfers between devices with their start and end apart: 28 -> 18, of which waited for: 8 -> 0; matrix products, arithmetic and copies ran while one was open for 17% -> 13% of each run, Pallas kernels for 18% -> 74%
where the time goes in v2:
time: 966 us; the launch traced here: 960 us
  Pallas kernels  768 us (80%)
  matrix products  55.9 us (6%)
  other arithmetic  51.5 us (5%)
  local copies, waits for them, and re-layouts  50.1 us (5%)
  between operations  17.2 us (2%)
  starting transfers between devices  14.2 us (1%)
    pallas_call x4, Pallas kernels, gather_group(): pl.pallas_call(kernel, out_shape=jax.ShapeDtypeStruct((2 * planes, count,...  150 us
    pallas_call x4, Pallas kernels, scatter_group(): pl.pallas_call(kernel, out_shape=jax.ShapeDtypeStruct((count, width), F32...  142 us
    pallas_call x4, Pallas kernels, scatter_plane(): pl.pallas_call(kernel, out_shape=jax.ShapeDtypeStruct((count, width), F32...  98.8 us
    pallas_call x3, Pallas kernels, gather_plane(): pl.pallas_call(kernel, out_shape=jax.ShapeDtypeStruct((8, count, width),...  79.6 us
    pallas_call x1, Pallas kernels, collect(): pl.pallas_call(kernel, out_shape=[jax.ShapeDtypeStruct((8, count, width),...  77.8 us
    pallas_call x2, Pallas kernels, experts_backward(): pl.pallas_call(kernel, grid=(local,), out_shape=[jax.ShapeDtypeStruct((bl...  63.6 us
    pallas_call x1, Pallas kernels, spread_first(): pl.pallas_call(kernel, out_shape=[jax.ShapeDtypeStruct((planes, 8, count,...  57 us
    pallas_call x1, Pallas kernels, gather_plane_first(): pl.pallas_call(kernel, out_shape=[jax.ShapeDtypeStruct((8, count, width),...  55.1 us
  transfers between devices with their start and end apart: 18, of which 0 were waited for; matrix products, arithmetic and copies ran while one was open for 13% of the time, Pallas kernels for 74%

profile of v2, /device:TPU:9, one launch (start us, length us, event | category | flops | bytes accessed | tf_op | source)
XLA Modules:
  0.0 959.7 jit_solution(3257902598061353801)
XLA Ops:
  7.2 3.5 fusion.194
  12.5 3.3 fusion.192
  23.6 57.0 %spread_first.1 = (bf16[4,8,48,384]{3,2,1,0:T(8,128)(2,1)S(1)}, bf16[8,48,384]{2,1,0:T(8,128)(2,1)S(1)}) custom-call(bf16[8,2,48,384]{3,2,1,0:T(8,128)(2,1)S(1)} %pad_maximum_fusion.4.p_ref), custom_call_target="tpu_custom_call" | custom-call | bytes 73800000 | tf_op jit(solution)/shard_map/spread_first/pallas_call | solution.py:427
  86.8 55.1 %gather_plane_first.1 = (bf16[8,128,1536]{2,1,0:T(8,128)(2,1)S(1)}, bf16[4,2,48,1536]{3,2,1,0:T(8,128)(2,1)S(1)}, bf16[4,8,48,384]{3,2,1,0:T(8,128)(2,1)S(1)}) custom-call(bf16[128,1536]{1,0:T(8,128)(2,1)S(1)} %fusion.100.x_ref, bf16[2,48,1536]{2,1,0:T(8,128)(2,1)S(1)} %copy-done.19, bf16[8,48,384]{2,1,0:T(8,128)(2,1)S(1)} %get-tuple-element.180.refs_0_), custom_call_target="tpu_custom_call" | custom-call | bytes 110700000 | tf_op jit(solution)/shard_map/gather_plane_first/pallas_call | solution.py:512
  150.2 1.7 copy-done.26
  154.2 21.6 %scatter_plane.4 = f32[128,1536]{1,0:T(8,128)S(1)} custom-call(bf16[8,128,1536]{2,1,0:T(8,128)(2,1)S(1)} %bitcast.301), custom_call_target="tpu_custom_call" | custom-call | bytes 73800000 | tf_op jit(solution)/shard_map/scatter_plane/pallas_call | solution.py:265
  176.8 56.0 %gather_group.4 = bf16[8,128,1664]{2,1,0:T(8,128)(2,1)S(1)} custom-call(bf16[128,1664]{1,0:T(8,128)(2,1)S(1)} %fusion.106.x_ref), custom_call_target="tpu_custom_call" | custom-call | bytes 121770000 | tf_op jit(solution)/shard_map/gather_group/pallas_call | solution.py:161
  232.9 2.0 slice.422.n_ref
  237.1 30.2 %gather_group.6.a_ref = bf16[8,128,1536]{2,1,0:T(8,128)(2,1)S(1)} custom-call(bf16[128,1536]{1,0:T(8,128)(2,1)S(1)} %collective-permute-done.4.x_ref), custom_call_target="tpu_custom_call" | custom-call | bytes 121770000 | tf_op jit(solution)/shard_map/gather_group/pallas_call | solution.py:161
  270.6 22.8 %experts_forward.2 = (bf16[8,128,1536]{2,1,0:T(8,128)(2,1)}, f32[3,512,512]{2,1,0:T(8,128)}, f32[3,512,512]{2,1,0:T(8,128)}, f32[8,128,128]{2,1,0:T(8,128)}, f32[8,32,128]{2,1,0:T(8,128)}) custom-call(bf16[8,128,1536]{2,1,0:T(8,128)(2,1)} %slice.422.n_ref, f32[8,128,128]{2,1,0:T(8,128)} %copy.169.c_ref, f32[8,32,128]{2,1,0:T(8,128)} %slice_bitcast_fusion.6.ct_ref, ...), custom_call_target="tpu_custom_call" | custom-call | bytes 59040000 | tf_op jit(solution)/shard_map/experts_forward/pallas_call | solution.py:787
  293.4 1.9 copy-done.7
  295.3 28.3 %scatter_group.4 = f32[128,1536]{1,0:T(8,128)S(1)} custom-call(bf16[8,128,1536]{2,1,0:T(8,128)(2,1)S(1)} %copy-done.7), custom_call_target="tpu_custom_call" | custom-call | bytes 118080000 | tf_op jit(solution)/shard_map/scatter_group/pallas_call | solution.py:185
  324.5 23.0 %gather_plane.3 = bf16[8,128,1536]{2,1,0:T(8,128)(2,1)S(1)} custom-call(bf16[128,1536]{1,0:T(8,128)(2,1)S(1)} %multiply_convert_fusion.1.x_ref), custom_call_target="tpu_custom_call" | custom-call | bytes 73800000 | tf_op jit(solution)/shard_map/gather_plane/pallas_call | solution.py:212
  357.5 18.7 %scatter_plane.5 = f32[128,1536]{1,0:T(8,128)S(1)} custom-call(bf16[8,128,1536]{2,1,0:T(8,128)(2,1)S(1)} %bitcast.302), custom_call_target="tpu_custom_call" | custom-call | bytes 73800000 | tf_op jit(solution)/shard_map/scatter_plane/pallas_call | solution.py:265
  377.4 31.5 %gather_group.5.n_ref = bf16[8,128,1536]{2,1,0:T(8,128)(2,1)S(1)} custom-call(bf16[128,1536]{1,0:T(8,128)(2,1)S(1)} %multiply_convert_fusion.x_ref), custom_call_target="tpu_custom_call" | custom-call | bytes 121770000 | tf_op jit(solution)/shard_map/gather_group/pallas_call | solution.py:161
  410.6 22.3 %experts_forward.3 = (bf16[8,128,1536]{2,1,0:T(8,128)(2,1)}, f32[3,512,512]{2,1,0:T(8,128)}, f32[3,512,512]{2,1,0:T(8,128)}, f32[8,128,128]{2,1,0:T(8,128)}, f32[8,32,128]{2,1,0:T(8,128)}) custom-call(bf16[8,128,1536]{2,1,0:T(8,128)(2,1)} %copy-done, f32[8,128,128]{2,1,0:T(8,128)} %copy.169.c_ref, f32[8,32,128]{2,1,0:T(8,128)} %slice_bitcast_fusion.6.ct_ref, ...), custom_call_target="tpu_custom_call" | custom-call | bytes 59040000 | tf_op jit(solution)/shard_map/experts_forward/pallas_call | solution.py:787
  432.8 31.9 %experts_backward.2 = (bf16[8,128,1664]{2,1,0:T(8,128)(2,1)}, bf16[4,3,384,512]{3,2,1,0:T(8,128)(2,1)}, bf16[4,3,384,512]{3,2,1,0:T(8,128)(2,1)}, bf16[4,3,512,384]{3,2,1,0:T(8,128)(2,1)}) custom-call(bf16[8,128,1536]{2,1,0:T(8,128)(2,1)} %copy-done, bf16[8,128,1536]{2,1,0:T(8,128)(2,1)} %copy-done.1, f32[8,128,128]{2,1,0:T(8,128)} %copy.169.c_ref, ...), custom_call_target="tpu_custom_call" | custom-call | bytes 110700000 | tf_op jit(solution)/shard_map/experts_backward/pallas_call | solution.py:896
  465.6 2.0 copy-done.4
  467.5 33.3 %scatter_group.6 = f32[128,1664]{1,0:T(8,128)S(1)} custom-call(bf16[8,128,1664]{2,1,0:T(8,128)(2,1)S(1)} %copy-done.4), custom_call_target="tpu_custom_call" | custom-call | bytes 118080000 | tf_op jit(solution)/shard_map/scatter_group/pallas_call | solution.py:185
  503.6 2.4 multiply_reduce_fusion.3
  506.0 2.0 copy-done.6
  508.0 31.6 %scatter_group.5 = f32[128,1536]{1,0:T(8,128)S(1)} custom-call(bf16[8,128,1536]{2,1,0:T(8,128)(2,1)S(1)} %copy-done.6), custom_call_target="tpu_custom_call" | custom-call | bytes 118080000 | tf_op jit(solution)/shard_map/scatter_group/pallas_call | solution.py:185
  541.6 33.7 %gather_plane.4 = bf16[8,128,1536]{2,1,0:T(8,128)(2,1)S(1)} custom-call(bf16[128,1536]{1,0:T(8,128)(2,1)S(1)} %get-tuple-element.266.x_ref), custom_call_target="tpu_custom_call" | custom-call | bytes 73800000 | tf_op jit(solution)/shard_map/gather_plane/pallas_call | solution.py:212
  580.9 5.4 fusion.3
  586.3 4.8 fusion.5
  591.2 2.1 fusion.80
  602.4 2.3 convolution_convert_fusion.3
  604.7 32.4 %scatter_plane.6 = f32[128,1536]{1,0:T(8,128)S(1)} custom-call(bf16[8,128,1536]{2,1,0:T(8,128)(2,1)S(1)} %bitcast.311), custom_call_target="tpu_custom_call" | custom-call | bytes 73800000 | tf_op jit(solution)/shard_map/scatter_plane/pallas_call | solution.py:265
  638.5 31.9 %gather_group.7.a_ref = bf16[8,128,1536]{2,1,0:T(8,128)(2,1)S(1)} custom-call(bf16[128,1536]{1,0:T(8,128)(2,1)S(1)} %get-tuple-element.264.x_ref), custom_call_target="tpu_custom_call" | custom-call | bytes 121770000 | tf_op jit(solution)/shard_map/gather_group/pallas_call | solution.py:161
  672.0 31.7 %experts_backward.3 = (bf16[8,128,1664]{2,1,0:T(8,128)(2,1)}, bf16[4,3,384,512]{3,2,1,0:T(8,128)(2,1)}, bf16[4,3,384,512]{3,2,1,0:T(8,128)(2,1)}, bf16[4,3,512,384]{3,2,1,0:T(8,128)(2,1)}) custom-call(bf16[8,128,1536]{2,1,0:T(8,128)(2,1)} %slice.422.n_ref, bf16[8,128,1536]{2,1,0:T(8,128)(2,1)} %copy-done.2, f32[8,128,128]{2,1,0:T(8,128)} %copy.169.c_ref, ...), custom_call_target="tpu_custom_call" | custom-call | bytes 110700000 | tf_op jit(solution)/shard_map/experts_backward/pallas_call | solution.py:896
  705.4 4.6 collective-permute-start.3
  710.0 2.7 copy.188
  712.7 48.4 %scatter_group.7 = f32[128,1664]{1,0:T(8,128)S(1)} custom-call(bf16[8,128,1664]{2,1,0:T(8,128)(2,1)S(1)} %copy-done.5), custom_call_target="tpu_custom_call" | custom-call | bytes 118080000 | tf_op jit(solution)/shard_map/scatter_group/pallas_call | solution.py:185
  762.2 1.8 multiply_reduce_fusion
  765.8 22.9 %gather_plane.5 = bf16[8,128,1536]{2,1,0:T(8,128)(2,1)S(1)} custom-call(bf16[128,1536]{1,0:T(8,128)(2,1)S(1)} %get-tuple-element.262.x_ref), custom_call_target="tpu_custom_call" | custom-call | bytes 73800000 | tf_op jit(solution)/shard_map/gather_plane/pallas_call | solution.py:212
  792.3 2.0 fusion.16
  795.3 2.0 fusion.87
  797.3 4.4 fusion
  802.2 1.8 fusion.2
  815.3 2.1 convolution_convert_fusion.2
  817.4 26.1 %scatter_plane.7 = f32[128,1536]{1,0:T(8,128)S(1)} custom-call(bf16[8,128,1536]{2,1,0:T(8,128)(2,1)S(1)} %bitcast.312), custom_call_target="tpu_custom_call" | custom-call | bytes 73800000 | tf_op jit(solution)/shard_map/scatter_plane/pallas_call | solution.py:265
  844.9 4.5 collective-permute-start.5
  851.1 77.8 %collect.1 = (bf16[8,48,384]{2,1,0:T(8,128)(2,1)S(1)}, bf16[8,48,384]{2,1,0:T(8,128)(2,1)S(1)}, bf16[48,1536]{1,0:T(8,128)(2,1)S(1)}, bf16[48,1536]{1,0:T(8,128)(2,1)S(1)}) custom-call(bf16[4,8,48,384]{3,2,1,0:T(8,128)(2,1)S(1)} %bitcast.308, bf16[4,8,48,384]{3,2,1,0:T(8,128)(2,1)S(1)} %bitcast.307, bf16[4,48,1536]{2,1,0:T(8,128)(2,1)S(1)} %bitcast.314, ...), custom_call_target="tpu_custom_call" | custom-call | bytes 147600000 | tf_op jit(solution)/shard_map/collect/pallas_call | solution.py:668
  937.0 2.0 bitcast_convert_fusion
  939.0 4.2 maximum_convert_fusion.2
  943.2 3.9 maximum_convert_fusion.1
  947.1 3.8 maximum_convert_fusion
  950.8 1.8 copy.216
  (525 shorter events, 99.7 us)
Async XLA Ops:
  7.2 263.4 %all-gather.13.cloned.1.call-start = ((), (), s32[]{:S(2)}) async-start(), calls=%async_computation.12 | async-start | bytes 5898240 | tf_op jit(solution)/shard_map/all_gather | solution.py:1103
  10.7 259.9 %all-gather.15.cloned.1.call-start = ((), (), s32[]{:S(2)}) async-start(), calls=%async_computation.13 | async-start | bytes 5898240 | tf_op jit(solution)/shard_map/all_gather | solution.py:1104
  12.5 258.2 %all-gather.17.cloned.1.call-start = ((), (), s32[]{:S(2)}) async-start(), calls=%async_computation.14 | async-start | bytes 5898240 | tf_op jit(solution)/shard_map/all_gather | solution.py:1105
  15.9 394.7 %all-gather.19.cloned.1.call-start = ((), (), s32[]{:S(2)}) async-start(), calls=%async_computation.15 | async-start | bytes 5898240 | tf_op jit(solution)/shard_map/all_gather | solution.py:1103
  16.4 394.1 %all-gather.21.cloned.1.call-start = ((), (), s32[]{:S(2)}) async-start(), calls=%async_computation.16 | async-start | bytes 5898240 | tf_op jit(solution)/shard_map/all_gather | solution.py:1104
  17.0 393.5 %all-gather.23.cloned.1.call-start = ((), (), s32[]{:S(2)}) async-start(), calls=%async_computation.17 | async-start | bytes 5898240 | tf_op jit(solution)/shard_map/all_gather | solution.py:1105
  17.1 66.3 %collective-permute-start.1 = (s32[1,4]{1,0:T(1,128)S(1)}, s32[1,4]{1,0:T(1,128)S(1)}, u32[]{:S(2)}, u32[]{:S(2)}) collective-permute-start(s32[1,4]{1,0:T(1,128)S(1)} %copy-done.158), channel_id=1, source_target_pairs={{0,0},{1,8},{2,16},{3,24},{8,1},{9,9},{10,17},{11,25},{16,2},{17,1... | collective-permute-start | bytes 56 | tf_op jit(solution)/shard_map/ppermute | solution.py:1053
  17.8 67.9 %collective-permute-start.2 = (s32[128,8]{0,1:T(8,128)S(1)}, s32[128,8]{0,1:T(8,128)S(1)}, u32[]{:S(2)}, u32[]{:S(2)}) collective-permute-start(s32[128,8]{0,1:T(8,128)S(1)} %bitcast.379), channel_id=1, source_target_pairs={{0,0},{1,8},{2,16},{3,24},{8,1},{9,9},{10,17},{11,25},{16,2},{17,1... | collective-permute-start | bytes 12296 | tf_op jit(solution)/shard_map/ppermute | solution.py:1053
  18.4 67.5 %collective-permute-start = (bf16[128,1536]{1,0:T(8,128)(2,1)}, bf16[128,1536]{1,0:T(8,128)(2,1)S(1)}, u32[]{:S(2)}, u32[]{:S(2)}) collective-permute-start(bf16[128,1536]{1,0:T(8,128)(2,1)} %bitcast), channel_id=1, source_target_pairs={{0,0},{1,8},{2,16},{3,24},{8,1},{9,9},{10,17},{11,25},{16,2},{17,1... | collective-permute-start | bytes 1179656 | tf_op jit(solution)/shard_map/ppermute | solution.py:1053
  20.1 216.9 %collective-permute-start.4 = (bf16[128,1536]{1,0:T(8,128)(2,1)}, bf16[128,1536]{1,0:T(8,128)(2,1)S(1)}, u32[]{:S(2)}, u32[]{:S(2)}) collective-permute-start(bf16[128,1536]{1,0:T(8,128)(2,1)} %bitcast.55), channel_id=1, source_target_pairs={{0,0},{1,8},{2,16},{3,24},{8,1},{9,9},{10,17},{11,25},{16,2},{17,1... | collective-permute-start | bytes 1179656 | tf_op jit(solution)/shard_map/ppermute | solution.py:1053
  21.8 682.0 %reduce-scatter.7.cloned.1.call-start = ((), (), s32[]{:S(2)}) async-start(), calls=%async_computation.6 | async-start | bytes 5898240 | tf_op jit(solution)/shard_map/reduce_scatter | solution.py:1111
  23.6 63.3 %copy-start.19 = (bf16[2,48,1536]{2,1,0:T(8,128)(2,1)S(1)}, bf16[2,48,1536]{2,1,0:T(8,128)(2,1)}, u32[]{:S(2)}) copy-start(bf16[2,48,1536]{2,1,0:T(8,128)(2,1)} %w_ref.1) | copy-start | bytes 884740
  80.6 62.6 %copy-start.10 = (bf16[4,8,48,384]{3,2,1,0:T(8,128)(2,1)}, bf16[4,8,48,384]{3,2,1,0:T(8,128)(2,1)S(1)}, u32[]{:S(2)}) copy-start(bf16[4,8,48,384]{3,2,1,0:T(8,128)(2,1)S(1)} %get-tuple-element.179) | copy-start | bytes 3538948
  81.2 62.1 %copy-start.107 = (f32[1536]{0:T(1024)}, f32[1536]{0:T(1024)S(1)}, u32[]{:S(2)}) copy-start(f32[1536]{0:T(1024)S(1)} %get-tuple-element.261) | copy-start | bytes 18436
  83.4 266.1 %copy-start.51 = (f32[1024,32]{0,1:T(8,128)}, f32[1024,32]{0,1:T(8,128)S(1)}, u32[]{:S(2)}) copy-start(f32[1024,32]{0,1:T(8,128)S(1)} %get-tuple-element.308) | copy-start | bytes 393220
  86.7 56.6 %copy-start.150 = (f32[128]{0:T(128)}, f32[128]{0:T(128)S(1)}, u32[]{:S(2)}) copy-start(f32[128]{0:T(128)S(1)} %get-tuple-element.312) | copy-start | bytes 1540
  142.0 125.3 %copy-start.12 = (bf16[4,8,48,384]{3,2,1,0:T(8,128)(2,1)}, bf16[4,8,48,384]{3,2,1,0:T(8,128)(2,1)S(1)}, u32[]{:S(2)}) copy-start(bf16[4,8,48,384]{3,2,1,0:T(8,128)(2,1)S(1)} %get-tuple-element.184) | copy-start | bytes 3538948
  176.0 147.6 %copy-start.35 = (f32[128,1536]{1,0:T(8,128)}, f32[128,1536]{1,0:T(8,128)S(1)}, u32[]{:S(2)}) copy-start(f32[128,1536]{1,0:T(8,128)S(1)} %get-tuple-element.273) | copy-start | bytes 2359300
  176.6 56.3 %copy-start.139 = (f32[128]{0:T(128)}, f32[128]{0:T(128)S(1)}, u32[]{:S(2)}) copy-start(f32[128]{0:T(128)S(1)} %get-tuple-element.314) | copy-start | bytes 1540
  176.7 56.1 %copy-start.49 = (bf16[128,1536]{1,0:T(8,128)(2,1)}, bf16[128,1536]{1,0:T(8,128)(2,1)S(1)}, u32[]{:S(2)}) copy-start(bf16[128,1536]{1,0:T(8,128)(2,1)S(1)} %multiply_convert_fusion.2) | copy-start | bytes 1179652
  237.1 56.4 %copy-start.15 = (bf16[128,1536]{1,0:T(8,128)(2,1)}, bf16[128,1536]{1,0:T(8,128)(2,1)S(1)}, u32[]{:S(2)}) copy-start(bf16[128,1536]{1,0:T(8,128)(2,1)S(1)} %collective-permute-done.4.x_ref) | copy-start | bytes 1179652
  270.0 54.4 %copy-start.109 = (f32[1536]{0:T(1024)}, f32[1536]{0:T(1024)S(1)}, u32[]{:S(2)}) copy-start(f32[1536]{0:T(1024)S(1)} %get-tuple-element.259) | copy-start | bytes 18436
  323.8 52.3 %copy-start.33 = (f32[128,1536]{1,0:T(8,128)}, f32[128,1536]{1,0:T(8,128)S(1)}, u32[]{:S(2)}) copy-start(f32[128,1536]{1,0:T(8,128)S(1)} %get-tuple-element.271) | copy-start | bytes 2359300
  464.8 239.1 %reduce-scatter.9.cloned.1.call-start = ((), (), s32[]{:S(2)}) async-start(), calls=%async_computation.7 | async-start | bytes 5898240 | tf_op jit(solution)/shard_map/reduce_scatter | solution.py:1112
  465.5 238.3 %reduce-scatter.11.cloned.1.call-start = ((), (), s32[]{:S(2)}) async-start(), calls=%async_computation.8 | async-start | bytes 5898240 | tf_op jit(solution)/shard_map/reduce_scatter | solution.py:1113
  502.5 436.5 %reduce-scatter.17.cloned.1.call-start = ((), (), s32[]{:S(2)}) async-start(), calls=%async_computation.11 | async-start | bytes 5898240 | tf_op jit(solution)/shard_map/reduce_scatter | solution.py:1113
  502.6 37.6 %copy-start.16 = (bf16[128,1536]{1,0:T(8,128)(2,1)S(1)}, bf16[128,1536]{1,0:T(8,128)(2,1)}, u32[]{:S(2)}) copy-start(bf16[128,1536]{1,0:T(8,128)(2,1)} %copy-done.15) | copy-start | bytes 1179652
  502.6 37.6 %copy-start.41 = (f32[128,1536]{1,0:T(8,128)S(1)}, f32[128,1536]{1,0:T(8,128)}, u32[]{:S(2)}) copy-start(f32[128,1536]{1,0:T(8,128)} %copy-done.40) | copy-start | bytes 2359300
  502.6 37.6 %copy-start.112 = (f32[1536]{0:T(1024)S(1)}, f32[1536]{0:T(1024)}, u32[]{:S(2)}) copy-start(f32[1536]{0:T(1024)} %get-tuple-element.258) | copy-start | bytes 18436
  502.6 37.6 %copy-start.142 = (f32[128]{0:T(128)S(1)}, f32[128]{0:T(128)}, u32[]{:S(2)}) copy-start(f32[128]{0:T(128)} %copy-done.141) | copy-start | bytes 1540
  502.6 37.6 %copy-start.155 = (f32[128]{0:T(128)S(1)}, f32[128]{0:T(128)}, u32[]{:S(2)}) copy-start(f32[128]{0:T(128)} %get-tuple-element.317) | copy-start | bytes 1540
  540.2 35.1 %copy-start.131 = (f32[3,512]{1,0:T(4,128)S(1)}, f32[3,512]{1,0:T(4,128)}, u32[]{:S(2)}) copy-start(f32[3,512]{1,0:T(4,128)} %copy-done.130) | copy-start | bytes 18436
  540.2 35.1 %copy-start.133 = (f32[3,512]{1,0:T(4,128)S(1)}, f32[3,512]{1,0:T(4,128)}, u32[]{:S(2)}) copy-start(f32[3,512]{1,0:T(4,128)} %copy-done.132) | copy-start | bytes 18436
  540.2 35.1 %copy-start.135 = (f32[3,512]{1,0:T(4,128)S(1)}, f32[3,512]{1,0:T(4,128)}, u32[]{:S(2)}) copy-start(f32[3,512]{1,0:T(4,128)} %copy-done.134) | copy-start | bytes 18436
  540.2 35.1 %copy-start.137 = (f32[3,512]{1,0:T(4,128)S(1)}, f32[3,512]{1,0:T(4,128)}, u32[]{:S(2)}) copy-start(f32[3,512]{1,0:T(4,128)} %copy-done.136) | copy-start | bytes 18436
  540.2 35.1 %copy-start.60 = (bf16[1,1,4,48,1536]{4,3,0,2,1:T(8,128)(2,1)S(1)}, bf16[1,1,4,48,1536]{4,3,0,2,1:T(8,128)(2,1)}, u32[]{:S(2)}) copy-start(bf16[1,1,4,48,1536]{4,3,0,2,1:T(8,128)(2,1)} %get-tuple-element.283) | copy-start | bytes 1769476
  604.7 32.6 %copy-start.54 = (f32[128,1536]{1,0:T(8,128)S(1)}, f32[128,1536]{1,0:T(8,128)}, u32[]{:S(2)}) copy-start(f32[128,1536]{1,0:T(8,128)} %get-tuple-element.267) | copy-start | bytes 2359300
  604.7 32.6 %copy-start.147 = (f32[128]{0:T(128)S(1)}, f32[128]{0:T(128)}, u32[]{:S(2)}) copy-start(f32[128]{0:T(128)} %copy-done.146) | copy-start | bytes 1540
  604.7 32.6 %copy-start.154 = (f32[128]{0:T(128)S(1)}, f32[128]{0:T(128)}, u32[]{:S(2)}) copy-start(f32[128]{0:T(128)} %get-tuple-element.315) | copy-start | bytes 1540
  703.9 239.3 %reduce-scatter.15.cloned.1.call-start = ((), (), s32[]{:S(2)}) async-start(), calls=%async_computation.10 | async-start | bytes 5898240 | tf_op jit(solution)/shard_map/reduce_scatter | solution.py:1112
  704.7 242.4 %reduce-scatter.13.cloned.1.call-start = ((), (), s32[]{:S(2)}) async-start(), calls=%async_computation.9 | async-start | bytes 5898240 | tf_op jit(solution)/shard_map/reduce_scatter | solution.py:1111
  704.8 87.5 %copy-start.114 = (f32[3,512]{1,0:T(4,128)}, f32[3,512]{1,0:T(4,128)S(1)}, u32[]{:S(2)}) copy-start(f32[3,512]{1,0:T(4,128)S(1)} %log_add_fusion.1) | copy-start | bytes 18436
  705.4 56.8 %copy-start.140 = (f32[128]{0:T(128)S(1)}, f32[128]{0:T(128)}, u32[]{:S(2)}) copy-start(f32[128]{0:T(128)} %copy-done.139) | copy-start | bytes 1540
  705.4 231.6 %collective-permute-start.3 = (bf16[128,1536]{1,0:T(8,128)(2,1)}, bf16[128,1536]{1,0:T(8,128)(2,1)}, u32[]{:S(2)}, u32[]{:S(2)}) collective-permute-start(bf16[128,1536]{1,0:T(8,128)(2,1)} %get-tuple-element.293), channel_id=1, source_target_pairs={{0,0},{1,8},{2,16},{3,24},{8,1},{9,9},{10,17},{11,25},{16,2},{17,1... | collective-permute-start | bytes 1179656 | tf_op jit(solution)/shard_map/ppermute | solution.py:1053
  712.6 49.6 %copy-start.36 = (f32[128,1536]{1,0:T(8,128)S(1)}, f32[128,1536]{1,0:T(8,128)}, u32[]{:S(2)}) copy-start(f32[128,1536]{1,0:T(8,128)} %copy-done.35) | copy-start | bytes 2359300
  712.6 52.0 %copy-start.56 = (f32[128,1536]{1,0:T(8,128)S(1)}, f32[128,1536]{1,0:T(8,128)}, u32[]{:S(2)}) copy-start(f32[128,1536]{1,0:T(8,128)} %get-tuple-element.265) | copy-start | bytes 2359300
  712.7 52.0 %copy-start.153 = (f32[128]{0:T(128)S(1)}, f32[128]{0:T(128)}, u32[]{:S(2)}) copy-start(f32[128]{0:T(128)} %get-tuple-element.313) | copy-start | bytes 1540
  844.9 92.1 %collective-permute-start.5 = (bf16[128,1536]{1,0:T(8,128)(2,1)}, bf16[128,1536]{1,0:T(8,128)(2,1)}, u32[]{:S(2)}, u32[]{:S(2)}) collective-permute-start(bf16[128,1536]{1,0:T(8,128)(2,1)} %fusion.104), channel_id=1, source_target_pairs={{0,0},{1,8},{2,16},{3,24},{8,1},{9,9},{10,17},{11,25},{16,2},{17,1... | collective-permute-start | bytes 1179656 | tf_op jit(solution)/shard_map/ppermute | solution.py:1053
  (133 other events, 677.8 us)
Sparse Core Ops, SparseCore 0:
  10.8 58.4 all-gather.12
  70.9 53.9 all-gather.14
  126.4 43.3 all-gather.16
  171.8 39.8 all-gather.18
  213.7 41.5 all-gather.20
  256.7 37.3 all-gather.22
  464.9 48.5 reduce-scatter.6
  516.8 60.4 reduce-scatter.8
  580.4 60.5 reduce-scatter.10
  704.0 48.3 reduce-scatter.16
  754.9 53.2 reduce-scatter.14
  810.8 68.5 reduce-scatter.12

commit v3 on v2

--- a/solution.py
+++ b/solution.py
@@ -96,7 +96,57 @@
                 rcopy(out.at[slot,sl],out.at[slot,sl],ss.at[idx,c],rs.at[idx,c],ring.sib_dev()).wait_recv()
     for cp in sends+started: cp.wait_send()
 
-def rs_ring(ring, K, part, buf, send, recv, slotf):
+class RingGather:
+    def __init__(self, ring, chunks, own, out, send, recv):
+        self.ring, self.k, self.own, self.out, self.send, self.recv = ring, chunks, own, out, send, recv
+        self.last = ring.n // 2
+        self.rows = own.shape[0] // chunks
+
+    def chunks(self, d, s):
+        if s < self.last:
+            return range(self.k)
+        return range(self.k // 2) if d == 0 else range(self.k // 2, self.k)
+
+    def copy(self, d, s, c):
+        sign = 1 - 2 * d
+        slot = self.ring.slot(self.ring.rho - (s - 1) * sign)
+        part = pl.ds(c * self.rows, self.rows)
+        source = self.own.at[part] if s == 1 else self.out.at[slot, part]
+        return rcopy(
+            source, self.out.at[slot, part], self.send.at[d, s - 1, c], self.recv.at[d, s - 1, c],
+            self.ring.dev(self.ring.rho + sign),
+        )
+
+    def arrive(self, d, s, c):
+        sign = 1 - 2 * d
+        ref = self.out.at[self.ring.slot(self.ring.rho - s * sign), pl.ds(c * self.rows, self.rows)]
+        rcopy(
+            ref, ref, self.send.at[d, s - 1, c], self.recv.at[d, s - 1, c],
+            self.ring.dev(self.ring.rho - sign),
+        ).wait_recv()
+
+    def step(self, s):
+        for c in range(self.k):
+            for d in (0, 1):
+                if c in self.chunks(d, s):
+                    if s > 1:
+                        self.arrive(d, s - 1, c)
+                    self.copy(d, s, c).start()
+
+    def finish(self):
+        for s in (self.last - 1, self.last):
+            for c in range(self.k):
+                for d in (0, 1):
+                    if c in self.chunks(d, s) and (s == self.last or c not in self.chunks(d, s + 1)):
+                        self.arrive(d, s, c)
+        for s in range(1, self.last + 1):
+            for c in range(self.k):
+                for d in (0, 1):
+                    if c in self.chunks(d, s):
+                        self.copy(d, s, c).wait_send()
+
+
+def rs_ring(ring, K, part, buf, send, recv, slotf, beside=None):
     n=ring.n; S=n//2; T=buf.shape[2]; rows=T//K; rho=ring.rho
     def chunks(d,s): return range(K) if s>1 else (range(K//2) if d==0 else range(K//2,K))
     sends=[]
@@ -121,6 +171,7 @@
                     src=part.at[slotf(dest),sl]
                 cp=rcopy(src,buf.at[d,s-1,sl],send.at[d,s-1,c],recv.at[d,s-1,c],ring.dev(rho+sg))
                 cp.start(); sends.append(cp)
+        if beside is not None: beside(s+1)
     for c in range(K):
         for d in (0,1):
             rd(d,S,c).wait_recv()
@@ -137,6 +188,81 @@
 DMA = pltpu.SemaphoreType.DMA
 
 
+class ShareGather:
+    def __init__(self, source, out, sems):
+        self.source, self.out = source, out
+        self.x_send, self.x_recv, self.s_send, self.s_recv, self.own, self.room = sems
+        x, c = lax.axis_index("xh"), lax.axis_index("co")
+        self.mine, self.across = x * 2 + c, (1 - x) * 2 + c
+        self.beside, self.beside_across = x * 2 + 1 - c, (1 - x) * 2 + 1 - c
+        self.chip, self.core = {"xh": 1 - x}, {"co": 1 - c}
+        self.parts = source.shape[0]
+
+    def to_chip(self, e):
+        return rcopy(
+            self.source.at[e], self.out.at[self.mine, e], self.x_send.at[e], self.x_recv.at[e],
+            self.chip,
+        )
+
+    def to_core(self, e):
+        if e == self.parts:
+            source, target = self.source, self.out.at[self.mine]
+        else:
+            source = target = self.out.at[self.across, e]
+        return rcopy(source, target, self.s_send.at[e], self.s_recv.at[e], self.core)
+
+    def keep(self, half):
+        ends = (self.source, self.room) if half == 0 else (self.room, self.out.at[self.mine])
+        return pltpu.make_async_copy(*ends, self.own.at[half])
+
+    def start(self):
+        for e in range(self.parts):
+            self.to_chip(e).start()
+        self.to_core(self.parts).start()
+        self.keep(0).start()
+
+    def forward(self):
+        self.keep(0).wait()
+        self.keep(1).start()
+        for e in range(self.parts):
+            ref = self.out.at[self.across, e]
+            rcopy(ref, ref, self.x_send.at[e], self.x_recv.at[e], self.chip).wait_recv()
+            self.to_core(e).start()
+
+    def finish(self):
+        for e in range(self.parts + 1):
+            ref = self.out.at[self.beside_across, e] if e < self.parts else self.out.at[self.beside]
+            rcopy(ref, ref, self.s_send.at[e], self.s_recv.at[e], self.core).wait_recv()
+        for e in range(self.parts):
+            self.to_chip(e).wait_send()
+        for e in range(self.parts + 1):
+            self.to_core(e).wait_send()
+        self.keep(1).wait()
+
+
+def share_devices():
+    return [{"xh": 1 - lax.axis_index("xh")}, {"co": 1 - lax.axis_index("co")}]
+
+
+def share_shapes(share):
+    if share is None:
+        return [], [], []
+    array = share[0]
+    parts = array.shape[1]
+    return (
+        [array],
+        [jax.ShapeDtypeStruct((4,) + array.shape[1:], BF16)],
+        [
+            DMA((parts,)),
+            DMA((parts,)),
+            DMA((parts + 1,)),
+            DMA((parts + 1,)),
+            DMA((2,)),
+            pltpu.VMEM(array.shape[1:], BF16),
+        ],
+    )
+
+
 def comm_params(number):
     return pltpu.CompilerParams(
         collective_id=number, has_side_effects=True, vmem_limit_bytes=40 << 20
@@ -147,92 +273,174 @@
     return pl.CostEstimate(flops=0, bytes_accessed=microseconds * 3_690_000, transcendentals=0)
 
 
-def gather_group(rows, planes, number=0):
+def gather_group(rows, planes, number, share=None):
     count, width = rows.shape
-
-    def kernel(x_ref, o_ref, send, recv, own):
+    more, outs, sems = share_shapes(share)
+
+    def kernel(x_ref, *refs):
+        if more:
+            w_ref, o_ref, b_ref, send, recv, own, *rest = refs
+        else:
+            o_ref, send, recv, own = refs
         ring = Ring8(planes)
-        barrier([ring.dev(ring.rho + 1), ring.dev(ring.rho - 1)])
+        devices = [ring.dev(ring.rho + 1), ring.dev(ring.rho - 1)]
+        barrier(devices + share_devices() * len(more))
         local = pltpu.make_async_copy(x_ref, o_ref.at[ring.slot(ring.rho)], own)
         local.start()
+        if more:
+            carried = ShareGather(w_ref.at[share[1]], b_ref, rest)
+            carried.start()
         ag_ring(ring, CHUNKS, x_ref, o_ref, send, recv)
+        if more:
+            carried.forward()
+            carried.finish()
         local.wait()
 
-    return pl.pallas_call(
+    results = pl.pallas_call(
         kernel,
-        out_shape=jax.ShapeDtypeStruct((2 * planes, count, width), BF16),
-        in_specs=[VMEM_SPEC],
-        out_specs=ANY_SPEC,
-        scratch_shapes=[DMA((2, planes, CHUNKS)), DMA((2, planes, CHUNKS)), DMA],
+        out_shape=[jax.ShapeDtypeStruct((2 * planes, count, width), BF16)] + outs,
+        in_specs=[VMEM_SPEC] + [ANY_SPEC] * len(more),
+        out_specs=[ANY_SPEC] * (1 + len(more)),
+        scratch_shapes=[DMA((2, planes, CHUNKS)), DMA((2, planes, CHUNKS)), DMA] + sems,
         compiler_params=comm_params(number),
         cost_estimate=busy(33),
         name="gather_group",
-    )(rows)
-
-
-def scatter_group(parts, planes, number):
+    )(rows, *more)
+    return results if more else results[0]
+
+
+def scatter_group(parts, planes, number, share=None):
     _, count, width = parts.shape
-
-    def kernel(p_ref, o_ref, buf, send, recv):
+    more, outs, sems = share_shapes(share)
+
+    def kernel(p_ref, *refs):
+        if more:
+            w_ref, o_ref, b_ref, buf, send, recv, *rest = refs
+        else:
+            o_ref, buf, send, recv = refs
         ring = Ring8(planes)
-        barrier([ring.dev(ring.rho + 1), ring.dev(ring.rho - 1)])
+        devices = [ring.dev(ring.rho + 1), ring.dev(ring.rho - 1)]
+        barrier(devices + share_devices() * len(more))
+        if more:
+            carried = ShareGather(w_ref.at[share[1]], b_ref, rest)
+            carried.start()
         rs_ring(ring, CHUNKS, p_ref, buf, send, recv, ring.slot)
         last = planes - 1
         o_ref[...] = (
             buf[0, last].astype(F32) + buf[1, last].astype(F32)
         ) + p_ref[ring.slot(ring.rho)].astype(F32)
-
-    return pl.pallas_call(
+        if more:
+            carried.forward()
+            carried.finish()
+
+    results = pl.pallas_call(
         kernel,
-        out_shape=jax.ShapeDtypeStruct((count, width), F32),
-        in_specs=[VMEM_SPEC],
-        out_specs=VMEM_SPEC,
+        out_shape=[jax.ShapeDtypeStruct((count, width), F32)] + outs,
+        in_specs=[VMEM_SPEC] + [ANY_SPEC] * len(more),
+        out_specs=[VMEM_SPEC] + [ANY_SPEC] * len(more),
         scratch_shapes=[
             pltpu.VMEM((2, planes, count, width), BF16),
             DMA((2, planes, CHUNKS)),
             DMA((2, planes, CHUNKS)),
-        ],
+        ]
+        + sems,
         compiler_params=comm_params(number),
         cost_estimate=busy(32),
         name="scatter_group",
-    )(parts)
-
-
-def gather_plane(rows):
+    )(parts, *more)
+    return results if more else results[0]
+
+
+def gather_plane(rows, tall=None):
     count, width = rows.shape
-
-    def kernel(x_ref, o_ref, send, recv, sib_send, sib_recv, own):
+    more = tall is not None
+
+    def kernel(x_ref, *refs):
+        if more:
+            w_ref, o_ref, t_ref, *refs = refs
+            *refs, f_send, f_recv, f_own = refs
+        else:
+            o_ref, *refs = refs
+        send, recv, sib_send, sib_recv, own = refs
         ring = Ring4()
-        barrier([ring.dev(ring.rho + 1), ring.dev(ring.rho - 1), ring.sib_dev()])
+        if more:
+            barrier([peer[0] for peer in plane_peers()])
+        else:
+            barrier([ring.dev(ring.rho + 1), ring.dev(ring.rho - 1), ring.sib_dev()])
         local = pltpu.make_async_copy(x_ref, o_ref.at[ring.slot(ring.rho)], own)
         local.start()
-        ag_ring(ring, CHUNKS, x_ref, o_ref, send, recv, (sib_send, sib_recv))
+        ends = []
+
+        def beside(turn):
+            if turn == 1 and more:
+                ends.append(hand_over(w_ref, t_ref, f_send, f_recv, f_own))
+
+        ag_ring(ring, CHUNKS, x_ref, o_ref, send, recv, (sib_send, sib_recv), beside)
         local.wait()
-
-    return pl.pallas_call(
+        for end in ends:
+            end()
+
+    shapes = [jax.ShapeDtypeStruct((8, count, width), BF16)]
+    if more:
+        shapes.append(jax.ShapeDtypeStruct(tall.shape, BF16))
+    results = pl.pallas_call(
         kernel,
-        out_shape=jax.ShapeDtypeStruct((8, count, width), BF16),
-        in_specs=[VMEM_SPEC],
-        out_specs=ANY_SPEC,
+        out_shape=shapes,
+        in_specs=[VMEM_SPEC] * len(shapes),
+        out_specs=[ANY_SPEC] + [VMEM_SPEC] * (len(shapes) - 1),
         scratch_shapes=[
             DMA((2, 2, CHUNKS)),
             DMA((2, 2, CHUNKS)),
             DMA((4, CHUNKS)),
             DMA((4, CHUNKS)),
             DMA,
-        ],
-        compiler_params=comm_params(3),
+        ]
+        + [DMA((3,)), DMA((3,)), DMA] * more,
+        compiler_params=comm_params(10 if more else 3),
         cost_estimate=busy(20),
         name="gather_plane",
-    )(rows)
+    )(rows, *([tall] if more else []))
+    return results if more else results[0]
 
 
 def scatter_plane(parts):
+    return scatter_plane_call(parts, [], 1, 4, None)[0]
+
+
+def scatter_plane_first(parts, slabs, out_weight, planes, share):
+    return scatter_plane_call(parts, [out_weight, *slabs], planes, 9, share)
+
+
+def scatter_plane_call(parts, beside, planes, number, share):
     _, count, width = parts.shape
-
-    def kernel(p_ref, o_ref, pair, buf, send, recv, sib_send, sib_recv):
+    extra = len(beside)
+    more, outs, sems = share_shapes(share)
+
+    def kernel(p_ref, *refs):
+        if more:
+            w_ref, refs = refs[0], refs[1:]
+        b_refs, o_ref, refs = refs[:extra], refs[extra], refs[extra + 1 :]
+        if more:
+            blocks, refs = refs[0], refs[1:]
+        if extra:
+            stores, refs = refs[:extra], refs[extra:]
+        pair, buf, send, recv, sib_send, sib_recv, refs = *refs[:6], refs[6:]
         ring = Ring4()
-        barrier([ring.dev(ring.rho + 1), ring.dev(ring.rho - 1), ring.sib_dev()])
+        if extra:
+            put, z_send, z_recv, *refs = refs
+            line_barrier(planes, [peer[0] for peer in plane_peers()])
+            if more:
+                carried = ShareGather(w_ref.at[share[1]], blocks, refs)
+                carried.start()
+            za = lax.axis_index("za")
+            puts = [
+                pltpu.make_async_copy(b_refs[i], stores[i].at[za], put.at[i]) for i in range(extra)
+            ]
+            for copy in puts:
+                copy.start()
+            line = LineGather(planes, stores, z_send, z_recv)
+        else:
+            barrier([ring.dev(ring.rho + 1), ring.dev(ring.rho - 1), ring.sib_dev()])
 
         def chip(r):
             x, b = ring.pos(r)
@@ -249,24 +457,45 @@
             )
             copy.start()
             copies.append(copy)
+        if extra:
+            for copy in puts:
+                copy.wait()
+            line.step(1)
         for i, copy in zip((2, 1, 3, 0), copies):
             place = chip(ring.rho + i)
             copy.wait_recv()
             pair[place] = (
                 pair[place].astype(F32) + p_ref[ring.slot(ring.rho + i)].astype(F32)
             ).astype(BF16)
-        rs_ring(ring, CHUNKS, pair, buf, send, recv, chip)
+        rs_ring(ring, CHUNKS, pair, buf, send, recv, chip, line.step if extra else None)
         o_ref[...] = (
             buf[0, 1].astype(F32) + buf[1, 1].astype(F32)
         ) + pair[chip(ring.rho)].astype(F32)
         for copy in copies:
             copy.wait_send()
-
+        if extra:
+            for turn in range(4, planes):
+                line.step(turn)
+            line.finish()
+        if more:
+            carried.forward()
+            carried.finish()
+
+    shapes, scratch = [], []
+    if extra:
+        shapes = [
+            jax.ShapeDtypeStruct((planes,) + array.shape, BF16) for array in beside
+        ]
+        scratch = [
+            DMA((extra,)),
+            DMA((extra, 2, planes - 1)),
+            DMA((extra, 2, planes - 1)),
+        ]
     return pl.pallas_call(
         kernel,
-        out_shape=jax.ShapeDtypeStruct((count, width), F32),
-        in_specs=[VMEM_SPEC],
-        out_specs=VMEM_SPEC,
+        out_shape=[jax.ShapeDtypeStruct((count, width), F32)] + outs + shapes,
+        in_specs=[VMEM_SPEC] + [ANY_SPEC] * len(more) + [VMEM_SPEC] * extra,
+        out_specs=[VMEM_SPEC] + [ANY_SPEC] * len(more) + [VMEM_SPEC] * len(shapes),
         scratch_shapes=[
             pltpu.VMEM((4, count, width), BF16),
             pltpu.VMEM((2, 2, count, width), BF16),
@@ -274,11 +503,13 @@
             DMA((2, 2, CHUNKS)),
             DMA((4,)),
             DMA((4,)),
-        ],
-        compiler_params=comm_params(4),
+        ]
+        + scratch
+        + sems,
+        compiler_params=comm_params(number),
         cost_estimate=busy(20),
-        name="scatter_plane",
-    )(parts)
+        name="scatter_plane_first" if extra else "scatter_plane",
+    )(parts, *more, *beside)
 
 
 def plane_peers():
@@ -378,163 +609,232 @@
                         self.copy(i, d, s).wait_send()
 
 
-def spread_first(pieces, planes):
-    _, layers, count, width = pieces.shape
-
-    def kernel(p_ref, a_ref, *refs):
-        later, (send, recv, own, z_send, z_recv) = refs[: layers - 1], refs[layers - 1 :]
+def flat_peers():
+    x, c = lax.axis_index("xh"), lax.axis_index("co")
+    peers = []
+    for k in (1, 2, 3):
+        px = x + (k // 2) * (1 - 2 * x)
+        pc = c + (k % 2) * (1 - 2 * c)
+        peers.append(({"xh": px, "co": pc}, px * 2 + pc))
+    return peers, x * 2 + c
+
+
+def hand_over(stage, target, send, recv, own):
+    peers, mine = flat_peers()
+    copies = []
+    for k, (device, f) in enumerate(peers):
+        copies.append(rcopy(stage.at[f], target.at[mine], send.at[k], recv.at[k], device))
+        copies[-1].start()
+    keep = pltpu.make_async_copy(stage.at[mine], target.at[mine], own)
+    keep.start()
+    return lambda: hand_over_end(peers, target, send, recv, keep, copies)
+
+
+def hand_over_end(peers, target, send, recv, keep, copies):
+    keep.wait()
+    for k, (device, f) in enumerate(peers):
+        ref = target.at[f]
+        rcopy(ref, ref, send.at[k], recv.at[k], device).wait_recv()
+    for copy in copies:
+        copy.wait_send()
+
+
+def enter(tokens, heads_part, other_part, out_weight, gain_lane, planes, share):
+    count, width = tokens.shape
+    more, outs, sems = share_shapes(share)
+    layers, rows = heads_part.shape[1:3]
+    extra = layers - 1
+
+    def kernel(x_ref, a_ref, b_ref, w_ref, *refs):
+        if more:
+            s_ref, refs = refs[0], refs[1:]
+        o_ref, stream_ref, t_ref, a_out, b_out, refs = *refs[:5], refs[5:]
+        a_late, b_late, refs = refs[:extra], refs[extra : 2 * extra], refs[2 * extra :]
+        if more:
+            blocks, refs = refs[0], refs[1:]
+        (
+            stage, normed, swap_send, swap_recv, send, recv, own, ring_send, ring_recv, sib_send,
+            sib_recv, put, za_send, za_recv, f_send, f_recv, *rest
+        ) = refs
         za = lax.axis_index("za")
+        x, c = lax.axis_index("xh"), lax.axis_index("co")
+        f = x * 2 + c
+        px, pc = za // 2, lax.rem(za, 2)
+        partner = {"za": f, "xh": px, "co": pc}
+        apart = ((za - f) * (za - f) + 8) // 9
+        ring = Ring4()
         peers = plane_peers()
-        line_barrier(planes, [peer[0] for peer in peers])
         group, place = own_places()
+
+        sem = pltpu.get_barrier_semaphore()
+        for peer in peers:
+            pl.semaphore_signal(sem, inc=1, device_id=peer[0], device_id_type=MESH)
+
+        @pl.when(za > 0)
+        def _():
+            pl.semaphore_signal(sem, inc=1, device_id={"za": za - 1}, device_id_type=MESH)
+
+        @pl.when(za < planes - 1)
+        def _():
+            pl.semaphore_signal(sem, inc=1, device_id={"za": za + 1}, device_id_type=MESH)
+
+        @pl.when(za != f)
+        def _():
+            pl.semaphore_signal(sem, inc=1, device_id=partner, device_id_type=MESH)
+
+        below, above = (za + planes - 1) // planes, (2 * planes - 2 - za) // planes
+        pl.semaphore_wait(sem, len(peers) + below + above + apart)
+
+        def swap():
+            return rcopy(x_ref, stream_ref, swap_send, swap_recv, partner)
+
+        @pl.when(za != f)
+        def _():
+            swap().start()
+
+        keep = pltpu.make_async_copy(x_ref, stream_ref, own.at[2 * layers])
+
+        @pl.when(za == f)
+        def _():
+            keep.start()
+
         copies = []
 
-        def target(layer, at):
-            return a_ref.at[za, at] if layer == 0 else later[layer - 1].at[at]
-
-        for layer in range(layers):
+        def target(kind, layer, at):
+            if layer == 0:
+                return (a_out, b_out)[kind].at[za, at]
+            return (a_late, b_late)[kind][layer - 1].at[at]
+
+        def scatter(kind, layer):
+            source = (a_ref, b_ref)[kind]
             for k, (device, their_group, _) in enumerate(peers):
                 copy = rcopy(
-                    p_ref.at[their_group, layer], target(layer, place),
-                    send.at[layer, k], recv.at[layer, k], device,
+                    source.at[their_group, layer], target(kind, layer, place),
+                    send.at[kind, layer, k], recv.at[kind, layer, k], device,
                 )
                 copy.start()
                 copies.append(copy)
-        locals_ = [
-            pltpu.make_async_copy(p_ref.at[group, layer], target(layer, place), own.at[layer])
-            for layer in range(layers)
-        ]
-        for copy in locals_:
-            copy.start()
-
-        def arrivals(layer):
+            local = pltpu.make_async_copy(
+                source.at[group, layer], target(kind, layer, place), own.at[kind * layers + layer]
+            )
+            local.start()
+            return local
+
+        def arrivals(kind, layer, local):
             for k, (device, _, their_place) in enumerate(peers):
-                ref = target(layer, their_place)
-                rcopy(ref, ref, send.at[layer, k], recv.at[layer, k], device).wait_recv()
-            locals_[layer].wait()
-
-        arrivals(0)
-        line = LineGather(planes, [a_ref], z_send, z_recv)
-        for s in range(1, planes):
-            line.step(s)
-            if s == 1:
+                ref = target(kind, layer, their_place)
+                rcopy(
+                    ref, ref, send.at[kind, layer, k], recv.at[kind, layer, k], device
+                ).wait_recv()
+            local.wait()
+
+        w_put = pltpu.make_async_copy(w_ref, stage.at[za], put)
+        w_put.start()
+        b_local = scatter(1, 0)
+        a_local = scatter(0, 0)
+        if more:
+            carried = ShareGather(s_ref.at[share[1]], blocks, rest)
+            carried.start()
+        tall = LineGather(planes, [stage], za_send.at[pl.ds(2, 1)], za_recv.at[pl.ds(2, 1)])
+        small = LineGather(planes, [b_out], za_send.at[pl.ds(0, 1)], za_recv.at[pl.ds(0, 1)])
+        line = LineGather(planes, [a_out], za_send.at[pl.ds(1, 1)], za_recv.at[pl.ds(1, 1)])
+        arrivals(1, 0, b_local)
+        for turn in range(1, planes):
+            small.step(turn)
+        w_put.wait()
+        tall.step(1)
+        arrivals(0, 0, a_local)
+        line.step(1)
+        for d in (0, 1):
+            small.wait_arrival(0, d, planes - 1)
+        columns = b_out[...].reshape(width, 128).astype(F32)
+        gain = columns.T[gain_lane : gain_lane + 1, :]
+
+        @pl.when(za != f)
+        def _():
+            swap().wait()
+
+        @pl.when(za == f)
+        def _():
+            keep.wait()
+
+        stream = stream_ref[...].astype(F32)
+        factor = lax.rsqrt(jnp.mean(stream * stream, axis=1, keepdims=True) + EPSILON)
+        normed[...] = (stream * factor * gain).astype(BF16)
+        local = pltpu.make_async_copy(normed, o_ref.at[ring.slot(ring.rho)], own.at[2 * layers])
+        local.start()
+        ends = []
+
+        def beside(turn):
+            if turn <= 2:
+                tall.step(turn + 1)
+                line.step(turn + 1)
+            if turn == 2:
                 for layer in range(1, layers):
-                    arrivals(layer)
+                    for kind in (1, 0):
+                        ends.append((kind, layer, scatter(kind, layer)))
+
+        ag_ring(ring, CHUNKS, normed, o_ref, ring_send, ring_recv, (sib_send, sib_recv), beside)
+        for turn in range(4, planes):
+            tall.step(turn)
+            line.step(turn)
+        tall.finish()
+        handed = hand_over(stage, t_ref, f_send, f_recv, own.at[2 * layers + 1])
+        local.wait()
         line.finish()
+        small.finish_sends()
+        for kind, layer, local in ends:
+            arrivals(kind, layer, local)
         for copy in copies:
             copy.wait_send()
-
-    return pl.pallas_call(
-        kernel,
-        out_shape=[jax.ShapeDtypeStruct((planes, 8, count, width), BF16)]
-        + [jax.ShapeDtypeStruct((8, count, width), BF16)] * (layers - 1),
-        in_specs=[VMEM_SPEC],
-        out_specs=[VMEM_SPEC] * layers,
-        scratch_shapes=[
-            DMA((layers, 7)),
-            DMA((layers, 7)),
-            DMA((layers,)),
-            DMA((1, 2, planes - 1)),
-            DMA((1, 2, planes - 1)),
-        ],
-        compiler_params=comm_params(5),
-        cost_estimate=busy(20),
-        name="spread_first",
-    )(pieces)
-
-
-def gather_plane_first(rows, later, out_weight, planes):
-    count, width = rows.shape
-    extra = len(later)
-
-    def kernel(x_ref, w_ref, *refs):
-        l_refs, refs = refs[:extra], refs[extra:]
-        o_ref, t_ref, refs = refs[0], refs[1], refs[2:]
-        s_refs, refs = refs[:extra], refs[extra:]
-        stage, send, recv, sib_send, sib_recv, own, put, z_send, z_recv, f_send, f_recv = refs
-        za = lax.axis_index("za")
-        x, c = lax.axis_index("xh"), lax.axis_index("co")
-        mine = x * 2 + c
-        ring = Ring4()
-        peers = plane_peers()
-        line_barrier(planes, [peer[0] for peer in peers])
-        puts = [
-            pltpu.make_async_copy(src, dst.at[za], put.at[i])
-            for i, (src, dst) in enumerate(
-                [(w_ref, stage)] + [(l_refs[i], s_refs[i]) for i in range(extra)]
-            )
-        ]
-        for copy in puts:
-            copy.start()
-        local = pltpu.make_async_copy(x_ref, o_ref.at[ring.slot(ring.rho)], own)
-        local.start()
-        line = LineGather(planes, [stage] + list(s_refs), z_send, z_recv)
-
-        def beside(turn):
-            if turn == 1:
-                for copy in puts:
-                    copy.wait()
-            line.step(turn)
-
-        ag_ring(ring, CHUNKS, x_ref, o_ref, send, recv, (sib_send, sib_recv), beside)
-        for turn in range(3, planes):
-            beside(turn)
-        local.wait()
-        for d in (0, 1):
-            line.wait_arrival(0, d, planes - 1)
-        copies = []
-        for k in (1, 2, 3):
-            px = x + (k // 2) * (1 - 2 * x)
-            pc = c + (k % 2) * (1 - 2 * c)
-            copies.append(
-                rcopy(
-                    stage.at[px * 2 + pc], t_ref.at[mine], f_send.at[k - 1], f_recv.at[k - 1],
-                    {"xh": px, "co": pc},
-                )
-            )
-            copies[-1].start()
-        keep = pltpu.make_async_copy(stage.at[mine], t_ref.at[mine], own)
-        keep.start()
-        keep.wait()
-        for k in (1, 2, 3):
-            px = x + (k // 2) * (1 - 2 * x)
-            pc = c + (k % 2) * (1 - 2 * c)
-            ref = t_ref.at[px * 2 + pc]
-            rcopy(ref, ref, f_send.at[k - 1], f_recv.at[k - 1], {"xh": px, "co": pc}).wait_recv()
-        for copy in copies:
-            copy.wait_send()
-        for i in range(1 + extra):
-            for d in (0, 1):
-                if i > 0:
-                    line.wait_arrival(i, d, planes - 1)
-        line.finish_sends()
-
-    return pl.pallas_call(
+        handed()
+        if more:
+            carried.forward()
+            carried.finish()
+
+    late = [
+        jax.ShapeDtypeStruct((8, rows, part.shape[-1]), BF16)
+        for part in (heads_part, other_part)
+        for _ in range(extra)
+    ]
+    results = pl.pallas_call(
         kernel,
         out_shape=[
             jax.ShapeDtypeStruct((8, count, width), BF16),
+            jax.ShapeDtypeStruct((count, width), BF16),
             jax.ShapeDtypeStruct((4,) + out_weight.shape, BF16),
+            jax.ShapeDtypeStruct((planes, 8, rows, heads_part.shape[-1]), BF16),
+            jax.ShapeDtypeStruct((planes, 8, rows, other_part.shape[-1]), BF16),
         ]
-        + [jax.ShapeDtypeStruct((planes,) + array.shape, BF16) for array in later],
-        in_specs=[VMEM_SPEC] * (2 + extra),
-        out_specs=[ANY_SPEC] + [VMEM_SPEC] * (1 + extra),
+        + late
+        + outs,
+        in_specs=[VMEM_SPEC] * 4 + [ANY_SPEC] * len(more),
+        out_specs=[ANY_SPEC] + [VMEM_SPEC] * (4 + len(late)) + [ANY_SPEC] * len(more),
         scratch_shapes=[
             pltpu.VMEM((planes,) + out_weight.shape, BF16),
+            pltpu.VMEM((count, width), BF16),
+            DMA,
+            DMA,
+            DMA((2, layers, 7)),
+            DMA((2, layers, 7)),
+            DMA((2 * layers + 2,)),
             DMA((2, 2, CHUNKS)),
             DMA((2, 2, CHUNKS)),
             DMA((4, CHUNKS)),
             DMA((4, CHUNKS)),
             DMA,
-            DMA((1 + extra,)),
-            DMA((1 + extra, 2, planes - 1)),
-            DMA((1 + extra, 2, planes - 1)),
+            DMA((3, 2, planes - 1)),
+            DMA((3, 2, planes - 1)),
             DMA((3,)),
             DMA((3,)),
-        ],
-        compiler_params=comm_params(6),
-        cost_estimate=busy(30),
-        name="gather_plane_first",
-    )(rows, out_weight, *later)
+        ]
+        + sems,
+        compiler_params=comm_params(5),
+        cost_estimate=busy(40),
+        name="enter",
+    )(tokens, heads_part, other_part, out_weight, *more)
+    first, rest = results[:5], results[5:]
+    return first, rest[:extra], rest[extra : 2 * extra], rest[2 * extra :]
 
 
 def collect(wide, tall, planes):
@@ -722,9 +1022,12 @@
     return lax.dot_general(a, b, (((1,), (1,)), ((), ())), preferred_element_type=F32)
 
 
-def plain_params(megabytes):
+def plain_params(megabytes, number=None):
     return pltpu.CompilerParams(
-        vmem_limit_bytes=megabytes << 20, dimension_semantics=("arbitrary",)
+        vmem_limit_bytes=megabytes << 20,
+        dimension_semantics=("arbitrary",),
+        collective_id=number,
+        has_side_effects=number is not None,
     )
 
 
@@ -736,19 +1039,47 @@
     return pl.BlockSpec((1,) + shape, lambda e: (e,) + (0,) * len(shape))
 
 
-def experts_forward(normed, codes, codes_t, router, gate_w, up_w, down_w, slots):
+def shares_of_expert(shape):
+    return pl.BlockSpec((shape[0], 1) + shape[2:], lambda e: (0, e, 0, 0))
+
+
+def side_by_side(ref):
+    return jnp.concatenate([ref[i, 0] for i in range(ref.shape[0])], axis=1)
+
+
+def experts_forward(normed, codes, codes_t, router, gate_w, up_w, down_w, beside, slots, planes, number, share=None):
     blocks, count, width = normed.shape
-    local, _, hidden_size = gate_w.shape
+    _, local, _, hidden_size = gate_w.shape
+    more, extra_outs, sems = share_shapes(share)
     lines = local * slots
     halves = 2
-    share = blocks // halves
-
-    def kernel(n_ref, c_ref, ct_ref, r_ref, gw_ref, uw_ref, dw_ref, out, g_out, u_out, p_out, pt_out, rows, back):
+    span = blocks // halves
+
+    def kernel(
+        n_ref, c_ref, ct_ref, r_ref, gw_ref, uw_ref, dw_ref, x_ref, *refs
+    ):
+        if more:
+            s_ref, refs = refs[0], refs[1:]
+        out, g_out, u_out, p_out, pt_out, b_out, *refs = refs
+        if more:
+            carried = ShareGather(s_ref.at[share[1]], refs[0], refs[6:])
+            refs = refs[1:]
+        rows, back, send, recv, own = refs[:5]
         e = pl.program_id(0)
+        ring = Ring8(planes)
+        gather = RingGather(ring, 2, x_ref, b_out, send, recv)
+        keep = pltpu.make_async_copy(x_ref, b_out.at[ring.slot(ring.rho)], own)
         first = (lax.axis_index("za") * 2 + lax.axis_index("yb")) * local
 
         @pl.when(e == 0)
         def _():
+            devices = [ring.dev(ring.rho + 1), ring.dev(ring.rho - 1)]
+            barrier(devices + share_devices() * len(more))
+            keep.start()
+            gather.step(1)
+            if more:
+                carried.start()
+
             @pl.loop(0, blocks)
             def _(b):
                 tokens = n_ref[b]
@@ -764,24 +1095,38 @@
                 ones = row_codes(lambda i: ct_ref[b, pl.ds(i, 1), :], first, local, slots)
                 rows[b] = dot(ones, tokens).astype(BF16)
 
+            gather.step(2)
+
         mine = pl.ds(pl.multiple_of(e * slots, slots), slots)
         for h in range(halves):
-            part = pl.ds(h * share, share)
-            held = rows[part, mine, :].reshape(share * slots, width)
-            gate = dot(held, gw_ref[0])
-            up = dot(held, uw_ref[0])
-            at = pl.ds(h * share * slots, share * slots)
+            part = pl.ds(h * span, span)
+            held = rows[part, mine, :].reshape(span * slots, width)
+            gate = dot(held, gw_ref[:, 0].reshape(width, hidden_size))
+            up = dot(held, uw_ref[:, 0].reshape(width, hidden_size))
+            at = pl.ds(h * span * slots, span * slots)
             g_out[0, at, :] = gate
             u_out[0, at, :] = up
             hidden = (gate * jax.nn.sigmoid(gate) * up).astype(BF16)
-            made = dot(hidden, dw_ref[0]).astype(BF16)
-            rows[part, mine, :] = made.reshape(share, slots, width)
+            made = dot(hidden, side_by_side(dw_ref)).astype(BF16)
+            rows[part, mine, :] = made.reshape(span, slots, width)
+
+        for turn in range(3, planes + 1):
+
+            @pl.when(e == min(turn - 3, local - 1))
+            def _():
+                gather.step(turn)
 
         @pl.when(e == local - 1)
         def _():
             @pl.loop(0, blocks)
             def _(b):
                 out[b] = dot(back[b], rows[b]).astype(BF16)
+
+            gather.finish()
+            keep.wait()
+            if more:
+                carried.forward()
+                carried.finish()
 
     wide = (local, blocks * slots, hidden_size)
     return pl.pallas_call(
@@ -793,47 +1138,58 @@
             jax.ShapeDtypeStruct(wide, F32),
             jax.ShapeDtypeStruct(codes.shape, F32),
             jax.ShapeDtypeStruct(codes_t.shape, F32),
-        ],
+            jax.ShapeDtypeStruct((blocks,) + beside.shape, BF16),
+        ]
+        + extra_outs,
         in_specs=[
             once(normed.shape),
             once(codes.shape),
             once(codes_t.shape),
             once(router.shape),
-            per_expert(gate_w.shape[1:]),
-            per_expert(up_w.shape[1:]),
-            per_expert(down_w.shape[1:]),
-        ],
+            shares_of_expert(gate_w.shape),
+            shares_of_expert(up_w.shape),
+            shares_of_expert(down_w.shape),
+            ANY_SPEC,
+        ]
+        + [ANY_SPEC] * len(more),
         out_specs=[
             once(normed.shape),
             per_expert(wide[1:]),
             per_expert(wide[1:]),
             once(codes.shape),
             once(codes_t.shape),
-        ],
+            ANY_SPEC,
+        ]
+        + [ANY_SPEC] * len(more),
         scratch_shapes=[
             pltpu.VMEM((blocks, lines, width), BF16),
             pltpu.VMEM((blocks, count, lines), BF16),
-        ],
-        compiler_params=plain_params(56),
+            DMA((2, planes, 2)),
+            DMA((2, planes, 2)),
+            DMA,
+        ]
+        + sems,
+        compiler_params=plain_params(56, number),
         cost_estimate=busy(16),
         name="experts_forward",
-    )(normed, codes, codes_t, router, gate_w, up_w, down_w)
+    )(normed, codes, codes_t, router, gate_w, up_w, down_w, beside, *more)
 
 
 def experts_backward(
     normed, arrived, codes, codes_t, probs_t, gate_w, up_w, down_w, gate_part, up_part, slots, shares
 ):
     blocks, count, width = normed.shape
-    local, _, hidden_size = gate_w.shape
+    pieces = len(arrived)
+    _, local, _, hidden_size = gate_w.shape
     lines = local * slots
     total = blocks * slots
     band = width // shares
     split = band % 128 == 0
 
     def kernel(
-        n_ref, a_ref, c_ref, ct_ref, pt_ref, gw_ref, uw_ref, dw_ref, g_ref, u_ref,
-        out, dg_out, du_out, dd_out, rows, outs, back, marks,
+        n_ref, c_ref, ct_ref, pt_ref, gw_ref, uw_ref, dw_ref, g_ref, u_ref, *refs
     ):
+        a_refs, (out, dg_out, du_out, dd_out, rows, outs, back, marks) = refs[:pieces], refs[pieces:]
         e = pl.program_id(0)
         first = (lax.axis_index("za") * 2 + lax.axis_index("yb")) * local
 
@@ -849,11 +1205,12 @@
 
                 back[b] = column_codes(c_ref[b], first, local, slots)
                 rows[b] = dot(row_codes(code, first, local, slots), n_ref[b]).astype(BF16)
-                outs[b] = dot(row_codes(code, first, local, slots, prob), a_ref[b]).astype(BF16)
+                upstream = jnp.concatenate([ref[b] for ref in a_refs], axis=0)
+                outs[b] = dot(row_codes(code, first, local, slots, prob), upstream).astype(BF16)
 
         mine = pl.ds(pl.multiple_of(e * slots, slots), slots)
         upstream = outs[:, mine, :].reshape(total, width)
-        hidden_grad = dot_t(upstream, dw_ref[0])
+        hidden_grad = dot_t(upstream, side_by_side(dw_ref))
         gate, up = g_ref[0], u_ref[0]
         logistic = jax.nn.sigmoid(gate)
         hidden = (gate * logistic * up).astype(BF16)
@@ -876,7 +1233,8 @@
                 dd_out[f, 0] = down[:, f * band : (f + 1) * band]
         else:
             dd_out[0] = down
-        back_rows = dot_t(gate_low, gw_ref[0]) + dot_t(up_low, uw_ref[0])
+        back_rows = dot_t(gate_low, gw_ref[:, 0].reshape(width, hidden_size))
+        back_rows = back_rows + dot_t(up_low, uw_ref[:, 0].reshape(width, hidden_size))
         rows[:, mine, :] = back_rows.astype(BF16).reshape(blocks, slots, width)
 
         @pl.when(e == local - 1)
@@ -892,7 +1250,8 @@
         down_shape = (shares, local, hidden_size, band)
         down_spec = pl.BlockSpec((shares, 1, hidden_size, band), lambda e: (0, e, 0, 0))
     else:
-        down_shape, down_spec = down_w.shape, per_expert(down_w.shape[1:])
+        down_shape = (local, hidden_size, width)
+        down_spec = per_expert(down_shape[1:])
     results = pl.pallas_call(
         kernel,
         grid=(local,),
@@ -904,16 +1263,16 @@
         ],
         in_specs=[
             once(normed.shape),
-            once(arrived.shape),
             once(codes.shape),
             once(codes_t.shape),
             once(probs_t.shape),
-            per_expert(gate_w.shape[1:]),
-            per_expert(up_w.shape[1:]),
-            per_expert(down_w.shape[1:]),
+            shares_of_expert(gate_w.shape),
+            shares_of_expert(up_w.shape),
+            shares_of_expert(down_w.shape),
             per_expert(gate_part.shape[1:]),
             per_expert(up_part.shape[1:]),
-        ],
+        ]
+        + [once(array.shape) for array in arrived],
         out_specs=[once((blocks, count, width + 128)), cut_spec, cut_spec, down_spec],
         scratch_shapes=[
             pltpu.VMEM((blocks, lines, width), BF16),
@@ -924,7 +1283,7 @@
         compiler_params=plain_params(60),
         cost_estimate=busy(30),
         name="experts_backward",
-    )(normed, arrived, codes, codes_t, probs_t, gate_w, up_w, down_w, gate_part, up_part)
+    )(normed, codes, codes_t, probs_t, gate_w, up_w, down_w, gate_part, up_part, *arrived)
     row_sums, gate_term, up_term, down_term = results
     if not split:
         down_term = jnp.moveaxis(
@@ -1052,8 +1411,6 @@
     def exchange(array):
         return lax.ppermute(array, ("za", "xh", "co"), swap)
 
-    stream = exchange(layer_in[0]).astype(F32)
-    upstream_low = exchange(cotangent[0])
     starts = exchange(doc_starts)[0]
     chosen = exchange(routes[0])
 
@@ -1091,19 +1448,28 @@
 
     def in_order(array):
         if groups > 1:
-            array = array.reshape(planes, 2, 4, groups, bands, padded)
+            array = array.reshape(planes, 2, 4, groups, bands, -1)
             array = jnp.swapaxes(array, 2, 3)
-        return array.reshape(width, padded)
-
-    first, *later = spread_first(pieces, planes)
-    slabs = [in_order(first)]
-
-    def fetch_experts(layer):
-        return (
-            lax.all_gather(gate_weight[layer], ("grp", "xh", "co"), axis=1, tiled=True),
-            lax.all_gather(up_weight[layer], ("grp", "xh", "co"), axis=1, tiled=True),
-            lax.all_gather(down_weight[layer], ("grp", "xh", "co"), axis=2, tiled=True),
-        )
+        return array.reshape(width, -1)
+
+    all_out = whole_rows(out_weight)
+    def carry(array, layer):
+        return (array, layer) if groups == 1 and layer < layers else None
+
+    firsts, late_heads, late_others, carried = enter(
+        layer_in[0],
+        pieces[..., : padded - 128],
+        pieces[..., padded - 128 :],
+        all_out[0],
+        used - 2 - (padded - 128),
+        planes,
+        carry(gate_weight, 0),
+    )
+    normed_first, stream, tall_rows, heads_slab, other_slab = firsts
+    stream = stream.astype(F32)
+    slabs = [(in_order(heads_slab), in_order(other_slab))]
+    upstream_low, tall_rows = lax.optimization_barrier((cotangent[0], tall_rows))
+    upstream_low = exchange(upstream_low)
 
     def sum_experts(gate_term, up_term, down_term):
         axes = ("grp", "xh", "co")
@@ -1131,26 +1497,33 @@
     angles = positions.astype(F32)[:, None] * inverse[None, :]
     cosine, sine = jnp.cos(angles), jnp.sin(angles)
 
-    states = []
-    out_rows = None
+    def fetch_experts(layer):
+        axes = ("grp", "xh", "co")
+        return [
+            lax.all_gather(gate_weight[layer], axes, axis=1, tiled=True)[None],
+            lax.all_gather(up_weight[layer], axes, axis=1, tiled=True)[None],
+            lax.all_gather(down_weight[layer], axes, axis=2, tiled=True)[None],
+        ]
+
+    states, arrived = [], []
+    out_rows = []
     for layer in range(layers):
-        gate_w, up_w, down_w = fetch_experts(layer)
-        small_part = slabs[layer][:, columns + 2 * kv :]
+        if groups > 1:
+            carried = fetch_experts(layer)
+        slab = jnp.concatenate(slabs[layer], axis=1)
+        small_part = slab[:, columns + 2 * kv :]
         attn_row = small_part[:, experts_all].astype(F32)
         ffn_row = small_part[:, experts_all + 1].astype(F32)
-        qkv_w = slabs[layer][:, : columns + 2 * kv]
+        qkv_w = slab[:, : columns + 2 * kv]
         router_w = jnp.pad(small_part[:, :experts_all], ((0, 0), (0, 128 - experts_all)))
         factor_one = norm_factor(stream)
-        own_one = (stream * factor_one * attn_row).astype(BF16)
         if layer == 0:
-            normed_one, tall_rows, *rest = gather_plane_first(
-                own_one, later, whole_rows(out_weight), planes
-            )
-            slabs += [in_order(array) for array in rest]
-            tall_rows = tall_rows.reshape(4, layers, groups, bands, width)
-            out_rows = jnp.transpose(tall_rows, (1, 2, 0, 3, 4)).reshape(layers, columns, width)
+            normed_one = normed_first
         else:
-            normed_one = gather_plane(own_one)
+            own_one = (stream * factor_one * attn_row).astype(BF16)
+            normed_one, tall_rows = gather_plane(own_one, tall_rows)
+        tall_rows = jnp.swapaxes(tall_rows.reshape(4, groups, bands, width), 0, 1)
+        out_rows.append(tall_rows.reshape(columns, width))
         normed_one = normed_one.reshape(length, width)
         qkv = jnp.dot(normed_one, qkv_w, preferred_element_type=F32)
         queries = rotate(qkv[:, :columns], cosine, sine).astype(BF16)
@@ -1160,18 +1533,44 @@
         mixed, logs = attend(queries, keys, values, documents)
         mixed = mixed.reshape(length, columns)
         branch = jnp.dot(mixed, out_rows[layer], preferred_element_type=F32).astype(BF16)
-        middle = stream + scatter_plane(branch.reshape(8, count, width))
+        branch = branch.reshape(8, count, width)
+        if layer + 1 < layers:
+            share = carry(up_weight, 0) if layer == 0 else None
+            branch, *later = scatter_plane_first(
+                branch, (late_heads[layer], late_others[layer]), all_out[layer + 1], planes, share
+            )
+            if share is not None:
+                carried, later = [carried[0], later[0]], later[1:]
+            tall_rows, *later = later
+            slabs.append([in_order(array) for array in later])
+        else:
+            branch = scatter_plane(branch)
+        middle = stream + branch
         factor_two = norm_factor(middle)
         own_two = (middle * factor_two * ffn_row).astype(BF16)
         if layer == 0:
-            both = gather_group(jnp.concatenate([own_two, codes], axis=1), planes, 8)
+            both = jnp.concatenate([own_two, codes], axis=1)
+            both = gather_group(both, planes, 8, carry(down_weight, 0))
+            if groups == 1:
+                both, last = both
+                carried = [*carried, last]
             normed_two, codes = both[..., :width], both[..., width:].astype(F32)
             codes_t = jnp.swapaxes(codes[..., :32], 1, 2)
         else:
-            normed_two = gather_group(own_two, planes)
-        total, gate_part, up_part, gate_probs, probs_t = experts_forward(
-            normed_two, codes, codes_t, router_w, gate_w, up_w, down_w, slots
-        )
+            share = carry(down_weight, layer)
+            normed_two = gather_group(own_two, planes, 12, share)
+            if share is not None:
+                normed_two, last = normed_two
+                carried = [*carried, last]
+        share = count // layers
+        gate_w, up_w, down_w = carried
+        share = count // layers
+        total, gate_part, up_part, gate_probs, probs_t, gathered, *carried = experts_forward(
+            normed_two, codes, codes_t, router_w, gate_w, up_w, down_w,
+            upstream_low[layer * share : (layer + 1) * share], slots, planes,
+            11 if layer == 0 else 13, carry(gate_weight, layer + 1),
+        )
+        arrived.append(gathered)
         own_probs = lax.dynamic_index_in_dim(gate_probs, place, 0, keepdims=False)[:, :experts_all]
         states.append(
             (
@@ -1180,7 +1579,12 @@
                 gate_w, up_w, down_w, attn_row, ffn_row, qkv_w, router_w,
             )
         )
-        stream = middle + scatter_group(total, planes, 1)
+        share = carry(up_weight, layer + 1)
+        added = scatter_group(total, planes, 14 if share is not None else 1, share)
+        if share is not None:
+            added, last = added
+            carried = [*carried, last]
+        stream = middle + added
 
     result = exchange(stream.astype(BF16))[None]
 
@@ -1193,7 +1597,8 @@
             factor_two, own_two, normed_two, own_probs, probs_t, gate_part, up_part,
             gate_w, up_w, down_w, attn_row, ffn_row, qkv_w, router_w,
         ) = states[layer]
-        arrived = gather_group(upstream.astype(BF16), planes)
+        if layer + 1 < layers:
+            arrived = [gather_group(upstream.astype(BF16), planes, 0)]
         row_sums, gate_term, up_term, down_term = experts_backward(
             normed_two, arrived, codes, codes_t, probs_t, gate_w, up_w, down_w, gate_part, up_part,
             slots, 4 * groups,

time: 966 us -> 953 us (0.987)
  Pallas kernels: 768 us -> 740 us
  local copies, waits for them, and re-layouts: 50.1 us -> 60.1 us
    pallas_call x17 -> x15, Pallas kernels: 582 us -> 535 us  [the longest x4 150 us: scatter_group(): pl.pallas_call(kernel, out_shape=[jax.ShapeDtypeStruct((count, width), F3...]
    pallas_call x2, Pallas kernels: 45 us -> 64.5 us  [experts_forward(): pl.pallas_call(kernel, grid=(local,), out_shape=[jax.ShapeDtypeStruct(nor...]
    unnamed x330 -> x303, local copies, waits for them, and re-layouts: 23.7 us -> 31.1 us
  transfers between devices with their start and end apart: 18 -> 11, of which waited for: 0 -> 0; matrix products, arithmetic and copies ran while one was open for 13% -> 13% of each run, Pallas kernels for 74% -> 56%
where the time goes in v3:
time: 953 us; the launch traced here: 947 us
  Pallas kernels  740 us (78%)
  local copies, waits for them, and re-layouts  60.1 us (6%)
  other arithmetic  55.4 us (6%)
  matrix products  54.4 us (6%)
  starting transfers between devices  18.9 us (2%)
  between operations  16.7 us (2%)
    pallas_call x4, Pallas kernels, scatter_group(): pl.pallas_call(kernel, out_shape=[jax.ShapeDtypeStruct((count, width), F3...  150 us
    pallas_call x4, Pallas kernels, scatter_plane_call(): pl.pallas_call(kernel, out_shape=[jax.ShapeDtypeStruct((count, width), F3...  125 us
    pallas_call x3, Pallas kernels, gather_group(): pl.pallas_call(kernel, out_shape=[jax.ShapeDtypeStruct((2 * planes, count...  110 us
    pallas_call x3, Pallas kernels, gather_plane(): pl.pallas_call(kernel, out_shape=shapes, in_specs=[VMEM_SPEC] * len(shape...  78 us
    pallas_call x1, Pallas kernels, collect(): pl.pallas_call(kernel, out_shape=[jax.ShapeDtypeStruct((8, count, width),...  77.8 us
    pallas_call x1, Pallas kernels, enter(): pl.pallas_call(kernel, out_shape=[jax.ShapeDtypeStruct((8, count, width),...  71.9 us
    pallas_call x2, Pallas kernels, experts_forward(): pl.pallas_call(kernel, grid=(local,), out_shape=[jax.ShapeDtypeStruct(nor...  64.5 us
    pallas_call x2, Pallas kernels, experts_backward(): pl.pallas_call(kernel, grid=(local,), out_shape=[jax.ShapeDtypeStruct((bl...  62 us
  transfers between devices with their start and end apart: 11, of which 0 were waited for; matrix products, arithmetic and copies ran while one was open for 13% of the time, Pallas kernels for 56%

profile of v3, /device:TPU:9, one launch (start us, length us, event | category | flops | bytes accessed | tf_op | source)
XLA Modules:
  0.0 946.6 jit_solution(13880906280624881898)
XLA Ops:
  7.2 2.0 collective-permute-start
  9.3 1.9 collective-permute-start.1
  21.9 71.9 %enter.1 = (bf16[8,128,1536]{2,1,0:T(8,128)(2,1)S(1)}, bf16[128,1536]{1,0:T(8,128)(2,1)S(1)}, bf16[4,48,1536]{2,1,0:T(8,128)(2,1)S(1)}, bf16[4,8,48,256]{3,2,1,0...) custom-call(bf16[128,1536]{1,0:T(8,128)(2,1)S(1)} %bitcast.326, ...), custom_call_target="tpu_custom_call" | custom-call | bytes 147600000 | tf_op jit(solution)/shard_map/enter/pallas_call | solution.py:800
  93.8 5.8 collective-permute-start.2
  115.9 46.5 %scatter_plane_first.1 = (f32[128,1536]{1,0:T(8,128)S(1)}, bf16[4,3,384,512]{3,2,1,0:T(8,128)(2,1)S(1)}, bf16[4,48,1536]{2,1,0:T(8,128)(2,1)S(1)}, bf16[4,8,48,2...) custom-call(bf16[8,128,1536]{2,1,0:T(8,128)(2,1)S(1)} %bitcast.300, bf16[2,3,384,512]{3,2,1,0:T(8,128)(2,1)S(1)} %copy-done.10, ...), custom_call_target="tpu_custom_call" | custom-call | bytes 73800000 | tf_op jit(solution)/shard_map/scatter_plane_first/pallas_call | solution.py:494
  162.4 2.2 copy-done.1
  170.5 40.8 %gather_group.3 = (bf16[8,128,1664]{2,1,0:T(8,128)(2,1)S(1)}, bf16[4,3,512,384]{3,2,1,0:T(8,128)(2,1)S(1)}) custom-call(bf16[128,1664]{1,0:T(8,128)(2,1)S(1)} %fusion.100.x_ref, bf16[2,3,512,384]{3,2,1,0:T(8,128)(2,1)S(1)} %copy-done.8), custom_call_target="tpu_custom_call" | custom-call | bytes 121770000 | tf_op jit(solution)/shard_map/gather_group/pallas_call | solution.py:299
  211.3 2.2 copy-done.2
  213.4 2.0 slice.410.n_ref
  215.4 3.8 copy.168
  223.7 36.9 %experts_forward.2 = (bf16[8,128,1536]{2,1,0:T(8,128)(2,1)}, f32[3,512,512]{2,1,0:T(8,128)}, f32[3,512,512]{2,1,0:T(8,128)}, f32[8,128,128]{2,1,0:T(8,128)}, f32...) custom-call(bf16[8,128,1536]{2,1,0:T(8,128)(2,1)} %slice.410.n_ref, ...), custom_call_target="tpu_custom_call" | custom-call | bytes 59040000 | tf_op jit(solution)/shard_map/experts_forward/pallas_call | solution.py:1132
  260.6 1.9 copy-done.22
  262.5 36.6 %scatter_group.4 = (f32[128,1536]{1,0:T(8,128)S(1)}, bf16[4,3,384,512]{3,2,1,0:T(8,128)(2,1)S(1)}) custom-call(bf16[8,128,1536]{2,1,0:T(8,128)(2,1)S(1)} %copy-done.22, bf16[2,3,384,512]{3,2,1,0:T(8,128)(2,1)S(1)} %copy-done.11), custom_call_target="tpu_custom_call" | custom-call | bytes 118080000 | tf_op jit(solution)/shard_map/scatter_group/pallas_call | solution.py:336
  300.6 24.6 %gather_plane.3 = (bf16[8,128,1536]{2,1,0:T(8,128)(2,1)S(1)}, bf16[4,48,1536]{2,1,0:T(8,128)(2,1)S(1)}) custom-call(bf16[128,1536]{1,0:T(8,128)(2,1)S(1)} %multiply_convert_fusion.1.x_ref, bf16[4,48,1536]{2,1,0:T(8,128)(2,1)S(1)} %copy-done.29), custom_call_target="tpu_custom_call" | custom-call | bytes 73800000 | tf_op jit(solution)/shard_map/gather_plane/pallas_call | solution.py:386
  337.0 18.7 %scatter_plane.3 = f32[128,1536]{1,0:T(8,128)S(1)} custom-call(bf16[8,128,1536]{2,1,0:T(8,128)(2,1)S(1)} %bitcast.301), custom_call_target="tpu_custom_call" | custom-call | bytes 73800000 | tf_op jit(solution)/shard_map/scatter_plane/pallas_call | solution.py:494
  356.9 37.2 %gather_group.4 = (bf16[8,128,1536]{2,1,0:T(8,128)(2,1)S(1)}, bf16[4,3,512,384]{3,2,1,0:T(8,128)(2,1)S(1)}) custom-call(bf16[128,1536]{1,0:T(8,128)(2,1)S(1)} %multiply_convert_fusion.x_ref, bf16[2,3,512,384]{3,2,1,0:T(8,128)(2,1)S(1)} %copy-done.9), custom_call_target="tpu_custom_call" | custom-call | bytes 121770000 | tf_op jit(solution)/shard_map/gather_group/pallas_call | solution.py:299
  394.2 2.2 copy-done.4
  398.0 27.6 %experts_forward.3 = (bf16[8,128,1536]{2,1,0:T(8,128)(2,1)}, f32[3,512,512]{2,1,0:T(8,128)}, f32[3,512,512]{2,1,0:T(8,128)}, f32[8,128,128]{2,1,0:T(8,128)}, f32...) custom-call(bf16[8,128,1536]{2,1,0:T(8,128)(2,1)} %copy-done.5, f32[8,128,128]{2,1,0:T(8,128)} %copy.169.c_ref, ...), custom_call_target="tpu_custom_call" | custom-call | bytes 59040000 | tf_op jit(solution)/shard_map/experts_forward/pallas_call | solution.py:1132
  425.6 31.0 %experts_backward.2 = (bf16[8,128,1664]{2,1,0:T(8,128)(2,1)}, bf16[4,3,384,512]{3,2,1,0:T(8,128)(2,1)}, bf16[4,3,384,512]{3,2,1,0:T(8,128)(2,1)}, bf16[4,3,512,384]{3,2,1,0:T(8,128)(2,1)}) custom-call(bf16[8,128,1536]{2,1,0:T(8,128)(2,1)} %copy-done.5, f32[8,128,128]{2,1,0:T(8,128)} %copy.169.c_ref, f32[8,32,128]{2,1,0:T(8,128)} %slice_bitcast_fusion.8.ct_ref, ...), custom_call_target="tpu_custom_call" | custom-call | bytes 110700000 | tf_op jit(solution)/shard_map/experts_backward/pallas_call | solution.py:1255
  457.4 2.0 copy-done.21
  459.5 31.3 %scatter_group.5 = f32[128,1536]{1,0:T(8,128)S(1)} custom-call(bf16[8,128,1536]{2,1,0:T(8,128)(2,1)S(1)} %copy-done.21), custom_call_target="tpu_custom_call" | custom-call | bytes 118080000 | tf_op jit(solution)/shard_map/scatter_group/pallas_call | solution.py:336
  490.8 33.9 %scatter_group.6 = f32[128,1664]{1,0:T(8,128)S(1)} custom-call(bf16[8,128,1664]{2,1,0:T(8,128)(2,1)S(1)} %copy-done.19), custom_call_target="tpu_custom_call" | custom-call | bytes 118080000 | tf_op jit(solution)/shard_map/scatter_group/pallas_call | solution.py:336
  527.0 2.1 multiply_reduce_fusion.3
  529.7 2.7 fusion.184
  532.3 32.6 %gather_plane.4 = bf16[8,128,1536]{2,1,0:T(8,128)(2,1)S(1)} custom-call(bf16[128,1536]{1,0:T(8,128)(2,1)S(1)} %get-tuple-element.310.x_ref), custom_call_target="tpu_custom_call" | custom-call | bytes 73800000 | tf_op jit(solution)/shard_map/gather_plane/pallas_call | solution.py:386
  570.6 4.8 fusion.3
  575.4 5.1 fusion.5
  590.1 2.0 convolution_convert_fusion.7
  592.1 32.2 %scatter_plane.4 = f32[128,1536]{1,0:T(8,128)S(1)} custom-call(bf16[8,128,1536]{2,1,0:T(8,128)(2,1)S(1)} %bitcast.318), custom_call_target="tpu_custom_call" | custom-call | bytes 73800000 | tf_op jit(solution)/shard_map/scatter_plane/pallas_call | solution.py:494
  624.8 32.2 %gather_group.5.refs_0_ = bf16[8,128,1536]{2,1,0:T(8,128)(2,1)S(1)} custom-call(bf16[128,1536]{1,0:T(8,128)(2,1)S(1)} %get-tuple-element.308.x_ref), custom_call_target="tpu_custom_call" | custom-call | bytes 121770000 | tf_op jit(solution)/shard_map/gather_group/pallas_call | solution.py:299
  658.6 31.0 %experts_backward.3 = (bf16[8,128,1664]{2,1,0:T(8,128)(2,1)}, bf16[4,3,384,512]{3,2,1,0:T(8,128)(2,1)}, bf16[4,3,384,512]{3,2,1,0:T(8,128)(2,1)}, bf16[4,3,512,384]{3,2,1,0:T(8,128)(2,1)}) custom-call(bf16[8,128,1536]{2,1,0:T(8,128)(2,1)} %slice.410.n_ref, f32[8,128,128]{2,1,0:T(8,128)} %copy.169.c_ref, f32[8,32,128]{2,1,0:T(8,128)} %slice_bitcast_fusion.8.ct_ref, ...), custom_call_target="tpu_custom_call" | custom-call | bytes 110700000 | tf_op jit(solution)/shard_map/experts_backward/pallas_call | solution.py:1255
  691.1 4.5 collective-permute-start.3
  695.6 2.1 copy-done.20
  697.6 48.7 %scatter_group.7 = f32[128,1664]{1,0:T(8,128)S(1)} custom-call(bf16[8,128,1664]{2,1,0:T(8,128)(2,1)S(1)} %copy-done.20), custom_call_target="tpu_custom_call" | custom-call | bytes 118080000 | tf_op jit(solution)/shard_map/scatter_group/pallas_call | solution.py:336
  749.0 20.8 %gather_plane.5 = bf16[8,128,1536]{2,1,0:T(8,128)(2,1)S(1)} custom-call(bf16[128,1536]{1,0:T(8,128)(2,1)S(1)} %get-tuple-element.306.x_ref), custom_call_target="tpu_custom_call" | custom-call | bytes 73800000 | tf_op jit(solution)/shard_map/gather_plane/pallas_call | solution.py:386
  773.3 2.0 fusion.16
  775.4 2.7 fusion.87
  778.0 2.5 copy.188
  781.3 5.0 fusion
  786.3 2.5 fusion.2
  788.9 2.1 fusion.78
  802.9 27.4 %scatter_plane.5 = f32[128,1536]{1,0:T(8,128)S(1)} custom-call(bf16[8,128,1536]{2,1,0:T(8,128)(2,1)S(1)} %bitcast.319), custom_call_target="tpu_custom_call" | custom-call | bytes 73800000 | tf_op jit(solution)/shard_map/scatter_plane/pallas_call | solution.py:494
  831.7 4.5 collective-permute-start.4
  837.9 77.8 %collect.1 = (bf16[8,48,384]{2,1,0:T(8,128)(2,1)S(1)}, bf16[8,48,384]{2,1,0:T(8,128)(2,1)S(1)}, bf16[48,1536]{1,0:T(8,128)(2,1)S(1)}, bf16[48,1536]{1,0:T(8,128)(2,1)S(1)}) custom-call(bf16[4,8,48,384]{3,2,1,0:T(8,128)(2,1)S(1)} %bitcast.317, bf16[4,8,48,384]{3,2,1,0:T(8,128)(2,1)S(1)} %bitcast.316, bf16[4,48,1536]{2,1,0:T(8,128)(2,1)S(1)} %bitcast.321, ...), custom_call_target="tpu_custom_call" | custom-call | bytes 147600000 | tf_op jit(solution)/shard_map/collect/pallas_call | solution.py:968
  923.9 2.0 bitcast_convert_fusion
  925.8 4.2 maximum_convert_fusion.2
  930.1 3.9 maximum_convert_fusion.1
  934.0 3.8 maximum_convert_fusion
  (473 shorter events, 105.9 us)
Async XLA Ops:
  7.2 14.7 %copy-start.7 = (bf16[2,3,384,512]{3,2,1,0:T(8,128)(2,1)S(1)}, bf16[2,3,384,512]{3,2,1,0:T(8,128)(2,1)}, u32[]{:S(2)}) copy-start(bf16[2,3,384,512]{3,2,1,0:T(8,128)(2,1)} %refs_0_.9) | copy-start | bytes 7077892
  7.2 14.7 %copy-start.30 = (bf16[1,128,1536]{2,1,0:T(8,128)(2,1)S(1)}, bf16[1,128,1536]{2,1,0:T(8,128)(2,1)}, u32[]{:S(2)}) copy-start(bf16[1,128,1536]{2,1,0:T(8,128)(2,1)} %param.38) | copy-start | bytes 1179652
  7.2 682.4 %reduce-scatter.7.cloned.1.call-start = ((), (), s32[]{:S(2)}) async-start(), calls=%async_computation.6 | async-start | bytes 5898240 | tf_op jit(solution)/shard_map/reduce_scatter | solution.py:1477
  7.2 97.8 %collective-permute-start = (s32[1,4]{1,0:T(1,128)}, s32[1,4]{1,0:T(1,128)}, u32[]{:S(2)}, u32[]{:S(2)}) collective-permute-start(s32[1,4]{1,0:T(1,128)} %param.40), channel_id=1, source_target_pairs={{0,0},{1,8},{2,16},{3,24},{8,1},{9,9},{10,17},{11,25},{16,2},{17,1... | collective-permute-start | bytes 56 | tf_op jit(solution)/shard_map/ppermute | solution.py:1412
  9.3 158.5 %collective-permute-start.1 = (s32[128,8]{0,1:T(8,128)}, s32[128,8]{0,1:T(8,128)}, u32[]{:S(2)}, u32[]{:S(2)}) collective-permute-start(s32[128,8]{0,1:T(8,128)} %bitcast.371), channel_id=1, source_target_pairs={{0,0},{1,8},{2,16},{3,24},{8,1},{9,9},{10,17},{11,25},{16,2},{17,1... | collective-permute-start | bytes 12296 | tf_op jit(solution)/shard_map/ppermute | solution.py:1412
  93.8 20.3 %copy-start.26 = (bf16[4,48,1536]{2,1,0:T(8,128)(2,1)}, bf16[4,48,1536]{2,1,0:T(8,128)(2,1)S(1)}, u32[]{:S(2)}) copy-start(bf16[4,48,1536]{2,1,0:T(8,128)(2,1)S(1)} %get-tuple-element.205) | copy-start | bytes 1769476
  93.8 70.8 %copy-start.17 = (bf16[128,1536]{1,0:T(8,128)(2,1)}, bf16[128,1536]{1,0:T(8,128)(2,1)S(1)}, u32[]{:S(2)}) copy-start(bf16[128,1536]{1,0:T(8,128)(2,1)S(1)} %get-tuple-element.200) | copy-start | bytes 1179652
  93.8 128.1 %collective-permute-start.2 = (bf16[128,1536]{1,0:T(8,128)(2,1)}, bf16[128,1536]{1,0:T(8,128)(2,1)}, u32[]{:S(2)}, u32[]{:S(2)}) collective-permute-start(bf16[128,1536]{1,0:T(8,128)(2,1)} %bitcast.25), channel_id=1, source_target_pairs={{0,0},{1,8},{2,16},{3,24},{8,1},{9,9},{10,17},{11,25},{16,2},{17,1... | collective-permute-start | bytes 1179656 | tf_op jit(solution)/shard_map/ppermute | solution.py:1412
  104.3 479.1 %copy-start.64 = (f32[1024,32]{0,1:T(8,128)}, f32[1024,32]{0,1:T(8,128)S(1)}, u32[]{:S(2)}) copy-start(f32[1024,32]{0,1:T(8,128)S(1)} %get-tuple-element.348) | copy-start | bytes 393220
  223.7 36.9 %copy-start.11 = (bf16[2,3,384,512]{3,2,1,0:T(8,128)(2,1)S(1)}, bf16[2,3,384,512]{3,2,1,0:T(8,128)(2,1)}, u32[]{:S(2)}) copy-start(bf16[2,3,384,512]{3,2,1,0:T(8,128)(2,1)} %refs_0_.10) | copy-start | bytes 7077892
  262.5 36.7 %copy-start.54 = (f32[128,1536]{1,0:T(8,128)S(1)}, f32[128,1536]{1,0:T(8,128)}, u32[]{:S(2)}) copy-start(f32[128,1536]{1,0:T(8,128)} %copy-done.53) | copy-start | bytes 2359300
  262.5 37.4 %copy-start.107 = (f32[1536]{0:T(1024)S(1)}, f32[1536]{0:T(1024)}, u32[]{:S(2)}) copy-start(f32[1536]{0:T(1024)} %get-tuple-element.305) | copy-start | bytes 18436
  299.1 27.4 %copy-start.3 = (bf16[4,3,384,512]{3,2,1,0:T(8,128)(2,1)}, bf16[4,3,384,512]{3,2,1,0:T(8,128)(2,1)S(1)}, u32[]{:S(2)}) copy-start(bf16[4,3,384,512]{3,2,1,0:T(8,128)(2,1)S(1)} %get-tuple-element.223.uw_ref) | copy-start | bytes 14155780
  299.2 26.1 %copy-start.15 = (bf16[4,8,48,128]{3,2,1,0:T(8,128)(2,1)S(1)}, bf16[4,8,48,128]{3,2,1,0:T(8,128)(2,1)}, u32[]{:S(2)}) copy-start(bf16[4,8,48,128]{3,2,1,0:T(8,128)(2,1)} %copy-done.14) | copy-start | bytes 1179652
  299.2 26.1 %copy-start.42 = (bf16[4,8,48,256]{3,2,1,0:T(8,128)(2,1)S(1)}, bf16[4,8,48,256]{3,2,1,0:T(8,128)(2,1)}, u32[]{:S(2)}) copy-start(bf16[4,8,48,256]{3,2,1,0:T(8,128)(2,1)} %copy-done.41) | copy-start | bytes 2359300
  299.4 56.3 %copy-start.51 = (f32[128,1536]{1,0:T(8,128)}, f32[128,1536]{1,0:T(8,128)S(1)}, u32[]{:S(2)}) copy-start(f32[128,1536]{1,0:T(8,128)S(1)} %get-tuple-element.315) | copy-start | bytes 2359300
  299.9 26.7 %copy-start.141 = (f32[128]{0:T(128)}, f32[128]{0:T(128)S(1)}, u32[]{:S(2)}) copy-start(f32[128]{0:T(128)S(1)} %get-tuple-element.356) | copy-start | bytes 1540
  337.0 19.8 %copy-start.109 = (f32[1536]{0:T(1024)S(1)}, f32[1536]{0:T(1024)}, u32[]{:S(2)}) copy-start(f32[1536]{0:T(1024)} %get-tuple-element.304) | copy-start | bytes 18436
  337.0 20.0 %copy-start.9 = (bf16[2,3,512,384]{3,2,1,0:T(8,128)(2,1)S(1)}, bf16[2,3,512,384]{3,2,1,0:T(8,128)(2,1)}, u32[]{:S(2)}) copy-start(bf16[2,3,512,384]{3,2,1,0:T(8,128)(2,1)} %refs_0_.11) | copy-start | bytes 7077892
  356.4 69.2 %copy-start.137 = (f32[128]{0:T(128)}, f32[128]{0:T(128)S(1)}, u32[]{:S(2)}) copy-start(f32[128]{0:T(128)S(1)} %get-tuple-element.358) | copy-start | bytes 1540
  456.6 233.0 %reduce-scatter.9.cloned.1.call-start = ((), (), s32[]{:S(2)}) async-start(), calls=%async_computation.7 | async-start | bytes 5898240 | tf_op jit(solution)/shard_map/reduce_scatter | solution.py:1478
  457.4 232.3 %reduce-scatter.11.cloned.1.call-start = ((), (), s32[]{:S(2)}) async-start(), calls=%async_computation.8 | async-start | bytes 5898240 | tf_op jit(solution)/shard_map/reduce_scatter | solution.py:1479
  457.4 33.4 %copy-start.19 = (bf16[8,128,1664]{2,1,0:T(8,128)(2,1)S(1)}, bf16[8,128,1664]{2,1,0:T(8,128)(2,1)}, u32[]{:S(2)}) copy-start(bf16[8,128,1664]{2,1,0:T(8,128)(2,1)} %get-tuple-element.231.p_ref) | copy-start | bytes 10223620
  525.4 400.4 %reduce-scatter.17.cloned.1.call-start = ((), (), s32[]{:S(2)}) async-start(), calls=%async_computation.11 | async-start | bytes 5898240 | tf_op jit(solution)/shard_map/reduce_scatter | solution.py:1479
  529.7 35.3 %copy-start.128 = (f32[3,512]{1,0:T(4,128)S(1)}, f32[3,512]{1,0:T(4,128)}, u32[]{:S(2)}) copy-start(f32[3,512]{1,0:T(4,128)} %copy-done.127) | copy-start | bytes 18436
  529.7 35.3 %copy-start.130 = (f32[3,512]{1,0:T(4,128)S(1)}, f32[3,512]{1,0:T(4,128)}, u32[]{:S(2)}) copy-start(f32[3,512]{1,0:T(4,128)} %copy-done.129) | copy-start | bytes 18436
  529.7 35.3 %copy-start.132 = (f32[3,512]{1,0:T(4,128)S(1)}, f32[3,512]{1,0:T(4,128)}, u32[]{:S(2)}) copy-start(f32[3,512]{1,0:T(4,128)} %copy-done.131) | copy-start | bytes 18436
  529.7 35.4 %copy-start.134 = (f32[3,512]{1,0:T(4,128)S(1)}, f32[3,512]{1,0:T(4,128)}, u32[]{:S(2)}) copy-start(f32[3,512]{1,0:T(4,128)} %copy-done.133) | copy-start | bytes 18436
  590.1 34.2 %copy-start.52 = (f32[128,1536]{1,0:T(8,128)S(1)}, f32[128,1536]{1,0:T(8,128)}, u32[]{:S(2)}) copy-start(f32[128,1536]{1,0:T(8,128)} %copy-done.51) | copy-start | bytes 2359300
  590.1 34.3 %copy-start.108 = (f32[1536]{0:T(1024)S(1)}, f32[1536]{0:T(1024)}, u32[]{:S(2)}) copy-start(f32[1536]{0:T(1024)} %get-tuple-element.305) | copy-start | bytes 18436
  592.1 32.4 %copy-start.66 = (f32[128,1536]{1,0:T(8,128)S(1)}, f32[128,1536]{1,0:T(8,128)}, u32[]{:S(2)}) copy-start(f32[128,1536]{1,0:T(8,128)} %get-tuple-element.311) | copy-start | bytes 2359300
  592.1 32.4 %copy-start.142 = (f32[128]{0:T(128)S(1)}, f32[128]{0:T(128)}, u32[]{:S(2)}) copy-start(f32[128]{0:T(128)} %copy-done.141) | copy-start | bytes 1540
  592.1 32.4 %copy-start.145 = (f32[128]{0:T(128)S(1)}, f32[128]{0:T(128)}, u32[]{:S(2)}) copy-start(f32[128]{0:T(128)} %get-tuple-element.355) | copy-start | bytes 1540
  689.8 240.3 %reduce-scatter.15.cloned.1.call-start = ((), (), s32[]{:S(2)}) async-start(), calls=%async_computation.10 | async-start | bytes 5898240 | tf_op jit(solution)/shard_map/reduce_scatter | solution.py:1478
  689.8 56.7 %copy-start.55 = (f32[128,1536]{1,0:T(8,128)S(1)}, f32[128,1536]{1,0:T(8,128)}, u32[]{:S(2)}) copy-start(f32[128,1536]{1,0:T(8,128)} %copy-done.53) | copy-start | bytes 2359300
  689.8 56.7 %copy-start.89 = (f32[128,128]{1,0:T(8,128)S(1)}, f32[128,128]{1,0:T(8,128)}, u32[]{:S(2)}) copy-start(f32[128,128]{1,0:T(8,128)} %get-tuple-element.381) | copy-start | bytes 196612
  689.8 56.7 %copy-start.136 = (f32[128]{0:T(128)S(1)}, f32[128]{0:T(128)}, u32[]{:S(2)}) copy-start(f32[128]{0:T(128)} %copy-done.135) | copy-start | bytes 1540
  690.3 56.2 %copy-start.13 = (bf16[4,8,48,128]{3,2,1,0:T(8,128)(2,1)S(1)}, bf16[4,8,48,128]{3,2,1,0:T(8,128)(2,1)}, u32[]{:S(2)}) copy-start(bf16[4,8,48,128]{3,2,1,0:T(8,128)(2,1)} %copy-done.12) | copy-start | bytes 1179652
  690.4 243.6 %reduce-scatter.13.cloned.1.call-start = ((), (), s32[]{:S(2)}) async-start(), calls=%async_computation.9 | async-start | bytes 5898240 | tf_op jit(solution)/shard_map/reduce_scatter | solution.py:1477
  690.5 82.9 %copy-start.111 = (f32[3,512]{1,0:T(4,128)}, f32[3,512]{1,0:T(4,128)S(1)}, u32[]{:S(2)}) copy-start(f32[3,512]{1,0:T(4,128)S(1)} %log_add_fusion.1) | copy-start | bytes 18436
  691.1 232.8 %collective-permute-start.3 = (bf16[128,1536]{1,0:T(8,128)(2,1)}, bf16[128,1536]{1,0:T(8,128)(2,1)}, u32[]{:S(2)}, u32[]{:S(2)}) collective-permute-start(bf16[128,1536]{1,0:T(8,128)(2,1)} %get-tuple-element.329), channel_id=1, source_target_pairs={{0,0},{1,8},{2,16},{3,24},{8,1},{9,9},{10,17},{11,25},{16,2},{17,1... | collective-permute-start | bytes 1179656 | tf_op jit(solution)/shard_map/ppermute | solution.py:1412
  697.6 50.2 %copy-start.144 = (f32[128]{0:T(128)S(1)}, f32[128]{0:T(128)}, u32[]{:S(2)}) copy-start(f32[128]{0:T(128)} %get-tuple-element.353) | copy-start | bytes 1540
  746.3 23.5 %copy-start.25 = (f32[128,1664]{1,0:T(8,128)}, f32[128,1664]{1,0:T(8,128)S(1)}, u32[]{:S(2)}) copy-start(f32[128,1664]{1,0:T(8,128)S(1)} %scatter_group.7) | copy-start | bytes 2555908
  747.9 22.0 %copy-start.27 = (bf16[4,48,1536]{2,1,0:T(8,128)(2,1)S(1)}, bf16[4,48,1536]{2,1,0:T(8,128)(2,1)}, u32[]{:S(2)}) copy-start(bf16[4,48,1536]{2,1,0:T(8,128)(2,1)} %copy-done.26) | copy-start | bytes 1769476
  801.3 29.0 %copy-start.18 = (bf16[128,1536]{1,0:T(8,128)(2,1)S(1)}, bf16[128,1536]{1,0:T(8,128)(2,1)}, u32[]{:S(2)}) copy-start(bf16[128,1536]{1,0:T(8,128)(2,1)} %copy-done.17) | copy-start | bytes 1179652
  801.3 29.1 %copy-start.115 = (f32[1536]{0:T(1024)S(1)}, f32[1536]{0:T(1024)}, u32[]{:S(2)}) copy-start(f32[1536]{0:T(1024)} %get-tuple-element.302) | copy-start | bytes 18436
  802.9 27.7 %copy-start.67 = (f32[128,1536]{1,0:T(8,128)S(1)}, f32[128,1536]{1,0:T(8,128)}, u32[]{:S(2)}) copy-start(f32[128,1536]{1,0:T(8,128)} %get-tuple-element.307) | copy-start | bytes 2359300
  831.7 92.2 %collective-permute-start.4 = (bf16[128,1536]{1,0:T(8,128)(2,1)}, bf16[128,1536]{1,0:T(8,128)(2,1)}, u32[]{:S(2)}, u32[]{:S(2)}) collective-permute-start(bf16[128,1536]{1,0:T(8,128)(2,1)} %fusion.96), channel_id=1, source_target_pairs={{0,0},{1,8},{2,16},{3,24},{8,1},{9,9},{10,17},{11,25},{16,2},{17,1... | collective-permute-start | bytes 1179656 | tf_op jit(solution)/shard_map/ppermute | solution.py:1412
  (113 other events, 332.2 us)
Sparse Core Ops, SparseCore 0:
  456.7 47.3 reduce-scatter.6
  506.8 60.4 reduce-scatter.8
  569.9 60.4 reduce-scatter.10
  689.8 47.4 reduce-scatter.16
  739.8 51.4 reduce-scatter.14
  793.8 68.6 reduce-scatter.12

commit v4 on v3

--- a/solution.py
+++ b/solution.py
@@ -1,4 +1,6 @@
-import functools, math
+import math
+
+import numpy as np
 import jax, jax.numpy as jnp
 from jax import lax
 from jax.experimental import pallas as pl
@@ -146,6 +148,78 @@
                         self.copy(d, s, c).wait_send()
 
 
+class RingScatter:
+    def __init__(self, ring, chunks, part, buf, stage, send, recv, load):
+        self.ring, self.k, self.part, self.buf, self.stage = ring, chunks, part, buf, stage
+        self.send, self.recv, self.load = send, recv, load
+        self.last = ring.n // 2
+        self.rows = stage.shape[1] // chunks
+
+    def chunks(self, d, s):
+        if s > 1:
+            return range(self.k)
+        return range(self.k // 2) if d == 0 else range(self.k // 2, self.k)
+
+    def slot(self, d, s):
+        return self.ring.slot(self.ring.rho + (1 - 2 * d) * (self.last + 1 - s))
+
+    def loading(self, d, s):
+        return pltpu.make_async_copy(
+            self.part.at[self.slot(d, s)], self.stage.at[d], self.load.at[d]
+        )
+
+    def copy(self, d, s, c):
+        rows = pl.ds(c * self.rows, self.rows)
+        if s > 1 and c in self.chunks(d, s - 1):
+            source = self.buf.at[d, s - 2, rows]
+        else:
+            source = self.part.at[self.slot(d, s), rows]
+        return rcopy(
+            source, self.buf.at[d, s - 1, rows], self.send.at[d, s - 1, c],
+            self.recv.at[d, s - 1, c], self.ring.dev(self.ring.rho + 1 - 2 * d),
+        )
+
+    def arrive(self, d, s, c):
+        ref = self.buf.at[d, s - 1, pl.ds(c * self.rows, self.rows)]
+        rcopy(
+            ref, ref, self.send.at[d, s - 1, c], self.recv.at[d, s - 1, c],
+            self.ring.dev(self.ring.rho - (1 - 2 * d)),
+        ).wait_recv()
+
+    def step(self, s):
+        if s > 1:
+            for d in (0, 1):
+                self.loading(d, s).wait()
+        for c in range(self.k):
+            for d in (0, 1):
+                if c not in self.chunks(d, s):
+                    continue
+                if s > 1 and c in self.chunks(d, s - 1):
+                    self.arrive(d, s - 1, c)
+                    rows = pl.ds(c * self.rows, self.rows)
+                    self.buf[d, s - 2, rows, :] = (
+                        self.buf[d, s - 2, rows, :].astype(F32)
+                        + self.stage[d, rows, :].astype(F32)
+                    ).astype(BF16)
+                self.copy(d, s, c).start()
+        for d in (0, 1):
+            if s < self.last or d == 0:
+                self.loading(d, s + 1).start()
+
+    def finish(self):
+        self.loading(0, self.last + 1).wait()
+        for d in (0, 1):
+            for c in range(self.k):
+                self.arrive(d, self.last, c)
+        for s in range(1, self.last + 1):
+            for d in (0, 1):
+                for c in self.chunks(d, s):
+                    self.copy(d, s, c).wait_send()
+        return (
+            self.buf[0, self.last - 1].astype(F32) + self.buf[1, self.last - 1].astype(F32)
+        ) + self.stage[0].astype(F32)
+
+
 def rs_ring(ring, K, part, buf, send, recv, slotf, beside=None):
     n=ring.n; S=n//2; T=buf.shape[2]; rows=T//K; rho=ring.rho
     def chunks(d,s): return range(K) if s>1 else (range(K//2) if d==0 else range(K//2,K))
@@ -182,7 +256,8 @@
 HIGHEST = lax.Precision.HIGHEST
 F32 = jnp.float32
 BF16 = jnp.bfloat16
-ANY_SPEC = pl.BlockSpec(memory_space=pl.ANY)
+ANY_SPEC = pl.BlockSpec(memory_space=pltpu.HBM)
+GATHERED_SPEC = pl.BlockSpec(memory_space=pl.ANY)
 VMEM_SPEC = pl.BlockSpec(memory_space=pltpu.VMEM)
 CHUNKS = 4
 DMA = pltpu.SemaphoreType.DMA
@@ -221,9 +296,15 @@
         self.to_core(self.parts).start()
         self.keep(0).start()
 
-    def forward(self):
+    def middle(self):
         self.keep(0).wait()
         self.keep(1).start()
+
+    def end(self):
+        self.forward()
+        self.finish()
+
+    def forward(self):
         for e in range(self.parts):
             ref = self.out.at[self.across, e]
             rcopy(ref, ref, self.x_send.at[e], self.x_recv.at[e], self.chip).wait_recv()
@@ -240,6 +321,71 @@
         self.keep(1).wait()
 
 
+class ShareScatter:
+    def __init__(self, source, out, rest):
+        self.source, self.out = source, out
+        (
+            self.own, self.came, self.far, self.load, self.s_send, self.s_recv, self.x_send,
+            self.x_recv, self.put,
+        ) = rest
+        x, c = lax.axis_index("xh"), lax.axis_index("co")
+        self.mine = ((1 - x) * 2 + c, x * 2 + c)
+        self.theirs = ((1 - x) * 2 + 1 - c, x * 2 + 1 - c)
+        self.chip, self.core = {"xh": 1 - x}, {"co": 1 - c}
+        self.parts = source.shape[1]
+
+    def loading(self, k):
+        return pltpu.make_async_copy(self.source.at[self.mine[k]], self.own.at[k], self.load.at[k])
+
+    def to_core(self, k, e):
+        return rcopy(
+            self.source.at[self.theirs[k], e], self.came.at[k, e], self.s_send.at[k, e],
+            self.s_recv.at[k, e], self.core,
+        )
+
+    def to_chip(self, e):
+        return rcopy(
+            self.own.at[0, e], self.far.at[e], self.x_send.at[e], self.x_recv.at[e], self.chip
+        )
+
+    def start(self):
+        for k in (0, 1):
+            self.loading(k).start()
+            for e in range(self.parts):
+                self.to_core(k, e).start()
+
+    def middle(self):
+        self.loading(0).wait()
+        for e in range(self.parts):
+            self.to_core(0, e).wait_recv()
+            self.own[0, e] = (
+                self.own[0, e].astype(F32) + self.came[0, e].astype(F32)
+            ).astype(BF16)
+            self.to_chip(e).start()
+
+    def end(self):
+        self.loading(1).wait()
+        for e in range(self.parts):
+            self.to_core(1, e).wait_recv()
+            self.to_chip(e).wait_recv()
+            self.own[1, e] = (
+                self.own[1, e].astype(F32) + self.came[1, e].astype(F32) + self.far[e].astype(F32)
+            ).astype(BF16)
+        store = pltpu.make_async_copy(self.own.at[1], self.out, self.put)
+        store.start()
+        for e in range(self.parts):
+            self.to_chip(e).wait_send()
+            for k in (0, 1):
+                self.to_core(k, e).wait_send()
+        store.wait()
+
+
+def carrier(share, source, out, rest):
+    if share[1] is None:
+        return ShareScatter(source, out, rest)
+    return ShareGather(source.at[share[1]], out, rest)
+
+
 def share_devices():
     return [{"xh": 1 - lax.axis_index("xh")}, {"co": 1 - lax.axis_index("co")}]
 
@@ -249,6 +395,22 @@
         return [], [], []
     array = share[0]
     parts = array.shape[1]
+    if share[1] is None:
+        return (
+            [array],
+            [jax.ShapeDtypeStruct(array.shape[1:], BF16)],
+            [
+                pltpu.VMEM((2,) + array.shape[1:], BF16),
+                pltpu.VMEM((2,) + array.shape[1:], BF16),
+                pltpu.VMEM(array.shape[1:], BF16),
+                DMA((2,)),
+                DMA((2, parts)),
+                DMA((2, parts)),
+                DMA((parts,)),
+                DMA((parts,)),
+                DMA,
+            ],
+        )
     return (
         [array],
         [jax.ShapeDtypeStruct((4,) + array.shape[1:], BF16)],
@@ -263,9 +425,9 @@
     )
 
 
-def comm_params(number):
+def comm_params(number, megabytes=40):
     return pltpu.CompilerParams(
-        collective_id=number, has_side_effects=True, vmem_limit_bytes=40 << 20
+        collective_id=number, has_side_effects=True, vmem_limit_bytes=megabytes << 20
     )
 
 
@@ -273,69 +435,104 @@
     return pl.CostEstimate(flops=0, bytes_accessed=microseconds * 3_690_000, transcendentals=0)
 
 
-def gather_group(rows, planes, number, share=None):
+def gather_group(rows, planes, number, share=None, beside=None):
     count, width = rows.shape
     more, outs, sems = share_shapes(share)
+    extra = [] if beside is None else [beside]
 
     def kernel(x_ref, *refs):
         if more:
-            w_ref, o_ref, b_ref, send, recv, own, *rest = refs
-        else:
-            o_ref, send, recv, own = refs
+            w_ref, refs = refs[0], refs[1:]
+        if extra:
+            y_ref, refs = refs[0], refs[1:]
+        o_ref, refs = refs[0], refs[1:]
+        if more:
+            b_ref, refs = refs[0], refs[1:]
+        if extra:
+            yo_ref, refs = refs[0], refs[1:]
+        send, recv, own, *rest = refs
+        if extra:
+            y_send, y_recv, y_own, *rest = rest
         ring = Ring8(planes)
         devices = [ring.dev(ring.rho + 1), ring.dev(ring.rho - 1)]
         barrier(devices + share_devices() * len(more))
         local = pltpu.make_async_copy(x_ref, o_ref.at[ring.slot(ring.rho)], own)
         local.start()
         if more:
-            carried = ShareGather(w_ref.at[share[1]], b_ref, rest)
+            carried = carrier(share, w_ref, b_ref, rest)
             carried.start()
-        ag_ring(ring, CHUNKS, x_ref, o_ref, send, recv)
+
+
+        if extra:
+            y_local = pltpu.make_async_copy(y_ref, yo_ref.at[ring.slot(ring.rho)], y_own)
+            y_local.start()
+            small = RingGather(ring, 2, y_ref, yo_ref, y_send, y_recv)
+
+        def turn_of(turn):
+            if extra:
+                small.step(turn)
+            if turn == 1 and more:
+                carried.middle()
+
+        ag_ring(ring, CHUNKS, x_ref, o_ref, send, recv, None, turn_of)
+        if extra:
+            small.finish()
+            y_local.wait()
         if more:
-            carried.forward()
-            carried.finish()
+            carried.end()
         local.wait()
 
     results = pl.pallas_call(
         kernel,
-        out_shape=[jax.ShapeDtypeStruct((2 * planes, count, width), BF16)] + outs,
-        in_specs=[VMEM_SPEC] + [ANY_SPEC] * len(more),
-        out_specs=[ANY_SPEC] * (1 + len(more)),
-        scratch_shapes=[DMA((2, planes, CHUNKS)), DMA((2, planes, CHUNKS)), DMA] + sems,
+        out_shape=[jax.ShapeDtypeStruct((2 * planes, count, width), BF16)]
+        + outs
+        + [jax.ShapeDtypeStruct((2 * planes,) + array.shape, BF16) for array in extra],
+        in_specs=[VMEM_SPEC] + [ANY_SPEC] * len(more) + [VMEM_SPEC] * len(extra),
+        out_specs=[GATHERED_SPEC] + [ANY_SPEC] * len(more) + [VMEM_SPEC] * len(extra),
+        scratch_shapes=[DMA((2, planes, CHUNKS)), DMA((2, planes, CHUNKS)), DMA]
+        + [DMA((2, planes, 2)), DMA((2, planes, 2)), DMA] * len(extra)
+        + sems,
         compiler_params=comm_params(number),
         cost_estimate=busy(33),
         name="gather_group",
-    )(rows, *more)
-    return results if more else results[0]
-
-
-def scatter_group(parts, planes, number, share=None):
+    )(rows, *more, *extra)
+    return results if more or extra else results[0]
+
+
+def scatter_group(parts, planes, number, shares=()):
     _, count, width = parts.shape
-    more, outs, sems = share_shapes(share)
+    held = [share_shapes(share) for share in shares]
+    more = [array for arrays, _, _ in held for array in arrays]
 
     def kernel(p_ref, *refs):
-        if more:
-            w_ref, o_ref, b_ref, buf, send, recv, *rest = refs
-        else:
-            o_ref, buf, send, recv = refs
+        w_refs, o_ref, refs = refs[: len(more)], refs[len(more)], refs[len(more) + 1 :]
+        b_refs, refs = refs[: len(more)], refs[len(more) :]
+        buf, send, recv, *rest = refs
         ring = Ring8(planes)
         devices = [ring.dev(ring.rho + 1), ring.dev(ring.rho - 1)]
-        barrier(devices + share_devices() * len(more))
-        if more:
-            carried = ShareGather(w_ref.at[share[1]], b_ref, rest)
-            carried.start()
-        rs_ring(ring, CHUNKS, p_ref, buf, send, recv, ring.slot)
+        barrier(devices + share_devices() * (len(more) > 0))
+        carried = []
+        for i, share in enumerate(shares):
+            some, rest = rest[: len(held[i][2])], rest[len(held[i][2]) :]
+            carried.append(carrier(share, w_refs[i], b_refs[i], some))
+            carried[-1].start()
+
+        def beside(turn):
+            if turn - 2 < len(carried):
+                carried[turn - 2].middle()
+
+        rs_ring(ring, CHUNKS, p_ref, buf, send, recv, ring.slot, beside)
         last = planes - 1
         o_ref[...] = (
             buf[0, last].astype(F32) + buf[1, last].astype(F32)
         ) + p_ref[ring.slot(ring.rho)].astype(F32)
-        if more:
-            carried.forward()
-            carried.finish()
+        for one in carried:
+            one.end()
 
     results = pl.pallas_call(
         kernel,
-        out_shape=[jax.ShapeDtypeStruct((count, width), F32)] + outs,
+        out_shape=[jax.ShapeDtypeStruct((count, width), F32)]
+        + [shape for _, shapes, _ in held for shape in shapes],
         in_specs=[VMEM_SPEC] + [ANY_SPEC] * len(more),
         out_specs=[VMEM_SPEC] + [ANY_SPEC] * len(more),
         scratch_shapes=[
@@ -343,7 +540,7 @@
             DMA((2, planes, CHUNKS)),
             DMA((2, planes, CHUNKS)),
         ]
-        + sems,
+        + [one for _, _, scratch in held for one in scratch],
         compiler_params=comm_params(number),
         cost_estimate=busy(32),
         name="scatter_group",
@@ -351,20 +548,26 @@
     return results if more else results[0]
 
 
-def gather_plane(rows, tall=None):
+def gather_plane(rows, tall=None, swap=None, planes=None):
     count, width = rows.shape
-    more = tall is not None
+    more, trades = tall is not None, swap is not None
 
     def kernel(x_ref, *refs):
         if more:
             w_ref, o_ref, t_ref, *refs = refs
             *refs, f_send, f_recv, f_own = refs
+        elif trades:
+            y_ref, o_ref, yo_ref, *refs = refs
+            *refs, y_send, y_recv = refs
         else:
             o_ref, *refs = refs
         send, recv, sib_send, sib_recv, own = refs
         ring = Ring4()
         if more:
             barrier([peer[0] for peer in plane_peers()])
+        elif trades:
+            line_barrier(planes, [peer[0] for peer in plane_peers()], True)
+            trade(y_ref, yo_ref, y_send, y_recv, lambda copy: copy.start())
         else:
             barrier([ring.dev(ring.rho + 1), ring.dev(ring.rho - 1), ring.sib_dev()])
         local = pltpu.make_async_copy(x_ref, o_ref.at[ring.slot(ring.rho)], own)
@@ -379,10 +582,14 @@
         local.wait()
         for end in ends:
             end()
+        if trades:
+            trade(y_ref, yo_ref, y_send, y_recv, lambda copy: copy.wait())
 
     shapes = [jax.ShapeDtypeStruct((8, count, width), BF16)]
     if more:
         shapes.append(jax.ShapeDtypeStruct(tall.shape, BF16))
+    if trades:
+        shapes.append(jax.ShapeDtypeStruct(swap.shape, BF16))
     results = pl.pallas_call(
         kernel,
         out_shape=shapes,
@@ -395,16 +602,18 @@
             DMA((4, CHUNKS)),
             DMA,
         ]
-        + [DMA((3,)), DMA((3,)), DMA] * more,
-        compiler_params=comm_params(10 if more else 3),
+        + [DMA((3,)), DMA((3,)), DMA] * more
+        + [DMA, DMA] * trades,
+        compiler_params=comm_params(10 if more else 16 if trades else 3),
         cost_estimate=busy(20),
         name="gather_plane",
-    )(rows, *([tall] if more else []))
-    return results if more else results[0]
-
-
-def scatter_plane(parts):
-    return scatter_plane_call(parts, [], 1, 4, None)[0]
+    )(rows, *([tall] if more else []), *([swap] if trades else []))
+    return results if more or trades else results[0]
+
+
+def scatter_plane(parts, share=None):
+    results = scatter_plane_call(parts, [], 1, 4 if share is None else 17, share)
+    return results[0] if share is None else results
 
 
 def scatter_plane_first(parts, slabs, out_weight, planes, share):
@@ -430,7 +639,7 @@
             put, z_send, z_recv, *refs = refs
             line_barrier(planes, [peer[0] for peer in plane_peers()])
             if more:
-                carried = ShareGather(w_ref.at[share[1]], blocks, refs)
+                carried = carrier(share, w_ref, blocks, refs)
                 carried.start()
             za = lax.axis_index("za")
             puts = [
@@ -457,6 +666,9 @@
             )
             copy.start()
             copies.append(copy)
+        if more and not extra:
+            carried = carrier(share, w_ref, blocks, refs)
+            carried.start()
         if extra:
             for copy in puts:
                 copy.wait()
@@ -467,7 +679,16 @@
             pair[place] = (
                 pair[place].astype(F32) + p_ref[ring.slot(ring.rho + i)].astype(F32)
             ).astype(BF16)
-        rs_ring(ring, CHUNKS, pair, buf, send, recv, chip, line.step if extra else None)
+        if more and extra:
+            carried.middle()
+
+        def beside(turn):
+            if extra:
+                line.step(turn)
+            elif more and turn == 2:
+                carried.middle()
+
+        rs_ring(ring, CHUNKS, pair, buf, send, recv, chip, beside)
         o_ref[...] = (
             buf[0, 1].astype(F32) + buf[1, 1].astype(F32)
         ) + pair[chip(ring.rho)].astype(F32)
@@ -478,8 +699,7 @@
                 line.step(turn)
             line.finish()
         if more:
-            carried.forward()
-            carried.finish()
+            carried.end()
 
     shapes, scratch = [], []
     if extra:
@@ -530,8 +750,28 @@
     return (x * 2 + c) * 2 + b, b * 4 + x * 2 + c
 
 
-def line_barrier(planes, devices):
+def trade(source, target, send, recv, act):
     za = lax.axis_index("za")
+    f = lax.axis_index("xh") * 2 + lax.axis_index("co")
+
+    @pl.when(za != f)
+    def _():
+        act(rcopy(source, target, send, recv, swap_partner()))
+
+    @pl.when(za == f)
+    def _():
+        act(pltpu.make_async_copy(source, target, send))
+
+
+def swap_partner():
+    za = lax.axis_index("za")
+    f = lax.axis_index("xh") * 2 + lax.axis_index("co")
+    return {"za": f, "xh": za // 2, "co": lax.rem(za, 2)}
+
+
+def line_barrier(planes, devices, swaps=False):
+    za = lax.axis_index("za")
+    f = lax.axis_index("xh") * 2 + lax.axis_index("co")
     sem = pltpu.get_barrier_semaphore()
     for device in devices:
         pl.semaphore_signal(sem, inc=1, device_id=device, device_id_type=MESH)
@@ -545,7 +785,15 @@
         pl.semaphore_signal(sem, inc=1, device_id={"za": za + 1}, device_id_type=MESH)
 
     below, above = (za + planes - 1) // planes, (2 * planes - 2 - za) // planes
-    pl.semaphore_wait(sem, len(devices) + below + above)
+    apart = 0
+    if swaps:
+
+        @pl.when(za != f)
+        def _():
+            pl.semaphore_signal(sem, inc=1, device_id=swap_partner(), device_id_type=MESH)
+
+        apart = ((za - f) * (za - f) + 8) // 9
+    pl.semaphore_wait(sem, len(devices) + below + above + apart)
 
 
 class LineGather:
@@ -639,17 +887,20 @@
         copy.wait_send()
 
 
-def enter(tokens, heads_part, other_part, out_weight, gain_lane, planes, share):
+def enter(tokens, heads_part, other_part, out_weight, others, gain_lane, planes, share):
     count, width = tokens.shape
     more, outs, sems = share_shapes(share)
+    also = len(others)
     layers, rows = heads_part.shape[1:3]
     extra = layers - 1
 
     def kernel(x_ref, a_ref, b_ref, w_ref, *refs):
+        y_refs, refs = refs[:also], refs[also:]
         if more:
             s_ref, refs = refs[0], refs[1:]
         o_ref, stream_ref, t_ref, a_out, b_out, refs = *refs[:5], refs[5:]
         a_late, b_late, refs = refs[:extra], refs[extra : 2 * extra], refs[2 * extra :]
+        y_outs, refs = refs[:also], refs[also:]
         if more:
             blocks, refs = refs[0], refs[1:]
         (
@@ -659,44 +910,26 @@
         za = lax.axis_index("za")
         x, c = lax.axis_index("xh"), lax.axis_index("co")
         f = x * 2 + c
-        px, pc = za // 2, lax.rem(za, 2)
-        partner = {"za": f, "xh": px, "co": pc}
-        apart = ((za - f) * (za - f) + 8) // 9
+        partner = swap_partner()
         ring = Ring4()
         peers = plane_peers()
         group, place = own_places()
-
-        sem = pltpu.get_barrier_semaphore()
-        for peer in peers:
-            pl.semaphore_signal(sem, inc=1, device_id=peer[0], device_id_type=MESH)
-
-        @pl.when(za > 0)
-        def _():
-            pl.semaphore_signal(sem, inc=1, device_id={"za": za - 1}, device_id_type=MESH)
-
-        @pl.when(za < planes - 1)
-        def _():
-            pl.semaphore_signal(sem, inc=1, device_id={"za": za + 1}, device_id_type=MESH)
-
-        @pl.when(za != f)
-        def _():
-            pl.semaphore_signal(sem, inc=1, device_id=partner, device_id_type=MESH)
-
-        below, above = (za + planes - 1) // planes, (2 * planes - 2 - za) // planes
-        pl.semaphore_wait(sem, len(peers) + below + above + apart)
-
-        def swap():
-            return rcopy(x_ref, stream_ref, swap_send, swap_recv, partner)
-
-        @pl.when(za != f)
-        def _():
-            swap().start()
-
-        keep = pltpu.make_async_copy(x_ref, stream_ref, own.at[2 * layers])
-
-        @pl.when(za == f)
-        def _():
-            keep.start()
+        line_barrier(planes, [peer[0] for peer in peers], True)
+
+        trades = [(x_ref, stream_ref), *zip(y_refs, y_outs)]
+
+        def trade(i, act):
+            source, target = trades[i]
+
+            @pl.when(za != f)
+            def _():
+                act(rcopy(source, target, swap_send.at[i], swap_recv.at[i], partner))
+
+            @pl.when(za == f)
+            def _():
+                act(pltpu.make_async_copy(source, target, swap_send.at[i]))
+
+        trade(0, lambda copy: copy.start())
 
         copies = []
 
@@ -733,7 +966,7 @@
         b_local = scatter(1, 0)
         a_local = scatter(0, 0)
         if more:
-            carried = ShareGather(s_ref.at[share[1]], blocks, rest)
+            carried = carrier(share, s_ref, blocks, rest)
             carried.start()
         tall = LineGather(planes, [stage], za_send.at[pl.ds(2, 1)], za_recv.at[pl.ds(2, 1)])
         small = LineGather(planes, [b_out], za_send.at[pl.ds(0, 1)], za_recv.at[pl.ds(0, 1)])
@@ -747,17 +980,14 @@
         line.step(1)
         for d in (0, 1):
             small.wait_arrival(0, d, planes - 1)
+        if more:
+            carried.middle()
         columns = b_out[...].reshape(width, 128).astype(F32)
         gain = columns.T[gain_lane : gain_lane + 1, :]
 
-        @pl.when(za != f)
-        def _():
-            swap().wait()
-
-        @pl.when(za == f)
-        def _():
-            keep.wait()
-
+        trade(0, lambda copy: copy.wait())
+        for i in range(1, 1 + also):
+            trade(i, lambda copy: copy.start())
         stream = stream_ref[...].astype(F32)
         factor = lax.rsqrt(jnp.mean(stream * stream, axis=1, keepdims=True) + EPSILON)
         normed[...] = (stream * factor * gain).astype(BF16)
@@ -788,9 +1018,10 @@
         for copy in copies:
             copy.wait_send()
         handed()
+        for i in range(1, 1 + also):
+            trade(i, lambda copy: copy.wait())
         if more:
-            carried.forward()
-            carried.finish()
+            carried.end()
 
     late = [
         jax.ShapeDtypeStruct((8, rows, part.shape[-1]), BF16)
@@ -807,14 +1038,15 @@
             jax.ShapeDtypeStruct((planes, 8, rows, other_part.shape[-1]), BF16),
         ]
         + late
+        + [jax.ShapeDtypeStruct(array.shape, array.dtype) for array in others]
         + outs,
-        in_specs=[VMEM_SPEC] * 4 + [ANY_SPEC] * len(more),
-        out_specs=[ANY_SPEC] + [VMEM_SPEC] * (4 + len(late)) + [ANY_SPEC] * len(more),
+        in_specs=[VMEM_SPEC] * (4 + also) + [ANY_SPEC] * len(more),
+        out_specs=[GATHERED_SPEC] + [VMEM_SPEC] * (4 + len(late) + also) + [ANY_SPEC] * len(more),
         scratch_shapes=[
             pltpu.VMEM((planes,) + out_weight.shape, BF16),
             pltpu.VMEM((count, width), BF16),
-            DMA,
-            DMA,
+            DMA((1 + also,)),
+            DMA((1 + also,)),
             DMA((2, layers, 7)),
             DMA((2, layers, 7)),
             DMA((2 * layers + 2,)),
@@ -832,28 +1064,64 @@
         compiler_params=comm_params(5),
         cost_estimate=busy(40),
         name="enter",
-    )(tokens, heads_part, other_part, out_weight, *more)
+    )(tokens, heads_part, other_part, out_weight, *others, *more)
     first, rest = results[:5], results[5:]
-    return first, rest[:extra], rest[extra : 2 * extra], rest[2 * extra :]
-
-
-def collect(wide, tall, planes):
+    late_heads, late_others, rest = rest[:extra], rest[extra : 2 * extra], rest[2 * extra :]
+    return first, late_heads, late_others, rest[:also], rest[also:]
+
+
+def collect(wide, tall, planes, shares=(), weights=None, tokens=None):
     layers = len(wide)
     count, width = wide[0].shape[2:]
     depth = tall[0].shape[2]
+    held = [share_shapes(share) for share in shares]
+    more = [array for arrays, _, _ in held for array in arrays]
+    more_outs = [shape for _, shapes, _ in held for shape in shapes]
+    last_stage = weights is not None
+    sizes = [array.shape[2] for array in weights] if last_stage else []
 
     def kernel(*refs):
         w_in, refs = refs[:layers], refs[layers:]
         t_in, refs = refs[:layers], refs[layers:]
+        own_refs, refs = refs[: len(sizes)], refs[len(sizes) :]
+        if last_stage:
+            x_ref, refs = refs[0], refs[1:]
+        g_in, refs = refs[: len(more)], refs[len(more) :]
+        f_out, refs = refs[: 2 + len(sizes)], refs[(2 + len(sizes)) * last_stage :]
+        if last_stage:
+            y_ref, refs = refs[0], refs[1:]
+            g_out, refs = refs[: len(more)], refs[len(more) :]
         w_out, refs = refs[:layers], refs[layers:]
         t_out, refs = refs[:layers], refs[layers:]
-        w_up, t_own, t_up, summed, own, f_send, f_recv, z_send, z_recv, p_send, p_recv = refs
+        if not last_stage:
+            g_out, refs = refs[: len(more)], refs[len(more) :]
+        w_up, t_own, t_up, summed, own, f_send, f_recv, z_send, z_recv, p_send, p_recv, *rest = refs
         za = lax.axis_index("za")
         x, c = lax.axis_index("xh"), lax.axis_index("co")
         mine = x * 2 + c
         peers = plane_peers()
-        line_barrier(planes, [peer[0] for peer in peers])
+        f = x * 2 + c
+        line_barrier(planes, [peer[0] for peer in peers], last_stage)
         group, place = own_places()
+        if last_stage:
+            swap_send, swap_recv, *rest = rest
+
+        def trade(act):
+            @pl.when(za != f)
+            def _():
+                act(rcopy(x_ref, y_ref, swap_send, swap_recv, swap_partner()))
+
+            @pl.when(za == f)
+            def _():
+                act(pltpu.make_async_copy(x_ref, y_ref, swap_send))
+
+        if last_stage:
+            trade(lambda copy: copy.start())
+        carried = []
+        for i, share in enumerate(shares):
+            some, rest = rest[: len(held[i][2])], rest[len(held[i][2]) :]
+            carried.append(carrier(share, g_in[i], g_out[i], some))
+            carried[-1].start()
         firsts, keeps = [], []
         for l in range(layers):
             for k in (1, 2, 3):
@@ -893,33 +1161,37 @@
             )
 
         last = planes - 1
-        for kind in (0, 1):
-            if kind == 1:
-                for l in range(layers):
-                    arrive(l)
-            for far in range(last):
+        def pass_on(l, kind, d, dest):
+            held, came = parts(l, kind)
+            sends = (za < dest) if d == 0 else (za > dest)
+            inner = (za > 0) if d == 0 else (za < last)
+            ref, copy = along(l, kind, d, dest)
+
+            @pl.when(sends & inner)
+            def _():
+                copy.wait_recv()
+                came[d, dest] = (
+                    came[d, dest].astype(F32) + held[dest].astype(F32)
+                ).astype(BF16)
+                copy.start()
+
+            @pl.when(sends & jnp.logical_not(inner))
+            def _():
+                rcopy(
+                    held.at[dest], ref, z_send.at[l, kind, d, dest],
+                    z_recv.at[l, kind, d, dest], {"za": za + (1 - 2 * d)},
+                ).start()
+
+        for far in range(last):
+            for kind in (0, 1):
+                if kind == 1 and far == 0:
+                    for l in range(layers):
+                        arrive(l)
                 for l in reversed(range(layers)):
                     for d in (0, 1):
-                        dest = last - far if d == 0 else far
-                        held, came = parts(l, kind)
-                        sends = (za < dest) if d == 0 else (za > dest)
-                        inner = (za > 0) if d == 0 else (za < last)
-                        ref, copy = along(l, kind, d, dest)
-
-                        @pl.when(sends & inner)
-                        def _():
-                            copy.wait_recv()
-                            came[d, dest] = (
-                                came[d, dest].astype(F32) + held[dest].astype(F32)
-                            ).astype(BF16)
-                            copy.start()
-
-                        @pl.when(sends & jnp.logical_not(inner))
-                        def _():
-                            rcopy(
-                                held.at[dest], ref, z_send.at[l, kind, d, dest],
-                                z_recv.at[l, kind, d, dest], {"za": za + (1 - 2 * d)},
-                            ).start()
+                        pass_on(l, kind, d, last - far if d == 0 else far)
+            if far < len(carried):
+                carried[far].middle()
 
         def total(l, kind, result):
             _, came = parts(l, kind)
@@ -933,6 +1205,21 @@
                         {"za": za - (1 - 2 * d)},
                     ).wait_recv()
                     result[...] = (result[...].astype(F32) + came[d, za].astype(F32)).astype(BF16)
+
+        def finish_layer(l):
+            heads = [w_out[l][h].astype(F32) for h in range(8)]
+            start, product = 0, jnp.zeros((count, 1), F32)
+            for i, size in enumerate(sizes):
+                stop = start + size // 8
+                made = jnp.concatenate([head[:, start:stop] for head in heads], axis=1)
+                f_out[i][l] = made
+                product = product + jnp.sum(own_refs[i][l].astype(F32) * made, axis=1, keepdims=True)
+                start = stop
+            f_out[len(sizes)][l] = t_out[l][...].astype(F32)
+            rest = sum(heads[1:], heads[0])[:, width - 128 :]
+            rest = pltpu.roll(rest, 64, 1) + pltpu.roll(rest, 32, 1)
+            lanes = lax.broadcasted_iota(jnp.int32, rest.shape, 1)
+            f_out[len(sizes) + 1][l] = jnp.where(lanes == 32, product, rest)
 
         outs = []
         for l in reversed(range(layers)):
@@ -965,13 +1252,29 @@
                         def _():
                             along(l, kind, d, dest)[1].wait_send()
 
+        if last_stage:
+            trade(lambda copy: copy.wait())
+            for l in range(layers):
+                finish_layer(l)
+        for one in carried:
+            one.end()
+
+    final_outs, plain_outs, plain_scratch = [], [], []
+    sums = [((8, count, width), BF16)] * layers + [((count, depth), BF16)] * layers
+    if last_stage:
+        final_outs = [
+            jax.ShapeDtypeStruct((layers, count, size), F32) for size in [*sizes, depth, 128]
+        ] + [jax.ShapeDtypeStruct(tokens.shape, BF16)]
+        plain_scratch = [pltpu.VMEM(*one) for one in sums]
+    else:
+        plain_outs = [jax.ShapeDtypeStruct(*one) for one in sums]
     return pl.pallas_call(
         kernel,
-        out_shape=[jax.ShapeDtypeStruct((8, count, width), BF16)] * layers
-        + [jax.ShapeDtypeStruct((count, depth), BF16)] * layers,
-        in_specs=[VMEM_SPEC] * (2 * layers),
-        out_specs=[VMEM_SPEC] * (2 * layers),
-        scratch_shapes=[
+        out_shape=final_outs + plain_outs + more_outs,
+        in_specs=[VMEM_SPEC] * (2 * layers + len(sizes) + last_stage) + [ANY_SPEC] * len(more),
+        out_specs=[VMEM_SPEC] * len(final_outs + plain_outs) + [ANY_SPEC] * len(more),
+        scratch_shapes=plain_scratch
+        + [
             pltpu.VMEM((layers, 2, planes, 8, count, width), BF16),
             pltpu.VMEM((layers, 4, count, depth), BF16),
             pltpu.VMEM((layers, 2, planes, count, depth), BF16),
@@ -983,11 +1286,13 @@
             DMA((layers, 2, 2, planes)),
             DMA((layers, 7)),
             DMA((layers, 7)),
-        ],
-        compiler_params=comm_params(7),
+        ]
+        + [DMA, DMA] * last_stage
+        + [one for _, _, scratch in held for one in scratch],
+        compiler_params=comm_params(7, 58),
         cost_estimate=busy(40),
         name="collect",
-    )(*wide, *tall)
+    )(*wide, *tall, *(weights or []), *([tokens] if last_stage else []), *more)
 
 
 def row_codes(code_rows, first, local, slots, weights=None):
@@ -1047,7 +1352,7 @@
     return jnp.concatenate([ref[i, 0] for i in range(ref.shape[0])], axis=1)
 
 
-def experts_forward(normed, codes, codes_t, router, gate_w, up_w, down_w, beside, slots, planes, number, share=None):
+def experts_forward(normed, codes, router, gate_w, up_w, down_w, beside, slots, planes, number, share=None):
     blocks, count, width = normed.shape
     _, local, _, hidden_size = gate_w.shape
     more, extra_outs, sems = share_shapes(share)
@@ -1056,15 +1361,15 @@
     span = blocks // halves
 
     def kernel(
-        n_ref, c_ref, ct_ref, r_ref, gw_ref, uw_ref, dw_ref, x_ref, *refs
+        n_ref, c_ref, r_ref, gw_ref, uw_ref, dw_ref, x_ref, *refs
     ):
         if more:
             s_ref, refs = refs[0], refs[1:]
         out, g_out, u_out, p_out, pt_out, b_out, *refs = refs
         if more:
-            carried = ShareGather(s_ref.at[share[1]], refs[0], refs[6:])
+            carried = carrier(share, s_ref, refs[0], refs[7:])
             refs = refs[1:]
-        rows, back, send, recv, own = refs[:5]
+        rows, back, codes_t, send, recv, own = refs[:6]
         e = pl.program_id(0)
         ring = Ring8(planes)
         gather = RingGather(ring, 2, x_ref, b_out, send, recv)
@@ -1083,8 +1388,9 @@
             @pl.loop(0, blocks)
             def _(b):
                 tokens = n_ref[b]
-                logits = dot(tokens, r_ref[...])
-                code = c_ref[b]
+                logits = pltpu.roll(dot(tokens, r_ref[...]), 128 - HEAD_SIZE, 1)
+                code = c_ref[b].astype(F32)
+                codes_t[...] = code.T
                 routed = code >= 0.0
                 highest = jnp.max(jnp.where(routed, logits, -1e30), axis=1, keepdims=True)
                 raised = jnp.where(routed, jnp.exp(logits - highest), 0.0)
@@ -1092,10 +1398,12 @@
                 p_out[b] = probs
                 pt_out[b] = probs.T[: pt_out.shape[1]]
                 back[b] = column_codes(code, first, local, slots, probs)
-                ones = row_codes(lambda i: ct_ref[b, pl.ds(i, 1), :], first, local, slots)
+                ones = row_codes(lambda i: codes_t[pl.ds(i, 1), :], first, local, slots)
                 rows[b] = dot(ones, tokens).astype(BF16)
 
             gather.step(2)
+            if more:
+                carried.middle()
 
         mine = pl.ds(pl.multiple_of(e * slots, slots), slots)
         for h in range(halves):
@@ -1125,8 +1433,7 @@
             gather.finish()
             keep.wait()
             if more:
-                carried.forward()
-                carried.finish()
+                carried.end()
 
     wide = (local, blocks * slots, hidden_size)
     return pl.pallas_call(
@@ -1137,14 +1444,13 @@
             jax.ShapeDtypeStruct(wide, F32),
             jax.ShapeDtypeStruct(wide, F32),
             jax.ShapeDtypeStruct(codes.shape, F32),
-            jax.ShapeDtypeStruct(codes_t.shape, F32),
+            jax.ShapeDtypeStruct((blocks, 32, count), F32),
             jax.ShapeDtypeStruct((blocks,) + beside.shape, BF16),
         ]
         + extra_outs,
         in_specs=[
             once(normed.shape),
             once(codes.shape),
-            once(codes_t.shape),
             once(router.shape),
             shares_of_expert(gate_w.shape),
             shares_of_expert(up_w.shape),
@@ -1157,13 +1463,14 @@
             per_expert(wide[1:]),
             per_expert(wide[1:]),
             once(codes.shape),
-            once(codes_t.shape),
+            once((blocks, 32, count)),
             ANY_SPEC,
         ]
         + [ANY_SPEC] * len(more),
         scratch_shapes=[
             pltpu.VMEM((blocks, lines, width), BF16),
             pltpu.VMEM((blocks, count, lines), BF16),
+            pltpu.VMEM((codes.shape[2], count), F32),
             DMA((2, planes, 2)),
             DMA((2, planes, 2)),
             DMA,
@@ -1172,14 +1479,16 @@
         compiler_params=plain_params(56, number),
         cost_estimate=busy(16),
         name="experts_forward",
-    )(normed, codes, codes_t, router, gate_w, up_w, down_w, beside, *more)
+    )(normed, codes, router, gate_w, up_w, down_w, beside, *more)
 
 
 def experts_backward(
-    normed, arrived, codes, codes_t, probs_t, gate_w, up_w, down_w, gate_part, up_part, slots, shares
+    normed, arrived, codes, probs_t, gate_w, up_w, down_w, gate_part, up_part, slots, shares,
+    late=None, planes=None,
 ):
     blocks, count, width = normed.shape
     pieces = len(arrived)
+    more = [] if late is None else [late]
     _, local, _, hidden_size = gate_w.shape
     lines = local * slots
     total = blocks * slots
@@ -1187,26 +1496,44 @@
     split = band % 128 == 0
 
     def kernel(
-        n_ref, c_ref, ct_ref, pt_ref, gw_ref, uw_ref, dw_ref, g_ref, u_ref, *refs
+        n_ref, c_ref, pt_ref, gw_ref, uw_ref, dw_ref, g_ref, u_ref, *refs
     ):
-        a_refs, (out, dg_out, du_out, dd_out, rows, outs, back, marks) = refs[:pieces], refs[pieces:]
+        a_refs, refs = refs[:pieces], refs[pieces:]
+        if more:
+            l_ref, refs = refs[0], refs[1:]
+        out, dg_out, du_out, dd_out, *refs = refs
+        if more:
+            l_out, refs = refs[0], refs[1:]
+        rows, outs, back, marks, codes_t, *refs = refs
+        if more:
+            ring = Ring8(planes)
+            scatter = RingScatter(ring, 2, l_ref, *refs)
         e = pl.program_id(0)
         first = (lax.axis_index("za") * 2 + lax.axis_index("yb")) * local
 
         @pl.when(e == 0)
         def _():
+            if more:
+                barrier([ring.dev(ring.rho + 1), ring.dev(ring.rho - 1)])
+                scatter.step(1)
+
             @pl.loop(0, blocks)
             def _(b):
+                codes_t[...] = c_ref[b].astype(F32).T
+
                 def code(i):
-                    return ct_ref[b, pl.ds(i, 1), :]
+                    return codes_t[pl.ds(i, 1), :]
 
                 def prob(i):
                     return pt_ref[b, pl.ds(i, 1), :]
 
-                back[b] = column_codes(c_ref[b], first, local, slots)
+                back[b] = column_codes(c_ref[b].astype(F32), first, local, slots)
                 rows[b] = dot(row_codes(code, first, local, slots), n_ref[b]).astype(BF16)
                 upstream = jnp.concatenate([ref[b] for ref in a_refs], axis=0)
                 outs[b] = dot(row_codes(code, first, local, slots, prob), upstream).astype(BF16)
+
+            if more:
+                scatter.step(2)
 
         mine = pl.ds(pl.multiple_of(e * slots, slots), slots)
         upstream = outs[:, mine, :].reshape(total, width)
@@ -1237,8 +1564,18 @@
         back_rows = back_rows + dot_t(up_low, uw_ref[:, 0].reshape(width, hidden_size))
         rows[:, mine, :] = back_rows.astype(BF16).reshape(blocks, slots, width)
 
+        if more:
+            for turn in range(3, planes + 1):
+
+                @pl.when(e == min(turn - 3, local - 1))
+                def _():
+                    scatter.step(turn)
+
         @pl.when(e == local - 1)
         def _():
+            if more:
+                l_out[...] = scatter.finish()
+
             @pl.loop(0, blocks)
             def _(b):
                 out[b, :, :width] = dot(back[b], rows[b]).astype(BF16)
@@ -1252,6 +1589,15 @@
     else:
         down_shape = (local, hidden_size, width)
         down_spec = per_expert(down_shape[1:])
+    late_scratch = []
+    if more:
+        late_scratch = [
+            pltpu.VMEM((2, planes, count, width), BF16),
+            pltpu.VMEM((2, count, width), BF16),
+            DMA((2, planes, 2)),
+            DMA((2, planes, 2)),
+            DMA((2,)),
+        ]
     results = pl.pallas_call(
         kernel,
         grid=(local,),
@@ -1260,11 +1606,11 @@
             jax.ShapeDtypeStruct(cut_shape, BF16),
             jax.ShapeDtypeStruct(cut_shape, BF16),
             jax.ShapeDtypeStruct(down_shape, BF16),
-        ],
+        ]
+        + [jax.ShapeDtypeStruct((count, width), F32)] * len(more),
         in_specs=[
             once(normed.shape),
             once(codes.shape),
-            once(codes_t.shape),
             once(probs_t.shape),
             shares_of_expert(gate_w.shape),
             shares_of_expert(up_w.shape),
@@ -1272,24 +1618,226 @@
             per_expert(gate_part.shape[1:]),
             per_expert(up_part.shape[1:]),
         ]
-        + [once(array.shape) for array in arrived],
-        out_specs=[once((blocks, count, width + 128)), cut_spec, cut_spec, down_spec],
+        + [once(array.shape) for array in arrived]
+        + [ANY_SPEC] * len(more),
+        out_specs=[once((blocks, count, width + 128)), cut_spec, cut_spec, down_spec]
+        + [once((count, width))] * len(more),
         scratch_shapes=[
             pltpu.VMEM((blocks, lines, width), BF16),
             pltpu.VMEM((blocks, lines, width), BF16),
             pltpu.VMEM((blocks, count, lines), BF16),
             pltpu.VMEM((blocks, lines, 128), BF16),
-        ],
-        compiler_params=plain_params(60),
+            pltpu.VMEM((codes.shape[2], count), F32),
+        ]
+        + late_scratch,
+        compiler_params=plain_params(62, 15 if more else None),
         cost_estimate=busy(30),
         name="experts_backward",
-    )(normed, codes, codes_t, probs_t, gate_w, up_w, down_w, gate_part, up_part, *arrived)
-    row_sums, gate_term, up_term, down_term = results
+    )(normed, codes, probs_t, gate_w, up_w, down_w, gate_part, up_part, *arrived, *more)
+    row_sums, gate_term, up_term, down_term, *added = results
     if not split:
         down_term = jnp.moveaxis(
             down_term.reshape(local, hidden_size, shares, band), 2, 0
         )
-    return row_sums, gate_term, up_term, down_term
+    return row_sums, gate_term, up_term, down_term, *added
+
+
+GROUP = 4 * HEAD_SIZE
+
+
+def turn_heads(values, cosine, sine, sign):
+    half = HEAD_SIZE // 2
+    lanes = lax.broadcasted_iota(jnp.int32, values.shape, 1)
+    first = lax.rem(lanes, HEAD_SIZE) < half
+    other = jnp.where(
+        first, -pltpu.roll(values, GROUP - half, 1), pltpu.roll(values, half, 1)
+    )
+    return values * cosine + sign * other * sine
+
+
+def spread_head(values, place):
+    lanes = lax.broadcasted_iota(jnp.int32, values.shape, 1) // HEAD_SIZE
+    alone = jnp.where(lanes == place, values, jnp.zeros_like(values))
+    return (
+        alone
+        + pltpu.roll(alone, HEAD_SIZE, 1)
+        + pltpu.roll(alone, 2 * HEAD_SIZE, 1)
+        + pltpu.roll(alone, 3 * HEAD_SIZE, 1)
+    )
+
+
+def only_head(values, h):
+    lanes = lax.broadcasted_iota(jnp.int32, values.shape, 1) // HEAD_SIZE
+    return jnp.where(lanes == h, values, jnp.zeros_like(values))
+
+
+def may_attend(starts_ref, first, rows, stop):
+    here = first + lax.broadcasted_iota(jnp.int32, (rows, 1), 0)
+    there = lax.broadcasted_iota(jnp.int32, (1, stop), 1)
+    mine, theirs = jnp.zeros_like(here), jnp.zeros_like(there)
+    for i in range(starts_ref.shape[1]):
+        start = starts_ref[0, i]
+        mine = mine + jnp.where(here >= start, 1, 0)
+        theirs = theirs + jnp.where(there >= start, 1, 0)
+    return (mine == theirs) & (there <= here)
+
+
+def probabilities(query_rows, keys, allowed):
+    scores = jnp.where(allowed, dot_t(query_rows, keys) * (1.0 / math.sqrt(HEAD_SIZE)), -1e30)
+    weights = jnp.exp(scores - jnp.max(scores, axis=1, keepdims=True))
+    return weights / jnp.sum(weights, axis=1, keepdims=True)
+
+
+SMEM_SPEC = pl.BlockSpec(memory_space=pltpu.SMEM)
+ROWS = 256
+
+
+def attention_forward(normed, slab, out_rows, starts, cosine, sine):
+    length, width = normed.shape
+    rows = min(ROWS, length)
+
+    def kernel(starts_ref, x_ref, w_ref, wv_ref, o_ref, c_ref, s_ref, out, heads, values, mixed, keys, spread):
+        @pl.loop(0, length // rows)
+        def _(i):
+            part = pl.ds(pl.multiple_of(i * rows, rows), rows)
+            turned = turn_heads(dot(x_ref[part, :], w_ref[...]), c_ref[part, :], s_ref[part, :], 1.0).astype(BF16)
+            heads[part, :] = turned
+            tail = dot(x_ref[part, :], wv_ref[...])
+            lanes = lax.broadcasted_iota(jnp.int32, tail.shape, 1)
+            value = jnp.where(lanes < HEAD_SIZE, tail, 0.0)
+            values[part, :] = value.astype(BF16)
+            keys[part, :] = spread_head(turned.astype(F32), 3).astype(BF16)
+            both = jnp.concatenate([value, jnp.zeros_like(value)], axis=1)
+            spread[part, :] = spread_head(both, 0).astype(BF16)
+
+        for i in range(length // rows):
+            first, stop = i * rows, (i + 1) * rows
+            allowed = may_attend(starts_ref, first, rows, stop)
+            queries = heads[first:stop, :]
+            total = jnp.zeros((rows, GROUP), F32)
+            for h in range(3):
+                probs = probabilities(only_head(queries, h), keys[:stop, :], allowed).astype(BF16)
+                total = total + dot(probs, only_head(spread[:stop, :], h))
+            low = total.astype(BF16)
+            mixed[first:stop, :] = low
+            out[first:stop, :] = dot(low[:, : 3 * HEAD_SIZE], o_ref[...]).astype(BF16)
+
+    return pl.pallas_call(
+        kernel,
+        out_shape=[
+            jax.ShapeDtypeStruct((length, width), BF16),
+            jax.ShapeDtypeStruct((length, GROUP), BF16),
+            jax.ShapeDtypeStruct((length, 128), BF16),
+            jax.ShapeDtypeStruct((length, GROUP), BF16),
+        ],
+        in_specs=[SMEM_SPEC] + [VMEM_SPEC] * 6,
+        out_specs=[VMEM_SPEC] * 4,
+        scratch_shapes=[pltpu.VMEM((length, GROUP), BF16), pltpu.VMEM((length, GROUP), BF16)],
+        compiler_params=pltpu.CompilerParams(vmem_limit_bytes=40 << 20),
+        cost_estimate=busy(10),
+        name="attend_forward",
+    )(starts, normed, *slab, out_rows, cosine, sine)
+
+
+def attention_backward(normed, slab, out_rows, starts, cosine, sine, heads, values, mixed, branch, rest):
+    length, width = normed.shape
+    rows = min(ROWS, length)
+    scale = 1.0 / math.sqrt(HEAD_SIZE)
+    used = 3 * HEAD_SIZE
+
+    def kernel(
+        starts_ref, x_ref, w_ref, wv_ref, o_ref, c_ref, s_ref, h_ref, v_ref, m_ref, b_ref, r_ref,
+        out, wide, tall, keys, spread, grads, key_sum, value_sum, low,
+    ):
+        @pl.loop(0, length // rows)
+        def _(i):
+            part = pl.ds(pl.multiple_of(i * rows, rows), rows)
+            keys[part, :] = spread_head(h_ref[part, :].astype(F32), 3).astype(BF16)
+            value = v_ref[part, :].astype(F32)
+            both = jnp.concatenate([value, jnp.zeros_like(value)], axis=1)
+            spread[part, :] = spread_head(both, 0).astype(BF16)
+            grad = dot_t(b_ref[part, :], o_ref[...])
+            grads[part, :] = jnp.concatenate(
+                [grad, jnp.zeros((rows, HEAD_SIZE), F32)], axis=1
+            ).astype(BF16)
+            key_sum[part, :] = jnp.zeros((rows, GROUP), F32)
+            value_sum[part, :] = jnp.zeros((rows, GROUP), F32)
+
+        for i in range(length // rows):
+            first, stop = i * rows, (i + 1) * rows
+            allowed = may_attend(starts_ref, first, rows, stop)
+            queries, upstream = h_ref[first:stop, :], grads[first:stop, :]
+            query_grad = jnp.zeros((rows, GROUP), F32)
+            for h in range(3):
+                query_rows, grad_rows = only_head(queries, h), only_head(upstream, h)
+                probs = probabilities(query_rows, keys[:stop, :], allowed)
+                prob_grad = dot_t(grad_rows, spread[:stop, :])
+                centre = jnp.sum(probs * prob_grad, axis=1, keepdims=True)
+                score_grad = (probs * (prob_grad - centre)).astype(BF16)
+                query_grad = query_grad + dot(score_grad, only_head(keys[:stop, :], h))
+                key_sum[:stop, :] += dot(score_grad.T, query_rows)
+                value_sum[:stop, :] += dot(probs.astype(BF16).T, grad_rows)
+            low[first:stop, :GROUP] = (query_grad * scale).astype(BF16)
+
+        @pl.loop(0, length // rows)
+        def _(i):
+            part = pl.ds(pl.multiple_of(i * rows, rows), rows)
+            keyed = key_sum[part, :]
+            keyed = (
+                pltpu.roll(keyed, HEAD_SIZE, 1)
+                + pltpu.roll(keyed, 2 * HEAD_SIZE, 1)
+                + pltpu.roll(keyed, 3 * HEAD_SIZE, 1)
+            ) * scale
+            lanes = lax.broadcasted_iota(jnp.int32, keyed.shape, 1)
+            raw = jnp.where(lanes < used, low[part, :GROUP].astype(F32), keyed)
+            raw = raw.astype(BF16).astype(F32)
+            low[part, :GROUP] = turn_heads(raw, c_ref[part, :], s_ref[part, :], -1.0).astype(BF16)
+            valued = value_sum[part, :]
+            valued = (
+                valued
+                + pltpu.roll(valued, GROUP - HEAD_SIZE, 1)
+                + pltpu.roll(valued, GROUP - 2 * HEAD_SIZE, 1)
+            )[:, :128]
+            lanes = lax.broadcasted_iota(jnp.int32, valued.shape, 1)
+            low[part, GROUP:] = jnp.where(lanes < HEAD_SIZE, valued, 0.0).astype(BF16)
+            grad = dot_t(low[part, :GROUP], w_ref[...]) + dot_t(low[part, GROUP:], wv_ref[...])
+            out[part, :] = grad.astype(BF16)
+
+        step = 256
+
+        @pl.loop(0, width // step)
+        def _(i):
+            part = pl.ds(pl.multiple_of(i * step, step), step)
+            made = dot(x_ref[:, part].T, low[...])
+            wide[part, :GROUP] = made[:, :GROUP].astype(BF16)
+            lanes = lax.broadcasted_iota(jnp.int32, (step, 128), 1)
+            beside = jnp.concatenate([r_ref[part, :], r_ref[part, :]], axis=1)
+            wide[part, GROUP:] = jnp.where(
+                lanes < HEAD_SIZE, made[:, GROUP:], beside.astype(F32)
+            ).astype(BF16)
+        tall[...] = dot(m_ref[...].T, b_ref[...])[:used].astype(BF16)
+
+    return pl.pallas_call(
+        kernel,
+        out_shape=[
+            jax.ShapeDtypeStruct((length, width), BF16),
+            jax.ShapeDtypeStruct((width, GROUP + 128), BF16),
+            jax.ShapeDtypeStruct((used, width), BF16),
+        ],
+        in_specs=[SMEM_SPEC] + [VMEM_SPEC] * 11,
+        out_specs=[VMEM_SPEC] * 3,
+        scratch_shapes=[
+            pltpu.VMEM((length, GROUP), BF16),
+            pltpu.VMEM((length, GROUP), BF16),
+            pltpu.VMEM((length, GROUP), BF16),
+            pltpu.VMEM((length, GROUP), F32),
+            pltpu.VMEM((length, GROUP), F32),
+            pltpu.VMEM((length, GROUP + 128), BF16),
+        ],
+        compiler_params=pltpu.CompilerParams(vmem_limit_bytes=50 << 20),
+        cost_estimate=busy(20),
+        name="attend_backward",
+    )(starts, normed, *slab, out_rows, cosine, sine, heads, values, mixed, branch, rest)
 
 
 def norm_factor(stream):
@@ -1300,79 +1848,6 @@
     scaled = gain_row * upstream
     inner_mean = jnp.mean(stream * scaled, axis=-1, keepdims=True)
     return factor * scaled - stream * (factor * factor * factor) * inner_mean
-
-
-def rotate(source, cosine, sine):
-    half = HEAD_SIZE // 2
-    shaped = source.reshape(source.shape[0], -1, HEAD_SIZE)
-    first, second = shaped[..., :half], shaped[..., half:]
-    c, s = cosine[:, None, :], sine[:, None, :]
-    turned = jnp.concatenate([first * c - second * s, second * c + first * s], axis=-1)
-    return turned.reshape(source.shape)
-
-
-def attend_blocks(length):
-    rows = min(512, length)
-    return [(i * rows, (i + 1) * rows) for i in range(length // rows)]
-
-
-def masked(scores, documents, start, stop):
-    ids = jnp.arange(stop, dtype=jnp.int32)
-    allowed = (documents[start:stop, None] == documents[None, :stop]) & (
-        ids[None, :] <= ids[start:stop, None]
-    )
-    return jnp.where(allowed[None], scores * (1.0 / math.sqrt(HEAD_SIZE)), -1e30)
-
-
-def attend(queries, keys, values, documents):
-    mixed, logs = [], []
-    for start, stop in attend_blocks(queries.shape[0]):
-        scores = masked(
-            jnp.einsum(
-                "qhd,kd->hqk", queries[start:stop], keys[:stop], preferred_element_type=F32
-            ),
-            documents,
-            start,
-            stop,
-        )
-        highest = jnp.max(scores, axis=-1, keepdims=True)
-        weights = jnp.exp(scores - highest)
-        totals = jnp.sum(weights, axis=-1, keepdims=True)
-        probs = (weights / totals).astype(BF16)
-        mixed.append(
-            jnp.einsum("hqk,kd->qhd", probs, values[:stop], preferred_element_type=F32).astype(BF16)
-        )
-        logs.append(highest + jnp.log(totals))
-    return jnp.concatenate(mixed, axis=0), logs
-
-
-def attend_back(queries, keys, values, documents, logs, mixed_grad):
-    scale = 1.0 / math.sqrt(HEAD_SIZE)
-    key_sum = jnp.zeros(keys.shape, F32)
-    value_sum = jnp.zeros(values.shape, F32)
-    query_list = []
-    for (start, stop), log in zip(attend_blocks(queries.shape[0]), logs):
-        query_rows, upstream = queries[start:stop], mixed_grad[start:stop]
-        scores = masked(
-            jnp.einsum("qhd,kd->hqk", query_rows, keys[:stop], preferred_element_type=F32),
-            documents,
-            start,
-            stop,
-        )
-        probs = jnp.exp(scores - log)
-        prob_grad = jnp.einsum("qhd,kd->hqk", upstream, values[:stop], preferred_element_type=F32)
-        centre = jnp.sum(probs * prob_grad, axis=-1, keepdims=True)
-        score_grad = (probs * (prob_grad - centre)).astype(BF16)
-        query_list.append(
-            jnp.einsum("hqk,kd->qhd", score_grad, keys[:stop], preferred_element_type=F32) * scale
-        )
-        key_sum = key_sum.at[:stop].add(
-            jnp.einsum("hqk,qhd->kd", score_grad, query_rows, preferred_element_type=F32) * scale
-        )
-        value_sum = value_sum.at[:stop].add(
-            jnp.einsum("hqk,qhd->kd", probs.astype(BF16), upstream, preferred_element_type=F32)
-        )
-    return jnp.concatenate(query_list, axis=0).astype(BF16), key_sum.astype(BF16), value_sum.astype(BF16)
 
 
 def per_device(
@@ -1401,8 +1876,7 @@
     local = gate_weight.shape[1]
     top = routes.shape[2]
     slots = -(-(count * top * 4 // (3 * experts_all) + 1) // 16) * 16
-    heads = query_weight.shape[2] // HEAD_SIZE // 8
-    columns = heads * HEAD_SIZE
+    columns = query_weight.shape[2] // 8
     kv = key_matrix.shape[2] // 8
     bands = query_weight.shape[1]
 
@@ -1411,8 +1885,6 @@
     def exchange(array):
         return lax.ppermute(array, ("za", "xh", "co"), swap)
 
-    starts = exchange(doc_starts)[0]
-    chosen = exchange(routes[0])
 
     small = jnp.stack([attn_gain, ffn_gain], axis=-1)
     used = columns + 2 * kv + experts_all + 2
@@ -1456,11 +1928,12 @@
     def carry(array, layer):
         return (array, layer) if groups == 1 and layer < layers else None
 
-    firsts, late_heads, late_others, carried = enter(
+    firsts, late_heads, late_others, swapped, carried = enter(
         layer_in[0],
         pieces[..., : padded - 128],
         pieces[..., padded - 128 :],
         all_out[0],
+        (cotangent[0], routes[0], doc_starts),
         used - 2 - (padded - 128),
         planes,
         carry(gate_weight, 0),
@@ -1468,8 +1941,10 @@
     normed_first, stream, tall_rows, heads_slab, other_slab = firsts
     stream = stream.astype(F32)
     slabs = [(in_order(heads_slab), in_order(other_slab))]
-    upstream_low, tall_rows = lax.optimization_barrier((cotangent[0], tall_rows))
-    upstream_low = exchange(upstream_low)
+    upstream_low, chosen, starts = swapped
+
+    def sum_share(term):
+        return lax.psum_scatter(term, ("xh", "co"), scatter_dimension=0)
 
     def sum_experts(gate_term, up_term, down_term):
         axes = ("grp", "xh", "co")
@@ -1487,15 +1962,12 @@
     rank = jnp.dot(before, named.astype(BF16), preferred_element_type=F32)
     codes = jnp.where(named > 0, rank, -1.0)
     codes = jnp.pad(codes, ((0, 0), (0, 128 - experts_all)), constant_values=-1.0).astype(BF16)
-    codes_t = None
-
-    positions = jnp.arange(length, dtype=jnp.int32)
-    documents = jnp.sum((starts[None, :] <= positions[:, None]).astype(jnp.int32), axis=1) - 1
-    inverse = 10000.0 ** (
-        -2.0 * jnp.arange(HEAD_SIZE // 2, dtype=F32) / HEAD_SIZE
+
+    angles = np.arange(length)[:, None] * 10000.0 ** (
+        -2.0 * np.arange(HEAD_SIZE // 2)[None, :] / HEAD_SIZE
     )
-    angles = positions.astype(F32)[:, None] * inverse[None, :]
-    cosine, sine = jnp.cos(angles), jnp.sin(angles)
+    cosine = jnp.asarray(np.tile(np.cos(angles), (1, 8)), F32)
+    sine = jnp.asarray(np.tile(np.sin(angles), (1, 8)), F32)
 
     def fetch_experts(layer):
         axes = ("grp", "xh", "co")
@@ -1510,12 +1982,11 @@
     for layer in range(layers):
         if groups > 1:
             carried = fetch_experts(layer)
-        slab = jnp.concatenate(slabs[layer], axis=1)
-        small_part = slab[:, columns + 2 * kv :]
+        slab = slabs[layer]
+        small_part = slab[1][:, columns + 2 * kv - GROUP :]
         attn_row = small_part[:, experts_all].astype(F32)
         ffn_row = small_part[:, experts_all + 1].astype(F32)
-        qkv_w = slab[:, : columns + 2 * kv]
-        router_w = jnp.pad(small_part[:, :experts_all], ((0, 0), (0, 128 - experts_all)))
+        router_w = small_part[:, :experts_all]
         factor_one = norm_factor(stream)
         if layer == 0:
             normed_one = normed_first
@@ -1525,14 +1996,10 @@
         tall_rows = jnp.swapaxes(tall_rows.reshape(4, groups, bands, width), 0, 1)
         out_rows.append(tall_rows.reshape(columns, width))
         normed_one = normed_one.reshape(length, width)
-        qkv = jnp.dot(normed_one, qkv_w, preferred_element_type=F32)
-        queries = rotate(qkv[:, :columns], cosine, sine).astype(BF16)
-        keys = rotate(qkv[:, columns : columns + kv], cosine, sine).astype(BF16)
-        values = qkv[:, columns + kv :].astype(BF16)
-        queries = queries.reshape(length, heads, HEAD_SIZE)
-        mixed, logs = attend(queries, keys, values, documents)
-        mixed = mixed.reshape(length, columns)
-        branch = jnp.dot(mixed, out_rows[layer], preferred_element_type=F32).astype(BF16)
+        tall = out_rows[layer]
+        branch, heads_low, values, mixed = attention_forward(
+            normed_one, slab, tall, starts, cosine, sine
+        )
         branch = branch.reshape(8, count, width)
         if layer + 1 < layers:
             share = carry(up_weight, 0) if layer == 0 else None
@@ -1549,13 +2016,10 @@
         factor_two = norm_factor(middle)
         own_two = (middle * factor_two * ffn_row).astype(BF16)
         if layer == 0:
-            both = jnp.concatenate([own_two, codes], axis=1)
-            both = gather_group(both, planes, 8, carry(down_weight, 0))
+            results = gather_group(own_two, planes, 8, carry(down_weight, 0), codes)
+            normed_two, codes = results[0], results[-1]
             if groups == 1:
-                both, last = both
-                carried = [*carried, last]
-            normed_two, codes = both[..., :width], both[..., width:].astype(F32)
-            codes_t = jnp.swapaxes(codes[..., :32], 1, 2)
+                carried = [*carried, results[1]]
         else:
             share = carry(down_weight, layer)
             normed_two = gather_group(own_two, planes, 12, share)
@@ -1566,7 +2030,7 @@
         gate_w, up_w, down_w = carried
         share = count // layers
         total, gate_part, up_part, gate_probs, probs_t, gathered, *carried = experts_forward(
-            normed_two, codes, codes_t, router_w, gate_w, up_w, down_w,
+            normed_two, codes, slab[1], gate_w, up_w, down_w,
             upstream_low[layer * share : (layer + 1) * share], slots, planes,
             11 if layer == 0 else 13, carry(gate_weight, layer + 1),
         )
@@ -1574,79 +2038,72 @@
         own_probs = lax.dynamic_index_in_dim(gate_probs, place, 0, keepdims=False)[:, :experts_all]
         states.append(
             (
-                stream, factor_one, normed_one, queries, keys, values, logs, mixed, middle,
-                factor_two, own_two, normed_two, own_probs, probs_t, gate_part, up_part,
-                gate_w, up_w, down_w, attn_row, ffn_row, qkv_w, router_w,
+                stream, factor_one, normed_one, heads_low, values, mixed, tall, middle,
+                factor_two, own_two, normed_two, own_probs, probs_t, gate_part, up_part, total,
+                gate_w, up_w, down_w, attn_row, ffn_row, slab, router_w,
             )
         )
-        share = carry(up_weight, layer + 1)
-        added = scatter_group(total, planes, 14 if share is not None else 1, share)
-        if share is not None:
-            added, last = added
-            carried = [*carried, last]
-        stream = middle + added
-
-    result = exchange(stream.astype(BF16))[None]
-
+        if layer + 1 < layers:
+            share = carry(up_weight, layer + 1)
+            added = scatter_group(total, planes, 14, () if share is None else (share,))
+            if share is not None:
+                added, last = added
+                carried = [*carried, last]
+            stream = middle + added
+
+    result, pending = None, None
     upstream = upstream_low.astype(F32)
-    expert_out, previous = [None] * layers, None
+    expert_out = [None] * layers
     wide_terms, tall_terms = [None] * layers, [None] * layers
     for layer in reversed(range(layers)):
         (
-            stream, factor_one, normed_one, queries, keys, values, logs, mixed, middle,
-            factor_two, own_two, normed_two, own_probs, probs_t, gate_part, up_part,
-            gate_w, up_w, down_w, attn_row, ffn_row, qkv_w, router_w,
+            stream, factor_one, normed_one, heads_low, values, mixed, tall, middle,
+            factor_two, own_two, normed_two, own_probs, probs_t, gate_part, up_part, total,
+            gate_w, up_w, down_w, attn_row, ffn_row, slab, router_w,
         ) = states[layer]
         if layer + 1 < layers:
-            arrived = [gather_group(upstream.astype(BF16), planes, 0)]
-        row_sums, gate_term, up_term, down_term = experts_backward(
-            normed_two, arrived, codes, codes_t, probs_t, gate_w, up_w, down_w, gate_part, up_part,
-            slots, 4 * groups,
+            sending = upstream.astype(BF16)
+            arrived = gather_group(sending, planes, 0, pending)
+            if pending is not None:
+                arrived, up_sum = arrived
+                expert_out[layer + 1] = (expert_out[layer + 1][0], up_sum, expert_out[layer + 1][2])
+            arrived = [arrived]
+        row_sums, gate_term, up_term, down_term, *added = experts_backward(
+            normed_two, arrived, codes, probs_t, gate_w, up_w, down_w, gate_part, up_part,
+            slots, 4 * groups, total if layer + 1 == layers else None, planes,
         )
-        terms = (gate_term, up_term, down_term)
-        if previous is not None:
-            terms, expert_out[layer + 1] = lax.optimization_barrier((terms, previous))
-        previous = expert_out[layer] = sum_experts(*terms)
-        summed = scatter_group(row_sums, planes, 2)
+        if added:
+            result = exchange((middle + added[0]).astype(BF16))
+        if groups > 1:
+            summed = scatter_group(row_sums, planes, 2)
+            expert_out[layer] = sum_experts(gate_term, up_term, down_term)
+        else:
+            second = gate_term if layer > 0 else up_term
+            summed, down_sum, second = scatter_group(
+                row_sums, planes, 2, ((down_term, None), (second, None))
+            )
+            pending = (up_term, None) if layer > 0 else (gate_term, None)
+            expert_out[layer] = (second, None, down_sum) if layer > 0 else (None, second, down_sum)
         weighted = summed[:, width : width + experts_all]
         weighted = weighted + summed[:, width + 64 : width + 64 + experts_all]
         logit_grad = weighted - own_probs * jnp.sum(weighted, axis=-1, keepdims=True)
         router_term = jnp.einsum("td,te->de", own_two.astype(F32), logit_grad, precision=HIGHEST)
         normed_two_grad = summed[:, :width] + jnp.einsum(
-            "te,de->td", logit_grad, router_w[:, :experts_all].astype(F32), precision=HIGHEST
+            "te,de->td", logit_grad, router_w.astype(F32), precision=HIGHEST
         )
         ffn_gain_term = jnp.sum(normed_two_grad * middle * factor_two, axis=0)
         middle_grad = upstream + norm_back(middle, factor_two, ffn_row, normed_two_grad)
         branch_low = gather_plane(middle_grad.astype(BF16)).reshape(length, width)
-        out_term = jnp.einsum("tc,td->cd", mixed, branch_low, preferred_element_type=F32)
-        mixed_grad = jnp.einsum(
-            "td,cd->tc", branch_low, out_rows[layer], preferred_element_type=F32
-        ).astype(BF16)
-        query_grad, key_grad, value_grad = attend_back(
-            queries, keys, values, documents, logs, mixed_grad.reshape(length, heads, HEAD_SIZE)
-        )
-        query_grad = query_grad.reshape(length, columns)
-        low = jnp.concatenate(
-            [
-                rotate(query_grad.astype(F32), cosine, -sine).astype(BF16),
-                rotate(key_grad.astype(F32), cosine, -sine).astype(BF16),
-                value_grad,
-            ],
-            axis=1,
-        )
-        qkv_term = jnp.einsum("td,tc->dc", normed_one, low, preferred_element_type=F32)
-        partial = jnp.einsum(
-            "tc,dc->td", low, qkv_w, preferred_element_type=F32
-        ).astype(BF16)
         rest = jnp.concatenate([router_term, ffn_gain_term[:, None]], axis=1)
         rest = jnp.pad(rest, ((0, 0), (0, 32 - experts_all - 1)))
         high = rest.astype(BF16)
         low_part = (rest - high.astype(F32)).astype(BF16)
-        qkv_term = jnp.concatenate([qkv_term.astype(BF16), high, low_part], axis=1)
-        partial, qkv_term, out_term = lax.optimization_barrier(
-            (partial, qkv_term, out_term.astype(BF16))
+        partial, qkv_term, out_term = attention_backward(
+            normed_one, slab, tall, starts, cosine, sine, heads_low, values, mixed, branch_low,
+            jnp.concatenate([high, low_part], axis=1),
         )
-        normed_one_grad = scatter_plane(partial.reshape(8, count, width))
+        partial = partial.reshape(8, count, width)
+        normed_one_grad = scatter_plane(partial)
         upstream = middle_grad + norm_back(stream, factor_one, attn_row, normed_one_grad)
         if groups > 1:
             qkv_term = jnp.swapaxes(
@@ -1656,40 +2113,51 @@
         wide_terms[layer] = qkv_term.reshape(planes, 8, band_rows, padded)
         tall_terms[layer] = out_term.reshape(4, band_rows, width)
 
-    sums = collect(wide_terms, tall_terms, planes)
+    if groups > 1:
+        sums = collect(wide_terms, tall_terms, planes)
+        input_grad = exchange(upstream.astype(BF16))
+    else:
+        query_out, key_out, value_out, tall_out, rest, input_grad, gate_sum = collect(
+            wide_terms, tall_terms, planes, (pending,),
+            (query_weight, key_matrix, value_matrix), upstream.astype(BF16),
+        )
+        expert_out[0] = (gate_sum, *expert_out[0][1:])
+        products = rest[..., 32]
     if groups > 1:
         sums = [
             lax.psum_scatter(array, "grp", scatter_dimension=array.ndim - 2, tiled=True)
             for array in sums
         ]
-    wide_sums = jnp.stack(sums[:layers]).astype(F32)
-
-    def by_heads(start, stop):
-        return jnp.swapaxes(wide_sums[..., start:stop], 1, 2).reshape(layers, bands, -1)
-
-    query_out = by_heads(0, columns)
-    key_out = by_heads(columns, columns + kv)
-    value_out = by_heads(columns + kv, columns + 2 * kv)
-    rest = jnp.sum(wide_sums[..., columns + 2 * kv :], axis=1)
-    rest = rest[..., :32] + rest[..., 32:64]
-    attn_out = (
-        jnp.sum(query_weight.astype(F32) * query_out, axis=-1)
-        + jnp.sum(key_matrix.astype(F32) * key_out, axis=-1)
-        + jnp.sum(value_matrix.astype(F32) * value_out, axis=-1)
-    ) / attn_gain.astype(F32)
+        wide_sums = jnp.stack(sums[:layers]).astype(F32)
+
+        def by_heads(start, stop):
+            return jnp.swapaxes(wide_sums[..., start:stop], 1, 2).reshape(layers, bands, -1)
+
+        query_out = by_heads(0, columns)
+        key_out = by_heads(columns, columns + kv)
+        value_out = by_heads(columns + kv, columns + 2 * kv)
+        tall_out = jnp.stack(sums[layers:]).astype(F32)
+        rest = jnp.sum(wide_sums[..., columns + 2 * kv :], axis=1)
+        rest = rest[..., :32] + rest[..., 32:64]
+        products = (
+            jnp.sum(query_weight.astype(F32) * query_out, axis=-1)
+            + jnp.sum(key_matrix.astype(F32) * key_out, axis=-1)
+            + jnp.sum(value_matrix.astype(F32) * value_out, axis=-1)
+        )
+    attn_out = products / attn_gain.astype(F32)
 
     def stacked(lists, i):
         return jnp.stack([lists[layer][i] for layer in range(layers)]).astype(F32)
 
     return (
-        result,
-        exchange(upstream.astype(BF16)).astype(F32)[None],
+        result[None],
+        input_grad.astype(F32)[None],
         attn_out,
         rest[..., experts_all],
         query_out,
         key_out,
         value_out,
-        jnp.stack(sums[layers:]).astype(F32),
+        tall_out,
         rest[..., :experts_all],
         stacked(expert_out, 0),
         stacked(expert_out, 1),

time: 953 us -> 936 us (0.982)
  Pallas kernels: 740 us -> 823 us
  matrix products: 54.4 us -> 3.34 us
  other arithmetic: 55.4 us -> 19.8 us
  between operations: 16.7 us -> 2.13 us
  starting transfers between devices: 18.9 us -> 4.49 us
  local copies, waits for them, and re-layouts: 60.1 us -> 74.5 us
    pallas_call x1 -> x5, Pallas kernels: 77.8 us -> 168 us  [the longest x1 101 us: collect(): pl.pallas_call(kernel, out_shape=final_outs + plain_outs + more_outs, in_...]
    dot_general x38 -> x2, matrix products: 52.6 us -> 2.44 us  [per_device(): jnp.einsum('te,de->td', logit_grad, router_w.astype(F32), precision=HIGHEST)]
    unnamed x303 -> x196, local copies, waits for them, and re-layouts: 31.1 us -> 61.9 us
    pallas_call x4, Pallas kernels: 125 us -> 109 us  [scatter_plane_call(): pl.pallas_call(kernel, out_shape=[jax.ShapeDtypeStruct((count, width), F3...]
    ppermute x5 -> x1, starting transfers between devices: 18.7 us -> 4.49 us  [exchange(): return lax.ppermute(array, ('za', 'xh', 'co'), swap)]
    pallas_call x3, Pallas kernels: 78 us -> 64.9 us  [gather_plane(): pl.pallas_call(kernel, out_shape=shapes, in_specs=[VMEM_SPEC] * len(shape...]
    convert_element_type x15 -> x1, other arithmetic: 12.9 us -> 1.14 us  [per_device(): sending = upstream.astype(BF16)]
    pallas_call x2, Pallas kernels: 62 us -> 73.6 us  [experts_backward(): pl.pallas_call(kernel, grid=(local,), out_shape=[jax.ShapeDtypeStruct((bl...]
  transfers between devices with their start and end apart: 11 -> 1, of which waited for: 0 -> 0; matrix products, arithmetic and copies ran while one was open for 13% -> 2% of each run, Pallas kernels for 56% -> 38%
where the time goes in v4:
time: 936 us; the launch traced here: 927 us
  Pallas kernels  823 us (88%)
  local copies, waits for them, and re-layouts  74.5 us (8%)
  other arithmetic  19.8 us (2%)
    pallas_call x3, Pallas kernels, scatter_group(): pl.pallas_call(kernel, out_shape=[jax.ShapeDtypeStruct((count, width), F3...  152 us
    pallas_call x3, Pallas kernels, gather_group(): pl.pallas_call(kernel, out_shape=[jax.ShapeDtypeStruct((2 * planes, count...  113 us
    pallas_call x4, Pallas kernels, scatter_plane_call(): pl.pallas_call(kernel, out_shape=[jax.ShapeDtypeStruct((count, width), F3...  109 us
    pallas_call x1, Pallas kernels, collect(): pl.pallas_call(kernel, out_shape=final_outs + plain_outs + more_outs, in_...  101 us
    pallas_call x1, Pallas kernels, enter(): pl.pallas_call(kernel, out_shape=[jax.ShapeDtypeStruct((8, count, width),...  78.9 us
    pallas_call x2, Pallas kernels, experts_backward(): pl.pallas_call(kernel, grid=(local,), out_shape=[jax.ShapeDtypeStruct((bl...  73.6 us
    pallas_call x3, Pallas kernels, gather_plane(): pl.pallas_call(kernel, out_shape=shapes, in_specs=[VMEM_SPEC] * len(shape...  64.9 us
    pallas_call x2, Pallas kernels, experts_forward(): pl.pallas_call(kernel, grid=(local,), out_shape=[jax.ShapeDtypeStruct(nor...  63.9 us
  transfers between devices with their start and end apart: 1, of which 0 were waited for; matrix products, arithmetic and copies ran while one was open for 2% of the time, Pallas kernels for 38%

profile of v4, /device:TPU:9, one launch (start us, length us, event | category | flops | bytes accessed | tf_op | source)
XLA Modules:
  0.0 927.0 jit_solution(10219296747106192914)
XLA Ops:
  6.0 1.7 slice_bitcast_fusion
  13.6 78.9 %enter.1 = (bf16[8,128,1536]{2,1,0:T(8,128)(2,1)S(1)}, bf16[128,1536]{1,0:T(8,128)(2,1)S(1)}, bf16[4,48,1536]{2,1,0:T(8,128)(2,1)S(1)}, bf16[4,8,48,256]{3,2,1,0...) custom-call(bf16[128,1536]{1,0:T(8,128)(2,1)S(1)} %bitcast.90, ...), custom_call_target="tpu_custom_call" | custom-call | bytes 147600000 | tf_op jit(solution)/shard_map/enter/pallas_call | solution.py:1031
  100.2 1.9 copy-done.12
  104.3 10.6 %attend_forward.2 = (bf16[1024,1536]{1,0:T(8,128)(2,1)S(1)}, bf16[1024,256]{1,0:T(8,128)(2,1)S(1)}, bf16[1024,128]{1,0:T(8,128)(2,1)S(1)}, bf16[1024,256]{1,0:T(8,128)(2,1)S(1)}) custom-call(s32[1,4]{1,0:T(1,128)S(1)} %get-tuple-element.89.starts_ref, bf16[1024,1536]{1,0:T(8,128)(2,1)S(1)} %bitcast.64, bf16[1536,256]{1,0:T(8,128)(2,1)S(1)} %bitcast.75, ...), custom_call_target="tpu_custom_call" | custom-call | bytes 36900000 | tf_op jit(solution)/shard_map/attend_forward/pallas_call | solution.py:1725
  116.5 50.2 %scatter_plane_first.1 = (f32[128,1536]{1,0:T(8,128)S(1)}, bf16[4,3,384,512]{3,2,1,0:T(8,128)(2,1)S(1)}, bf16[4,48,1536]{2,1,0:T(8,128)(2,1)S(1)}, bf16[4,8,48,2...) custom-call(bf16[8,128,1536]{2,1,0:T(8,128)(2,1)S(1)} %bitcast.71, bf16[2,3,384,512]{3,2,1,0:T(8,128)(2,1)S(1)} %copy-done.19, ...), custom_call_target="tpu_custom_call" | custom-call | bytes 73800000 | tf_op jit(solution)/shard_map/scatter_plane_first/pallas_call | solution.py:714
  166.8 2.2 copy-done
  171.5 40.0 %gather_group.3 = (bf16[8,128,1536]{2,1,0:T(8,128)(2,1)S(1)}, bf16[4,3,512,384]{3,2,1,0:T(8,128)(2,1)S(1)}, bf16[8,128,128]{2,1,0:T(8,128)(2,1)S(1)}) custom-call(bf16[128,1536]{1,0:T(8,128)(2,1)S(1)} %multiply_convert_fusion.2.x_ref, bf16[2,3,512,384]{3,2,1,0:T(8,128)(2,1)S(1)} %copy-done.18, bf16[128,128]{1,0:T(8,128)(2,1)S(1)} %pad.12.refs_1_), custom_call_target="tpu_custom_call" | custom-call | bytes 121770000 | tf_op jit(solution)/shard_map/gather_group/pallas_call | solution.py:485
  211.6 2.2 copy-done.1
  213.8 1.6 copy-done.10
  216.1 36.7 %experts_forward.2 = (bf16[8,128,1536]{2,1,0:T(8,128)(2,1)}, f32[3,512,512]{2,1,0:T(8,128)}, f32[3,512,512]{2,1,0:T(8,128)}, f32[8,128,128]{2,1,0:T(8,128)}, f32...) custom-call(bf16[8,128,1536]{2,1,0:T(8,128)(2,1)} %copy-done.10, ...), custom_call_target="tpu_custom_call" | custom-call | bytes 59040000 | tf_op jit(solution)/shard_map/experts_forward/pallas_call | solution.py:1439
  252.8 1.9 copy-done.30
  254.7 36.5 %scatter_group.3 = (f32[128,1536]{1,0:T(8,128)S(1)}, bf16[4,3,384,512]{3,2,1,0:T(8,128)(2,1)S(1)}) custom-call(bf16[8,128,1536]{2,1,0:T(8,128)(2,1)S(1)} %copy-done.30, bf16[2,3,384,512]{3,2,1,0:T(8,128)(2,1)S(1)} %copy-done.19), custom_call_target="tpu_custom_call" | custom-call | bytes 118080000 | tf_op jit(solution)/shard_map/scatter_group/pallas_call | solution.py:532
  291.2 2.2 copy-done.2
  294.4 24.6 %gather_plane.3 = (bf16[8,128,1536]{2,1,0:T(8,128)(2,1)S(1)}, bf16[4,48,1536]{2,1,0:T(8,128)(2,1)S(1)}) custom-call(bf16[128,1536]{1,0:T(8,128)(2,1)S(1)} %multiply_convert_fusion.1.x_ref, bf16[4,48,1536]{2,1,0:T(8,128)(2,1)S(1)} %copy-done.56), custom_call_target="tpu_custom_call" | custom-call | bytes 73800000 | tf_op jit(solution)/shard_map/gather_plane/pallas_call | solution.py:593
  319.1 10.7 %attend_forward.3 = (bf16[1024,1536]{1,0:T(8,128)(2,1)S(1)}, bf16[1024,256]{1,0:T(8,128)(2,1)S(1)}, bf16[1024,128]{1,0:T(8,128)(2,1)S(1)}, bf16[1024,256]{1,0:T(8,128)(2,1)S(1)}) custom-call(s32[1,4]{1,0:T(1,128)S(1)} %get-tuple-element.89.starts_ref, bf16[1024,1536]{1,0:T(8,128)(2,1)S(1)} %bitcast.65, bf16[1536,256]{1,0:T(8,128)(2,1)S(1)} %bitcast.77, ...), custom_call_target="tpu_custom_call" | custom-call | bytes 36900000 | tf_op jit(solution)/shard_map/attend_forward/pallas_call | solution.py:1725
  329.8 18.7 %scatter_plane.3 = f32[128,1536]{1,0:T(8,128)S(1)} custom-call(bf16[8,128,1536]{2,1,0:T(8,128)(2,1)S(1)} %bitcast.74), custom_call_target="tpu_custom_call" | custom-call | bytes 73800000 | tf_op jit(solution)/shard_map/scatter_plane/pallas_call | solution.py:714
  348.9 37.0 %gather_group.4 = (bf16[8,128,1536]{2,1,0:T(8,128)(2,1)S(1)}, bf16[4,3,512,384]{3,2,1,0:T(8,128)(2,1)S(1)}) custom-call(bf16[128,1536]{1,0:T(8,128)(2,1)S(1)} %multiply_convert_fusion.x_ref, bf16[2,3,512,384]{3,2,1,0:T(8,128)(2,1)S(1)} %copy-done.18), custom_call_target="tpu_custom_call" | custom-call | bytes 121770000 | tf_op jit(solution)/shard_map/gather_group/pallas_call | solution.py:485
  385.9 2.1 copy-done.3
  388.0 1.6 copy-done.16
  389.6 27.2 %experts_forward.3 = (bf16[8,128,1536]{2,1,0:T(8,128)(2,1)}, f32[3,512,512]{2,1,0:T(8,128)}, f32[3,512,512]{2,1,0:T(8,128)}, f32[8,128,128]{2,1,0:T(8,128)}, f32...) custom-call(bf16[8,128,1536]{2,1,0:T(8,128)(2,1)} %copy-done.16, bf16[8,128,128]{2,1,0:T(8,128)(2,1)} %copy-done.22, ...), custom_call_target="tpu_custom_call" | custom-call | bytes 59040000 | tf_op jit(solution)/shard_map/experts_forward/pallas_call | solution.py:1439
  416.8 41.9 %experts_backward.2 = (bf16[8,128,1664]{2,1,0:T(8,128)(2,1)}, bf16[4,3,384,512]{3,2,1,0:T(8,128)(2,1)}, bf16[4,3,384,512]{3,2,1,0:T(8,128)(2,1)}, bf16[4,3,512,384]{3,2,1,0:T(8,128)(2,1)}, f32[128,1536]{1,0:T(8,128)}) custom-call(bf16[8,128,1536]{2,1,0:T(8,128)(2,1)} %copy-done.16, bf16[8,128,128]{2,1,0:T(8,128)(2,1)} %copy-done.22, ...), custom_call_target="tpu_custom_call" | custom-call | bytes 110700000 | tf_op jit(solution)/shard_map/experts_backward/pallas_call | solution.py:1601
  458.7 2.3 copy-done.20
  461.1 2.0 copy-done.25
  463.0 58.5 %scatter_group.4 = (f32[128,1664]{1,0:T(8,128)S(1)}, bf16[3,512,384]{2,1,0:T(8,128)(2,1)S(1)}, bf16[3,384,512]{2,1,0:T(8,128)(2,1)S(1)}) custom-call(bf16[8,128,1664]{2,1,0:T(8,128)(2,1)S(1)} %copy-done.25, bf16[4,3,512,384]{3,2,1,0:T(8,128)(2,1)S(1)} %copy-done.20, bf16[4,3,384,512]{3,2,1,0:T(8,128)(2,1)} %get-tuple-element.129.refs_1_), custom_call_target="tpu_custom_call" | custom-call | bytes 118080000 | tf_op jit(solution)/shard_map/scatter_group/pallas_call | solution.py:532
  526.1 2.8 fusion.16
  529.0 4.5 collective-permute-start
  534.4 21.8 %gather_plane.4 = bf16[8,128,1536]{2,1,0:T(8,128)(2,1)S(1)} custom-call(bf16[128,1536]{1,0:T(8,128)(2,1)S(1)} %get-tuple-element.240.x_ref), custom_call_target="tpu_custom_call" | custom-call | bytes 73800000 | tf_op jit(solution)/shard_map/gather_plane/pallas_call | solution.py:593
  556.2 1.7 copy-done.15
  558.2 22.6 %attend_backward.2 = (bf16[1024,1536]{1,0:T(8,128)(2,1)}, bf16[1536,384]{1,0:T(8,128)(2,1)}, bf16[192,1536]{1,0:T(8,128)(2,1)S(1)}) custom-call(s32[1,4]{1,0:T(1,128)S(1)} %get-tuple-element.89.starts_ref, bf16[1024,1536]{1,0:T(8,128)(2,1)} %bitcast.66, bf16[1536,256]{1,0:T(8,128)(2,1)S(1)} %bitcast.78, bf16[1536,128]{1,0:T(8,128)(2,1)S(1)} %bitcast.62, ...), custom_call_target="tpu_custom_call" | custom-call | bytes 73800000 | tf_op jit(solution)/shard_map/attend_backward/pallas_call | solution.py:1820
  580.8 2.1 copy-done.29
  582.9 21.3 %scatter_plane.4 = f32[128,1536]{1,0:T(8,128)S(1)} custom-call(bf16[8,128,1536]{2,1,0:T(8,128)(2,1)S(1)} %bitcast.73), custom_call_target="tpu_custom_call" | custom-call | bytes 73800000 | tf_op jit(solution)/shard_map/scatter_plane/pallas_call | solution.py:714
  605.6 35.8 %gather_group.5 = (bf16[8,128,1536]{2,1,0:T(8,128)(2,1)S(1)}, bf16[3,384,512]{2,1,0:T(8,128)(2,1)S(1)}) custom-call(bf16[128,1536]{1,0:T(8,128)(2,1)S(1)} %get-tuple-element.238.x_ref, bf16[4,3,384,512]{3,2,1,0:T(8,128)(2,1)S(1)} %bitcast.70), custom_call_target="tpu_custom_call" | custom-call | bytes 121770000 | tf_op jit(solution)/shard_map/gather_group/pallas_call | solution.py:485
  641.4 1.7 copy-done.27
  643.1 31.7 %experts_backward.3 = (bf16[8,128,1664]{2,1,0:T(8,128)(2,1)}, bf16[4,3,384,512]{3,2,1,0:T(8,128)(2,1)}, bf16[4,3,384,512]{3,2,1,0:T(8,128)(2,1)}, bf16[4,3,512,384]{3,2,1,0:T(8,128)(2,1)}) custom-call(bf16[8,128,1536]{2,1,0:T(8,128)(2,1)} %copy-done.10, bf16[8,128,128]{2,1,0:T(8,128)(2,1)} %copy-done.22, f32[8,32,128]{2,1,0:T(8,128)} %get-tuple-element.136.pt_ref, ...), custom_call_target="tpu_custom_call" | custom-call | bytes 110700000 | tf_op jit(solution)/shard_map/experts_backward/pallas_call | solution.py:1601
  674.8 2.3 copy-done.21
  677.1 2.0 copy-done.26
  679.1 57.4 %scatter_group.5 = (f32[128,1664]{1,0:T(8,128)S(1)}, bf16[3,512,384]{2,1,0:T(8,128)(2,1)S(1)}, bf16[3,384,512]{2,1,0:T(8,128)(2,1)S(1)}) custom-call(bf16[8,128,1664]{2,1,0:T(8,128)(2,1)S(1)} %copy-done.26, bf16[4,3,512,384]{3,2,1,0:T(8,128)(2,1)S(1)} %copy-done.21, bf16[4,3,384,512]{3,2,1,0:T(8,128)(2,1)} %get-tuple-element.143.refs_1_), custom_call_target="tpu_custom_call" | custom-call | bytes 118080000 | tf_op jit(solution)/shard_map/scatter_group/pallas_call | solution.py:532
  741.4 1.9 fusion.14
  743.3 18.5 %gather_plane.5 = bf16[8,128,1536]{2,1,0:T(8,128)(2,1)S(1)} custom-call(bf16[128,1536]{1,0:T(8,128)(2,1)S(1)} %get-tuple-element.236.x_ref), custom_call_target="tpu_custom_call" | custom-call | bytes 73800000 | tf_op jit(solution)/shard_map/gather_plane/pallas_call | solution.py:593
  761.8 1.7 copy-done.14
  763.7 22.4 %attend_backward.3 = (bf16[1024,1536]{1,0:T(8,128)(2,1)}, bf16[1536,384]{1,0:T(8,128)(2,1)}, bf16[192,1536]{1,0:T(8,128)(2,1)S(1)}) custom-call(s32[1,4]{1,0:T(1,128)S(1)} %get-tuple-element.89.starts_ref, bf16[1024,1536]{1,0:T(8,128)(2,1)} %bitcast.63, bf16[1536,256]{1,0:T(8,128)(2,1)S(1)} %bitcast.76, bf16[1536,128]{1,0:T(8,128)(2,1)S(1)} %bitcast.57, ...), custom_call_target="tpu_custom_call" | custom-call | bytes 73800000 | tf_op jit(solution)/shard_map/attend_backward/pallas_call | solution.py:1820
  786.1 2.1 copy-done.28
  788.2 18.5 %scatter_plane.5 = f32[128,1536]{1,0:T(8,128)S(1)} custom-call(bf16[8,128,1536]{2,1,0:T(8,128)(2,1)S(1)} %bitcast.72), custom_call_target="tpu_custom_call" | custom-call | bytes 73800000 | tf_op jit(solution)/shard_map/scatter_plane/pallas_call | solution.py:714
  808.1 101.4 %collect.1 = (f32[2,48,1536]{2,1,0:T(8,128)}, f32[2,48,512]{2,1,0:T(8,128)}, f32[2,48,512]{2,1,0:T(8,128)}, f32[2,48,1536]{2,1,0:T(8,128)}, f32[2,48,128]{2,1,0:...) custom-call(bf16[4,8,48,384]{3,2,1,0:T(8,128)(2,1)} %bitcast.95, bf16[4,8,48,384]{3,2,1,0:T(8,128)(2,1)} %bitcast.94, ...), custom_call_target="tpu_custom_call" | custom-call | bytes 147600000 | tf_op jit(solution)/shard_map/collect/pallas_call | solution.py:1271
  913.2 2.5 maximum_convert_fusion.1
  915.7 2.5 maximum_convert_fusion.2
  918.3 2.5 maximum_convert_fusion
  921.8 1.8 copy.98
  (242 shorter events, 48.6 us)
Async XLA Ops:
  0.6 9.0 copy-start.76
  9.6 90.6 %copy-start.4 = (f32[1024,256]{1,0:T(8,128)S(1)}, f32[1024,256]{1,0:T(8,128)}, u32[]{:S(2)}) copy-start(f32[1024,256]{1,0:T(8,128)} %constant.48.clone.s_ref) | copy-start | bytes 3145732
  9.6 90.6 %copy-start.5 = (f32[1024,256]{1,0:T(8,128)S(1)}, f32[1024,256]{1,0:T(8,128)}, u32[]{:S(2)}) copy-start(f32[1024,256]{1,0:T(8,128)} %constant.47.clone.c_ref) | copy-start | bytes 3145732
  97.7 17.2 %copy-start.6 = (bf16[4,8,48,128]{3,2,1,0:T(8,128)(2,1)}, bf16[4,8,48,128]{3,2,1,0:T(8,128)(2,1)S(1)}, u32[]{:S(2)}) copy-start(bf16[4,8,48,128]{3,2,1,0:T(8,128)(2,1)S(1)} %get-tuple-element.92) | copy-start | bytes 1179652
  97.7 17.2 %copy-start.42 = (bf16[128,1536]{1,0:T(8,128)(2,1)}, bf16[128,1536]{1,0:T(8,128)(2,1)S(1)}, u32[]{:S(2)}) copy-start(bf16[128,1536]{1,0:T(8,128)(2,1)S(1)} %get-tuple-element.104) | copy-start | bytes 1179652
  104.3 12.2 %copy-start.19 = (bf16[2,3,384,512]{3,2,1,0:T(8,128)(2,1)S(1)}, bf16[2,3,384,512]{3,2,1,0:T(8,128)(2,1)}, u32[]{:S(2)}) copy-start(bf16[2,3,384,512]{3,2,1,0:T(8,128)(2,1)} %refs_0_.8) | copy-start | bytes 7077892
  104.3 12.2 %copy-start.72 = (bf16[8,48,256]{2,1,0:T(8,128)(2,1)S(1)}, bf16[8,48,256]{2,1,0:T(8,128)(2,1)}, u32[]{:S(2)}) copy-start(bf16[8,48,256]{2,1,0:T(8,128)(2,1)} %copy-done.71) | copy-start | bytes 589828
  104.3 12.2 %copy-start.74 = (bf16[8,48,128]{2,1,0:T(8,128)(2,1)S(1)}, bf16[8,48,128]{2,1,0:T(8,128)(2,1)}, u32[]{:S(2)}) copy-start(bf16[8,48,128]{2,1,0:T(8,128)(2,1)} %copy-done.73) | copy-start | bytes 294916
  116.5 52.6 %copy-start.67 = (bf16[1024,128]{1,0:T(8,128)(2,1)}, bf16[1024,128]{1,0:T(8,128)(2,1)S(1)}, u32[]{:S(2)}) copy-start(bf16[1024,128]{1,0:T(8,128)(2,1)S(1)} %get-tuple-element.125.v_ref) | copy-start | bytes 786436
  168.9 42.6 %copy-start.34 = (bf16[4,8,48,256]{3,2,1,0:T(8,128)(2,1)}, bf16[4,8,48,256]{3,2,1,0:T(8,128)(2,1)S(1)}, u32[]{:S(2)}) copy-start(bf16[4,8,48,256]{3,2,1,0:T(8,128)(2,1)S(1)} %get-tuple-element.110) | copy-start | bytes 2359300
  168.9 42.6 %copy-start.55 = (bf16[4,48,1536]{2,1,0:T(8,128)(2,1)}, bf16[4,48,1536]{2,1,0:T(8,128)(2,1)S(1)}, u32[]{:S(2)}) copy-start(bf16[4,48,1536]{2,1,0:T(8,128)(2,1)S(1)} %get-tuple-element.108.refs_0_) | copy-start | bytes 1769476
  168.9 150.1 %copy-start.8 = (bf16[4,8,48,128]{3,2,1,0:T(8,128)(2,1)}, bf16[4,8,48,128]{3,2,1,0:T(8,128)(2,1)S(1)}, u32[]{:S(2)}) copy-start(bf16[4,8,48,128]{3,2,1,0:T(8,128)(2,1)S(1)} %get-tuple-element.107) | copy-start | bytes 1179652
  171.5 40.0 %copy-start.23 = (bf16[128,1536]{1,0:T(8,128)(2,1)}, bf16[128,1536]{1,0:T(8,128)(2,1)S(1)}, u32[]{:S(2)}) copy-start(bf16[128,1536]{1,0:T(8,128)(2,1)S(1)} %multiply_convert_fusion.2.x_ref) | copy-start | bytes 1179652
  254.7 38.7 %copy-start.80 = (f32[128,1536]{1,0:T(8,128)S(1)}, f32[128,1536]{1,0:T(8,128)}, u32[]{:S(2)}) copy-start(f32[128,1536]{1,0:T(8,128)} %copy-done.79) | copy-start | bytes 2359300
  293.4 25.7 %copy-start.35 = (bf16[4,8,48,256]{3,2,1,0:T(8,128)(2,1)S(1)}, bf16[4,8,48,256]{3,2,1,0:T(8,128)(2,1)}, u32[]{:S(2)}) copy-start(bf16[4,8,48,256]{3,2,1,0:T(8,128)(2,1)} %copy-done.34) | copy-start | bytes 2359300
  293.5 55.0 %copy-start.77 = (f32[128,1536]{1,0:T(8,128)}, f32[128,1536]{1,0:T(8,128)S(1)}, u32[]{:S(2)}) copy-start(f32[128,1536]{1,0:T(8,128)S(1)} %get-tuple-element.245) | copy-start | bytes 2359300
  319.0 10.8 %copy-start.13 = (bf16[8,128,1536]{2,1,0:T(8,128)(2,1)}, bf16[8,128,1536]{2,1,0:T(8,128)(2,1)S(1)}, u32[]{:S(2)}) copy-start(bf16[8,128,1536]{2,1,0:T(8,128)(2,1)S(1)} %get-tuple-element.109) | copy-start | bytes 9437188
  319.0 10.8 %copy-start.40 = (bf16[4,48,1536]{2,1,0:T(8,128)(2,1)}, bf16[4,48,1536]{2,1,0:T(8,128)(2,1)S(1)}, u32[]{:S(2)}) copy-start(bf16[4,48,1536]{2,1,0:T(8,128)(2,1)S(1)} %get-tuple-element.111) | copy-start | bytes 1769476
  329.8 18.9 %copy-start.61 = (bf16[1024,256]{1,0:T(8,128)(2,1)}, bf16[1024,256]{1,0:T(8,128)(2,1)S(1)}, u32[]{:S(2)}) copy-start(bf16[1024,256]{1,0:T(8,128)(2,1)S(1)} %get-tuple-element.132.h_ref) | copy-start | bytes 1572868
  329.8 18.9 %copy-start.63 = (bf16[1024,256]{1,0:T(8,128)(2,1)}, bf16[1024,256]{1,0:T(8,128)(2,1)S(1)}, u32[]{:S(2)}) copy-start(bf16[1024,256]{1,0:T(8,128)(2,1)S(1)} %get-tuple-element.134.m_ref) | copy-start | bytes 1572868
  329.8 18.9 %copy-start.69 = (bf16[1024,128]{1,0:T(8,128)(2,1)}, bf16[1024,128]{1,0:T(8,128)(2,1)S(1)}, u32[]{:S(2)}) copy-start(bf16[1024,128]{1,0:T(8,128)(2,1)S(1)} %get-tuple-element.133.v_ref) | copy-start | bytes 786436
  348.7 176.5 %copy-start.82 = (f32[128,1536]{1,0:T(8,128)}, f32[128,1536]{1,0:T(8,128)S(1)}, u32[]{:S(2)}) copy-start(f32[128,1536]{1,0:T(8,128)S(1)} %get-tuple-element.243) | copy-start | bytes 2359300
  463.0 62.3 %copy-start.9 = (bf16[4,8,48,128]{3,2,1,0:T(8,128)(2,1)S(1)}, bf16[4,8,48,128]{3,2,1,0:T(8,128)(2,1)}, u32[]{:S(2)}) copy-start(bf16[4,8,48,128]{3,2,1,0:T(8,128)(2,1)} %copy-done.8) | copy-start | bytes 1179652
  463.0 63.1 %copy-start.43 = (bf16[128,1536]{1,0:T(8,128)(2,1)S(1)}, bf16[128,1536]{1,0:T(8,128)(2,1)}, u32[]{:S(2)}) copy-start(bf16[128,1536]{1,0:T(8,128)(2,1)} %copy-done.42) | copy-start | bytes 1179652
  529.0 392.8 %collective-permute-start = (bf16[128,1536]{1,0:T(8,128)(2,1)}, bf16[128,1536]{1,0:T(8,128)(2,1)}, u32[]{:S(2)}, u32[]{:S(2)}) collective-permute-start(bf16[128,1536]{1,0:T(8,128)(2,1)} %get-tuple-element.248), channel_id=1, source_target_pairs={{0,0},{1,8},{2,16},{3,24},{8,1},{9,9},{10,17},{11,25},{16,2},{17,1... | collective-permute-start | bytes 1179656 | tf_op jit(solution)/shard_map/ppermute | solution.py:1886
  534.3 23.8 %copy-start.36 = (bf16[4,8,48,256]{3,2,1,0:T(8,128)(2,1)S(1)}, bf16[4,8,48,256]{3,2,1,0:T(8,128)(2,1)}, u32[]{:S(2)}) copy-start(bf16[4,8,48,256]{3,2,1,0:T(8,128)(2,1)} %copy-done.34) | copy-start | bytes 2359300
  534.3 23.8 %copy-start.41 = (bf16[4,48,1536]{2,1,0:T(8,128)(2,1)S(1)}, bf16[4,48,1536]{2,1,0:T(8,128)(2,1)}, u32[]{:S(2)}) copy-start(bf16[4,48,1536]{2,1,0:T(8,128)(2,1)} %copy-done.40) | copy-start | bytes 1769476
  534.3 23.8 %copy-start.62 = (bf16[1024,256]{1,0:T(8,128)(2,1)S(1)}, bf16[1024,256]{1,0:T(8,128)(2,1)}, u32[]{:S(2)}) copy-start(bf16[1024,256]{1,0:T(8,128)(2,1)} %copy-done.61) | copy-start | bytes 1572868
  534.3 23.8 %copy-start.64 = (bf16[1024,256]{1,0:T(8,128)(2,1)S(1)}, bf16[1024,256]{1,0:T(8,128)(2,1)}, u32[]{:S(2)}) copy-start(bf16[1024,256]{1,0:T(8,128)(2,1)} %copy-done.63) | copy-start | bytes 1572868
  534.3 23.8 %copy-start.70 = (bf16[1024,128]{1,0:T(8,128)(2,1)S(1)}, bf16[1024,128]{1,0:T(8,128)(2,1)}, u32[]{:S(2)}) copy-start(bf16[1024,128]{1,0:T(8,128)(2,1)} %copy-done.69) | copy-start | bytes 786436
  558.1 47.5 %slice-start = ((s8[4718592]{0:T(1024)(128)(4,1)}), s8[4194304]{0:T(1024)(128)(4,1)S(1)}, s32[]{:S(2)}) async-start(s8[4718592]{0:T(1024)(128)(4,1)} %bitcast.69), calls=%async_computation | async-start | bytes 8388608
  558.2 46.1 %copy-start.78 = (f32[128,1536]{1,0:T(8,128)S(1)}, f32[128,1536]{1,0:T(8,128)}, u32[]{:S(2)}) copy-start(f32[128,1536]{1,0:T(8,128)} %copy-done.77) | copy-start | bytes 2359300
  558.2 46.2 %copy-start.83 = (f32[128,1536]{1,0:T(8,128)S(1)}, f32[128,1536]{1,0:T(8,128)}, u32[]{:S(2)}) copy-start(f32[128,1536]{1,0:T(8,128)} %get-tuple-element.241) | copy-start | bytes 2359300
  558.2 47.4 %slice-start.1 = ((s8[4718592]{0:T(1024)(128)(4,1)}), s8[524288]{0:T(1024)(128)(4,1)S(1)}, s32[]{:S(2)}) async-start(s8[4718592]{0:T(1024)(128)(4,1)} %bitcast.69), calls=%async_computation.1 | async-start | bytes 1048576
  580.8 24.7 %copy-start.52 = (bf16[192,1536]{1,0:T(8,128)(2,1)}, bf16[192,1536]{1,0:T(8,128)(2,1)S(1)}, u32[]{:S(2)}) copy-start(bf16[192,1536]{1,0:T(8,128)(2,1)S(1)} %get-tuple-element.149) | copy-start | bytes 1769476
  679.1 59.8 %copy-start.24 = (bf16[128,1536]{1,0:T(8,128)(2,1)S(1)}, bf16[128,1536]{1,0:T(8,128)(2,1)}, u32[]{:S(2)}) copy-start(bf16[128,1536]{1,0:T(8,128)(2,1)} %copy-done.23) | copy-start | bytes 1179652
  679.1 59.8 %copy-start.85 = (f32[128,128]{1,0:T(8,128)S(1)}, f32[128,128]{1,0:T(8,128)}, u32[]{:S(2)}) copy-start(f32[128,128]{1,0:T(8,128)} %get-tuple-element.263) | copy-start | bytes 196612
  679.1 60.2 %copy-start.7 = (bf16[4,8,48,128]{3,2,1,0:T(8,128)(2,1)S(1)}, bf16[4,8,48,128]{3,2,1,0:T(8,128)(2,1)}, u32[]{:S(2)}) copy-start(bf16[4,8,48,128]{3,2,1,0:T(8,128)(2,1)} %copy-done.6) | copy-start | bytes 1179652
  679.1 60.2 %copy-start.81 = (f32[128,1536]{1,0:T(8,128)S(1)}, f32[128,1536]{1,0:T(8,128)}, u32[]{:S(2)}) copy-start(f32[128,1536]{1,0:T(8,128)} %copy-done.79) | copy-start | bytes 2359300
  743.3 20.4 %copy-start.33 = (bf16[4,8,48,256]{3,2,1,0:T(8,128)(2,1)S(1)}, bf16[4,8,48,256]{3,2,1,0:T(8,128)(2,1)}, u32[]{:S(2)}) copy-start(bf16[4,8,48,256]{3,2,1,0:T(8,128)(2,1)} %copy-done.31) | copy-start | bytes 2359300
  743.3 20.4 %copy-start.39 = (bf16[4,48,1536]{2,1,0:T(8,128)(2,1)S(1)}, bf16[4,48,1536]{2,1,0:T(8,128)(2,1)}, u32[]{:S(2)}) copy-start(bf16[4,48,1536]{2,1,0:T(8,128)(2,1)} %copy-done.37) | copy-start | bytes 1769476
  743.3 20.4 %copy-start.58 = (bf16[1024,256]{1,0:T(8,128)(2,1)S(1)}, bf16[1024,256]{1,0:T(8,128)(2,1)}, u32[]{:S(2)}) copy-start(bf16[1024,256]{1,0:T(8,128)(2,1)} %copy-done.57) | copy-start | bytes 1572868
  743.3 20.4 %copy-start.60 = (bf16[1024,256]{1,0:T(8,128)(2,1)S(1)}, bf16[1024,256]{1,0:T(8,128)(2,1)}, u32[]{:S(2)}) copy-start(bf16[1024,256]{1,0:T(8,128)(2,1)} %copy-done.59) | copy-start | bytes 1572868
  743.3 20.4 %copy-start.68 = (bf16[1024,128]{1,0:T(8,128)(2,1)S(1)}, bf16[1024,128]{1,0:T(8,128)(2,1)}, u32[]{:S(2)}) copy-start(bf16[1024,128]{1,0:T(8,128)(2,1)} %copy-done.67) | copy-start | bytes 786436
  786.1 21.9 %copy-start.53 = (bf16[192,1536]{1,0:T(8,128)(2,1)}, bf16[192,1536]{1,0:T(8,128)(2,1)S(1)}, u32[]{:S(2)}) copy-start(bf16[192,1536]{1,0:T(8,128)(2,1)S(1)} %get-tuple-element.148) | copy-start | bytes 1769476
  808.1 103.0 %copy-start.91 = (bf16[2,48]{1,0:T(2,128)(2,1)S(1)}, bf16[2,48]{1,0:T(2,128)(2,1)}, u32[]{:S(2)}) copy-start(bf16[2,48]{1,0:T(2,128)(2,1)} %param.20) | copy-start | bytes 580
  808.1 105.1 %copy-start.51 = (bf16[3,384,512]{2,1,0:T(8,128)(2,1)S(1)}, bf16[3,384,512]{2,1,0:T(8,128)(2,1)}, u32[]{:S(2)}) copy-start(bf16[3,384,512]{2,1,0:T(8,128)(2,1)} %copy-done.50) | copy-start | bytes 3538948
  918.3 5.2 copy-start.87
  (47 other events, 82.0 us)

commit v5 on v4

--- a/solution.py
+++ b/solution.py
@@ -769,22 +769,25 @@
     return {"za": f, "xh": za // 2, "co": lax.rem(za, 2)}
 
 
-def line_barrier(planes, devices, swaps=False):
+def line_barrier(planes, devices, swaps=False, line=True):
     za = lax.axis_index("za")
     f = lax.axis_index("xh") * 2 + lax.axis_index("co")
     sem = pltpu.get_barrier_semaphore()
     for device in devices:
         pl.semaphore_signal(sem, inc=1, device_id=device, device_id_type=MESH)
 
-    @pl.when(za > 0)
-    def _():
-        pl.semaphore_signal(sem, inc=1, device_id={"za": za - 1}, device_id_type=MESH)
-
-    @pl.when(za < planes - 1)
-    def _():
-        pl.semaphore_signal(sem, inc=1, device_id={"za": za + 1}, device_id_type=MESH)
-
-    below, above = (za + planes - 1) // planes, (2 * planes - 2 - za) // planes
+    below, above = 0, 0
+    if line:
+
+        @pl.when(za > 0)
+        def _():
+            pl.semaphore_signal(sem, inc=1, device_id={"za": za - 1}, device_id_type=MESH)
+
+        @pl.when(za < planes - 1)
+        def _():
+            pl.semaphore_signal(sem, inc=1, device_id={"za": za + 1}, device_id_type=MESH)
+
+        below, above = (za + planes - 1) // planes, (2 * planes - 2 - za) // planes
     apart = 0
     if swaps:
 
@@ -1484,11 +1487,13 @@
 
 def experts_backward(
     normed, arrived, codes, probs_t, gate_w, up_w, down_w, gate_part, up_part, slots, shares,
-    late=None, planes=None,
+    late=None, planes=None, share=None, swap=None,
 ):
     blocks, count, width = normed.shape
     pieces = len(arrived)
     more = [] if late is None else [late]
+    shared, shared_outs, shared_scratch = share_shapes(share)
+    swaps = [] if swap is None else [swap]
     _, local, _, hidden_size = gate_w.shape
     lines = local * slots
     total = blocks * slots
@@ -1501,13 +1506,21 @@
         a_refs, refs = refs[:pieces], refs[pieces:]
         if more:
             l_ref, refs = refs[0], refs[1:]
+        w_ref, refs = refs[: len(shared)], refs[len(shared) :]
+        y_ref, refs = refs[: len(swaps)], refs[len(swaps) :]
         out, dg_out, du_out, dd_out, *refs = refs
         if more:
             l_out, refs = refs[0], refs[1:]
+        b_ref, refs = refs[: len(shared)], refs[len(shared) :]
+        yo_ref, refs = refs[: len(swaps)], refs[len(swaps) :]
         rows, outs, back, marks, codes_t, *refs = refs
         if more:
             ring = Ring8(planes)
             scatter = RingScatter(ring, 2, l_ref, *refs)
+        if swaps:
+            swap_send, swap_recv, *refs = refs
+        if shared:
+            carried = carrier(share, w_ref[0], b_ref[0], refs)
         e = pl.program_id(0)
         first = (lax.axis_index("za") * 2 + lax.axis_index("yb")) * local
 
@@ -1516,6 +1529,12 @@
             if more:
                 barrier([ring.dev(ring.rho + 1), ring.dev(ring.rho - 1)])
                 scatter.step(1)
+            if swaps or shared:
+                line_barrier(planes, share_devices(), len(swaps) > 0, False)
+            if shared:
+                carried.start()
+            if swaps:
+                trade(y_ref[0], yo_ref[0], swap_send, swap_recv, lambda copy: copy.start())
 
             @pl.loop(0, blocks)
             def _(b):
@@ -1534,6 +1553,8 @@
 
             if more:
                 scatter.step(2)
+            if shared:
+                carried.middle()
 
         mine = pl.ds(pl.multiple_of(e * slots, slots), slots)
         upstream = outs[:, mine, :].reshape(total, width)
@@ -1575,6 +1596,10 @@
         def _():
             if more:
                 l_out[...] = scatter.finish()
+            if shared:
+                carried.end()
+            if swaps:
+                trade(y_ref[0], yo_ref[0], swap_send, swap_recv, lambda copy: copy.wait())
 
             @pl.loop(0, blocks)
             def _(b):
@@ -1607,7 +1632,9 @@
             jax.ShapeDtypeStruct(cut_shape, BF16),
             jax.ShapeDtypeStruct(down_shape, BF16),
         ]
-        + [jax.ShapeDtypeStruct((count, width), F32)] * len(more),
+        + [jax.ShapeDtypeStruct((count, width), F32)] * len(more)
+        + shared_outs
+        + [jax.ShapeDtypeStruct(array.shape, BF16) for array in swaps],
         in_specs=[
             once(normed.shape),
             once(codes.shape),
@@ -1619,9 +1646,10 @@
             per_expert(up_part.shape[1:]),
         ]
         + [once(array.shape) for array in arrived]
-        + [ANY_SPEC] * len(more),
+        + [ANY_SPEC] * (len(more) + len(shared) + len(swaps)),
         out_specs=[once((blocks, count, width + 128)), cut_spec, cut_spec, down_spec]
-        + [once((count, width))] * len(more),
+        + [once((count, width))] * len(more)
+        + [ANY_SPEC] * (len(shared) + len(swaps)),
         scratch_shapes=[
             pltpu.VMEM((blocks, lines, width), BF16),
             pltpu.VMEM((blocks, lines, width), BF16),
@@ -1629,11 +1657,13 @@
             pltpu.VMEM((blocks, lines, 128), BF16),
             pltpu.VMEM((codes.shape[2], count), F32),
         ]
-        + late_scratch,
-        compiler_params=plain_params(62, 15 if more else None),
+        + late_scratch
+        + [DMA, DMA] * len(swaps)
+        + shared_scratch,
+        compiler_params=plain_params(62, 15 if more else 19 if shared or swaps else None),
         cost_estimate=busy(30),
         name="experts_backward",
-    )(normed, codes, probs_t, gate_w, up_w, down_w, gate_part, up_part, *arrived, *more)
+    )(normed, codes, probs_t, gate_w, up_w, down_w, gate_part, up_part, *arrived, *more, *shared, *swaps)
     row_sums, gate_term, up_term, down_term, *added = results
     if not split:
         down_term = jnp.moveaxis(
@@ -1739,16 +1769,23 @@
     )(starts, normed, *slab, out_rows, cosine, sine)
 
 
-def attention_backward(normed, slab, out_rows, starts, cosine, sine, heads, values, mixed, branch, rest):
+def attention_backward(normed, slab, out_rows, starts, cosine, sine, heads, values, mixed, branch, rest, share=None):
     length, width = normed.shape
     rows = min(ROWS, length)
     scale = 1.0 / math.sqrt(HEAD_SIZE)
     used = 3 * HEAD_SIZE
-
-    def kernel(
-        starts_ref, x_ref, w_ref, wv_ref, o_ref, c_ref, s_ref, h_ref, v_ref, m_ref, b_ref, r_ref,
-        out, wide, tall, keys, spread, grads, key_sum, value_sum, low,
-    ):
+    more, more_outs, more_scratch = share_shapes(share)
+
+    def kernel(starts_ref, x_ref, w_ref, wv_ref, o_ref, c_ref, s_ref, h_ref, v_ref, m_ref, b_ref, r_ref, *refs):
+        in_ref, refs = refs[: len(more)], refs[len(more) :]
+        out, wide, tall, *refs = refs
+        sum_ref, refs = refs[: len(more)], refs[len(more) :]
+        keys, spread, grads, key_sum, value_sum, low, *refs = refs
+        if more:
+            barrier(share_devices())
+            carried = carrier(share, in_ref[0], sum_ref[0], refs)
+            carried.start()
+
         @pl.loop(0, length // rows)
         def _(i):
             part = pl.ds(pl.multiple_of(i * rows, rows), rows)
@@ -1762,6 +1799,9 @@
             ).astype(BF16)
             key_sum[part, :] = jnp.zeros((rows, GROUP), F32)
             value_sum[part, :] = jnp.zeros((rows, GROUP), F32)
+
+        if more:
+            carried.middle()
 
         for i in range(length // rows):
             first, stop = i * rows, (i + 1) * rows
@@ -1816,6 +1856,8 @@
                 lanes < HEAD_SIZE, made[:, GROUP:], beside.astype(F32)
             ).astype(BF16)
         tall[...] = dot(m_ref[...].T, b_ref[...])[:used].astype(BF16)
+        if more:
+            carried.end()
 
     return pl.pallas_call(
         kernel,
@@ -1823,9 +1865,10 @@
             jax.ShapeDtypeStruct((length, width), BF16),
             jax.ShapeDtypeStruct((width, GROUP + 128), BF16),
             jax.ShapeDtypeStruct((used, width), BF16),
-        ],
-        in_specs=[SMEM_SPEC] + [VMEM_SPEC] * 11,
-        out_specs=[VMEM_SPEC] * 3,
+        ]
+        + more_outs,
+        in_specs=[SMEM_SPEC] + [VMEM_SPEC] * 11 + [ANY_SPEC] * len(more),
+        out_specs=[VMEM_SPEC] * 3 + [ANY_SPEC] * len(more),
         scratch_shapes=[
             pltpu.VMEM((length, GROUP), BF16),
             pltpu.VMEM((length, GROUP), BF16),
@@ -1833,11 +1876,14 @@
             pltpu.VMEM((length, GROUP), F32),
             pltpu.VMEM((length, GROUP), F32),
             pltpu.VMEM((length, GROUP + 128), BF16),
-        ],
-        compiler_params=pltpu.CompilerParams(vmem_limit_bytes=50 << 20),
+        ]
+        + more_scratch,
+        compiler_params=comm_params(1, 50)
+        if more
+        else pltpu.CompilerParams(vmem_limit_bytes=50 << 20),
         cost_estimate=busy(20),
         name="attend_backward",
-    )(starts, normed, *slab, out_rows, cosine, sine, heads, values, mixed, branch, rest)
+    )(starts, normed, *slab, out_rows, cosine, sine, heads, values, mixed, branch, rest, *more)
 
 
 def norm_factor(stream):
@@ -2068,22 +2114,19 @@
                 arrived, up_sum = arrived
                 expert_out[layer + 1] = (expert_out[layer + 1][0], up_sum, expert_out[layer + 1][2])
             arrived = [arrived]
+        outermost = layer + 1 == layers
         row_sums, gate_term, up_term, down_term, *added = experts_backward(
             normed_two, arrived, codes, probs_t, gate_w, up_w, down_w, gate_part, up_part,
-            slots, 4 * groups, total if layer + 1 == layers else None, planes,
+            slots, 4 * groups, total if outermost else None, planes, None, result,
         )
-        if added:
-            result = exchange((middle + added[0]).astype(BF16))
+        result = (middle + added[0]).astype(BF16) if outermost else added[0]
         if groups > 1:
             summed = scatter_group(row_sums, planes, 2)
             expert_out[layer] = sum_experts(gate_term, up_term, down_term)
+            beside = None
         else:
-            second = gate_term if layer > 0 else up_term
-            summed, down_sum, second = scatter_group(
-                row_sums, planes, 2, ((down_term, None), (second, None))
-            )
-            pending = (up_term, None) if layer > 0 else (gate_term, None)
-            expert_out[layer] = (second, None, down_sum) if layer > 0 else (None, second, down_sum)
+            summed, down_sum = scatter_group(row_sums, planes, 2, ((down_term, None),))
+            pending, beside = (up_term, None), (gate_term, None)
         weighted = summed[:, width : width + experts_all]
         weighted = weighted + summed[:, width + 64 : width + 64 + experts_all]
         logit_grad = weighted - own_probs * jnp.sum(weighted, axis=-1, keepdims=True)
@@ -2098,10 +2141,12 @@
         rest = jnp.pad(rest, ((0, 0), (0, 32 - experts_all - 1)))
         high = rest.astype(BF16)
         low_part = (rest - high.astype(F32)).astype(BF16)
-        partial, qkv_term, out_term = attention_backward(
+        partial, qkv_term, out_term, *sums = attention_backward(
             normed_one, slab, tall, starts, cosine, sine, heads_low, values, mixed, branch_low,
-            jnp.concatenate([high, low_part], axis=1),
+            jnp.concatenate([high, low_part], axis=1), beside,
         )
+        if beside is not None:
+            expert_out[layer] = (sums[0], None, down_sum)
         partial = partial.reshape(8, count, width)
         normed_one_grad = scatter_plane(partial)
         upstream = middle_grad + norm_back(stream, factor_one, attn_row, normed_one_grad)
@@ -2117,11 +2162,11 @@
         sums = collect(wide_terms, tall_terms, planes)
         input_grad = exchange(upstream.astype(BF16))
     else:
-        query_out, key_out, value_out, tall_out, rest, input_grad, gate_sum = collect(
+        query_out, key_out, value_out, tall_out, rest, input_grad, up_sum = collect(
             wide_terms, tall_terms, planes, (pending,),
             (query_weight, key_matrix, value_matrix), upstream.astype(BF16),
         )
-        expert_out[0] = (gate_sum, *expert_out[0][1:])
+        expert_out[0] = (expert_out[0][0], up_sum, expert_out[0][2])
         products = rest[..., 32]
     if groups > 1:
         sums = [

time: 936 us -> 911 us (0.973)
  Pallas kernels: 823 us -> 803 us
    pallas_call x3, Pallas kernels: 152 us -> 112 us  [scatter_group(): pl.pallas_call(kernel, out_shape=[jax.ShapeDtypeStruct((count, width), F3...]
    pallas_call x2, Pallas kernels: 45 us -> 73.4 us  [attention_backward(): pl.pallas_call(kernel, out_shape=[jax.ShapeDtypeStruct((length, width), B...]
    unnamed x196 -> x206, local copies, waits for them, and re-layouts: 61.9 us -> 59.5 us
  transfers between devices with their start and end apart: 1 -> 0, of which waited for: 0 -> 0; matrix products, arithmetic and copies ran while one was open for 2% -> 0% of each run, Pallas kernels for 38% -> 0%
where the time goes in v5:
time: 911 us; the launch traced here: 899 us
  Pallas kernels  803 us (88%)
  local copies, waits for them, and re-layouts  70.5 us (8%)
  other arithmetic  20.5 us (2%)
    pallas_call x3, Pallas kernels, scatter_group(): pl.pallas_call(kernel, out_shape=[jax.ShapeDtypeStruct((count, width), F3...  112 us
    pallas_call x3, Pallas kernels, gather_group(): pl.pallas_call(kernel, out_shape=[jax.ShapeDtypeStruct((2 * planes, count...  111 us
    pallas_call x4, Pallas kernels, scatter_plane_call(): pl.pallas_call(kernel, out_shape=[jax.ShapeDtypeStruct((count, width), F3...  108 us
    pallas_call x1, Pallas kernels, collect(): pl.pallas_call(kernel, out_shape=final_outs + plain_outs + more_outs, in_...  97.7 us
    pallas_call x1, Pallas kernels, enter(): pl.pallas_call(kernel, out_shape=[jax.ShapeDtypeStruct((8, count, width),...  78.9 us
    pallas_call x2, Pallas kernels, experts_backward(): pl.pallas_call(kernel, grid=(local,), out_shape=[jax.ShapeDtypeStruct((bl...  74.8 us
    pallas_call x2, Pallas kernels, attention_backward(): pl.pallas_call(kernel, out_shape=[jax.ShapeDtypeStruct((length, width), B...  73.4 us
    pallas_call x2, Pallas kernels, experts_forward(): pl.pallas_call(kernel, grid=(local,), out_shape=[jax.ShapeDtypeStruct(nor...  63.9 us

profile of v5, /device:TPU:9, one launch (start us, length us, event | category | flops | bytes accessed | tf_op | source)
XLA Modules:
  0.0 898.6 jit_solution(6851072468367257197)
XLA Ops:
  6.4 1.7 slice_bitcast_fusion
  8.7 1.7 copy-done.17
  13.2 78.9 %enter.1 = (bf16[8,128,1536]{2,1,0:T(8,128)(2,1)S(1)}, bf16[128,1536]{1,0:T(8,128)(2,1)S(1)}, bf16[4,48,1536]{2,1,0:T(8,128)(2,1)S(1)}, bf16[4,8,48,256]{3,2,1,0...) custom-call(bf16[128,1536]{1,0:T(8,128)(2,1)S(1)} %bitcast.88, ...), custom_call_target="tpu_custom_call" | custom-call | bytes 147600000 | tf_op jit(solution)/shard_map/enter/pallas_call | solution.py:1034
  92.1 1.6 copy-done.10
  100.4 1.9 copy-done.11
  104.5 10.5 %attend_forward.2 = (bf16[1024,1536]{1,0:T(8,128)(2,1)S(1)}, bf16[1024,256]{1,0:T(8,128)(2,1)S(1)}, bf16[1024,128]{1,0:T(8,128)(2,1)S(1)}, bf16[1024,256]{1,0:T(8,128)(2,1)S(1)}) custom-call(s32[1,4]{1,0:T(1,128)S(1)} %get-tuple-element.90.starts_ref, bf16[1024,1536]{1,0:T(8,128)(2,1)S(1)} %bitcast.64, bf16[1536,256]{1,0:T(8,128)(2,1)S(1)} %bitcast.71, ...), custom_call_target="tpu_custom_call" | custom-call | bytes 36900000 | tf_op jit(solution)/shard_map/attend_forward/pallas_call | solution.py:1755
  116.7 50.2 %scatter_plane_first.1 = (f32[128,1536]{1,0:T(8,128)S(1)}, bf16[4,3,384,512]{3,2,1,0:T(8,128)(2,1)S(1)}, bf16[4,48,1536]{2,1,0:T(8,128)(2,1)S(1)}, bf16[4,8,48,2...) custom-call(bf16[8,128,1536]{2,1,0:T(8,128)(2,1)S(1)} %bitcast.75, bf16[2,3,384,512]{3,2,1,0:T(8,128)(2,1)S(1)} %copy-done.19, ...), custom_call_target="tpu_custom_call" | custom-call | bytes 73800000 | tf_op jit(solution)/shard_map/scatter_plane_first/pallas_call | solution.py:714
  166.9 2.2 copy-done
  171.7 40.0 %gather_group.3 = (bf16[8,128,1536]{2,1,0:T(8,128)(2,1)S(1)}, bf16[4,3,512,384]{3,2,1,0:T(8,128)(2,1)S(1)}, bf16[8,128,128]{2,1,0:T(8,128)(2,1)S(1)}) custom-call(bf16[128,1536]{1,0:T(8,128)(2,1)S(1)} %multiply_convert_fusion.2.x_ref, bf16[2,3,512,384]{3,2,1,0:T(8,128)(2,1)S(1)} %copy-done.18, bf16[128,128]{1,0:T(8,128)(2,1)S(1)} %pad.12.refs_1_), custom_call_target="tpu_custom_call" | custom-call | bytes 121770000 | tf_op jit(solution)/shard_map/gather_group/pallas_call | solution.py:485
  211.7 2.2 copy-done.1
  213.9 1.6 copy-done.15
  216.3 36.7 %experts_forward.2 = (bf16[8,128,1536]{2,1,0:T(8,128)(2,1)}, f32[3,512,512]{2,1,0:T(8,128)}, f32[3,512,512]{2,1,0:T(8,128)}, f32[8,128,128]{2,1,0:T(8,128)}, f32...) custom-call(bf16[8,128,1536]{2,1,0:T(8,128)(2,1)} %copy-done.15, ...), custom_call_target="tpu_custom_call" | custom-call | bytes 59040000 | tf_op jit(solution)/shard_map/experts_forward/pallas_call | solution.py:1442
  253.0 1.9 copy-done.35
  254.9 36.5 %scatter_group.3 = (f32[128,1536]{1,0:T(8,128)S(1)}, bf16[4,3,384,512]{3,2,1,0:T(8,128)(2,1)S(1)}) custom-call(bf16[8,128,1536]{2,1,0:T(8,128)(2,1)S(1)} %copy-done.35, bf16[2,3,384,512]{3,2,1,0:T(8,128)(2,1)S(1)} %copy-done.19), custom_call_target="tpu_custom_call" | custom-call | bytes 118080000 | tf_op jit(solution)/shard_map/scatter_group/pallas_call | solution.py:532
  291.3 2.2 copy-done.2
  294.6 24.6 %gather_plane.3 = (bf16[8,128,1536]{2,1,0:T(8,128)(2,1)S(1)}, bf16[4,48,1536]{2,1,0:T(8,128)(2,1)S(1)}) custom-call(bf16[128,1536]{1,0:T(8,128)(2,1)S(1)} %multiply_convert_fusion.1.x_ref, bf16[4,48,1536]{2,1,0:T(8,128)(2,1)S(1)} %copy-done.55), custom_call_target="tpu_custom_call" | custom-call | bytes 73800000 | tf_op jit(solution)/shard_map/gather_plane/pallas_call | solution.py:593
  319.3 10.7 %attend_forward.3 = (bf16[1024,1536]{1,0:T(8,128)(2,1)S(1)}, bf16[1024,256]{1,0:T(8,128)(2,1)S(1)}, bf16[1024,128]{1,0:T(8,128)(2,1)S(1)}, bf16[1024,256]{1,0:T(8,128)(2,1)S(1)}) custom-call(s32[1,4]{1,0:T(1,128)S(1)} %get-tuple-element.90.starts_ref, bf16[1024,1536]{1,0:T(8,128)(2,1)S(1)} %bitcast.65, bf16[1536,256]{1,0:T(8,128)(2,1)S(1)} %bitcast.73, ...), custom_call_target="tpu_custom_call" | custom-call | bytes 36900000 | tf_op jit(solution)/shard_map/attend_forward/pallas_call | solution.py:1755
  330.0 18.7 %scatter_plane.3 = f32[128,1536]{1,0:T(8,128)S(1)} custom-call(bf16[8,128,1536]{2,1,0:T(8,128)(2,1)S(1)} %bitcast.78), custom_call_target="tpu_custom_call" | custom-call | bytes 73800000 | tf_op jit(solution)/shard_map/scatter_plane/pallas_call | solution.py:714
  349.1 37.0 %gather_group.4 = (bf16[8,128,1536]{2,1,0:T(8,128)(2,1)S(1)}, bf16[4,3,512,384]{3,2,1,0:T(8,128)(2,1)S(1)}) custom-call(bf16[128,1536]{1,0:T(8,128)(2,1)S(1)} %multiply_convert_fusion.x_ref, bf16[2,3,512,384]{3,2,1,0:T(8,128)(2,1)S(1)} %copy-done.18), custom_call_target="tpu_custom_call" | custom-call | bytes 121770000 | tf_op jit(solution)/shard_map/gather_group/pallas_call | solution.py:485
  386.1 2.1 copy-done.3
  388.2 1.6 copy-done.16
  389.8 27.2 %experts_forward.3 = (bf16[8,128,1536]{2,1,0:T(8,128)(2,1)}, f32[3,512,512]{2,1,0:T(8,128)}, f32[3,512,512]{2,1,0:T(8,128)}, f32[8,128,128]{2,1,0:T(8,128)}, f32...) custom-call(bf16[8,128,1536]{2,1,0:T(8,128)(2,1)} %copy-done.16, bf16[8,128,128]{2,1,0:T(8,128)(2,1)} %copy-done.22, ...), custom_call_target="tpu_custom_call" | custom-call | bytes 59040000 | tf_op jit(solution)/shard_map/experts_forward/pallas_call | solution.py:1442
  417.9 41.9 %experts_backward.2 = (bf16[8,128,1664]{2,1,0:T(8,128)(2,1)}, bf16[4,3,384,512]{3,2,1,0:T(8,128)(2,1)}, bf16[4,3,384,512]{3,2,1,0:T(8,128)(2,1)}, bf16[4,3,512,384]{3,2,1,0:T(8,128)(2,1)}, f32[128,1536]{1,0:T(8,128)}) custom-call(bf16[8,128,1536]{2,1,0:T(8,128)(2,1)} %copy-done.16, bf16[8,128,128]{2,1,0:T(8,128)(2,1)} %copy-done.22, ...), custom_call_target="tpu_custom_call" | custom-call | bytes 110700000 | tf_op jit(solution)/shard_map/experts_backward/pallas_call | solution.py:1626
  459.8 2.3 copy-done.20
  462.2 2.0 copy-done.25
  464.1 37.2 %scatter_group.4 = (f32[128,1664]{1,0:T(8,128)S(1)}, bf16[3,512,384]{2,1,0:T(8,128)(2,1)S(1)}) custom-call(bf16[8,128,1664]{2,1,0:T(8,128)(2,1)S(1)} %copy-done.25, bf16[4,3,512,384]{3,2,1,0:T(8,128)(2,1)S(1)} %copy-done.20), custom_call_target="tpu_custom_call" | custom-call | bytes 118080000 | tf_op jit(solution)/shard_map/scatter_group/pallas_call | solution.py:532
  505.1 19.1 %gather_plane.4 = bf16[8,128,1536]{2,1,0:T(8,128)(2,1)S(1)} custom-call(bf16[128,1536]{1,0:T(8,128)(2,1)S(1)} %get-tuple-element.242.x_ref), custom_call_target="tpu_custom_call" | custom-call | bytes 73800000 | tf_op jit(solution)/shard_map/gather_plane/pallas_call | solution.py:593
  524.3 1.7 copy-done.14
  526.0 36.9 %attend_backward.2 = (bf16[1024,1536]{1,0:T(8,128)(2,1)}, bf16[1536,384]{1,0:T(8,128)(2,1)}, bf16[192,1536]{1,0:T(8,128)(2,1)S(1)}, bf16[3,384,512]{2,1,0:T(8,128)(2,1)}) custom-call(s32[1,4]{1,0:T(1,128)S(1)} %copy-done.76, bf16[1024,1536]{1,0:T(8,128)(2,1)} %bitcast.66, bf16[1536,256]{1,0:T(8,128)(2,1)S(1)} %bitcast.74, bf16[1536,128]{1,0:T(8,128)(2,1)S(1)} %bitcast.62, ...), custom_call_target="tpu_custom_call" | custom-call | bytes 73800000 | tf_op jit(solution)/shard_map/attend_backward/pallas_call | solution.py:1862
  562.9 2.1 copy-done.34
  565.0 19.8 %scatter_plane.4 = f32[128,1536]{1,0:T(8,128)S(1)} custom-call(bf16[8,128,1536]{2,1,0:T(8,128)(2,1)S(1)} %bitcast.77), custom_call_target="tpu_custom_call" | custom-call | bytes 73800000 | tf_op jit(solution)/shard_map/scatter_plane/pallas_call | solution.py:714
  586.1 33.7 %gather_group.5 = (bf16[8,128,1536]{2,1,0:T(8,128)(2,1)S(1)}, bf16[3,384,512]{2,1,0:T(8,128)(2,1)S(1)}) custom-call(bf16[128,1536]{1,0:T(8,128)(2,1)S(1)} %get-tuple-element.240.x_ref, bf16[4,3,384,512]{3,2,1,0:T(8,128)(2,1)S(1)} %bitcast.70), custom_call_target="tpu_custom_call" | custom-call | bytes 121770000 | tf_op jit(solution)/shard_map/gather_group/pallas_call | solution.py:485
  619.8 1.7 copy-done.36
  622.5 32.9 %experts_backward.3 = (bf16[8,128,1664]{2,1,0:T(8,128)(2,1)}, bf16[4,3,384,512]{3,2,1,0:T(8,128)(2,1)}, bf16[4,3,384,512]{3,2,1,0:T(8,128)(2,1)}, bf16[4,3,512,384]{3,2,1,0:T(8,128)(2,1)}, bf16[128,1536]{1,0:T(8,128)(2,1)}) custom-call(bf16[8,128,1536]{2,1,0:T(8,128)(2,1)} %copy-done.15, bf16[8,128,128]{2,1,0:T(8,128)(2,1)} %copy-done.22, ...), custom_call_target="tpu_custom_call" | custom-call | bytes 110700000 | tf_op jit(solution)/shard_map/experts_backward/pallas_call | solution.py:1626
  655.4 2.3 copy-done.21
  657.7 2.0 copy-done.26
  659.7 38.3 %scatter_group.5 = (f32[128,1664]{1,0:T(8,128)S(1)}, bf16[3,512,384]{2,1,0:T(8,128)(2,1)S(1)}) custom-call(bf16[8,128,1664]{2,1,0:T(8,128)(2,1)S(1)} %copy-done.26, bf16[4,3,512,384]{3,2,1,0:T(8,128)(2,1)S(1)} %copy-done.21), custom_call_target="tpu_custom_call" | custom-call | bytes 118080000 | tf_op jit(solution)/shard_map/scatter_group/pallas_call | solution.py:532
  702.4 2.5 maximum_convert_fusion.2
  704.9 18.4 %gather_plane.5 = bf16[8,128,1536]{2,1,0:T(8,128)(2,1)S(1)} custom-call(bf16[128,1536]{1,0:T(8,128)(2,1)S(1)} %get-tuple-element.238.x_ref), custom_call_target="tpu_custom_call" | custom-call | bytes 73800000 | tf_op jit(solution)/shard_map/gather_plane/pallas_call | solution.py:593
  723.3 1.7 copy-done.13
  725.0 36.5 %attend_backward.3 = (bf16[1024,1536]{1,0:T(8,128)(2,1)}, bf16[1536,384]{1,0:T(8,128)(2,1)}, bf16[192,1536]{1,0:T(8,128)(2,1)S(1)}, bf16[3,384,512]{2,1,0:T(8,128)(2,1)}) custom-call(s32[1,4]{1,0:T(1,128)S(1)} %copy-done.76, bf16[1024,1536]{1,0:T(8,128)(2,1)} %bitcast.63, bf16[1536,256]{1,0:T(8,128)(2,1)S(1)} %bitcast.72, bf16[1536,128]{1,0:T(8,128)(2,1)S(1)} %bitcast.57, ...), custom_call_target="tpu_custom_call" | custom-call | bytes 73800000 | tf_op jit(solution)/shard_map/attend_backward/pallas_call | solution.py:1862
  761.6 2.1 copy-done.33
  763.7 19.7 %scatter_plane.5 = f32[128,1536]{1,0:T(8,128)S(1)} custom-call(bf16[8,128,1536]{2,1,0:T(8,128)(2,1)S(1)} %bitcast.76), custom_call_target="tpu_custom_call" | custom-call | bytes 73800000 | tf_op jit(solution)/shard_map/scatter_plane/pallas_call | solution.py:714
  784.7 97.7 %collect.1 = (f32[2,48,1536]{2,1,0:T(8,128)}, f32[2,48,512]{2,1,0:T(8,128)}, f32[2,48,512]{2,1,0:T(8,128)}, f32[2,48,1536]{2,1,0:T(8,128)}, f32[2,48,128]{2,1,0:...) custom-call(bf16[4,8,48,384]{3,2,1,0:T(8,128)(2,1)} %bitcast.93, bf16[4,8,48,384]{3,2,1,0:T(8,128)(2,1)} %bitcast.92, ...), custom_call_target="tpu_custom_call" | custom-call | bytes 147600000 | tf_op jit(solution)/shard_map/collect/pallas_call | solution.py:1274
  882.4 1.6 slice_reduce_fusion
  886.0 2.0 bitcast_convert_fusion
  888.0 3.9 maximum_convert_fusion.1
  892.0 2.5 maximum_convert_fusion
  (250 shorter events, 42.7 us)
Async XLA Ops:
  0.7 8.0 copy-start.77
  13.2 87.2 %copy-start.4 = (f32[1024,256]{1,0:T(8,128)S(1)}, f32[1024,256]{1,0:T(8,128)}, u32[]{:S(2)}) copy-start(f32[1024,256]{1,0:T(8,128)} %constant.48.clone.s_ref) | copy-start | bytes 3145732
  13.2 87.2 %copy-start.5 = (f32[1024,256]{1,0:T(8,128)S(1)}, f32[1024,256]{1,0:T(8,128)}, u32[]{:S(2)}) copy-start(f32[1024,256]{1,0:T(8,128)} %constant.47.clone.c_ref) | copy-start | bytes 3145732
  97.4 17.7 %copy-start.6 = (bf16[4,8,48,128]{3,2,1,0:T(8,128)(2,1)}, bf16[4,8,48,128]{3,2,1,0:T(8,128)(2,1)S(1)}, u32[]{:S(2)}) copy-start(bf16[4,8,48,128]{3,2,1,0:T(8,128)(2,1)S(1)} %get-tuple-element.93) | copy-start | bytes 1179652
  97.4 17.7 %copy-start.42 = (bf16[128,1536]{1,0:T(8,128)(2,1)}, bf16[128,1536]{1,0:T(8,128)(2,1)S(1)}, u32[]{:S(2)}) copy-start(bf16[128,1536]{1,0:T(8,128)(2,1)S(1)} %get-tuple-element.105) | copy-start | bytes 1179652
  97.4 221.9 %copy-start.75 = (s32[1,4]{1,0:T(1,128)}, s32[1,4]{1,0:T(1,128)S(1)}, u32[]{:S(2)}) copy-start(s32[1,4]{1,0:T(1,128)S(1)} %get-tuple-element.90.starts_ref) | copy-start | bytes 52
  104.5 12.2 %copy-start.19 = (bf16[2,3,384,512]{3,2,1,0:T(8,128)(2,1)S(1)}, bf16[2,3,384,512]{3,2,1,0:T(8,128)(2,1)}, u32[]{:S(2)}) copy-start(bf16[2,3,384,512]{3,2,1,0:T(8,128)(2,1)} %refs_0_.8) | copy-start | bytes 7077892
  104.5 12.2 %copy-start.52 = (bf16[48,1536]{1,0:T(8,128)(2,1)S(1)}, bf16[48,1536]{1,0:T(8,128)(2,1)}, u32[]{:S(2)}) copy-start(bf16[48,1536]{1,0:T(8,128)(2,1)} %get-tuple-element.253.refs_1_) | copy-start | bytes 442372
  104.5 12.2 %copy-start.71 = (bf16[8,48,256]{2,1,0:T(8,128)(2,1)S(1)}, bf16[8,48,256]{2,1,0:T(8,128)(2,1)}, u32[]{:S(2)}) copy-start(bf16[8,48,256]{2,1,0:T(8,128)(2,1)} %copy-done.70) | copy-start | bytes 589828
  104.5 12.2 %copy-start.73 = (bf16[8,48,128]{2,1,0:T(8,128)(2,1)S(1)}, bf16[8,48,128]{2,1,0:T(8,128)(2,1)}, u32[]{:S(2)}) copy-start(bf16[8,48,128]{2,1,0:T(8,128)(2,1)} %copy-done.72) | copy-start | bytes 294916
  116.7 52.6 %copy-start.66 = (bf16[1024,128]{1,0:T(8,128)(2,1)}, bf16[1024,128]{1,0:T(8,128)(2,1)S(1)}, u32[]{:S(2)}) copy-start(bf16[1024,128]{1,0:T(8,128)(2,1)S(1)} %get-tuple-element.141.v_ref) | copy-start | bytes 786436
  169.1 42.6 %copy-start.54 = (bf16[4,48,1536]{2,1,0:T(8,128)(2,1)}, bf16[4,48,1536]{2,1,0:T(8,128)(2,1)S(1)}, u32[]{:S(2)}) copy-start(bf16[4,48,1536]{2,1,0:T(8,128)(2,1)S(1)} %get-tuple-element.112.refs_0_) | copy-start | bytes 1769476
  169.1 150.1 %copy-start.8 = (bf16[4,8,48,128]{3,2,1,0:T(8,128)(2,1)}, bf16[4,8,48,128]{3,2,1,0:T(8,128)(2,1)S(1)}, u32[]{:S(2)}) copy-start(bf16[4,8,48,128]{3,2,1,0:T(8,128)(2,1)S(1)} %get-tuple-element.111) | copy-start | bytes 1179652
  169.3 46.9 %copy-start.80 = (f32[128,1536]{1,0:T(8,128)}, f32[128,1536]{1,0:T(8,128)S(1)}, u32[]{:S(2)}) copy-start(f32[128,1536]{1,0:T(8,128)S(1)} %get-tuple-element.249) | copy-start | bytes 2359300
  171.7 40.0 %copy-start.23 = (bf16[128,1536]{1,0:T(8,128)(2,1)}, bf16[128,1536]{1,0:T(8,128)(2,1)S(1)}, u32[]{:S(2)}) copy-start(bf16[128,1536]{1,0:T(8,128)(2,1)S(1)} %multiply_convert_fusion.2.x_ref) | copy-start | bytes 1179652
  254.9 38.7 %copy-start.81 = (f32[128,1536]{1,0:T(8,128)S(1)}, f32[128,1536]{1,0:T(8,128)}, u32[]{:S(2)}) copy-start(f32[128,1536]{1,0:T(8,128)} %copy-done.80) | copy-start | bytes 2359300
  293.5 25.7 %copy-start.31 = (bf16[4,8,48,256]{3,2,1,0:T(8,128)(2,1)S(1)}, bf16[4,8,48,256]{3,2,1,0:T(8,128)(2,1)}, u32[]{:S(2)}) copy-start(bf16[4,8,48,256]{3,2,1,0:T(8,128)(2,1)} %copy-done.30) | copy-start | bytes 2359300
  293.7 55.0 %copy-start.78 = (f32[128,1536]{1,0:T(8,128)}, f32[128,1536]{1,0:T(8,128)S(1)}, u32[]{:S(2)}) copy-start(f32[128,1536]{1,0:T(8,128)S(1)} %get-tuple-element.247) | copy-start | bytes 2359300
  319.2 10.8 %copy-start.12 = (bf16[8,128,1536]{2,1,0:T(8,128)(2,1)}, bf16[8,128,1536]{2,1,0:T(8,128)(2,1)S(1)}, u32[]{:S(2)}) copy-start(bf16[8,128,1536]{2,1,0:T(8,128)(2,1)S(1)} %get-tuple-element.113) | copy-start | bytes 9437188
  319.2 10.8 %copy-start.40 = (bf16[4,48,1536]{2,1,0:T(8,128)(2,1)}, bf16[4,48,1536]{2,1,0:T(8,128)(2,1)S(1)}, u32[]{:S(2)}) copy-start(bf16[4,48,1536]{2,1,0:T(8,128)(2,1)S(1)} %get-tuple-element.115) | copy-start | bytes 1769476
  330.0 18.9 %copy-start.60 = (bf16[1024,256]{1,0:T(8,128)(2,1)}, bf16[1024,256]{1,0:T(8,128)(2,1)S(1)}, u32[]{:S(2)}) copy-start(bf16[1024,256]{1,0:T(8,128)(2,1)S(1)} %get-tuple-element.131.h_ref) | copy-start | bytes 1572868
  330.0 18.9 %copy-start.62 = (bf16[1024,256]{1,0:T(8,128)(2,1)}, bf16[1024,256]{1,0:T(8,128)(2,1)S(1)}, u32[]{:S(2)}) copy-start(bf16[1024,256]{1,0:T(8,128)(2,1)S(1)} %get-tuple-element.133.m_ref) | copy-start | bytes 1572868
  330.0 18.9 %copy-start.68 = (bf16[1024,128]{1,0:T(8,128)(2,1)}, bf16[1024,128]{1,0:T(8,128)(2,1)S(1)}, u32[]{:S(2)}) copy-start(bf16[1024,128]{1,0:T(8,128)(2,1)S(1)} %get-tuple-element.132.v_ref) | copy-start | bytes 786436
  464.1 37.8 %copy-start.9 = (bf16[4,8,48,128]{3,2,1,0:T(8,128)(2,1)S(1)}, bf16[4,8,48,128]{3,2,1,0:T(8,128)(2,1)}, u32[]{:S(2)}) copy-start(bf16[4,8,48,128]{3,2,1,0:T(8,128)(2,1)} %copy-done.8) | copy-start | bytes 1179652
  504.8 21.1 %copy-start.32 = (bf16[4,8,48,256]{3,2,1,0:T(8,128)(2,1)S(1)}, bf16[4,8,48,256]{3,2,1,0:T(8,128)(2,1)}, u32[]{:S(2)}) copy-start(bf16[4,8,48,256]{3,2,1,0:T(8,128)(2,1)} %copy-done.30) | copy-start | bytes 2359300
  504.8 21.1 %copy-start.41 = (bf16[4,48,1536]{2,1,0:T(8,128)(2,1)S(1)}, bf16[4,48,1536]{2,1,0:T(8,128)(2,1)}, u32[]{:S(2)}) copy-start(bf16[4,48,1536]{2,1,0:T(8,128)(2,1)} %copy-done.40) | copy-start | bytes 1769476
  504.8 21.1 %copy-start.61 = (bf16[1024,256]{1,0:T(8,128)(2,1)S(1)}, bf16[1024,256]{1,0:T(8,128)(2,1)}, u32[]{:S(2)}) copy-start(bf16[1024,256]{1,0:T(8,128)(2,1)} %copy-done.60) | copy-start | bytes 1572868
  504.8 21.1 %copy-start.63 = (bf16[1024,256]{1,0:T(8,128)(2,1)S(1)}, bf16[1024,256]{1,0:T(8,128)(2,1)}, u32[]{:S(2)}) copy-start(bf16[1024,256]{1,0:T(8,128)(2,1)} %copy-done.62) | copy-start | bytes 1572868
  504.8 21.1 %copy-start.69 = (bf16[1024,128]{1,0:T(8,128)(2,1)S(1)}, bf16[1024,128]{1,0:T(8,128)(2,1)}, u32[]{:S(2)}) copy-start(bf16[1024,128]{1,0:T(8,128)(2,1)} %copy-done.68) | copy-start | bytes 786436
  504.8 21.1 %copy-start.76 = (s32[1,4]{1,0:T(1,128)S(1)}, s32[1,4]{1,0:T(1,128)}, u32[]{:S(2)}) copy-start(s32[1,4]{1,0:T(1,128)} %copy-done.75) | copy-start | bytes 52
  505.1 81.0 %slice-start = ((s8[4718592]{0:T(1024)(128)(4,1)}), s8[4194304]{0:T(1024)(128)(4,1)S(1)}, s32[]{:S(2)}) async-start(s8[4718592]{0:T(1024)(128)(4,1)} %bitcast.69), calls=%async_computation | async-start | bytes 8388608
  525.9 58.8 %copy-start.79 = (f32[128,1536]{1,0:T(8,128)S(1)}, f32[128,1536]{1,0:T(8,128)}, u32[]{:S(2)}) copy-start(f32[128,1536]{1,0:T(8,128)} %copy-done.78) | copy-start | bytes 2359300
  526.0 59.0 %copy-start.83 = (f32[128,1536]{1,0:T(8,128)S(1)}, f32[128,1536]{1,0:T(8,128)}, u32[]{:S(2)}) copy-start(f32[128,1536]{1,0:T(8,128)} %get-tuple-element.243) | copy-start | bytes 2359300
  526.0 60.1 %slice-start.1 = ((s8[4718592]{0:T(1024)(128)(4,1)}), s8[524288]{0:T(1024)(128)(4,1)S(1)}, s32[]{:S(2)}) async-start(s8[4718592]{0:T(1024)(128)(4,1)} %bitcast.69), calls=%async_computation.1 | async-start | bytes 1048576
  562.8 23.3 %copy-start.50 = (bf16[192,1536]{1,0:T(8,128)(2,1)}, bf16[192,1536]{1,0:T(8,128)(2,1)S(1)}, u32[]{:S(2)}) copy-start(bf16[192,1536]{1,0:T(8,128)(2,1)S(1)} %get-tuple-element.151) | copy-start | bytes 1769476
  659.7 38.6 %copy-start.24 = (bf16[128,1536]{1,0:T(8,128)(2,1)S(1)}, bf16[128,1536]{1,0:T(8,128)(2,1)}, u32[]{:S(2)}) copy-start(bf16[128,1536]{1,0:T(8,128)(2,1)} %copy-done.23) | copy-start | bytes 1179652
  659.7 39.0 %copy-start.7 = (bf16[4,8,48,128]{3,2,1,0:T(8,128)(2,1)S(1)}, bf16[4,8,48,128]{3,2,1,0:T(8,128)(2,1)}, u32[]{:S(2)}) copy-start(bf16[4,8,48,128]{3,2,1,0:T(8,128)(2,1)} %copy-done.6) | copy-start | bytes 1179652
  659.7 39.0 %copy-start.82 = (f32[128,1536]{1,0:T(8,128)S(1)}, f32[128,1536]{1,0:T(8,128)}, u32[]{:S(2)}) copy-start(f32[128,1536]{1,0:T(8,128)} %copy-done.80) | copy-start | bytes 2359300
  704.9 20.1 %copy-start.29 = (bf16[4,8,48,256]{3,2,1,0:T(8,128)(2,1)S(1)}, bf16[4,8,48,256]{3,2,1,0:T(8,128)(2,1)}, u32[]{:S(2)}) copy-start(bf16[4,8,48,256]{3,2,1,0:T(8,128)(2,1)} %copy-done.27) | copy-start | bytes 2359300
  704.9 20.1 %copy-start.39 = (bf16[4,48,1536]{2,1,0:T(8,128)(2,1)S(1)}, bf16[4,48,1536]{2,1,0:T(8,128)(2,1)}, u32[]{:S(2)}) copy-start(bf16[4,48,1536]{2,1,0:T(8,128)(2,1)} %copy-done.37) | copy-start | bytes 1769476
  704.9 20.1 %copy-start.57 = (bf16[1024,256]{1,0:T(8,128)(2,1)S(1)}, bf16[1024,256]{1,0:T(8,128)(2,1)}, u32[]{:S(2)}) copy-start(bf16[1024,256]{1,0:T(8,128)(2,1)} %copy-done.56) | copy-start | bytes 1572868
  704.9 20.1 %copy-start.59 = (bf16[1024,256]{1,0:T(8,128)(2,1)S(1)}, bf16[1024,256]{1,0:T(8,128)(2,1)}, u32[]{:S(2)}) copy-start(bf16[1024,256]{1,0:T(8,128)(2,1)} %copy-done.58) | copy-start | bytes 1572868
  704.9 20.1 %copy-start.67 = (bf16[1024,128]{1,0:T(8,128)(2,1)S(1)}, bf16[1024,128]{1,0:T(8,128)(2,1)}, u32[]{:S(2)}) copy-start(bf16[1024,128]{1,0:T(8,128)(2,1)} %copy-done.66) | copy-start | bytes 786436
  725.0 58.6 %copy-start.85 = (f32[128,1536]{1,0:T(8,128)S(1)}, f32[128,1536]{1,0:T(8,128)}, u32[]{:S(2)}) copy-start(f32[128,1536]{1,0:T(8,128)} %get-tuple-element.239) | copy-start | bytes 2359300
  761.5 22.1 %copy-start.51 = (bf16[192,1536]{1,0:T(8,128)(2,1)}, bf16[192,1536]{1,0:T(8,128)(2,1)S(1)}, u32[]{:S(2)}) copy-start(bf16[192,1536]{1,0:T(8,128)(2,1)S(1)} %get-tuple-element.150) | copy-start | bytes 1769476
  761.5 21.8 %copy-start.95 = (f32[1536]{0:T(1024)S(1)}, f32[1536]{0:T(1024)}, u32[]{:S(2)}) copy-start(f32[1536]{0:T(1024)} %get-tuple-element.232) | copy-start | bytes 18436
  784.7 99.3 %copy-start.96 = (bf16[2,48]{1,0:T(2,128)(2,1)S(1)}, bf16[2,48]{1,0:T(2,128)(2,1)}, u32[]{:S(2)}) copy-start(bf16[2,48]{1,0:T(2,128)(2,1)} %param.20) | copy-start | bytes 580
  784.7 103.3 %copy-start.47 = (bf16[3,384,512]{2,1,0:T(8,128)(2,1)S(1)}, bf16[3,384,512]{2,1,0:T(8,128)(2,1)}, u32[]{:S(2)}) copy-start(bf16[3,384,512]{2,1,0:T(8,128)(2,1)} %copy-done.46) | copy-start | bytes 3538948
  (51 other events, 100.6 us)
